TPU v7x, 32 devices: a whole 2x2x4 slice. The times are simulated.
32 devices in a mesh: pipe: 2 (over core), batch: 4 (over y, x), space: 4 (over z).
Axes of the slice: x: 2, y: 2, z: 4, core: 2. Of those that a mesh axis runs over, the one named last changes fastest.
Arguments:
- images: bfloat16 [64, 8, 64, 256], P('batch', 'space'), may hold values from -6 to 6
- image_counts: int32 [4, 4], P('batch'), may hold values from 1 to 4, as said below
- labels: int32 [64, 40], P('batch'), may hold values 0 or 1
- fw_picks: int32 [20], replicated, may hold values from 0 to 39
- conv_down: bfloat16 [3, 3, 256, 512], replicated, may hold values from -0.125 to 0.125
- conv_mid: bfloat16 [3, 3, 512, 512], replicated, may hold values from -0.09375 to 0.09375
- shortcut: bfloat16 [256, 512], replicated, may hold values from -0.375 to 0.375
- gains_down: float32 [3, 512], replicated, may hold values from 0.5 to 1.5
- biases_down: float32 [3, 512], replicated, may hold values from -3 to 3
- conv_first: bfloat16 [3, 3, 512, 512], replicated, may hold values from -0.09375 to 0.09375
- conv_second: bfloat16 [3, 3, 512, 512], replicated, may hold values from -0.09375 to 0.09375
- gains_plain: float32 [2, 512], replicated, may hold values from 0.5 to 1.5
- biases_plain: float32 [2, 512], replicated, may hold values from -3 to 3
- head_weight: float32 [512, 40], replicated, may hold values from -0.25 to 0.25
- head_bias: float32 [40], replicated, may hold values from -3 to 3
Outputs:
- pooled: float32 [64, 512], P('batch', 'pipe')
- images_grad: float32 [64, 8, 64, 256], P('batch', 'space', None, 'pipe')
- conv_down_grad: float32 [3, 3, 256, 512], P(None, None, None, 'pipe')
- conv_mid_grad: float32 [3, 3, 512, 512], P(None, None, None, 'pipe')
- shortcut_grad: float32 [256, 512], P(None, 'pipe')
- gains_down_grad: float32 [3, 512], P(None, 'pipe')
- biases_down_grad: float32 [3, 512], P(None, 'pipe')
- conv_first_grad: float32 [3, 3, 512, 512], P(None, None, None, 'pipe')
- conv_second_grad: float32 [3, 3, 512, 512], P(None, None, None, 'pipe')
- gains_plain_grad: float32 [2, 512], P(None, 'pipe')
- biases_plain_grad: float32 [2, 512], P(None, 'pipe')
- head_weight_grad: float32 [512, 40], P('pipe')
- head_bias_grad: float32 [40], P('pipe')
Inputs may be any that keep to these rules, and one draw needn't show every extreme that they name: Within each batch index and micro-batch the first image_counts slots are live; some batch index fills all 4 slots of some micro-batch.
All inputs are finite; a program needn't handle non-finite values. No bound on the sum of `labels` on one device may be relied on, other than what follows from the above.
Results may differ from a plain program's by a relative error of at most 0.013.
Values may be sent and summed in bfloat16 or wider, within the bound.
No kernel may reach another device: no remote copies, remote signals or barrier semaphores. Data moves between devices by JAX's collectives and lax.ppermute only.
A program may use at most 448 MiB of HBM per device.

v0:
```python
import jax
import jax.numpy as jnp
from jax import lax
from jax.sharding import PartitionSpec as P

EPSILON = 1e-05
NUMBERS = ("NHWC", "HWIO", "NHWC")
HIGHEST = lax.Precision.HIGHEST


def shortened(x):

    def short(part):
        return part.astype(jnp.bfloat16) if part.dtype == jnp.float32 else part

    return jax.tree.map(short, x)


def extended_2(cells, sides, width):
    for axis, dim in sides:
        count = lax.axis_size(axis)
        ends = count - 1
        head = lax.slice_in_dim(cells, 0, width, axis=dim)
        tail = lax.slice_in_dim(cells, cells.shape[dim] - width, cells.shape[dim], axis=dim)
        cells = jnp.concatenate(
            [
                lax.ppermute(tail, axis, [(i, (i + 1) % count) for i in range(ends)]),
                cells,
                lax.ppermute(head, axis, [((i + 1) % count, i) for i in range(ends)]),
            ],
            axis=dim,
        )
    return cells


def shifted(block, axis, distance):
    devices = range(lax.axis_size(axis))
    route = [(i - distance, i) for i in devices if i - distance in devices]
    return lax.ppermute(block, axis, route)


def silu_slope(values):
    sigmoid = jax.nn.sigmoid(values)
    return sigmoid * (1.0 + values * (1.0 - sigmoid))


def select_by(flag, first, second):
    return jax.tree.map(lambda left, right: jnp.where(flag, left, right), first, second)


def pad_columns(tensor, pad_before, pad_after):
    return jnp.pad(tensor, ((0, 0), (0, 0), (pad_before, pad_after), (0, 0)))


def with_rims(tensor):
    rimmed = extended_2(shortened(tensor), (("space", 1),), 1).astype(tensor.dtype)
    return pad_columns(rimmed, 1, 1)


def conv_valid(extended, kernel, stride):
    return lax.conv_general_dilated(
        extended,
        kernel,
        (stride, stride),
        "VALID",
        dimension_numbers=NUMBERS,
        preferred_element_type=jnp.float32,
    )


def flipped(kernel):
    return jnp.swapaxes(kernel[::-1, ::-1], 2, 3)


def conv_back(grad_low, kernel):
    return conv_valid(with_rims(grad_low), flipped(kernel), 1)


def kernel_grad(extended, grad_low, stride):
    out_rows = grad_low.shape[1]
    out_cols = grad_low.shape[2]
    tap_rows = []
    for row_tap in range(3):
        tap_line = []
        for col_tap in range(3):
            window = lax.slice(
                extended,
                (0, row_tap, col_tap, 0),
                (
                    extended.shape[0],
                    row_tap + stride * (out_rows - 1) + 1,
                    col_tap + stride * (out_cols - 1) + 1,
                    extended.shape[3],
                ),
                (1, stride, stride, 1),
            )
            tap_line.append(
                jnp.einsum("nhwi,nhwo->io", window, grad_low, preferred_element_type=jnp.float32)
            )
        tap_rows.append(jnp.stack(tap_line))
    return jnp.stack(tap_rows)


def down_extend(images_mb):
    from_above = shifted(images_mb[:, -1:], "space", 1)
    return pad_columns(jnp.concatenate([from_above, images_mb], axis=1), 1, 0)


def down_input_grad(grad_low, kernel):
    spread = lax.conv_general_dilated(
        grad_low,
        flipped(kernel),
        (1, 1),
        ((2, 2), (2, 2)),
        lhs_dilation=(2, 2),
        dimension_numbers=NUMBERS,
        preferred_element_type=jnp.float32,
    )
    from_below = shifted(spread[:, :1, 1:].astype(jnp.bfloat16), "space", -1).astype(jnp.float32)
    interior = spread[:, 1:, 1:]
    return interior.at[:, -1:].add(from_below)


def norm_stats(conv_outs, living):
    weight = living[:, None, None, None]
    pixels = conv_outs[0].shape[1] * conv_outs[0].shape[2]
    counted_here = jnp.sum(living) * pixels
    firsts = jnp.stack([jnp.sum(conv_out * weight, axis=(0, 1, 2)) for conv_out in conv_outs])
    totals, counted = lax.psum((firsts, counted_here), ("batch", "space"))
    average = totals / counted
    deviations = jnp.stack(
        [
            jnp.sum((conv_out - average[position]) ** 2 * weight, axis=(0, 1, 2))
            for position, conv_out in enumerate(conv_outs)
        ]
    )
    variance = lax.psum(deviations, ("batch", "space")) / counted
    inverse = lax.rsqrt(variance + EPSILON)
    normed = [
        (conv_out - average[position]) * inverse[position]
        for position, conv_out in enumerate(conv_outs)
    ]
    return (normed, inverse, counted)


def norm_back(upstreams, normed_list, inverse, gains, counted, living):
    weight = living[:, None, None, None]
    grad_sums = jnp.stack([jnp.sum(upstream * weight, axis=(0, 1, 2)) for upstream in upstreams])
    cross_sums = jnp.stack(
        [
            jnp.sum(upstream * normed * weight, axis=(0, 1, 2))
            for upstream, normed in zip(upstreams, normed_list)
        ]
    )
    grad_total, cross_total = lax.psum((grad_sums, cross_sums), ("batch", "space"))
    results = []
    for position in range(len(upstreams)):
        correction = weight * (
            grad_total[position] / counted
            + normed_list[position] * (cross_total[position] / counted)
        )
        results.append(gains[position] * inverse[position] * (upstreams[position] - correction))
    return (results, cross_sums, grad_sums)


def frank_wolfe(gram, picks):
    tasks = gram.shape[0]
    labels_index = jnp.arange(tasks, dtype=jnp.int32)

    def advance(step_index, weights):
        chosen = picks[step_index]
        pulled = jnp.dot(gram, weights, precision=HIGHEST)
        energy = jnp.dot(weights, pulled, precision=HIGHEST)
        onehot = (labels_index == chosen).astype(jnp.float32)
        toward = jnp.sum(pulled * onehot)
        corner = jnp.sum(jnp.diagonal(gram) * onehot)
        denom = jnp.maximum(energy - 2.0 * toward + corner, 0.05 * corner)
        ratio = jnp.clip((energy - toward) / denom, 0.0, 1.0)
        return (1.0 - ratio) * weights + ratio * onehot

    return lax.fori_loop(0, picks.shape[0], advance, jnp.full((tasks,), 1.0 / tasks, jnp.float32))


def down_forward(images_mb, living, conv_down, conv_mid, shortcut, gains_down, biases_down):
    extended = down_extend(images_mb)
    first_out = conv_valid(extended, conv_down, 2)
    first_norm, first_inv, counted = norm_stats([first_out], living)
    first_pre = first_norm[0] * gains_down[0] + biases_down[0]
    first_act = jax.nn.silu(first_pre).astype(jnp.bfloat16)
    mid_ext = with_rims(first_act)
    mid_out = conv_valid(mid_ext, conv_mid, 1)
    short_in = images_mb[:, ::2, ::2]
    short_out = jnp.einsum("nhwi,io->nhwo", short_in, shortcut, preferred_element_type=jnp.float32)
    pair_norm, pair_inv, counted = norm_stats([mid_out, short_out], living)
    joined = (
        pair_norm[0] * gains_down[1]
        + biases_down[1]
        + pair_norm[1] * gains_down[2]
        + biases_down[2]
    )
    return dict(
        extended=extended,
        first_pre=first_pre,
        first_norm=first_norm,
        first_inv=first_inv,
        mid_ext=mid_ext,
        short_in=short_in,
        pair_norm=pair_norm,
        pair_inv=pair_inv,
        counted=counted,
        joined=joined,
    )


def plain_forward(entry, living, conv_first, conv_second, gains_plain, biases_plain):
    first_ext = with_rims(entry)
    first_out = conv_valid(first_ext, conv_first, 1)
    first_norm, first_inv, counted = norm_stats([first_out], living)
    first_pre = first_norm[0] * gains_plain[0] + biases_plain[0]
    first_act = jax.nn.silu(first_pre).astype(jnp.bfloat16)
    second_ext = with_rims(first_act)
    second_out = conv_valid(second_ext, conv_second, 1)
    second_norm, second_inv, counted = norm_stats([second_out], living)
    joined = second_norm[0] * gains_plain[1] + biases_plain[1] + entry.astype(jnp.float32)
    return dict(
        first_ext=first_ext,
        first_pre=first_pre,
        first_norm=first_norm,
        first_inv=first_inv,
        second_ext=second_ext,
        second_norm=second_norm,
        second_inv=second_inv,
        counted=counted,
        joined=joined,
    )


def segment_sum(member_one, member_two, member_three, member_four):
    return lax.psum((member_one, member_two, member_three, member_four), ("batch", "space"))


def per_device(
    images,
    image_counts,
    labels,
    fw_picks,
    conv_down,
    conv_mid,
    shortcut,
    gains_down,
    biases_down,
    conv_first,
    conv_second,
    gains_plain,
    biases_plain,
    head_weight,
    head_bias,
):
    micros = image_counts.shape[1]
    per_micro = images.shape[0] // micros
    out_rows = images.shape[1] // 2
    out_cols = images.shape[2] // 2
    channels = conv_mid.shape[3]
    tasks = head_weight.shape[1]
    image_pixels = out_rows * lax.axis_size("space") * out_cols
    scale = float(image_pixels * tasks)
    is_first = lax.axis_index("pipe") == 0
    on_top = lax.axis_index("space") == 0
    slots = jnp.arange(per_micro, dtype=jnp.int32)
    living_list = [
        (slots < image_counts[0, moment]).astype(jnp.float32) for moment in range(micros)
    ]
    images_list = [
        images[moment * per_micro : (moment + 1) * per_micro] for moment in range(micros)
    ]
    targets = labels.astype(jnp.float32)
    target_list = [
        targets[moment * per_micro : (moment + 1) * per_micro] for moment in range(micros)
    ]
    flowing = jnp.zeros((per_micro, out_rows, out_cols, channels), jnp.bfloat16)
    zero_pool = jnp.zeros((per_micro, channels), jnp.float32)
    zero_logit = jnp.zeros((per_micro, tasks), jnp.float32)
    zero_image = jnp.zeros(images_list[0].shape, jnp.float32)
    arrived = []
    pooled_list = []
    partial_list = []
    logit_list = []
    for moment in range(micros + 1):

        def down_branch(moment=moment):
            if moment == micros:
                return (flowing, zero_pool, zero_pool, zero_logit)
            kept = down_forward(
                images_list[moment],
                living_list[moment],
                conv_down,
                conv_mid,
                shortcut,
                gains_down,
                biases_down,
            )
            return (
                jax.nn.silu(kept["joined"]).astype(jnp.bfloat16),
                zero_pool,
                zero_pool,
                zero_logit,
            )

        def plain_branch(moment=moment):
            if moment == 0:
                return (flowing, zero_pool, zero_pool, zero_logit)
            kept = plain_forward(
                arrived[moment - 1],
                living_list[moment - 1],
                conv_first,
                conv_second,
                gains_plain,
                biases_plain,
            )
            output = jax.nn.silu(kept["joined"])
            partial_value = jnp.sum(output, axis=(1, 2))
            pooled = lax.psum(partial_value, "space") / image_pixels
            logits = jnp.dot(pooled, head_weight, precision=HIGHEST) + head_bias
            return (flowing, pooled, partial_value, logits)

        payload, pooled, partial_value, logits = select_by(is_first, down_branch(), plain_branch())
        if moment < micros:
            arrived.append(shifted(payload, "pipe", 1))
        if moment > 0:
            pooled_list.append(pooled)
            partial_list.append(partial_value)
            logit_list.append(logits)
    error_list = [
        living_list[moment][:, None] * (jax.nn.sigmoid(logit_list[moment]) - target_list[moment])
        for moment in range(micros)
    ]
    cross_local = jnp.zeros((tasks, tasks), jnp.float32)
    for moment in range(micros):
        cross_local = cross_local + jnp.einsum(
            "nt,ns->ts", error_list[moment], error_list[moment], precision=HIGHEST
        )
    gram = lax.psum(cross_local, "batch") * jnp.dot(head_weight.T, head_weight, precision=HIGHEST)
    alpha = frank_wolfe(gram, fw_picks)
    grads = (
        jnp.zeros(conv_down.shape, jnp.float32),
        jnp.zeros(conv_mid.shape, jnp.float32),
        jnp.zeros(shortcut.shape, jnp.float32),
        jnp.zeros(gains_down.shape, jnp.float32),
        jnp.zeros(biases_down.shape, jnp.float32),
        jnp.zeros(conv_first.shape, jnp.float32),
        jnp.zeros(conv_second.shape, jnp.float32),
        jnp.zeros(gains_plain.shape, jnp.float32),
        jnp.zeros(biases_plain.shape, jnp.float32),
        jnp.zeros(head_weight.shape, jnp.float32),
        jnp.zeros(head_bias.shape, jnp.float32),
    )
    returned = []
    image_grad_list = [zero_image for moment in range(micros)]
    for moment in range(micros + 1):

        def down_branch(moment=moment, grads=grads):
            if moment == 0:
                return (flowing, grads, zero_image)
            current = micros - moment
            living = living_list[current]
            kept = down_forward(
                images_list[current], living, conv_down, conv_mid, shortcut, gains_down, biases_down
            )
            grad_joined = returned[moment - 1].astype(jnp.float32) * silu_slope(kept["joined"])
            pair_grads, pair_cross, pair_sums = norm_back(
                [grad_joined, grad_joined],
                kept["pair_norm"],
                kept["pair_inv"],
                gains_down[1:3],
                kept["counted"],
                living,
            )
            mid_low = pair_grads[0].astype(jnp.bfloat16)
            short_low = pair_grads[1].astype(jnp.bfloat16)
            mid_kernel = kernel_grad(kept["mid_ext"], mid_low, 1)
            short_kernel = jnp.einsum(
                "nhwi,nhwo->io", kept["short_in"], short_low, preferred_element_type=jnp.float32
            )
            act_grad = conv_back(mid_low, conv_mid)
            first_grad = act_grad * silu_slope(kept["first_pre"])
            first_grads, first_cross, first_sums = norm_back(
                [first_grad],
                kept["first_norm"],
                kept["first_inv"],
                gains_down[0:1],
                kept["counted"],
                living,
            )
            first_low = first_grads[0].astype(jnp.bfloat16)
            down_kernel = kernel_grad(kept["extended"], first_low, 2)
            image_grad = down_input_grad(first_low, conv_down)
            image_grad = image_grad.at[:, ::2, ::2].add(
                jnp.einsum("nhwo,io->nhwi", short_low, shortcut, preferred_element_type=jnp.float32)
            )
            updated = (
                grads[0] + down_kernel,
                grads[1] + mid_kernel,
                grads[2] + short_kernel,
                grads[3] + jnp.concatenate([first_cross, pair_cross]),
                grads[4] + jnp.concatenate([first_sums, pair_sums]),
            ) + grads[5:]
            return (flowing, updated, image_grad)

        def plain_branch(moment=moment, grads=grads):
            if moment == micros:
                return (flowing, grads, zero_image)
            current = micros - 1 - moment
            living = living_list[current]
            grad_logits = scale * alpha * error_list[current]
            head_w = jnp.einsum(
                "nc,nt->ct", partial_list[current] / image_pixels, grad_logits, precision=HIGHEST
            )
            head_b = jnp.where(on_top, jnp.sum(grad_logits, axis=0), 0.0)
            grad_pool = (
                jnp.einsum("nt,ct->nc", grad_logits, head_weight, precision=HIGHEST) / image_pixels
            )
            kept = plain_forward(
                arrived[current], living, conv_first, conv_second, gains_plain, biases_plain
            )
            grad_joined = grad_pool[:, None, None, :] * silu_slope(kept["joined"])
            second_grads, second_cross, second_sums = norm_back(
                [grad_joined],
                kept["second_norm"],
                kept["second_inv"],
                gains_plain[1:2],
                kept["counted"],
                living,
            )
            second_low = second_grads[0].astype(jnp.bfloat16)
            second_kernel = kernel_grad(kept["second_ext"], second_low, 1)
            act_grad = conv_back(second_low, conv_second)
            first_grad = act_grad * silu_slope(kept["first_pre"])
            first_grads, first_cross, first_sums = norm_back(
                [first_grad],
                kept["first_norm"],
                kept["first_inv"],
                gains_plain[0:1],
                kept["counted"],
                living,
            )
            first_low = first_grads[0].astype(jnp.bfloat16)
            first_kernel = kernel_grad(kept["first_ext"], first_low, 1)
            entry_grad = conv_back(first_low, conv_first) + grad_joined
            updated = grads[:5] + (
                grads[5] + first_kernel,
                grads[6] + second_kernel,
                grads[7] + jnp.concatenate([first_cross, second_cross]),
                grads[8] + jnp.concatenate([first_sums, second_sums]),
                grads[9] + head_w,
                grads[10] + head_b,
            )
            return (entry_grad.astype(jnp.bfloat16), updated, zero_image)

        payload, grads, image_grad = select_by(is_first, down_branch(), plain_branch())
        if moment < micros:
            returned.append(
                jax.tree.map(
                    lambda part, own: part.astype(own.dtype),
                    shifted(shortened(payload), "pipe", -1),
                    payload,
                )
            )
        if moment > 0:
            image_grad_list[micros - moment] = image_grad
    down_summed = segment_sum(grads[0], grads[1], grads[2], jnp.stack([grads[3], grads[4]]))
    heads = jnp.concatenate([grads[9], grads[10][None, :]], axis=0)
    plain_summed = segment_sum(grads[5], grads[6], heads, jnp.stack([grads[7], grads[8]]))
    summed_down = (
        down_summed[0],
        down_summed[1],
        down_summed[2],
        down_summed[3][0],
        down_summed[3][1],
    ) + grads[5:]
    summed_plain = grads[:5] + (
        plain_summed[0],
        plain_summed[1],
        plain_summed[3][0],
        plain_summed[3][1],
        plain_summed[2][:-1],
        plain_summed[2][-1],
    )
    grads = select_by(is_first, summed_down, summed_plain)
    images_grad = jnp.concatenate(image_grad_list, axis=0)
    pooled_all = jnp.concatenate(pooled_list, axis=0)
    shares = (
        lax.psum_scatter(
            images_grad.astype(jnp.bfloat16), "pipe", scatter_dimension=3, tiled=True
        ).astype(jnp.float32),
        lax.psum_scatter(
            pooled_all.astype(jnp.bfloat16), "pipe", scatter_dimension=1, tiled=True
        ).astype(jnp.float32),
        lax.psum_scatter(
            grads[0].astype(jnp.bfloat16), "pipe", scatter_dimension=3, tiled=True
        ).astype(jnp.float32),
        lax.psum_scatter(
            grads[1].astype(jnp.bfloat16), "pipe", scatter_dimension=3, tiled=True
        ).astype(jnp.float32),
        lax.psum_scatter(
            grads[2].astype(jnp.bfloat16), "pipe", scatter_dimension=1, tiled=True
        ).astype(jnp.float32),
        lax.psum_scatter(
            grads[3].astype(jnp.bfloat16), "pipe", scatter_dimension=1, tiled=True
        ).astype(jnp.float32),
        lax.psum_scatter(
            grads[4].astype(jnp.bfloat16), "pipe", scatter_dimension=1, tiled=True
        ).astype(jnp.float32),
        lax.psum_scatter(
            grads[5].astype(jnp.bfloat16), "pipe", scatter_dimension=3, tiled=True
        ).astype(jnp.float32),
        lax.psum_scatter(
            grads[6].astype(jnp.bfloat16), "pipe", scatter_dimension=3, tiled=True
        ).astype(jnp.float32),
        lax.psum_scatter(
            grads[7].astype(jnp.bfloat16), "pipe", scatter_dimension=1, tiled=True
        ).astype(jnp.float32),
        lax.psum_scatter(
            grads[8].astype(jnp.bfloat16), "pipe", scatter_dimension=1, tiled=True
        ).astype(jnp.float32),
        lax.psum_scatter(
            grads[9].astype(jnp.bfloat16), "pipe", scatter_dimension=0, tiled=True
        ).astype(jnp.float32),
        lax.psum_scatter(
            grads[10].astype(jnp.bfloat16), "pipe", scatter_dimension=0, tiled=True
        ).astype(jnp.float32),
    )
    weight_part = shares[2:]
    return (
        shares[1],
        shares[0],
        weight_part[0],
        weight_part[1],
        weight_part[2],
        weight_part[3],
        weight_part[4],
        weight_part[5],
        weight_part[6],
        weight_part[7],
        weight_part[8],
        weight_part[9],
        weight_part[10],
    )


def solution(mesh):
    placed = (
        P("batch", "space", None, None),
        P("batch", None),
        P("batch", None),
        P(),
        P(),
        P(),
        P(),
        P(),
        P(),
        P(),
        P(),
        P(),
        P(),
        P(),
        P(),
    )
    return jax.shard_map(
        per_device,
        mesh=mesh,
        in_specs=placed,
        out_specs=(
            P("batch", "pipe"),
            P("batch", "space", None, "pipe"),
            P(None, None, None, "pipe"),
            P(None, None, None, "pipe"),
            P(None, "pipe"),
            P(None, "pipe"),
            P(None, "pipe"),
            P(None, None, None, "pipe"),
            P(None, None, None, "pipe"),
            P(None, "pipe"),
            P(None, "pipe"),
            P("pipe", None),
            P("pipe"),
        ),
        check_vma=False,
    )
```

profile of v0, /device:TPU:0, one launch (start us, length us, event | category | flops | bytes accessed | tf_op | source)
XLA Modules:
  0.0 4131.0 jit_solution(2563400582316059943)
XLA Ops:
  10.2 5.6 collective-permute-start.24
  42.9 37.3 all-reduce.29
  81.9 38.8 psum.544
  139.1 38.7 psum.545
  179.7 36.9 psum.546
  233.5 5.5 collective-permute-done.5
  241.7 36.8 psum.549
  279.2 38.7 psum.550
  321.8 4.8 collective-permute-start.6
  337.3 36.8 psum.551
  379.0 39.2 all-reduce.28
  419.9 36.8 psum.560
  476.0 39.2 psum.561
  518.0 36.7 psum.564
  578.6 37.0 psum.565
  617.4 38.5 psum.566
  661.5 5.6 collective-permute-start.14
  681.3 38.0 all-reduce.27
  723.3 38.7 psum.576
  781.4 39.2 psum.579
  823.5 36.7 psum.580
  886.9 36.7 psum.581
  925.5 38.8 psum.584
  969.9 5.4 collective-permute-start.22
  1054.0 37.3 all-reduce.26
  1110.4 39.2 psum.595
  1152.4 36.7 psum.596
  1202.5 4.9 collective-permute-done.29
  1213.1 36.8 psum.599
  1251.7 38.9 psum.600
  1308.9 39.3 psum.601
  1349.9 37.5 all-reduce.25
  1395.5 17.6 all-reduce.30
  1417.3 14.6 psum.606
  1432.1 191.7 %while.18 = (s32[]{:T(128)}, f32[40]{0:T(128)S(1)}, f32[40,40]{1,0:T(8,128)S(1)}, s32[20]{0:T(128)}, s32[]{:T(128)}, /*index=5*/f32[]{:T(128)}, f32[]{:T(128)}, s32[]{:T(128)}, f32[]{:T(128)}, f32[]{:T(128)}) while((s32[]{:T(128)}, f32[40]{0:T(128)S(1)}, f32[40,40]{1,0:T(8,128)S(1)}, s32[20]{0:T(128)}, s32[]{:T(128)}, ...), condition=%wide.region_93.94_spmd.clone, body=%wide.region_90.93_spmd.clone.sunk | while | flops 19970 | bytes 8124 | solution.py:181
  1632.7 39.7 all-reduce.24
  1677.6 5.2 collective-permute-start.32
  1688.1 5.6 collective-permute-start.56
  1756.0 73.2 %all-reduce.34.cloned.1.call-done = f32[513,40]{0,1:T(8,128)} async-done(((f32[513,40]{0,1:T(8,128)}), f32[513,40]{0,1:T(8,128)}) %all-reduce.34.cloned.1.call-update) | async-done | bytes 82096 | tf_op jit(solution)/shard_map/psum | solution.py:239
  1842.6 40.9 all-reduce.23
  1911.6 72.2 %all-reduce.22 = (f32[1,512]{1,0:T(1,128)}, f32[1,512]{1,0:T(1,128)}, f32[2,512]{1,0:T(2,128)}, f32[2,512]{1,0:T(2,128)}, f32[1,512]{1,0:T(1,128)}, /*index=5*/f32[1,512]{1,0:T(1,128)}) all-reduce(f32[1,512]{1,0:T(1,128)} %bitcast.2673, f32[1,512]{1,0:T(1,128)} %bitcast.2670, ...), channel_id=1, replica_groups=mesh['pipe'=2,'batch'=4,'space'=4] {'batch','space'}, use_global_device_ids=true, to_apply=%region_113.114 | all-reduce | flops 4096 | bytes 32768 | tf_op jit(solution)/shard_map/psum | solution.py:155
  1991.3 5.2 collective-permute-start.37
  2000.4 5.2 collective-permute-start.48
  2049.2 11.0 add_select_fusion
  2065.8 5.0 collective-permute-start.40
  2083.7 73.4 %all-reduce.21 = (f32[1,512]{1,0:T(1,128)}, f32[1,512]{1,0:T(1,128)}, f32[1,512]{1,0:T(1,128)}, f32[1,512]{1,0:T(1,128)}, f32[1,512]{1,0:T(1,128)S(1)}, /*index=5*/f32[1,512]{1,0:T(1,128)S(1)}) all-reduce(f32[1,512]{1,0:T(1,128)S(1)} %bitcast.2757, ...), channel_id=1, replica_groups=mesh['pipe'=2,'batch'=4,'space'=4] {'batch','space'}, use_global_device_ids=true, to_apply=%region_153.154 | all-reduce | flops 3072 | bytes 24576 | tf_op jit(solution)/shard_map/psum | solution.py:155
  2163.5 5.2 collective-permute-start.50
  2177.9 5.2 collective-permute-start.42
  2221.6 11.0 add_select_fusion.3
  2260.2 73.8 %all-reduce.20 = (f32[2,512]{1,0:T(2,128)}, f32[2,512]{1,0:T(2,128)}, f32[2,512]{1,0:T(2,128)S(1)}, f32[2,512]{1,0:T(2,128)S(1)}, f32[2,512]{1,0:T(2,128)S(1)}, /*index=5*/f32[2,512]{1,0:T(2,128)S(1)}) all-reduce(f32[2,512]{1,0:T(2,128)} %pad_maximum_fusion.27, ...), channel_id=1, replica_groups=mesh['pipe'=2,'batch'=4,'space'=4] {'batch','space'}, use_global_device_ids=true, to_apply=%region_157.158 | all-reduce | flops 6144 | bytes 49152 | tf_op jit(solution)/shard_map/psum | solution.py:155
  2339.6 5.2 collective-permute-start.53
  2348.6 5.2 collective-permute-start.45
  2384.3 11.0 add_select_fusion.6
  2401.9 4.9 collective-permute-start.61
  2421.8 73.8 %all-reduce.19 = (f32[1,512]{1,0:T(1,128)S(1)}, f32[1,512]{1,0:T(1,128)S(1)}, f32[1,512]{1,0:T(1,128)S(1)}, f32[1,512]{1,0:T(1,128)S(1)}, f32[1,512]{1,0:T(1,128...) all-reduce(f32[1,512]{1,0:T(1,128)S(1)} %bitcast.2739, ...), channel_id=1, replica_groups=mesh['pipe'=2,'batch'=4,'space'=4] {'batch','space'}, use_global_device_ids=true, to_apply=%region_162.163 | all-reduce | flops 4096 | bytes 32768 | tf_op jit(solution)/shard_map/psum | solution.py:155
  2537.1 1352.9 %all-reduce.35 = (bf16[256,512]{0,1:T(8,128)(2,1)}, bf16[3,3,256,512]{3,2,1,0:T(8,128)(2,1)}, bf16[3,3,512,512]{3,2,1,0:T(8,128)(2,1)}, bf16[2,3,512]{2,1,0:T(4,...) all-reduce(f32[256,512]{0,1:T(8,128)S(1)} %copy-done.77, ...), channel_id=1, replica_groups=mesh['pipe'=2,'batch'=4,'space'=4] {'batch','space'}, use_global_device_ids=true, to_apply=%region_171.172 | all-reduce | flops 8393728 | bytes 50362368 | tf_op jit(solution)/shard_map/psum | solution.py:239
  3988.1 12.0 copy.547
  4000.1 15.8 reshape.3203
  4016.0 9.9 select_convert_fusion.3
  4025.9 16.4 select_convert_fusion
  4042.6 16.9 select_convert_fusion.1
  4059.5 19.3 select_convert_fusion.2
  4095.2 5.4 reshape.3204
  4100.6 5.8 copy.548
  (2129 shorter events, 987.1 us)
Async XLA Ops:
  8.1 1821.1 %all-reduce.34.cloned.1.call-start = ((), (), s32[]{:S(2)}) async-start(), calls=%async_computation.18 | async-start | bytes 204800 | tf_op jit(solution)/shard_map/psum | solution.py:239
  10.2 121.5 %collective-permute-start.24 = (bf16[4,1,64,256]{3,2,0,1:T(8,128)(2,1)}, bf16[4,1,64,256]{3,2,0,1:T(8,128)(2,1)}, u32[]{:S(2)}, u32[]{:S(2)}) collective-permute-start(bf16[4,1,64,256]{3,2,0,1:T(8,128)(2,1)} %get-tuple-element.371), channel_id=1, source_target_pairs={{0,1},{1,2},{2,3},{4,5},{5,6},{6,7},{8,9},{9,10},{10,11},{12,13},{... | collective-permute-start | bytes 393224 | tf_op jit(solution)/shard_map/ppermute | solution.py:39
  15.8 114.4 %collective-permute-start.16 = (bf16[4,1,64,256]{3,2,0,1:T(8,128)(2,1)}, bf16[4,1,64,256]{3,2,0,1:T(8,128)(2,1)}, u32[]{:S(2)}, u32[]{:S(2)}) collective-permute-start(bf16[4,1,64,256]{3,2,0,1:T(8,128)(2,1)} %get-tuple-element.372), channel_id=1, source_target_pairs={{0,1},{1,2},{2,3},{4,5},{5,6},{6,7},{8,9},{9,10},{10,11},{12,13},{... | collective-permute-start | bytes 393224 | tf_op jit(solution)/shard_map/ppermute | solution.py:39
  19.3 19.4 collective-permute-start.8
  22.7 14.9 collective-permute-start
  124.3 9.0 collective-permute-start.2
  125.6 7.7 collective-permute-start.1
  225.3 8.1 collective-permute-start.4
  320.5 11.0 collective-permute-start.7
  321.8 9.7 collective-permute-start.6
  461.9 7.7 collective-permute-start.10
  561.0 7.1 collective-permute-start.12
  564.9 7.4 collective-permute-start.13
  660.2 14.3 collective-permute-start.15
  661.5 13.0 collective-permute-start.14
  767.2 7.7 collective-permute-start.18
  768.5 7.1 collective-permute-start.17
  968.7 78.6 %collective-permute-start.23 = (bf16[4,1,32,512]{3,2,0,1:T(8,128)(2,1)}, bf16[4,1,32,512]{3,2,0,1:T(8,128)(2,1)}, u32[]{:S(2)}, u32[]{:S(2)}) collective-permute-start(bf16[4,1,32,512]{3,2,0,1:T(8,128)(2,1)} %slice_bitcast_fusion.10), channel_id=1, source_target_pairs={{1,0},{2,1},{3,2},{5,4},{6,5},{7,6},{9,8},{10,9},{11,10},{13,12},{... | collective-permute-start | bytes 393224 | tf_op jit(solution)/shard_map/ppermute | solution.py:29
  969.9 77.3 %collective-permute-start.22 = (bf16[4,1,32,512]{3,2,0,1:T(8,128)(2,1)}, bf16[4,1,32,512]{3,2,0,1:T(8,128)(2,1)}, u32[]{:S(2)}, u32[]{:S(2)}) collective-permute-start(bf16[4,1,32,512]{3,2,0,1:T(8,128)(2,1)} %slice_bitcast_fusion.10), channel_id=1, source_target_pairs={{0,1},{1,2},{2,3},{4,5},{5,6},{6,7},{8,9},{9,10},{10,11},{12,13},{... | collective-permute-start | bytes 393224 | tf_op jit(solution)/shard_map/ppermute | solution.py:27
  1095.5 7.3 collective-permute-start.26
  1097.0 7.1 collective-permute-start.25
  1294.2 7.2 collective-permute-start.31
  1676.3 154.6 %collective-permute-start.33 = (bf16[4,1,32,512]{3,2,0,1:T(8,128)(2,1)S(1)}, bf16[4,1,32,512]{3,2,0,1:T(8,128)(2,1)}, u32[]{:S(2)}, u32[]{:S(2)}) collective-permute-start(bf16[4,1,32,512]{3,2,0,1:T(8,128)(2,1)S(1)} %fusion.228), channel_id=1, source_target_pairs={{1,0},{2,1},{3,2},{5,4},{6,5},{7,6},{9,8},{10,9},{11,10},{13,12},{... | collective-permute-start | bytes 393224 | tf_op jit(solution)/shard_map/ppermute | solution.py:29
  1677.6 153.3 %collective-permute-start.32 = (bf16[4,1,32,512]{3,2,0,1:T(8,128)(2,1)S(1)}, bf16[4,1,32,512]{3,2,0,1:T(8,128)(2,1)}, u32[]{:S(2)}, u32[]{:S(2)}) collective-permute-start(bf16[4,1,32,512]{3,2,0,1:T(8,128)(2,1)S(1)} %fusion.228), channel_id=1, source_target_pairs={{0,1},{1,2},{2,3},{4,5},{5,6},{6,7},{8,9},{9,10},{10,11},{12,13},{... | collective-permute-start | bytes 393224 | tf_op jit(solution)/shard_map/ppermute | solution.py:27
  1686.9 145.6 %collective-permute-start.57 = (bf16[4,1,32,512]{3,2,0,1:T(8,128)(2,1)}, bf16[4,1,32,512]{3,2,0,1:T(8,128)(2,1)}, u32[]{:S(2)}, u32[]{:S(2)}) collective-permute-start(bf16[4,1,32,512]{3,2,0,1:T(8,128)(2,1)} %fusion.186), channel_id=1, source_target_pairs={{1,0},{2,1},{3,2},{5,4},{6,5},{7,6},{9,8},{10,9},{11,10},{13,12},{... | collective-permute-start | bytes 393224 | tf_op jit(solution)/shard_map/ppermute | solution.py:29
  1688.1 144.3 %collective-permute-start.56 = (bf16[4,1,32,512]{3,2,0,1:T(8,128)(2,1)}, bf16[4,1,32,512]{3,2,0,1:T(8,128)(2,1)}, u32[]{:S(2)}, u32[]{:S(2)}) collective-permute-start(bf16[4,1,32,512]{3,2,0,1:T(8,128)(2,1)} %fusion.186), channel_id=1, source_target_pairs={{0,1},{1,2},{2,3},{4,5},{5,6},{6,7},{8,9},{9,10},{10,11},{12,13},{... | collective-permute-start | bytes 393224 | tf_op jit(solution)/shard_map/ppermute | solution.py:27
  1729.2 2351.5 %reduce-scatter.23.cloned.1.call-start = ((), (), s32[]{:S(2)}) async-start(), calls=%async_computation.12 | async-start | bytes 24576 | tf_op jit(solution)/shard_map/reduce_scatter | solution.py:495
  1734.7 2351.3 %reduce-scatter.35.cloned.1.call-start = ((), (), s32[]{:S(2)}) async-start(), calls=%async_computation.19 | async-start | bytes 61440 | tf_op jit(solution)/shard_map/reduce_scatter | solution.py:525
  1830.8 2256.6 %reduce-scatter.45.cloned.1.call-start = ((), (), s32[]{:S(2)}) async-start(), calls=%async_computation.24 | async-start | bytes 196608
  1887.9 14.7 collective-permute-start.35
  1889.3 13.3 collective-permute-start.34
  1989.9 75.9 %collective-permute-start.38 = (bf16[4,1,32,512]{3,2,0,1:T(8,128)(2,1)}, bf16[4,1,32,512]{3,2,0,1:T(8,128)(2,1)}, u32[]{:S(2)}, u32[]{:S(2)}) collective-permute-start(bf16[4,1,32,512]{3,2,0,1:T(8,128)(2,1)} %get-tuple-element.396), channel_id=1, source_target_pairs={{1,0},{2,1},{3,2},{5,4},{6,5},{7,6},{9,8},{10,9},{11,10},{13,12},{... | collective-permute-start | bytes 393224 | tf_op jit(solution)/shard_map/ppermute | solution.py:29
  1991.3 79.4 %collective-permute-start.37 = (bf16[4,1,32,512]{3,2,0,1:T(8,128)(2,1)}, bf16[4,1,32,512]{3,2,0,1:T(8,128)(2,1)}, u32[]{:S(2)}, u32[]{:S(2)}) collective-permute-start(bf16[4,1,32,512]{3,2,0,1:T(8,128)(2,1)} %get-tuple-element.396), channel_id=1, source_target_pairs={{0,1},{1,2},{2,3},{4,5},{5,6},{6,7},{8,9},{9,10},{10,11},{12,13},{... | collective-permute-start | bytes 393224 | tf_op jit(solution)/shard_map/ppermute | solution.py:27
  1999.1 73.3 %collective-permute-start.49 = (bf16[4,1,32,512]{3,2,0,1:T(8,128)(2,1)S(1)}, bf16[4,1,32,512]{3,2,0,1:T(8,128)(2,1)}, u32[]{:S(2)}, u32[]{:S(2)}) collective-permute-start(bf16[4,1,32,512]{3,2,0,1:T(8,128)(2,1)S(1)} %fusion.200), channel_id=1, source_target_pairs={{1,0},{2,1},{3,2},{5,4},{6,5},{7,6},{9,8},{10,9},{11,10},{13,12},{... | collective-permute-start | bytes 393224 | tf_op jit(solution)/shard_map/ppermute | solution.py:29
  2000.4 72.0 %collective-permute-start.48 = (bf16[4,1,32,512]{3,2,0,1:T(8,128)(2,1)S(1)}, bf16[4,1,32,512]{3,2,0,1:T(8,128)(2,1)}, u32[]{:S(2)}, u32[]{:S(2)}) collective-permute-start(bf16[4,1,32,512]{3,2,0,1:T(8,128)(2,1)S(1)} %fusion.200), channel_id=1, source_target_pairs={{0,1},{1,2},{2,3},{4,5},{5,6},{6,7},{8,9},{9,10},{10,11},{12,13},{... | collective-permute-start | bytes 393224 | tf_op jit(solution)/shard_map/ppermute | solution.py:27
  2009.0 64.9 %collective-permute-start.41 = (bf16[4,1,32,512]{3,2,0,1:T(8,128)(2,1)S(1)}, bf16[4,1,32,512]{3,2,0,1:T(8,128)(2,1)}, u32[]{:S(2)}, u32[]{:S(2)}) collective-permute-start(bf16[4,1,32,512]{3,2,0,1:T(8,128)(2,1)S(1)} %fusion.214), channel_id=1, source_target_pairs={{1,0},{2,1},{3,2},{5,4},{6,5},{7,6},{9,8},{10,9},{11,10},{13,12},{... | collective-permute-start | bytes 393224 | tf_op jit(solution)/shard_map/ppermute | solution.py:29
  2065.8 8.2 collective-permute-start.40
  2162.2 70.3 %collective-permute-start.51 = (bf16[4,1,32,512]{3,2,0,1:T(8,128)(2,1)}, bf16[4,1,32,512]{3,2,0,1:T(8,128)(2,1)}, u32[]{:S(2)}, u32[]{:S(2)}) collective-permute-start(bf16[4,1,32,512]{3,2,0,1:T(8,128)(2,1)} %slice_bitcast_fusion.57), channel_id=1, source_target_pairs={{1,0},{2,1},{3,2},{5,4},{6,5},{7,6},{9,8},{10,9},{11,10},{13,12},{... | collective-permute-start | bytes 393224 | tf_op jit(solution)/shard_map/ppermute | solution.py:29
  2163.5 73.6 %collective-permute-start.50 = (bf16[4,1,32,512]{3,2,0,1:T(8,128)(2,1)}, bf16[4,1,32,512]{3,2,0,1:T(8,128)(2,1)}, u32[]{:S(2)}, u32[]{:S(2)}) collective-permute-start(bf16[4,1,32,512]{3,2,0,1:T(8,128)(2,1)} %slice_bitcast_fusion.57), channel_id=1, source_target_pairs={{0,1},{1,2},{2,3},{4,5},{5,6},{6,7},{8,9},{9,10},{10,11},{12,13},{... | collective-permute-start | bytes 393224 | tf_op jit(solution)/shard_map/ppermute | solution.py:27
  2176.6 62.1 %collective-permute-start.43 = (bf16[4,1,32,512]{3,2,0,1:T(8,128)(2,1)}, bf16[4,1,32,512]{3,2,0,1:T(8,128)(2,1)}, u32[]{:S(2)}, u32[]{:S(2)}) collective-permute-start(bf16[4,1,32,512]{3,2,0,1:T(8,128)(2,1)} %slice_bitcast_fusion.58), channel_id=1, source_target_pairs={{1,0},{2,1},{3,2},{5,4},{6,5},{7,6},{9,8},{10,9},{11,10},{13,12},{... | collective-permute-start | bytes 393224 | tf_op jit(solution)/shard_map/ppermute | solution.py:29
  2177.9 60.8 %collective-permute-start.42 = (bf16[4,1,32,512]{3,2,0,1:T(8,128)(2,1)}, bf16[4,1,32,512]{3,2,0,1:T(8,128)(2,1)}, u32[]{:S(2)}, u32[]{:S(2)}) collective-permute-start(bf16[4,1,32,512]{3,2,0,1:T(8,128)(2,1)} %slice_bitcast_fusion.58), channel_id=1, source_target_pairs={{0,1},{1,2},{2,3},{4,5},{5,6},{6,7},{8,9},{9,10},{10,11},{12,13},{... | collective-permute-start | bytes 393224 | tf_op jit(solution)/shard_map/ppermute | solution.py:27
  2199.9 40.4 collective-permute-start.59
  2232.5 7.8 collective-permute-start.58
  2247.0 9.3 collective-permute-start.60
  2250.8 7.1 collective-permute-start.44
  2338.1 63.8 %collective-permute-start.54 = (bf16[4,1,32,512]{3,2,0,1:T(8,128)(2,1)S(1)}, bf16[4,1,32,512]{3,2,0,1:T(8,128)(2,1)}, u32[]{:S(2)}, u32[]{:S(2)}) collective-permute-start(bf16[4,1,32,512]{3,2,0,1:T(8,128)(2,1)S(1)} %get-tuple-element.400), channel_id=1, source_target_pairs={{1,0},{2,1},{3,2},{5,4},{6,5},{7,6},{9,8},{10,9},{11,10},{13,12},{... | collective-permute-start | bytes 393224 | tf_op jit(solution)/shard_map/ppermute | solution.py:29
  2339.6 67.3 %collective-permute-start.53 = (bf16[4,1,32,512]{3,2,0,1:T(8,128)(2,1)S(1)}, bf16[4,1,32,512]{3,2,0,1:T(8,128)(2,1)}, u32[]{:S(2)}, u32[]{:S(2)}) collective-permute-start(bf16[4,1,32,512]{3,2,0,1:T(8,128)(2,1)S(1)} %get-tuple-element.400), channel_id=1, source_target_pairs={{0,1},{1,2},{2,3},{4,5},{5,6},{6,7},{8,9},{9,10},{10,11},{12,13},{... | collective-permute-start | bytes 393224 | tf_op jit(solution)/shard_map/ppermute | solution.py:27
  2347.3 61.1 %collective-permute-start.46 = (bf16[4,1,32,512]{3,2,0,1:T(8,128)(2,1)S(1)}, bf16[4,1,32,512]{3,2,0,1:T(8,128)(2,1)}, u32[]{:S(2)}, u32[]{:S(2)}) collective-permute-start(bf16[4,1,32,512]{3,2,0,1:T(8,128)(2,1)S(1)} %get-tuple-element.398), channel_id=1, source_target_pairs={{1,0},{2,1},{3,2},{5,4},{6,5},{7,6},{9,8},{10,9},{11,10},{13,12},{... | collective-permute-start | bytes 393224 | tf_op jit(solution)/shard_map/ppermute | solution.py:29
  2348.6 59.8 %collective-permute-start.45 = (bf16[4,1,32,512]{3,2,0,1:T(8,128)(2,1)S(1)}, bf16[4,1,32,512]{3,2,0,1:T(8,128)(2,1)}, u32[]{:S(2)}, u32[]{:S(2)}) collective-permute-start(bf16[4,1,32,512]{3,2,0,1:T(8,128)(2,1)S(1)} %get-tuple-element.398), channel_id=1, source_target_pairs={{0,1},{1,2},{2,3},{4,5},{5,6},{6,7},{8,9},{9,10},{10,11},{12,13},{... | collective-permute-start | bytes 393224 | tf_op jit(solution)/shard_map/ppermute | solution.py:27
  2396.6 13.4 collective-permute-start.62
  2401.9 8.1 collective-permute-start.61
  3899.3 78.8 %collective-permute-start.63 = (bf16[4,1,64,256]{3,0,2,1:T(4,128)(2,1)}, bf16[4,1,64,256]{3,0,2,1:T(4,128)(2,1)}, u32[]{:S(2)}, u32[]{:S(2)}) collective-permute-start(bf16[4,1,64,256]{3,0,2,1:T(4,128)(2,1)} %slice.1343), channel_id=1, source_target_pairs={{1,0},{2,1},{3,2},{5,4},{6,5},{7,6},{9,8},{10,9},{11,10},{13,12},{... | collective-permute-start | bytes 393224 | tf_op jit(solution)/shard_map/ppermute | solution.py:39
  3902.9 186.1 %reduce-scatter.43.cloned.1.call-start = ((), (), s32[]{:S(2)}) async-start(), calls=%async_computation.23 | async-start | bytes 196608
  3909.4 60.9 %collective-permute-start.55 = (bf16[4,1,64,256]{3,0,2,1:T(4,128)(2,1)}, bf16[4,1,64,256]{3,0,2,1:T(4,128)(2,1)}, u32[]{:S(2)}, u32[]{:S(2)}) collective-permute-start(bf16[4,1,64,256]{3,0,2,1:T(4,128)(2,1)} %slice.1324), channel_id=1, source_target_pairs={{1,0},{2,1},{3,2},{5,4},{6,5},{7,6},{9,8},{10,9},{11,10},{13,12},{... | collective-permute-start | bytes 393224 | tf_op jit(solution)/shard_map/ppermute | solution.py:39
  3911.5 178.9 %reduce-scatter.41.cloned.1.call-start = ((), (), s32[]{:S(2)}) async-start(), calls=%async_computation.22 | async-start | bytes 196608
  3917.8 44.6 %collective-permute-start.47 = (bf16[4,1,64,256]{3,0,2,1:T(4,128)(2,1)}, bf16[4,1,64,256]{3,0,2,1:T(4,128)(2,1)}, u32[]{:S(2)}, u32[]{:S(2)}) collective-permute-start(bf16[4,1,64,256]{3,0,2,1:T(4,128)(2,1)} %slice.1305), channel_id=1, source_target_pairs={{1,0},{2,1},{3,2},{5,4},{6,5},{7,6},{9,8},{10,9},{11,10},{13,12},{... | collective-permute-start | bytes 393224 | tf_op jit(solution)/shard_map/ppermute | solution.py:39
  3920.0 172.0 %reduce-scatter.39.cloned.1.call-start = ((), (), s32[]{:S(2)}) async-start(), calls=%async_computation.21 | async-start | bytes 196608
  3926.1 30.7 collective-permute-start.39
  3928.2 165.3 %reduce-scatter.29.cloned.1.call-start = ((), (), s32[]{:S(2)}) async-start(), calls=%async_computation.15 | async-start | bytes 393216 | tf_op jit(solution)/shard_map/reduce_scatter | solution.py:504
  3956.3 138.9 %reduce-scatter.37.cloned.1.call-start = ((), (), s32[]{:S(2)}) async-start(), calls=%async_computation.20 | async-start | bytes 1572864
  4015.9 91.6 %reduce-scatter.25.cloned.1.call-start = ((), (), s32[]{:S(2)}) async-start(), calls=%async_computation.13 | async-start | bytes 3538944 | tf_op jit(solution)/shard_map/reduce_scatter | solution.py:498
  4025.9 84.7 %reduce-scatter.33.cloned.1.call-start = ((), (), s32[]{:S(2)}) async-start(), calls=%async_computation.17 | async-start | bytes 7077888 | tf_op jit(solution)/shard_map/reduce_scatter | solution.py:516
  4042.3 72.5 %reduce-scatter.31.cloned.1.call-start = ((), (), s32[]{:S(2)}) async-start(), calls=%async_computation.16 | async-start | bytes 7077888 | tf_op jit(solution)/shard_map/reduce_scatter | solution.py:513
  4059.5 59.6 %reduce-scatter.27.cloned.1.call-start = ((), (), s32[]{:S(2)}) async-start(), calls=%async_computation.14 | async-start | bytes 7077888 | tf_op jit(solution)/shard_map/reduce_scatter | solution.py:501
  (516 other events, 38638.5 us)
Sparse Core Ops, SparseCore 0:
  1729.3 99.8 all-reduce.33
Sparse Core Ops, SparseCore 1:
  1734.8 3.7 reduce-scatter.22
  1830.9 7.1 reduce-scatter.34
  3902.9 17.1 reduce-scatter.44
  3922.3 8.5 reduce-scatter.42
  3933.1 8.6 reduce-scatter.40
  3944.0 8.6 reduce-scatter.38
  3956.4 22.4 reduce-scatter.28
  4016.0 23.3 reduce-scatter.36
  4042.1 10.9 reduce-scatter.24
  4056.0 14.4 reduce-scatter.32
  4072.7 16.2 reduce-scatter.30
  4091.9 16.7 reduce-scatter.26
where the time goes:
time: 4170 us; the launch traced here: 4130 us
  blocking collectives  2750 us (66%)
  other arithmetic  425 us (10%)
  local copies, waits for them, and re-layouts  331 us (8%)
  matrix products  240 us (6%)
  starting transfers between devices  179 us (4%)
  waiting for transfers between devices  100 us (2%)
  loops' own time  79.4 us (2%)
    psum x1, blocking collectives, segment_sum(): lax.psum((member_one, member_two, member_three, member_four), ('batch', '...  1350 us
    psum x14, blocking collectives, norm_stats(): totals, counted = lax.psum((firsts, counted_here), ('batch', 'space'))  532 us
    psum x12, blocking collectives, norm_stats(): variance = lax.psum(deviations, ('batch', 'space')) / counted  454 us
    psum x6, blocking collectives, norm_back(): lax.psum((grad_sums, cross_sums), ('batch', 'space'))  374 us
    ppermute x24, starting transfers between devices, extended_2(): lax.ppermute(tail, axis, [(i, (i + 1) % count) for i in range(ends)])  116 us
    unnamed x1070, local copies, waits for them, and re-layouts  99.3 us
    dot_general x144, matrix products, kernel_grad(): jnp.einsum('nhwi,nhwo->io', window, grad_low, preferred_element_type=jnp....  93.5 us
    conv_general_dilated x28, matrix products, conv_valid(): lax.conv_general_dilated(extended, kernel, (stride, stride), 'VALID', dim...  86.5 us
  transfers between devices with their start and end apart: 77, of which 13 were waited for; matrix products, arithmetic and copies ran while one was open for 17% of the time, Pallas kernels for 0%

commit v1 on v0

v1 whole, which is shorter than its diff:
```python
import jax
import jax.numpy as jnp
from jax import lax
from jax.experimental import pallas as pl
from jax.experimental.pallas import tpu as pltpu
from jax.sharding import PartitionSpec as P

EPSILON = 1e-05
NUMBERS = ("NHWC", "HWIO", "NHWC")
HIGHEST = lax.Precision.HIGHEST
F32 = jnp.float32
BF16 = jnp.bfloat16


def silu_slope(values):
    sigmoid = jax.nn.sigmoid(values)
    return sigmoid * (1.0 + values * (1.0 - sigmoid))


def frank_wolfe_kernel(picks_ref, gram_ref, alpha_ref):
    tasks = gram_ref.shape[0]
    lanes = lax.broadcasted_iota(jnp.int32, (1, tasks), 1)
    gram = gram_ref[...]
    alpha = jnp.full((1, tasks), 1.0 / tasks, F32)
    pulled = jnp.sum(gram, axis=0, keepdims=True) * (1.0 / tasks)
    energy = jnp.sum(pulled * alpha, axis=1, keepdims=True)

    def advance(step, carry):
        alpha, pulled, energy = carry
        chosen = picks_ref[step]
        row = gram_ref[pl.ds(chosen, 1), :]
        onehot = (lanes == chosen).astype(F32)
        toward = jnp.sum(pulled * onehot, axis=1, keepdims=True)
        corner = jnp.sum(row * onehot, axis=1, keepdims=True)
        denom = jnp.maximum(energy - 2.0 * toward + corner, 0.05 * corner)
        ratio = jnp.clip((energy - toward) / denom, 0.0, 1.0)
        rest = 1.0 - ratio
        alpha = rest * alpha + ratio * onehot
        pulled = rest * pulled + ratio * row
        energy = rest * rest * energy + 2.0 * rest * ratio * toward + ratio * ratio * corner
        return alpha, pulled, energy

    alpha, _, _ = lax.fori_loop(0, picks_ref.shape[0], advance, (alpha, pulled, energy))
    alpha_ref[...] = alpha


def frank_wolfe(gram, picks):
    tasks = gram.shape[0]
    return pl.pallas_call(
        frank_wolfe_kernel,
        out_shape=jax.ShapeDtypeStruct((1, tasks), F32),
        in_specs=[
            pl.BlockSpec(memory_space=pltpu.SMEM),
            pl.BlockSpec(memory_space=pltpu.VMEM),
        ],
        out_specs=pl.BlockSpec(memory_space=pltpu.VMEM),
    )(picks, gram)


class Layout:
    def __init__(self, micros):
        self.micros = micros
        self.spaces = lax.axis_size("space")
        self.groups = self.spaces // micros
        self.inner = [
            [group * micros + zone for zone in range(micros)] for group in range(self.groups)
        ]
        self.outer = [
            [group * micros + zone for group in range(self.groups)] for zone in range(micros)
        ]
        self.zone = lax.axis_index("space") % micros

    def group_sum(self, tree):
        if self.groups == 1:
            return tree
        return lax.psum(tree, "space", axis_index_groups=self.outer)

    def row_from(self, block, step):
        span = step * self.micros
        route = [
            (i, i + span) for i in range(self.spaces) if 0 <= i + span < self.spaces
        ]
        if not route:
            return jnp.zeros_like(block)
        return lax.ppermute(block, "space", route)

    def rims(self, tensor):
        above = self.row_from(tensor[:, -1:], 1)
        below = self.row_from(tensor[:, :1], -1)
        grown = jnp.concatenate([above, tensor, below], axis=1)
        return jnp.pad(grown, ((0, 0), (0, 0), (1, 1), (0, 0)))


def conv_valid(extended, kernel, stride):
    return lax.conv_general_dilated(
        extended,
        kernel,
        (stride, stride),
        "VALID",
        dimension_numbers=NUMBERS,
        preferred_element_type=F32,
    )


def flipped(kernel):
    return jnp.swapaxes(kernel[::-1, ::-1], 2, 3)


def kernel_grad(extended, grad_low, stride):
    rows, cols = grad_low.shape[1], grad_low.shape[2]
    taps = []
    for row_tap in range(3):
        for col_tap in range(3):
            window = extended[
                :,
                row_tap : row_tap + stride * (rows - 1) + 1 : stride,
                col_tap : col_tap + stride * (cols - 1) + 1 : stride,
            ]
            taps.append(jnp.einsum("nhwi,nhwo->io", window, grad_low, preferred_element_type=F32))
    return jnp.stack(taps)


def norm_forward(layout, conv_out, weight, counted):
    total = layout.group_sum(jnp.sum(conv_out * weight, axis=(0, 1, 2)))
    centered = conv_out - total / counted
    spread = layout.group_sum(jnp.sum(centered * centered * weight, axis=(0, 1, 2)))
    inverse = lax.rsqrt(spread / counted + EPSILON)
    return centered * inverse, inverse


def norm_back(layout, upstream, normed, inverse, gain, weight, counted):
    grad_sum = jnp.sum(upstream * weight, axis=(0, 1, 2))
    cross_sum = jnp.sum(upstream * normed * weight, axis=(0, 1, 2))
    grad_total, cross_total = layout.group_sum((grad_sum, cross_sum))
    correction = weight * (grad_total / counted + normed * (cross_total / counted))
    low = (gain * inverse * (upstream - correction)).astype(BF16)
    return low, cross_sum, grad_sum


def per_device(
    images,
    image_counts,
    labels,
    fw_picks,
    conv_down,
    conv_mid,
    shortcut,
    gains_down,
    biases_down,
    conv_first,
    conv_second,
    gains_plain,
    biases_plain,
    head_weight,
    head_bias,
):
    layout = Layout(image_counts.shape[1])
    micros, zone = layout.micros, layout.zone
    batches, pipes = lax.axis_size("batch"), lax.axis_size("pipe")
    batch = lax.axis_index("batch")
    pipe = lax.axis_index("pipe")
    per_micro = images.shape[0] // micros
    count = per_micro * batches
    entering, channels = conv_down.shape[2], conv_mid.shape[3]
    tasks = head_weight.shape[1]
    half = channels // pipes
    own = pipe * half

    def own_out(kernel, axis):
        size = kernel.shape[axis] // pipes
        return lax.dynamic_slice_in_dim(kernel, pipe * size, size, axis)

    def whole(tensor, axis=3):
        return lax.all_gather(tensor, "pipe", axis=axis, tiled=True)

    def share(tensor):
        size = tensor.shape[3] // batches
        return lax.dynamic_slice_in_dim(tensor, batch * size, size, 3)

    mine = lax.all_to_all(
        images, "space", 0, 1, axis_index_groups=layout.inner, tiled=True
    )
    mine = lax.all_gather(mine, "batch", axis=0, tiled=True)
    counts = lax.all_gather(image_counts, "batch", axis=0, tiled=True)
    counts = lax.dynamic_slice_in_dim(counts, zone, 1, 1)[:, 0]
    marks = lax.dynamic_slice_in_dim(labels, zone * per_micro, per_micro, 0)
    targets = lax.all_gather(marks, "batch", axis=0, tiled=True).astype(F32)
    slots = jnp.arange(per_micro, dtype=jnp.int32)
    living = (slots[None, :] < counts[:, None]).astype(F32).reshape(count)
    weight = living[:, None, None, None]
    out_rows, out_cols = mine.shape[1] // 2, mine.shape[2] // 2
    image_pixels = out_rows * layout.groups * out_cols
    counted = jnp.sum(living) * image_pixels
    scale = float(image_pixels * tasks)

    gain_d, bias_d = own_out(gains_down, 1), own_out(biases_down, 1)
    gain_p, bias_p = own_out(gains_plain, 1), own_out(biases_plain, 1)

    above = layout.row_from(mine[:, -1:], 1)
    down_ext = jnp.pad(
        jnp.concatenate([above, mine], axis=1), ((0, 0), (0, 0), (1, 0), (0, 0))
    )
    down_out = conv_valid(down_ext, own_out(conv_down, 3), 2)
    down_norm, down_inv = norm_forward(layout, down_out, weight, counted)
    down_pre = down_norm * gain_d[0] + bias_d[0]
    mid_ext = layout.rims(whole(jax.nn.silu(down_pre).astype(BF16)))
    mid_out = conv_valid(mid_ext, own_out(conv_mid, 3), 1)
    short_in = mine[:, ::2, ::2]
    short_out = jnp.einsum(
        "nhwi,io->nhwo", short_in, own_out(shortcut, 1), preferred_element_type=F32
    )
    mid_norm, mid_inv = norm_forward(layout, mid_out, weight, counted)
    short_norm, short_inv = norm_forward(layout, short_out, weight, counted)
    section_pre = mid_norm * gain_d[1] + bias_d[1] + short_norm * gain_d[2] + bias_d[2]
    section = jax.nn.silu(section_pre).astype(BF16)
    first_ext = layout.rims(whole(section))
    first_out = conv_valid(first_ext, own_out(conv_first, 3), 1)
    first_norm, first_inv = norm_forward(layout, first_out, weight, counted)
    first_pre = first_norm * gain_p[0] + bias_p[0]
    second_ext = layout.rims(whole(jax.nn.silu(first_pre).astype(BF16)))
    second_out = conv_valid(second_ext, own_out(conv_second, 3), 1)
    second_norm, second_inv = norm_forward(layout, second_out, weight, counted)
    block_pre = second_norm * gain_p[1] + bias_p[1] + section.astype(F32)
    pooled = layout.group_sum(jnp.sum(jax.nn.silu(block_pre), axis=(1, 2))) / image_pixels

    pooled_all = whole(pooled, 1)
    logits = jnp.dot(pooled_all, head_weight, precision=HIGHEST) + head_bias
    errors = living[:, None] * (jax.nn.sigmoid(logits) - targets)
    cross = jnp.einsum("nt,ns->ts", errors, errors, precision=HIGHEST)
    cross = lax.psum(cross, "space", axis_index_groups=layout.inner)
    gram = cross * jnp.dot(head_weight.T, head_weight, precision=HIGHEST)
    alpha = frank_wolfe(gram, fw_picks)
    grad_logits = scale * alpha * errors
    head_w = jnp.einsum("nc,nt->ct", pooled, grad_logits, precision=HIGHEST)
    head_b = jnp.sum(grad_logits, axis=0)
    head_own = own_out(head_weight, 0)
    grad_pool = jnp.einsum("nt,ct->nc", grad_logits, head_own, precision=HIGHEST) / image_pixels

    grad_block = grad_pool[:, None, None, :] * silu_slope(block_pre)
    second_low, second_cross, second_sum = norm_back(
        layout, grad_block, second_norm, second_inv, gain_p[1], weight, counted
    )
    second_kernel = kernel_grad(share(second_ext), second_low, 1)
    act_grad = conv_valid(layout.rims(whole(second_low)), flipped(own_out(conv_second, 2)), 1)
    first_low, first_cross, first_sum = norm_back(
        layout, act_grad * silu_slope(first_pre), first_norm, first_inv, gain_p[0], weight, counted
    )
    first_kernel = kernel_grad(share(first_ext), first_low, 1)
    entry_grad = conv_valid(layout.rims(whole(first_low)), flipped(own_out(conv_first, 2)), 1)
    entry_grad = (entry_grad + grad_block).astype(BF16).astype(F32)
    grad_section = entry_grad * silu_slope(section_pre)
    mid_low, mid_cross, mid_sum = norm_back(
        layout, grad_section, mid_norm, mid_inv, gain_d[1], weight, counted
    )
    short_low, short_cross, short_sum = norm_back(
        layout, grad_section, short_norm, short_inv, gain_d[2], weight, counted
    )
    mid_kernel = kernel_grad(share(mid_ext), mid_low, 1)
    short_kernel = jnp.einsum(
        "nhwi,nhwo->io", share(short_in), short_low, preferred_element_type=F32
    )
    act_grad = conv_valid(layout.rims(whole(mid_low)), flipped(own_out(conv_mid, 2)), 1)
    down_low, down_cross, down_sum = norm_back(
        layout, act_grad * silu_slope(down_pre), down_norm, down_inv, gain_d[0], weight, counted
    )
    down_kernel = kernel_grad(share(down_ext), down_low, 2)

    kept = lax.dynamic_slice_in_dim(whole(down_low), batch * per_micro, per_micro, 0)
    below = layout.row_from(kept[:, :1], -1)
    spread = lax.conv_general_dilated(
        jnp.concatenate([kept, below], axis=1),
        flipped(own_out(conv_down, 2)),
        (1, 1),
        ((2, 2), (2, 2)),
        lhs_dilation=(2, 2),
        dimension_numbers=NUMBERS,
        preferred_element_type=F32,
    )[:, 1 : 2 * out_rows + 1, 1:]
    short_kept = lax.dynamic_slice_in_dim(whole(short_low), batch * per_micro, per_micro, 0)
    spread = spread.at[:, ::2, ::2].add(
        jnp.einsum(
            "nhwo,io->nhwi", short_kept, own_out(shortcut, 0), preferred_element_type=F32
        )
    )
    images_grad = lax.all_to_all(
        spread.astype(BF16), "space", 1, 0, axis_index_groups=layout.inner, tiled=True
    ).astype(F32)

    def total(kernel, axis):
        summed = lax.psum(kernel.astype(BF16), "space")
        return lax.all_gather(summed, "batch", axis=axis, tiled=True).astype(F32)

    pooled_out = lax.dynamic_slice_in_dim(pooled, batch * per_micro, per_micro, 0)
    pooled_out = lax.all_gather(
        pooled_out, "space", axis_index_groups=layout.inner, axis=0, tiled=True
    )
    head_w, head_b = lax.psum((head_w, head_b), "space", axis_index_groups=layout.inner)
    gains_d, sums_d, gains_p, sums_p = lax.psum(
        (
            jnp.stack([down_cross, mid_cross, short_cross]),
            jnp.stack([down_sum, mid_sum, short_sum]),
            jnp.stack([first_cross, second_cross]),
            jnp.stack([first_sum, second_sum]),
        ),
        "space",
    )
    return (
        pooled_out,
        images_grad,
        total(down_kernel, 1).reshape(3, 3, entering, half),
        total(mid_kernel, 1).reshape(3, 3, channels, half),
        total(short_kernel, 0),
        gains_d,
        sums_d,
        total(first_kernel, 1).reshape(3, 3, channels, half),
        total(second_kernel, 1).reshape(3, 3, channels, half),
        gains_p,
        sums_p,
        head_w,
        own_out(head_b, 0),
    )


def solution(mesh):
    placed = (
        P("batch", "space", None, None),
        P("batch", None),
        P("batch", None),
    ) + (P(),) * 12
    return jax.shard_map(
        per_device,
        mesh=mesh,
        in_specs=placed,
        out_specs=(
            P("batch", "pipe"),
            P("batch", "space", None, "pipe"),
            P(None, None, None, "pipe"),
            P(None, None, None, "pipe"),
            P(None, "pipe"),
            P(None, "pipe"),
            P(None, "pipe"),
            P(None, None, None, "pipe"),
            P(None, None, None, "pipe"),
            P(None, "pipe"),
            P(None, "pipe"),
            P("pipe", None),
            P("pipe"),
        ),
        check_vma=False,
    )
```

time: 4170 us -> 595 us (0.14)
  blocking collectives: 2750 us -> 135 us
  other arithmetic: 425 us -> 57.1 us
  local copies, waits for them, and re-layouts: 331 us -> 50.8 us
  starting transfers between devices: 179 us -> 6.55 us
  matrix products: 240 us -> 108 us
  waiting for transfers between devices: 100 us -> 207 us
  loops' own time: 79.4 us -> 0 us
    psum x35 -> x3, blocking collectives: 2740 us -> 55.5 us  [the longest x1 20.4 us: per_device(): cross = lax.psum(cross, 'space', axis_index_groups=layout.inner)]
    ppermute x64 -> x0, starting transfers between devices: 178 us -> none  [the longest x24 116 us: extended_2(): lax.ppermute(tail, axis, [(i, (i + 1) % count) for i in range(ends)])]
    all_gather x0 -> x13, waiting for transfers between devices: none -> 120 us  [the longest x4 48.3 us: total(): return lax.all_gather(summed, 'batch', axis=axis, tiled=True).astype(F32)]
    convert_element_type x43 -> x12, other arithmetic: 112 us -> 14.8 us  [the longest x4 7.69 us: norm_back(): low = (gain * inverse * (upstream - correction)).astype(BF16)]
    dot_general x193 -> x44, matrix products: 144 us -> 48.6 us  [the longest x36 41.3 us: kernel_grad(): jnp.einsum('nhwi,nhwo->io', window, grad_low, preferred_element_type=F32)]
    unnamed x1070 -> x160, local copies, waits for them, and re-layouts: 99.3 us -> 6.57 us
    another operation x1 -> x0, loops' own time: 79.4 us -> none  [frank_wolfe(): lax.fori_loop(0, picks.shape[0], advance, jnp.full((tasks,), 1.0 / tasks,...]
    another operation x78 -> x4, other arithmetic: 77.7 us -> 0.03 us  [the longest x1 0.01 us: per_device(): jnp.stack([down_cross, mid_cross, short_cross])]
  transfers between devices with their start and end apart: 77 -> 15, of which waited for: 13 -> 7; matrix products, arithmetic and copies ran while one was open for 17% -> 19% of each run, Pallas kernels for 0% -> 0%
where the time goes in v1:
time: 595 us; the launch traced here: 584 us
  waiting for transfers between devices  207 us (35%)
  blocking collectives  135 us (23%)
  matrix products  108 us (18%)
  other arithmetic  57.1 us (10%)
  local copies, waits for them, and re-layouts  50.8 us (9%)
  between operations  16.2 us (3%)
  starting transfers between devices  6.55 us (1%)
    psum x1, waiting for transfers between devices, total(): summed = lax.psum(kernel.astype(BF16), 'space')  84.2 us
    conv_general_dilated x7, matrix products, conv_valid(): lax.conv_general_dilated(extended, kernel, (stride, stride), 'VALID', dim...  57.4 us
    all_gather x4, waiting for transfers between devices, total(): return lax.all_gather(summed, 'batch', axis=axis, tiled=True).astype(F32)  48.3 us
    all_gather x1, waiting for transfers between devices, per_device(): mine = lax.all_gather(mine, 'batch', axis=0, tiled=True)  41.3 us
    dot_general x36, matrix products, kernel_grad(): jnp.einsum('nhwi,nhwo->io', window, grad_low, preferred_element_type=F32)  41.3 us
    all_to_all x1, blocking collectives, per_device(): lax.all_to_all(images, 'space', 0, 1, axis_index_groups=layout.inner, til...  32.2 us
    all_gather x8, waiting for transfers between devices, whole(): return lax.all_gather(tensor, 'pipe', axis=axis, tiled=True)  30 us
    slice x1, local copies, waits for them, and re-layouts, per_device(): short_in = mine[:, ::2, ::2]  27.9 us
  transfers between devices with their start and end apart: 15, of which 7 were waited for; matrix products, arithmetic and copies ran while one was open for 19% of the time, Pallas kernels for 0%

profile of v1, /device:TPU:0, one launch (start us, length us, event | category | flops | bytes accessed | tf_op | source)
XLA Modules:
  0.0 583.6 jit_solution(10814132197994489257)
XLA Ops:
  7.2 32.2 %all_to_all.27 = bf16[16,2,64,256]{3,2,1,0:T(8,128)(2,1)S(1)} all-to-all(bf16[16,2,64,256]{3,2,1,0:T(8,128)(2,1)} %param.15), channel_id=1, replica_groups={{0,1,2,3},{4,5,6,7},{8,9,10,11},{12,13,14,15},{16,17,18,19},{20,21,22,2..., dimensions={0} | all-to-all | bytes 2097152 | tf_op jit(solution)/shard_map/all_to_all | solution.py:180
  39.4 1.0 copy.194
  40.6 7.9 %all-gather = s32[4,1,4]{2,1,0:T(1,128)S(1)} all-gather(s32[1,1,4]{2,1,0:T(1,128)S(1)} %bitcast.701), channel_id=1, replica_groups=mesh['pipe'=2,'batch'=4,'space'=4] {'batch'}, dimensions={0}, use_global_device_ids=true | all-gather | bytes 80 | tf_op jit(solution)/shard_map/all_gather | solution.py:184
  51.1 41.3 %all-gather.17.cloned.1.call-done = bf16[16,8,64,256]{3,2,1,0:T(8,128)(2,1)} async-done(((bf16[4,8,64,256]{3,2,1,0:T(8,128)(2,1)}), bf16[16,8,64,256]{3,2,1,0:T(8,128)(2,1)}) %all-gather.17.cloned.1.call-update) | async-done | bytes 4194320 | tf_op jit(solution)/shard_map/all_gather | solution.py:183
  92.5 5.6 multiply_reduce_fusion.18
  99.4 1.6 multiply_convert_fusion.6
  101.1 27.9 %slice.153 = bf16[16,4,32,256]{3,2,1,0:T(8,128)(2,1)S(1)} slice(bf16[16,8,64,256]{3,2,1,0:T(8,128)(2,1)} %all-gather.17.cloned.1.call-done), slice={[0:16:1], [0:8:2], [0:64:2], [0:256:1]} | slice | bytes 2097152 | tf_op jit(solution)/shard_map/slice | solution.py:208
  129.1 2.0 multiply_reduce_fusion.14
  131.1 1.3 copy-done.12
  133.5 8.0 %multiply_reduce_fusion.16 = (f32[256]{0:T(256)S(1)}, f32[16,4,32,256]{3,0,2,1:T(8,128)S(1)}) fusion(f32[16]{0:T(128)S(1)} %reshape.217, bf16[3,3,512,512]{3,2,1,0:T(8,128)(2,1)} %param.20, s32[]{:T(128)S(6)} %select_n.23, bf16[16,1,32,512]{3,0,2,1:T(8,128)(2,1)S(1)} %broadcast.176, bf16[16,4,32,512]{3,0,2,1:T(8,128)(2,1)} %all-gather.19.cloned.1.call-done), kind=kOutput, calls=%fused_computation.76 | convolution fusion | flops 4741660672 | bytes 7078980 | tf_op jit(solution)/shard_map/conv_general_dilated | solution.py:95
  143.9 2.0 multiply_convert_fusion.5
  146.4 10.0 %all-gather.21.cloned.1.call-done = bf16[16,4,32,512]{3,0,2,1:T(8,128)(2,1)} async-done(((bf16[16,4,32,256]{3,0,2,1:T(8,128)(2,1)}), bf16[16,4,32,512]{3,0,2,1:T(8,128)(2,1)}) %all-gather.21.cloned.1.call-update) | async-done | bytes 2097168 | tf_op jit(solution)/shard_map/all_gather | solution.py:174
  156.4 7.9 %multiply_reduce_fusion.12 = (f32[256]{0:T(256)S(1)}, f32[16,4,32,256]{3,0,2,1:T(8,128)S(1)}) fusion(f32[16]{0:T(128)S(1)} %reshape.217, bf16[3,3,512,512]{3,2,1,0:T(8,128)(2,1)} %param.24, s32[]{:T(128)S(6)} %select_n.23, bf16[16,1,32,512]{3,0,2,1:T(8,128)(2,1)S(1)} %broadcast.176, bf16[16,4,32,512]{3,0,2,1:T(8,128)(2,1)} %all-gather.21.cloned.1.call-done), kind=kOutput, calls=%fused_computation.70 | convolution fusion | flops 4741660672 | bytes 7078980 | tf_op jit(solution)/shard_map/conv_general_dilated | solution.py:95
  165.5 1.6 multiply_convert_fusion.4
  168.0 8.3 %all-gather.2 = s32[4,4,40]{2,1,0:T(4,128)S(1)} all-gather(s32[1,4,40]{2,1,0:T(4,128)S(1)} %fusion.190), channel_id=1, replica_groups=mesh['pipe'=2,'batch'=4,'space'=4] {'batch'}, dimensions={0}, use_global_device_ids=true | all-gather | bytes 3200 | tf_op jit(solution)/shard_map/all_gather | solution.py:187
  176.3 5.1 copy.195
  181.4 2.1 pad_dynamic-slice_fusion
  183.5 7.9 %multiply_reduce_fusion.10 = (f32[256]{0:T(256)S(1)}, f32[16,4,32,256]{3,0,2,1:T(8,128)S(1)}) fusion(f32[16]{0:T(128)S(1)} %reshape.217, bf16[3,3,512,512]{3,2,1,0:T(8,128)(2,1)} %param.25, s32[]{:T(128)S(6)} %select_n.23, bf16[16,1,32,512]{3,0,2,1:T(8,128)(2,1)S(1)} %broadcast.176, bf16[16,4,32,512]{3,0,2,1:T(8,128)(2,1)} %all-gather.23.cloned.1.call-done), kind=kOutput, calls=%fused_computation.65 | convolution fusion | flops 4741660672 | bytes 7078980 | tf_op jit(solution)/shard_map/conv_general_dilated | solution.py:95
  194.2 1.8 all_gather.60
  197.1 20.4 %psum.84 = f32[40,40]{1,0:T(8,128)} all-reduce(f32[40,40]{1,0:T(8,128)} %fusion.202), channel_id=1, replica_groups={{0,1,2,3},{4,5,6,7},{8,9,10,11},{12,13,14,15},{16,17,18,19},{20,21,22,2..., use_global_device_ids=true, to_apply=%region_12.13 | all-reduce | flops 1600 | bytes 12800 | tf_op jit(solution)/shard_map/psum | solution.py:230
  217.5 1.5 convolution_multiply_fusion.gram_ref
  219.1 3.3 shard_map.246
  223.8 3.0 multiply_reduce_fusion.7
  226.8 3.1 multiply_convert_fusion.3
  230.0 6.0 %pad_maximum_fusion.3 = (bf16[16,6,32,512]{3,0,2,1:T(8,128)(2,1)S(1)}, bf16[16,6,32,512]{3,0,2,1:T(8,128)(2,1)}, bf16[16,6,32,512]{3,0,2,1:T(8,128)(2,1)}) fusion(bf16[16,1,32,512]{3,0,2,1:T(8,128)(2,1)} %copy-done.21, bf16[16,4,32,512]{3,0,2,1:T(8,128)(2,1)} %all-gather.23.cloned.1.call-done, bf16[16,4,32,512]{3,0,2,1:T(8,128)(2,1)} %all-gather.21.cloned.1.call-done, ...), kind=kLoop, calls=%fused_computation.4 | loop fusion | flops 9437184 | bytes 16252928 | tf_op jit(solution)/shard_map/concatenate | solution.py:90
  243.9 1.0 fusion.56
  245.0 8.6 %multiply_reduce_fusion.5 = (f32[256]{0:T(256)S(1)}, f32[256]{0:T(256)S(1)}, f32[16,4,32,256]{3,0,2,1:T(8,128)S(1)}) fusion(f32[16]{0:T(128)S(1)} %reshape.217, f32[256]{0:T(256)S(1)} %copy-done.55, f32[16,4,32,256]{3,0,2,1:T(8,128)} %copy-done.19, f32[256]{0:T(256)S(1)} %copy-done.36, f32[256]{0:T(256)S(1)} %bitcast.693, f32[256]{0:T(256)S(1)} %bitcast.683, ...), kind=kOutput, calls=%fused_computation.55 | convolution fusion | flops 4749524992 | bytes 9181252 | tf_op jit(solution)/shard_map/conv_general_dilated | solution.py:95
  253.6 1.6 multiply_convert_fusion.2
  255.5 2.5 fusion.90
  261.1 1.0 fusion.82
  266.5 11.0 %fusion.18 = (f32[256]{0:T(256)S(1)}, f32[256]{0:T(256)S(1)}, f32[256]{0:T(256)S(1)}, f32[16,4,32,256]{3,0,2,1:T(8,128)S(1)}) fusion(f32[256,16,4,32]{0,1,3,2:T(8,128)} %copy-done.12, f32[256]{0:T(256)S(1)} %copy-done.57, f32[256]{0:T(256)S(1)} %copy-done.41, f32[16]{0:T(128)S(1)} %reshape.217, f32[256]{0:T(256)S(1)} %copy-done.59, ...), kind=kOutput, calls=%fused_computation.38 | convolution fusion | flops 4762632192 | bytes 14449732 | tf_op jit(solution)/shard_map/conv_general_dilated | solution.py:95
  277.6 2.5 fusion.23
  280.4 2.6 fusion.108
  283.0 1.0 fusion.106
  284.0 1.0 fusion.104
  285.0 1.0 fusion.102
  286.0 1.0 fusion.100
  287.0 1.0 fusion.98
  288.0 1.0 fusion.96
  289.1 1.0 fusion.94
  290.1 1.0 fusion.92
  291.1 8.5 %multiply_reduce_fusion.1 = (f32[256]{0:T(256)S(1)}, f32[256]{0:T(256)S(1)}, f32[16,4,32,256]{3,0,2,1:T(8,128)S(1)}) fusion(f32[16]{0:T(128)S(1)} %reshape.217, f32[256]{0:T(256)S(1)} %copy-done.53, f32[16,4,32,256]{3,0,2,1:T(8,128)} %copy-done.17, f32[256]{0:T(256)S(1)} %copy-done.34, f32[256]{0:T(256)S(1)} %bitcast.687, f32[256]{0:T(256)S(1)} %bitcast.674, ...), kind=kOutput, calls=%fused_computation.46 | convolution fusion | flops 4749524992 | bytes 9181252 | tf_op jit(solution)/shard_map/conv_general_dilated | solution.py:95
  300.3 2.4 fusion.136
  302.7 2.0 fusion.134
  312.9 84.2 %all-reduce.9.cloned.1.call-done = (bf16[9,64,256]{2,1,0:T(8,128)(2,1)}, bf16[9,128,256]{2,1,0:T(8,128)(2,1)}, bf16[9,128,256]{2,1,0:T(8,128)(2,1)}, bf16[9,128,256]{2,1,0:T(8,128)(2,1)}) async-done(((bf16[9,64,256]{2,1,0:T(8,128)(2,1)}, bf16[9,128,256]{2,1,0:T(8,128)(2,1)}, bf16[9,128,256]{2,1,0:T(8,128)(2,1)}, bf16[9,128,256]{2,1,0:T(8,128)(2,1)}), (bf16[9,64,256]{2,1,0:T(8,128)(2,1)}, ...) | async-done | bytes 2064400 | tf_op jit(solution)/shard_map/psum | solution.py:290
  399.5 9.1 %all-gather.33.cloned.1.call-done = bf16[16,4,32,512]{3,0,2,1:T(8,128)(2,1)} async-done(((bf16[16,4,32,256]{3,0,2,1:T(8,128)(2,1)}), bf16[16,4,32,512]{3,0,2,1:T(8,128)(2,1)}) %all-gather.33.cloned.1.call-update) | async-done | bytes 2097168 | tf_op jit(solution)/shard_map/all_gather | solution.py:174
  408.7 1.5 constant_dynamic-slice_fusion.3
  411.4 10.9 %all-gather.31.cloned.1.call-done = bf16[16,4,32,512]{3,0,2,1:T(8,128)(2,1)} async-done(((bf16[16,4,32,256]{3,0,2,1:T(8,128)(2,1)}), bf16[16,4,32,512]{3,0,2,1:T(8,128)(2,1)}) %all-gather.31.cloned.1.call-update) | async-done | bytes 2097168 | tf_op jit(solution)/shard_map/all_gather | solution.py:174
  422.2 1.5 dynamic-slice_bitcast_fusion
  424.4 1.8 convolution_select_fusion
  427.7 8.9 %scatter_fusion = f32[4,8,64,128]{3,0,2,1:T(4,128)S(1)} fusion(f32[4,8,64,128]{3,0,2,1:T(4,128)S(1)} %bitcast.649, s32[128]{0:T(128)S(1)} %reshape.231, f32[128,4,128]{2,1,0:T(4,128)} %copy.202), kind=kCustom, calls=%fused_computation | custom fusion | flops 65536 | bytes 787456 | tf_op jit(solution)/shard_map/scatter-add | solution.py:280
  437.6 4.9 all-to-all-start.1
  442.5 20.3 %all-gather.1 = f32[4,4,256]{2,1,0:T(4,128)S(1)} all-gather(f32[1,4,256]{2,1,0:T(4,128)S(1)} %fusion.186), channel_id=1, replica_groups={{0,1,2,3},{4,5,6,7},{8,9,10,11},{12,13,14,15},{16,17,18,19},{20,21,22,2..., dimensions={0}, use_global_device_ids=true | all-gather | bytes 20480 | tf_op jit(solution)/shard_map/all_gather | solution.py:294
  463.4 2.1 fusion.118
  465.5 18.2 %psum.87 = bf16[64,256]{1,0:T(8,128)(2,1)S(1)} all-reduce(bf16[64,256]{1,0:T(8,128)(2,1)S(1)} %fusion.118), channel_id=1, replica_groups=mesh['pipe'=2,'batch'=4,'space'=4] {'space'}, use_global_device_ids=true, to_apply=%region_25.26 | all-reduce | flops 16384 | bytes 65536 | tf_op jit(solution)/shard_map/psum | solution.py:290
  483.7 9.4 %all_gather.69 = bf16[256,256]{1,0:T(8,128)(2,1)S(1)} all-gather(bf16[64,256]{1,0:T(8,128)(2,1)S(1)} %psum.87), channel_id=1, replica_groups=mesh['pipe'=2,'batch'=4,'space'=4] {'batch'}, dimensions={0}, use_global_device_ids=true | all-gather | bytes 163840 | tf_op jit(solution)/shard_map/all_gather | solution.py:291
  493.8 16.9 %all-reduce.5 = (f32[3,256]{1,0:T(4,128)}, f32[3,256]{1,0:T(4,128)}, f32[2,256]{1,0:T(2,128)}, f32[2,256]{1,0:T(2,128)}, f32[256,40]{0,1:T(8,128)}, /*index=5*/f32[40]{0:T(128)S(1)}) all-reduce(f32[3,256]{1,0:T(4,128)S(1)} %pad_maximum_fusion.21, ...), channel_id=1, replica_groups=mesh['pipe'=2,'batch'=4,'space'=4] {'space'}, use_global_device_ids=true, to_apply=%region_26.27 | all-reduce | flops 12840 | bytes 102720 | tf_op jit(solution)/shard_map/psum | solution.py:298
  511.4 1.1 copy.203
  512.5 2.9 convert.189
  515.4 4.3 convert.192
  519.7 13.2 %all-gather.39.cloned.1.call-done = bf16[9,512,256]{2,1,0:T(8,128)(2,1)} async-done(((bf16[9,128,256]{2,1,0:T(8,128)(2,1)}), bf16[9,512,256]{2,1,0:T(8,128)(2,1)}) %all-gather.39.cloned.1.call-update) | async-done | bytes 2359312 | tf_op jit(solution)/shard_map/all_gather | solution.py:291
  532.9 4.3 convert.191
  537.2 35.1 %all-gather.37.cloned.1.call-done = bf16[9,512,256]{2,1,0:T(8,128)(2,1)} async-done(((bf16[9,128,256]{2,1,0:T(8,128)(2,1)}), bf16[9,512,256]{2,1,0:T(8,128)(2,1)}) %all-gather.37.cloned.1.call-update) | async-done | bytes 2359312 | tf_op jit(solution)/shard_map/all_gather | solution.py:291
  572.3 4.3 convert.190
  (279 shorter events, 48.3 us)
Async XLA Ops:
  7.2 85.3 %copy-start = (bf16[3,3,256,512]{3,2,1,0:T(8,128)(2,1)S(1)}, bf16[3,3,256,512]{3,2,1,0:T(8,128)(2,1)}, u32[]{:S(2)}) copy-start(bf16[3,3,256,512]{3,2,1,0:T(8,128)(2,1)} %param.19) | copy-start | bytes 7077892
  7.2 85.3 %all-gather.17.cloned.1.call-start = ((), (), s32[]{:S(2)}) async-start(), calls=%async_computation.2 | async-start | bytes 5242880 | tf_op jit(solution)/shard_map/all_gather | solution.py:183
  40.5 92.9 %all-gather.19.cloned.1.call-start = ((), (), s32[]{:S(2)}) async-start(), calls=%async_computation.3 | async-start | bytes 3145728 | tf_op jit(solution)/shard_map/all_gather | solution.py:174
  51.1 48.2 %copy-start.44 = (f32[1,256]{1,0:T(1,128)}, f32[1,256]{1,0:T(1,128)S(1)}, u32[]{:S(2)}) copy-start(f32[1,256]{1,0:T(1,128)S(1)} %get-tuple-element.72) | copy-start | bytes 3076
  51.1 48.2 %copy-start.62 = (f32[1,256]{1,0:T(1,128)}, f32[1,256]{1,0:T(1,128)S(1)}, u32[]{:S(2)}) copy-start(f32[1,256]{1,0:T(1,128)S(1)} %get-tuple-element.50) | copy-start | bytes 3076
  51.1 91.5 %copy-start.46 = (f32[1,256]{1,0:T(1,128)}, f32[1,256]{1,0:T(1,128)S(1)}, u32[]{:S(2)}) copy-start(f32[1,256]{1,0:T(1,128)S(1)} %get-tuple-element.70) | copy-start | bytes 3076
  51.1 91.5 %copy-start.48 = (f32[1,256]{1,0:T(1,128)}, f32[1,256]{1,0:T(1,128)S(1)}, u32[]{:S(2)}) copy-start(f32[1,256]{1,0:T(1,128)S(1)} %get-tuple-element.71) | copy-start | bytes 3076
  51.1 91.5 %copy-start.64 = (f32[1,256]{1,0:T(1,128)}, f32[1,256]{1,0:T(1,128)S(1)}, u32[]{:S(2)}) copy-start(f32[1,256]{1,0:T(1,128)S(1)} %get-tuple-element.51) | copy-start | bytes 3076
  51.1 91.5 %copy-start.66 = (f32[1,256]{1,0:T(1,128)}, f32[1,256]{1,0:T(1,128)S(1)}, u32[]{:S(2)}) copy-start(f32[1,256]{1,0:T(1,128)S(1)} %get-tuple-element.52) | copy-start | bytes 3076
  99.3 1.8 copy-start.52
  101.1 55.3 %all-gather.21.cloned.1.call-start = ((), (), s32[]{:S(2)}) async-start(), calls=%async_computation.4 | async-start | bytes 3145728 | tf_op jit(solution)/shard_map/all_gather | solution.py:174
  129.1 2.0 copy-start.23
  131.1 11.6 %copy-start.40 = (f32[256]{0:T(256)}, f32[256]{0:T(256)S(1)}, u32[]{:S(2)}) copy-start(f32[256]{0:T(256)S(1)} %broadcast_divide_fusion.11) | copy-start | bytes 3076
  133.4 9.2 %copy-start.56 = (f32[256]{0:T(256)}, f32[256]{0:T(256)S(1)}, u32[]{:S(2)}) copy-start(f32[256]{0:T(256)S(1)} %get-tuple-element.33) | copy-start | bytes 3076
  133.5 50.0 %copy-start.21 = (bf16[16,1,32,512]{3,0,2,1:T(8,128)(2,1)}, bf16[16,1,32,512]{3,0,2,1:T(8,128)(2,1)S(1)}, u32[]{:S(2)}) copy-start(bf16[16,1,32,512]{3,0,2,1:T(8,128)(2,1)S(1)} %broadcast.176) | copy-start | bytes 1572868
  141.5 2.4 copy-start.13
  141.5 4.3 copy-start.42
  142.6 3.2 copy-start.58
  143.9 2.4 copy-start.74
  143.9 2.4 copy-start.75
  145.9 37.6 %all-gather.23.cloned.1.call-start = ((), (), s32[]{:S(2)}) async-start(), calls=%async_computation.5 | async-start | bytes 3145728 | tf_op jit(solution)/shard_map/all_gather | solution.py:174
  146.4 19.1 %copy-start.50 = (f32[1,256]{1,0:T(1,128)}, f32[1,256]{1,0:T(1,128)S(1)}, u32[]{:S(2)}) copy-start(f32[1,256]{1,0:T(1,128)S(1)} %get-tuple-element.74) | copy-start | bytes 3076
  146.4 19.1 %copy-start.68 = (f32[1,256]{1,0:T(1,128)}, f32[1,256]{1,0:T(1,128)S(1)}, u32[]{:S(2)}) copy-start(f32[1,256]{1,0:T(1,128)S(1)} %get-tuple-element.55) | copy-start | bytes 3076
  146.4 46.1 %copy-start.27 = (f32[1,256]{1,0:T(1,128)}, f32[1,256]{1,0:T(1,128)S(1)}, u32[]{:S(2)}) copy-start(f32[1,256]{1,0:T(1,128)S(1)} %get-tuple-element.73) | copy-start | bytes 3076
  146.4 46.1 %copy-start.30 = (f32[1,256]{1,0:T(1,128)}, f32[1,256]{1,0:T(1,128)S(1)}, u32[]{:S(2)}) copy-start(f32[1,256]{1,0:T(1,128)S(1)} %get-tuple-element.56) | copy-start | bytes 3076
  164.2 2.9 copy-start.35
  167.2 77.7 %all-gather.25.cloned.1.call-start = ((), (), s32[]{:S(2)}) async-start(), calls=%async_computation.6 | async-start | bytes 3145728 | tf_op jit(solution)/shard_map/all_gather | solution.py:174
  191.3 2.9 copy-start.7
  191.4 2.0 copy-start.9
  191.9 4.2 copy-start.24
  191.9 4.2 copy-start.76
  192.5 29.8 %copy-start.37 = (f32[256]{0:T(256)}, f32[256]{0:T(256)S(1)}, u32[]{:S(2)}) copy-start(f32[256]{0:T(256)S(1)} %get-tuple-element.41) | copy-start | bytes 3076
  222.3 4.5 copy-start.8
  222.3 4.5 copy-start.28
  222.3 4.5 copy-start.31
  223.6 3.2 copy-start.38
  229.9 6.0 %copy-start.3 = (bf16[16,4,32,256]{3,0,2,1:T(8,128)(2,1)S(1)}, bf16[16,4,32,256]{3,0,2,1:T(8,128)(2,1)}, u32[]{:S(2)}) copy-start(bf16[16,4,32,256]{3,0,2,1:T(8,128)(2,1)} %multiply_convert_fusion.3) | copy-start | bytes 3145732
  230.0 36.3 %all-gather.27.cloned.1.call-start = ((), (), s32[]{:S(2)}) async-start(), calls=%async_computation.7 | async-start | bytes 3145728 | tf_op jit(solution)/shard_map/all_gather | solution.py:174
  244.9 8.7 %copy-start.71 = (f32[256]{0:T(256)S(1)}, f32[256]{0:T(256)}, u32[]{:S(2)}) copy-start(f32[256]{0:T(256)} %get-tuple-element.38) | copy-start | bytes 3076
  245.0 8.7 %copy-start.20 = (f32[16,4,32,256]{3,0,2,1:T(8,128)S(1)}, f32[16,4,32,256]{3,0,2,1:T(8,128)}, u32[]{:S(2)}) copy-start(f32[16,4,32,256]{3,0,2,1:T(8,128)} %copy-done.19) | copy-start | bytes 6291460
  255.2 35.9 %all-gather.29.cloned.1.call-start = ((), (), s32[]{:S(2)}) async-start(), calls=%async_computation.8 | async-start | bytes 3145728 | tf_op jit(solution)/shard_map/all_gather | solution.py:174
  255.5 2.6 copy-start.2
  255.5 2.6 copy-start.4
  266.2 11.3 %copy-start.72 = (f32[256]{0:T(256)S(1)}, f32[256]{0:T(256)}, u32[]{:S(2)}) copy-start(f32[256]{0:T(256)} %get-tuple-element.32) | copy-start | bytes 3076
  266.4 11.1 %copy-start.14 = (f32[256,16,4,32]{0,1,3,2:T(8,128)S(1)}, f32[256,16,4,32]{0,1,3,2:T(8,128)}, u32[]{:S(2)}) copy-start(f32[256,16,4,32]{0,1,3,2:T(8,128)} %copy-done.12) | copy-start | bytes 6291460
  266.4 11.1 %copy-start.16 = (f32[16,4,32,256]{3,0,2,1:T(8,128)S(1)}, f32[16,4,32,256]{3,0,2,1:T(8,128)}, u32[]{:S(2)}) copy-start(f32[16,4,32,256]{3,0,2,1:T(8,128)} %copy-done.15) | copy-start | bytes 6291460
  266.5 11.1 %copy-start.73 = (f32[256]{0:T(256)S(1)}, f32[256]{0:T(256)}, u32[]{:S(2)}) copy-start(f32[256]{0:T(256)} %get-tuple-element.36) | copy-start | bytes 3076
  280.0 117.1 %all-reduce.9.cloned.1.call-start = ((), (), s32[]{:S(2)}) async-start(), calls=%async_computation.15 | async-start | bytes 4128768 | tf_op jit(solution)/shard_map/psum | solution.py:290
  280.3 2.6 copy-start.1
  280.4 2.6 copy-start.5
  291.1 8.6 %copy-start.70 = (f32[256]{0:T(256)S(1)}, f32[256]{0:T(256)}, u32[]{:S(2)}) copy-start(f32[256]{0:T(256)} %get-tuple-element.34) | copy-start | bytes 3076
  291.1 8.5 %copy-start.18 = (f32[16,4,32,256]{3,0,2,1:T(8,128)S(1)}, f32[16,4,32,256]{3,0,2,1:T(8,128)}, u32[]{:S(2)}) copy-start(f32[16,4,32,256]{3,0,2,1:T(8,128)} %copy-done.17) | copy-start | bytes 6291460
  300.3 10.3 %copy-start.6 = (bf16[16,4,32,256]{3,0,2,1:T(8,128)(2,1)}, bf16[16,4,32,256]{3,0,2,1:T(8,128)(2,1)S(1)}, u32[]{:S(2)}) copy-start(bf16[16,4,32,256]{3,0,2,1:T(8,128)(2,1)S(1)} %multiply_convert_fusion) | copy-start | bytes 3145732
  300.3 4.4 copy-start.11
  311.5 97.1 %all-gather.33.cloned.1.call-start = ((), (), s32[]{:S(2)}) async-start(), calls=%async_computation.10 | async-start | bytes 3145728 | tf_op jit(solution)/shard_map/all_gather | solution.py:174
  311.6 87.7 %copy-start.61 = (f32[40]{0:T(128)S(1)}, f32[40]{0:T(128)}, u32[]{:S(2)}) copy-start(f32[40]{0:T(128)} %copy-done.60) | copy-start | bytes 484
  312.3 97.9 %copy-start.26 = (bf16[256,512]{1,0:T(8,128)(2,1)S(1)}, bf16[256,512]{1,0:T(8,128)(2,1)}, u32[]{:S(2)}) copy-start(bf16[256,512]{1,0:T(8,128)(2,1)} %param.21) | copy-start | bytes 786436
  312.3 109.9 %all-gather.31.cloned.1.call-start = ((), (), s32[]{:S(2)}) async-start(), calls=%async_computation.9 | async-start | bytes 3145728 | tf_op jit(solution)/shard_map/all_gather | solution.py:174
  312.9 199.6 %all-gather.35.cloned.1.call-start = ((), (), s32[]{:S(2)}) async-start(), calls=%async_computation.11 | async-start | bytes 1474560 | tf_op jit(solution)/shard_map/all_gather | solution.py:291
  397.2 118.2 %all-gather.41.cloned.1.call-start = ((), (), s32[]{:S(2)}) async-start(), calls=%async_computation.14 | async-start | bytes 2949120 | tf_op jit(solution)/shard_map/all_gather | solution.py:291
  397.7 135.2 %all-gather.39.cloned.1.call-start = ((), (), s32[]{:S(2)}) async-start(), calls=%async_computation.13 | async-start | bytes 2949120 | tf_op jit(solution)/shard_map/all_gather | solution.py:291
  398.5 173.8 %all-gather.37.cloned.1.call-start = ((), (), s32[]{:S(2)}) async-start(), calls=%async_computation.12 | async-start | bytes 2949120 | tf_op jit(solution)/shard_map/all_gather | solution.py:291
  411.4 13.0 %copy-start.25 = (pred[32,10]{0,1:T(8,128)(4,1)S(1)}, pred[32,10]{0,1:T(8,128)(4,1)}, u32[]{:S(2)}) copy-start(pred[32,10]{0,1:T(8,128)(4,1)} %constant.85) | copy-start | bytes 964
  437.6 73.7 %all-to-all-start.1 = ((bf16[4,8,64,128]{3,0,2,1:T(4,128)(2,1)}), bf16[4,8,64,128]{3,0,2,1:T(4,128)(2,1)S(1)}, u32[]{:S(2)}, u32[]{:S(2)}) async-start(bf16[4,8,64,128]{3,0,2,1:T(4,128)(2,1)} %convert_element_type.107), calls=%async_computation.1 | async-start | bytes 1048576 | tf_op jit(solution)/shard_map/all_to_all | solution.py:285
  (29 other events, 34.1 us)
Sparse Core Ops, SparseCore 0:
  40.6 51.8 all-gather.16
  101.2 10.3 all-gather.18
  146.0 10.3 all-gather.20
  167.3 11.5 all-gather.22
  230.1 7.5 all-gather.24
  255.3 7.8 all-gather.26
  280.2 8.4 all-gather.28
  311.7 85.4 all-reduce.8
  399.3 9.2 all-gather.32
  410.7 11.5 all-gather.30
  424.2 28.9 all-gather.34
  455.1 38.5 all-gather.40
  495.6 37.2 all-gather.38
  534.8 37.4 all-gather.36

commit v2 on v1

--- a/solution.py
+++ b/solution.py
@@ -135,6 +135,874 @@
     correction = weight * (grad_total / counted + normed * (cross_total / counted))
     low = (gain * inverse * (upstream - correction)).astype(BF16)
     return low, cross_sum, grad_sum
+
+
+MESH_LIMIT = 56 * 2**20
+VM = pl.BlockSpec(memory_space=pltpu.VMEM)
+SM = pl.BlockSpec(memory_space=pltpu.SMEM)
+NT = (((1,), (1,)), ((), ()))
+TN = (((0,), (0,)), ((), ()))
+OWN_PX, OTHER_PX, ALL_PX = 8, 9, 10
+
+
+def call(kernel, outs, operands, scratch=(), flops=0, name=None):
+    nbytes = sum(x.size * x.dtype.itemsize for x in operands)
+    return pl.pallas_call(
+        kernel,
+        out_shape=tuple(jax.ShapeDtypeStruct(shape, dtype) for shape, dtype in outs),
+        in_specs=[SM if x.ndim == 1 else VM for x in operands],
+        out_specs=tuple(VM for _ in outs),
+        scratch_shapes=list(scratch),
+        compiler_params=pltpu.CompilerParams(vmem_limit_bytes=MESH_LIMIT),
+        cost_estimate=pl.CostEstimate(
+            flops=int(flops), bytes_accessed=int(nbytes), transcendentals=0
+        ),
+        name=name,
+    )(*operands)
+
+
+def fold(rows):
+    return rows[0:8] + rows[8:16] + rows[16:24] + rows[24:32]
+
+
+def total_row(part):
+    return jnp.sum(part, axis=0, keepdims=True)
+
+
+def band(row):
+    return slice(row * 32, row * 32 + 32)
+
+
+def put_band(x_ref, image, row, value):
+    zero = jnp.zeros_like(value)
+    x_ref[image, band(row), 512:1024] = value
+    if row < 3:
+        x_ref[image, band(row + 1), 0:512] = value
+    else:
+        x_ref[image, band(0), 0:512] = zero
+    if row > 0:
+        x_ref[image, band(row - 1), 1024:1536] = value
+    else:
+        x_ref[image, band(3), 1024:1536] = zero
+
+
+def columns_joined(left, middle, right):
+    count = middle.shape[0]
+    column = lax.broadcasted_iota(jnp.int32, (count, 1), 0) % 32
+    joined = middle
+    if left is not None:
+        joined = joined + jnp.where(column == 0, 0.0, pltpu.roll(left, 1, 0))
+    if right is not None:
+        joined = joined + jnp.where(column == 31, 0.0, pltpu.roll(right, count - 1, 0))
+    return joined
+
+
+def conv_core(x_ref, w_ref, out_ref, back):
+    for part in range(2):
+        images = slice(4 * part, 4 * part + 4)
+
+        def tap(col):
+            value = None
+            for row in range(3):
+                lhs = x_ref[images, :, row * 512 : (row + 1) * 512].reshape(512, 512)
+                if back:
+                    term = lax.dot_general(
+                        lhs, w_ref[2 - row, 2 - col], NT, preferred_element_type=F32
+                    )
+                else:
+                    term = jnp.dot(lhs, w_ref[row, col], preferred_element_type=F32)
+                value = term if value is None else value + term
+            return value
+
+        out = columns_joined(tap(0), tap(1), tap(2))
+        out_ref[images] = out.reshape(4, 128, 512)
+
+
+def stats_of(facts_ref, out_ref, stat_ref, row):
+    def add(image, part):
+        for r in range(4):
+            part = part + fold(out_ref[image, band(r), :]) * facts_ref[image]
+        return part
+
+    first = total_row(lax.fori_loop(0, 8, add, jnp.zeros((8, 512), F32)))
+    mean = first / jnp.maximum(facts_ref[OWN_PX], 1.0)
+
+    def deviate(image, part):
+        for r in range(4):
+            away = out_ref[image, band(r), :] - mean
+            part = part + fold(away * away) * facts_ref[image]
+        return part
+
+    second = total_row(lax.fori_loop(0, 8, deviate, jnp.zeros((8, 512), F32)))
+    stat_ref[row : row + 1, :] = first
+    stat_ref[row + 1 : row + 2, :] = second
+
+
+def norm_of(facts_ref, own_ref, other_ref, row):
+    own_px, other_px, all_px = facts_ref[OWN_PX], facts_ref[OTHER_PX], facts_ref[ALL_PX]
+    own, other = own_ref[row : row + 1, :], other_ref[row : row + 1, :]
+    mean = (own + other) / all_px
+    apart = own / jnp.maximum(own_px, 1.0) - other / jnp.maximum(other_px, 1.0)
+    spread = own_ref[row + 1 : row + 2, :] + other_ref[row + 1 : row + 2, :]
+    variance = (spread + apart * apart * (own_px * other_px / all_px)) / all_px
+    return mean, lax.rsqrt(variance + EPSILON)
+
+
+def sigmoid(values):
+    return 1.0 / (1.0 + jnp.exp(-values))
+
+
+def slope_of(values):
+    gate = sigmoid(values)
+    return gate * (1.0 + values * (1.0 - gate))
+
+
+def pieces_kernel(where_ref, images_ref, o0, o1, o2, o3, wide):
+    pipe, zone = where_ref[0], where_ref[2]
+    for rel, out in enumerate((o0, o1, o2, o3)):
+        first = (zone ^ rel) * 4 + pipe * 2
+        for i in range(2):
+            for row in range(2):
+                for part in range(2):
+                    lanes = slice(part * 128, part * 128 + 128)
+                    wide[...] = images_ref[first + i, row, :, lanes].astype(F32)
+                    for par in range(2):
+                        value = wide[pl.ds(par, 32, stride=2), :]
+                        start = par * 256 + part * 128
+                        out[i, row, :, start : start + 128] = value.astype(BF16)
+
+
+def down_kernel(facts_ref, where_ref, *refs):
+    pieces, (w_ref, s_ref, img_ref, out_ref, short_ref, stat_ref, x_ref) = refs[:16], refs[16:]
+    batch, zone = where_ref[1], where_ref[2]
+    for kb in range(4):
+        for kz in range(4):
+            piece = pieces[kb * 4 + kz]
+            row = zone ^ kz
+            here = pl.ds(pl.multiple_of(row * 32, 32), 32)
+            after = pl.ds(pl.multiple_of(((row + 1) % 4) * 32, 32), 32)
+            for i in range(2):
+                image = (batch ^ kb) * 2 + i
+                odd = piece[i, 1]
+                img_ref[image, here, 0:512] = piece[i, 0]
+                img_ref[image, here, 512:1024] = odd
+                x_ref[image, after, :] = jnp.where(row == 3, jnp.zeros_like(odd), odd)
+    for part in range(2):
+        images = slice(4 * part, 4 * part + 4)
+        blocks = (
+            x_ref[images].reshape(512, 512),
+            img_ref[images, :, 0:512].reshape(512, 512),
+            img_ref[images, :, 512:1024].reshape(512, 512),
+        )
+        left, middle = None, None
+        for row in range(3):
+            a = jnp.dot(blocks[row][:, 256:], w_ref[row, 0], preferred_element_type=F32)
+            m = jnp.dot(
+                blocks[row], w_ref[row, 1:3].reshape(512, 512), preferred_element_type=F32
+            )
+            left = a if left is None else left + a
+            middle = m if middle is None else middle + m
+        out_ref[images] = columns_joined(left, middle, None).reshape(4, 128, 512)
+        short = jnp.dot(blocks[1][:, :256], s_ref[...], preferred_element_type=F32)
+        short_ref[images] = short.reshape(4, 128, 512)
+    stats_of(facts_ref, out_ref, stat_ref, 0)
+    stats_of(facts_ref, short_ref, stat_ref, 2)
+    stat_ref[4:8, :] = jnp.zeros((4, 512), F32)
+
+
+def layer_kernel(which, facts_ref, in_ref, own_ref, other_ref, g_ref, b_ref, w_ref,
+                 act_ref, out_ref, stat_ref, norm_ref, x_ref):
+    mean, inverse = norm_of(facts_ref, own_ref, other_ref, 0)
+    gain, bias = g_ref[which : which + 1, :], b_ref[which : which + 1, :]
+
+    def activate(image, carry):
+        for r in range(4):
+            pre = (in_ref[image, band(r), :] - mean) * inverse * gain + bias
+            act = (pre * sigmoid(pre)).astype(BF16)
+            act_ref[image, band(r), :] = act
+            put_band(x_ref, image, r, act)
+        return carry
+
+    lax.fori_loop(0, 8, activate, 0)
+    norm_ref[0:1, :] = mean
+    norm_ref[1:2, :] = inverse
+    norm_ref[2:8, :] = jnp.zeros((6, 512), F32)
+    conv_core(x_ref, w_ref, out_ref, False)
+    stats_of(facts_ref, out_ref, stat_ref, 0)
+    stat_ref[2:8, :] = jnp.zeros((6, 512), F32)
+
+
+def join_kernel(facts_ref, mid_ref, short_ref, own_m, other_m, own_d, other_d, g_ref, b_ref,
+                w_ref, act_ref, out_ref, stat_ref, norm_ref, x_ref):
+    mean_m, inv_m = norm_of(facts_ref, own_m, other_m, 0)
+    mean_s, inv_s = norm_of(facts_ref, own_d, other_d, 2)
+    gain_m, gain_s = g_ref[1:2, :], g_ref[2:3, :]
+    bias_m, bias_s = b_ref[1:2, :], b_ref[2:3, :]
+
+    def activate(image, carry):
+        for r in range(4):
+            pre = (mid_ref[image, band(r), :] - mean_m) * inv_m * gain_m + bias_m
+            pre = pre + (short_ref[image, band(r), :] - mean_s) * inv_s * gain_s + bias_s
+            act = (pre * sigmoid(pre)).astype(BF16)
+            act_ref[image, band(r), :] = act
+            put_band(x_ref, image, r, act)
+        return carry
+
+    lax.fori_loop(0, 8, activate, 0)
+    norm_ref[0:1, :] = mean_m
+    norm_ref[1:2, :] = inv_m
+    norm_ref[2:3, :] = mean_s
+    norm_ref[3:4, :] = inv_s
+    norm_ref[4:8, :] = jnp.zeros((4, 512), F32)
+    conv_core(x_ref, w_ref, out_ref, False)
+    stats_of(facts_ref, out_ref, stat_ref, 0)
+    stat_ref[2:8, :] = jnp.zeros((6, 512), F32)
+
+
+def block_kernel(facts_ref, in_ref, section_ref, own_ref, other_ref, g_ref, b_ref,
+                 pack_ref, norm_ref):
+    mean, inverse = norm_of(facts_ref, own_ref, other_ref, 0)
+    gain, bias = g_ref[1:2, :], b_ref[1:2, :]
+    norm_ref[0:1, :] = mean
+    norm_ref[1:2, :] = inverse
+    norm_ref[2:8, :] = jnp.zeros((6, 512), F32)
+
+    def gather(image, carry):
+        pooled = jnp.zeros((8, 512), F32)
+        slopes, crossed = pooled, pooled
+        for r in range(4):
+            normed = (in_ref[image, band(r), :] - mean) * inverse
+            pre = normed * gain + bias + section_ref[image, band(r), :].astype(F32)
+            gate = sigmoid(pre)
+            slope = gate * (1.0 + pre * (1.0 - gate))
+            pooled = pooled + fold(pre * gate)
+            slopes = slopes + fold(slope)
+            crossed = crossed + fold(slope * normed)
+        pack_ref[pl.ds(image, 1), :] = total_row(pooled) / 128.0
+        pack_ref[pl.ds(image + 8, 1), :] = total_row(slopes)
+        pack_ref[pl.ds(image + 16, 1), :] = total_row(crossed)
+        return carry
+
+    lax.fori_loop(0, 8, gather, 0)
+
+
+def logits_kernel(where_ref, own_ref, other_ref, living_ref, labels_ref, hw_ref, hb_ref,
+                  all_ref, errors_ref, cross_ref):
+    pipe = where_ref[0]
+    for block in range(3):
+        rows = slice(block * 8, block * 8 + 8)
+        all_ref[block, pl.ds(pl.multiple_of(pipe * 8, 8), 8), :] = own_ref[rows, :]
+        all_ref[block, pl.ds(pl.multiple_of((1 - pipe) * 8, 8), 8), :] = other_ref[rows, :]
+    logits = (
+        jnp.dot(all_ref[0], hw_ref[...], precision=HIGHEST, preferred_element_type=F32)
+        + hb_ref[...]
+    )
+    errors = living_ref[...] * (sigmoid(logits) - labels_ref[...])
+    errors_ref[...] = errors
+    cross_ref[...] = lax.dot_general(
+        errors, errors, TN, precision=HIGHEST, preferred_element_type=F32
+    )
+
+
+def head_kernel(picks_ref, where_ref, facts_ref, c0, c1, c2, c3, heads_ref, hw_ref, errors_ref,
+                all_ref, in_ref, section_ref, norm_ref, g_ref, b_ref,
+                low_ref, pool_ref, small_ref, alpha_ref, gram_ref):
+    tasks = gram_ref.shape[0]
+    pipe = where_ref[0]
+    gram_ref[...] = ((c0[...] + c1[...]) + (c2[...] + c3[...])) * heads_ref[...]
+    frank_wolfe_kernel(picks_ref, gram_ref, alpha_ref)
+    grad_logits = (128.0 * tasks) * alpha_ref[...] * errors_ref[...]
+    pooled, slopes, crossed = all_ref[0], all_ref[1], all_ref[2]
+    grad_pool = (
+        lax.dot_general(
+            grad_logits, hw_ref[...], NT, precision=HIGHEST, preferred_element_type=F32
+        )
+        / 128.0
+    )
+    grad_sum = total_row(grad_pool * slopes)
+    cross_sum = total_row(grad_pool * crossed)
+    small_ref[0:tasks, :] = lax.dot_general(
+        grad_logits, pooled, TN, precision=HIGHEST, preferred_element_type=F32
+    )
+    small_ref[tasks : tasks + 1, :] = grad_sum
+    small_ref[tasks + 1 : tasks + 2, :] = cross_sum
+    small_ref[tasks + 2 :, :] = jnp.zeros((small_ref.shape[0] - tasks - 2, 512), F32)
+    for start in (0, 256):
+        small_ref[tasks + 2 : tasks + 3, start : start + tasks] = total_row(grad_logits)
+    pool_ref[...] = jnp.where(pipe == 0, grad_pool[0:8], grad_pool[8:16])
+
+    mean, inverse = norm_ref[0:1, :], norm_ref[1:2, :]
+    gain, bias = g_ref[1:2, :], b_ref[1:2, :]
+    all_px = facts_ref[ALL_PX]
+    front = gain * inverse
+    mean_grad, mean_cross = grad_sum / all_px, cross_sum / all_px
+
+    def back(image, carry):
+        up = pool_ref[pl.ds(image, 1), :]
+        for r in range(4):
+            normed = (in_ref[image, band(r), :] - mean) * inverse
+            pre = normed * gain + bias + section_ref[image, band(r), :].astype(F32)
+            grad = up * slope_of(pre)
+            fix = facts_ref[image] * (mean_grad + normed * mean_cross)
+            low_ref[image, band(r), :] = (front * (grad - fix)).astype(BF16)
+        return carry
+
+    lax.fori_loop(0, 8, back, 0)
+
+
+def back_norm(facts_ref, in_ref, up_ref, norm_ref, own_ref, other_ref, gain, rows, sinks):
+    mean, inverse = norm_ref[rows : rows + 1, :], norm_ref[rows + 1 : rows + 2, :]
+    all_px = facts_ref[ALL_PX]
+    front = gain * inverse
+    cross_row = 1 + rows // 2
+    mean_grad = (own_ref[0:1, :] + other_ref[0:1, :]) / all_px
+    mean_cross = (
+        own_ref[cross_row : cross_row + 1, :] + other_ref[cross_row : cross_row + 1, :]
+    ) / all_px
+
+    def back(image, carry):
+        for r in range(4):
+            normed = (in_ref[image, band(r), :] - mean) * inverse
+            fix = facts_ref[image] * (mean_grad + normed * mean_cross)
+            sinks(image, r, (front * (up_ref[image, band(r), :] - fix)).astype(BF16))
+        return carry
+
+    lax.fori_loop(0, 8, back, 0)
+
+
+def second_back_kernel(facts_ref, low_ref, in_ref, norm_ref, g_ref, b_ref, w_ref,
+                       up_ref, sum_ref, x_ref, conv_ref):
+    def fill(image, carry):
+        for r in range(4):
+            put_band(x_ref, image, r, low_ref[image, band(r), :])
+        return carry
+
+    lax.fori_loop(0, 8, fill, 0)
+    conv_core(x_ref, w_ref, conv_ref, True)
+    slope_sums(facts_ref, in_ref, norm_ref, g_ref[0:1, :], b_ref[0:1, :], conv_ref, up_ref, sum_ref)
+
+
+def slope_sums(facts_ref, in_ref, norm_ref, gain, bias, conv_ref, up_ref, sum_ref):
+    mean, inverse = norm_ref[0:1, :], norm_ref[1:2, :]
+
+    def slope(image, carry):
+        grads, crosses = carry
+        for r in range(4):
+            normed = (in_ref[image, band(r), :] - mean) * inverse
+            up = conv_ref[image, band(r), :] * slope_of(normed * gain + bias)
+            up_ref[image, band(r), :] = up
+            living = facts_ref[image]
+            grads = grads + fold(up) * living
+            crosses = crosses + fold(up * normed) * living
+        return grads, crosses
+
+    zero = jnp.zeros((8, 512), F32)
+    grads, crosses = lax.fori_loop(0, 8, slope, (zero, zero))
+    sum_ref[0:1, :] = total_row(grads)
+    sum_ref[1:2, :] = total_row(crosses)
+    sum_ref[2:8, :] = jnp.zeros((6, 512), F32)
+
+
+def first_back_kernel(facts_ref, up_in, in_ref, norm_ref, own_ref, other_ref, gp_ref, w_ref,
+                      second_ref, norm2_ref, section_ref, bp_ref, pool_ref,
+                      mid_ref, short_ref, normd_ref, gd_ref, bd_ref,
+                      low_ref, up_ref, sum_ref, x_ref, conv_ref):
+    def keep(image, r, low):
+        low_ref[image, band(r), :] = low
+        put_band(x_ref, image, r, low)
+
+    back_norm(facts_ref, in_ref, up_in, norm_ref, own_ref, other_ref, gp_ref[0:1, :], 0, keep)
+    conv_core(x_ref, w_ref, conv_ref, True)
+    mean2, inv2 = norm2_ref[0:1, :], norm2_ref[1:2, :]
+    gain2, bias2 = gp_ref[1:2, :], bp_ref[1:2, :]
+    mean_m, inv_m = normd_ref[0:1, :], normd_ref[1:2, :]
+    mean_s, inv_s = normd_ref[2:3, :], normd_ref[3:4, :]
+    gain_m, gain_s = gd_ref[1:2, :], gd_ref[2:3, :]
+    bias_m, bias_s = bd_ref[1:2, :], bd_ref[2:3, :]
+
+    def join(image, carry):
+        grads, cross_m, cross_s = carry
+        pool = pool_ref[pl.ds(image, 1), :]
+        for r in range(4):
+            pre2 = (second_ref[image, band(r), :] - mean2) * inv2 * gain2 + bias2
+            pre2 = pre2 + section_ref[image, band(r), :].astype(F32)
+            entry = conv_ref[image, band(r), :] + pool * slope_of(pre2)
+            entry = entry.astype(BF16).astype(F32)
+            norm_m = (mid_ref[image, band(r), :] - mean_m) * inv_m
+            norm_s = (short_ref[image, band(r), :] - mean_s) * inv_s
+            pre = norm_m * gain_m + bias_m + norm_s * gain_s + bias_s
+            up = entry * slope_of(pre)
+            up_ref[image, band(r), :] = up
+            living = facts_ref[image]
+            grads = grads + fold(up) * living
+            cross_m = cross_m + fold(up * norm_m) * living
+            cross_s = cross_s + fold(up * norm_s) * living
+        return grads, cross_m, cross_s
+
+    zero = jnp.zeros((8, 512), F32)
+    grads, cross_m, cross_s = lax.fori_loop(0, 8, join, (zero, zero, zero))
+    sum_ref[0:1, :] = total_row(grads)
+    sum_ref[1:2, :] = total_row(cross_m)
+    sum_ref[2:3, :] = total_row(cross_s)
+    sum_ref[3:8, :] = jnp.zeros((5, 512), F32)
+
+
+def mid_back_kernel(facts_ref, up_in, mid_ref, short_ref, normd_ref, own_ref, other_ref, gd_ref,
+                    w_ref, in_ref, norm1_ref, bd_ref,
+                    low_ref, low_s_ref, up_ref, sum_ref, x_ref, conv_ref):
+    def keep(image, r, low):
+        low_ref[image, band(r), :] = low
+        put_band(x_ref, image, r, low)
+
+    def keep_short(image, r, low):
+        low_s_ref[image, band(r), :] = low
+
+    back_norm(facts_ref, mid_ref, up_in, normd_ref, own_ref, other_ref, gd_ref[1:2, :], 0, keep)
+    back_norm(
+        facts_ref, short_ref, up_in, normd_ref, own_ref, other_ref, gd_ref[2:3, :], 2, keep_short
+    )
+    conv_core(x_ref, w_ref, conv_ref, True)
+    slope_sums(
+        facts_ref, in_ref, norm1_ref, gd_ref[0:1, :], bd_ref[0:1, :], conv_ref, up_ref, sum_ref
+    )
+
+
+def down_back_kernel(where_ref, facts_ref, up_in, in_ref, norm1_ref, own_ref, other_ref, gd_ref,
+                     low_s_ref, w_ref, s_ref, low_ref, own_out, other_out):
+    pipe, batch, zone = where_ref[0], where_ref[1], where_ref[2]
+
+    def keep(image, r, low):
+        low_ref[image, band(r), :] = low
+
+    back_norm(facts_ref, in_ref, up_in, norm1_ref, own_ref, other_ref, gd_ref[0:1, :], 0, keep)
+    mine = pl.ds(batch * 2, 2)
+    here = low_ref[mine]
+    below = jnp.concatenate([here[:, 32:], jnp.zeros((2, 32, 512), BF16)], axis=1)
+    here, below = here.reshape(256, 512), below.reshape(256, 512)
+    short = low_s_ref[mine].reshape(256, 512)
+
+    def back(lhs, row, col):
+        return lax.dot_general(lhs, w_ref[row, col], NT, preferred_element_type=F32)
+
+    even_even = back(here, 1, 1) + lax.dot_general(
+        short, s_ref[...], NT, preferred_element_type=F32
+    )
+    even_odd = columns_joined(None, back(here, 1, 2), back(here, 1, 0))
+    odd_even = back(here, 2, 1) + back(below, 0, 1)
+    odd_odd = columns_joined(
+        None, back(here, 2, 2) + back(below, 0, 2), back(here, 2, 0) + back(below, 0, 0)
+    )
+    planes = ((even_even, even_odd), (odd_even, odd_odd))
+    for row in range(2):
+        for par in range(2):
+            plane = planes[row][par].reshape(2, 4, 32, 256).astype(BF16)
+            halves = (plane[..., 0:128], plane[..., 128:256])
+            own = jnp.where(pipe == 0, halves[0], halves[1])
+            other = jnp.where(pipe == 0, halves[1], halves[0])
+            lanes = slice(par * 128, par * 128 + 128)
+            for z in range(4):
+                own_out[z ^ zone, :, row, :, lanes] = own[:, z]
+                other_out[z ^ zone, :, row, :, lanes] = other[:, z]
+
+
+def image_grad_kernel(where_ref, *refs):
+    pieces, out_ref = refs[:8], refs[8]
+    pipe, zone = where_ref[0], where_ref[2]
+    for rel in range(4):
+        for side in range(2):
+            first = (zone ^ rel) * 4 + (pipe if side == 0 else 1 - pipe) * 2
+            for i in range(2):
+                for row in range(2):
+                    for par in range(2):
+                        out_ref[first + i, row, pl.ds(par, 32, stride=2), :] = pieces[
+                            rel * 2 + side
+                        ][i, row, :, par * 128 : (par + 1) * 128].astype(F32)
+
+
+def slot_of(quarter, zone):
+    rel = quarter ^ zone
+    return (rel >> 1) | ((rel & 1) << 1)
+
+
+def shifted_window(turned, down, right):
+    pixel = lax.broadcasted_iota(jnp.int32, (1, 128), 1)
+    column, row = pixel % 32 + right, pixel // 32 + down
+    inside = (column >= 0) & (column < 32) & (row >= 0) & (row < 4)
+    amount = (256 - down * 32 - right) % 128
+    moved = turned if isinstance(amount, int) and amount == 0 else pltpu.roll(turned, amount, 1)
+    return jnp.where(inside, moved, 0.0).astype(BF16)
+
+
+def split_out(pipe, zone, unit, result_own, result_other, own_ref, other_ref):
+    for quarter in range(4):
+        slot = slot_of(quarter, zone)
+        rows = slice(quarter * 32, quarter * 32 + 32)
+        own_ref[slot, unit] = result_own[rows]
+        other_ref[slot, unit] = result_other[rows].astype(BF16)
+
+
+def kernel_grad_kernel(where_ref, act_ref, low_ref, own_ref, other_ref, turned_ref):
+    pipe, batch, zone = where_ref[0], where_ref[1], where_ref[2]
+    lanes = pl.ds(pl.multiple_of(batch * 128, 128), 128)
+
+    def turn(image, carry):
+        turned = act_ref[image, :, lanes].astype(F32).T
+        pixels = pl.ds(pl.multiple_of(image * 128, 128), 128)
+        for row in range(3):
+            for col in range(3):
+                turned_ref[row * 3 + col, :, pixels] = shifted_window(turned, row - 1, col - 1)
+        return carry
+
+    lax.fori_loop(0, 8, turn, 0)
+    lhs = turned_ref[...].reshape(9 * 128, 1024)
+    results = []
+    for side in (pipe, 1 - pipe):
+        columns = pl.ds(pl.multiple_of(side * 256, 256), 256)
+        rhs = low_ref[:, :, columns].reshape(1024, 256)
+        results.append(jnp.dot(lhs, rhs, preferred_element_type=F32))
+    for unit in range(9):
+        rows = slice(unit * 128, unit * 128 + 128)
+        split_out(pipe, zone, unit, results[0][rows], results[1][rows], own_ref, other_ref)
+
+
+DOWN_UNITS = (
+    ((0, 0, 0, 4), (2, -1, 0, 1), (2, 0, 0, 7), (0, 0, 0, 9), (1, 0, 0, 5)),
+    ((1, 0, -1, 3), (3, -1, -1, 0), (3, -1, 0, 2), (3, 0, -1, 6), (3, 0, 0, 8)),
+)
+
+
+def down_grad_kernel(where_ref, img_ref, low_ref, low_s_ref, own_ref, other_ref, turned_ref):
+    pipe, batch, zone = where_ref[0], where_ref[1], where_ref[2]
+    upper, part = batch // 2, batch % 2
+
+    for turn_kind in range(2):
+
+        @pl.when(upper == turn_kind)
+        def _(units=DOWN_UNITS[turn_kind]):
+            def turn(image, carry):
+                pixels = pl.ds(pl.multiple_of(image * 128, 128), 128)
+                seen = {}
+                for unit, (plane, down, right, _) in enumerate(units):
+                    if plane not in seen:
+                        lanes = pl.ds(pl.multiple_of(plane * 256 + part * 128, 128), 128)
+                        seen[plane] = img_ref[image, :, lanes].astype(F32).T
+                    turned_ref[unit, :, pixels] = shifted_window(seen[plane], down, right)
+                return carry
+
+            lax.fori_loop(0, 8, turn, 0)
+
+    short_unit = [tap for _, _, _, tap in DOWN_UNITS[0]].index(9)
+    for unit in range(5):
+        lhs = turned_ref[unit]
+        results = []
+        for side in (pipe, 1 - pipe):
+            columns = pl.ds(pl.multiple_of(side * 256, 256), 256)
+            rhs = low_ref[:, :, columns].reshape(1024, 256)
+            if unit == short_unit:
+                rhs_s = low_s_ref[:, :, columns].reshape(1024, 256)
+                rhs = jnp.where(upper == 0, rhs_s, rhs)
+            results.append(jnp.dot(lhs, rhs, preferred_element_type=F32))
+        split_out(pipe, zone, unit, results[0], results[1], own_ref, other_ref)
+
+
+def gathered_blocks(zone, batch, refs):
+    fin, near = refs[0], refs[1]
+    sets = {0: (None, refs[2]), 1: (refs[3], refs[6]), 2: (refs[4], refs[7]), 3: (refs[5], refs[8])}
+    for kb in range(4):
+        first, second = sets[kb]
+        for rel in range(4):
+            owner, quarter = batch ^ kb, zone ^ rel
+            if rel % 2 == 1:
+                yield owner, quarter, second, rel // 2
+            elif first is not None:
+                yield owner, quarter, first, rel // 2
+            else:
+                yield owner, quarter, (fin if rel == 0 else near), None
+
+
+def assemble_kernel(where_ref, *refs):
+    pieces, out_ref = refs[:9], refs[9]
+    batch, zone = where_ref[1], where_ref[2]
+    for owner, quarter, ref, index in gathered_blocks(zone, batch, pieces):
+        rows = pl.ds(pl.multiple_of(owner * 128 + quarter * 32, 32), 32)
+        value = ref[...] if index is None else ref[index]
+        out_ref[:, rows, :] = value.astype(F32)
+
+
+def assemble_down_kernel(where_ref, *refs):
+    pieces, (out_ref, short_ref) = refs[:9], refs[9:]
+    batch, zone = where_ref[1], where_ref[2]
+    for owner, quarter, ref, index in gathered_blocks(zone, batch, pieces):
+        upper, part = owner // 2, owner % 2
+        rows = pl.ds(pl.multiple_of(part * 128 + quarter * 32, 32), 32)
+        value = (ref[...] if index is None else ref[index]).astype(F32)
+        for kind in range(2):
+
+            @pl.when(upper == kind)
+            def _(value=value, rows=rows, units=DOWN_UNITS[kind]):
+                for unit, (_, _, _, tap) in enumerate(units):
+                    if tap == 9:
+                        short_ref[rows, :] = value[unit]
+                    else:
+                        out_ref[tap, rows, :] = value[unit]
+
+
+def fast_device(images, image_counts, labels, fw_picks, conv_down, conv_mid, shortcut, gains_down,
+                biases_down, conv_first, conv_second, gains_plain, biases_plain, head_weight,
+                head_bias):
+    pipe, batch, zone = (lax.axis_index(axis) for axis in ("pipe", "batch", "space"))
+    tasks = head_weight.shape[1]
+
+    def over(axis, rel, x):
+        size = lax.axis_size(axis)
+        return lax.ppermute(x, axis, [(i, i ^ rel) for i in range(size)])
+
+    def by_index(parts, own):
+        stacked = jnp.stack(parts)
+        return jnp.take(stacked, jnp.arange(4) ^ own, axis=0)
+
+    where = jnp.stack([pipe, batch, zone, zone]).astype(jnp.int32)
+
+    pieces = call(
+        pieces_kernel,
+        [((2, 2, 32, 512), BF16)] * 4,
+        [where, images],
+        [pltpu.VMEM((64, 128), F32)],
+        name="pieces",
+    )
+    moved = [pieces[0]] + [over("space", rel, pieces[rel]) for rel in (1, 2, 3)]
+    gathered = [[moved[rel] for rel in range(4)]]
+    for kb in (1, 2, 3):
+        gathered.append([over("batch", kb, moved[rel]) for rel in range(4)])
+
+    marks = lax.dynamic_slice_in_dim(labels, zone * 4, 4, 0)
+    count = lax.dynamic_slice_in_dim(image_counts, zone, 1, 1)
+    marks = jnp.concatenate([marks, jnp.broadcast_to(count, (1, tasks))], axis=0)
+    marks = by_index([marks] + [over("batch", kb, marks) for kb in (1, 2, 3)], batch)
+    counts = marks[:, 4, 0]
+    slots = jnp.arange(4, dtype=jnp.int32).reshape(2, 1, 2)
+    living = (slots < counts[None, :, None]).astype(F32).reshape(2, 8)
+    targets = marks[:, :4].reshape(4, 2, 2, tasks).transpose(1, 0, 2, 3).reshape(16, tasks)
+    targets = targets.astype(F32)
+    alive = jnp.sum(living, axis=1) * 128.0
+    mine = jnp.where(pipe == 0, living[0], living[1])
+    own_px = jnp.where(pipe == 0, alive[0], alive[1])
+    facts = jnp.concatenate(
+        [mine, jnp.stack([own_px, alive[0] + alive[1] - own_px, alive[0] + alive[1]])]
+    )
+    facts = jnp.pad(facts, (0, 5))
+
+    big = ((8, 128, 512), F32)
+    low = ((8, 128, 512), BF16)
+    rows = ((8, 512), F32)
+    x_scratch = pltpu.VMEM((8, 128, 1536), BF16)
+    conv_scratch = pltpu.VMEM((8, 128, 512), F32)
+    conv_flops = 2 * 1024 * 4608 * 512
+
+    def partner(x):
+        return over("pipe", 1, x)
+
+    img, down_out, short_out, stat_d = call(
+        down_kernel,
+        [((8, 128, 1024), BF16), big, big, rows],
+        [facts, where] + [piece for line in gathered for piece in line] + [conv_down, shortcut],
+        [pltpu.VMEM((8, 128, 512), BF16)],
+        conv_flops // 2,
+        "down",
+    )
+    other_d = partner(stat_d)
+    down_act, mid_out, stat_m, norm_d = call(
+        lambda *refs: layer_kernel(0, *refs),
+        [low, big, rows, rows],
+        [facts, down_out, stat_d, other_d, gains_down, biases_down, conv_mid],
+        [x_scratch],
+        conv_flops,
+        "mid",
+    )
+    other_m = partner(stat_m)
+    section, first_out, stat_f, norm_j = call(
+        join_kernel,
+        [low, big, rows, rows],
+        [facts, mid_out, short_out, stat_m, other_m, stat_d, other_d, gains_down, biases_down,
+         conv_first],
+        [x_scratch],
+        conv_flops,
+        "first",
+    )
+    other_f = partner(stat_f)
+    plain_act, second_out, stat_s, norm_f = call(
+        lambda *refs: layer_kernel(0, *refs),
+        [low, big, rows, rows],
+        [facts, first_out, stat_f, other_f, gains_plain, biases_plain, conv_second],
+        [x_scratch],
+        conv_flops,
+        "second",
+    )
+    other_s = partner(stat_s)
+    pack, norm_s = call(
+        block_kernel,
+        [((24, 512), F32), rows],
+        [facts, second_out, section, stat_s, other_s, gains_plain, biases_plain],
+        name="block",
+    )
+    other_pack = partner(pack)
+    all_pack, errors, cross = call(
+        logits_kernel,
+        [((3, 16, 512), F32), ((16, tasks), F32), ((tasks, tasks), F32)],
+        [where, pack, other_pack, living.reshape(16, 1), targets, head_weight,
+         head_bias.reshape(1, tasks)],
+        name="logits",
+    )
+    crosses = [cross] + [over("space", rel, cross) for rel in (1, 2, 3)]
+    heads = jnp.dot(head_weight.T, head_weight, precision=HIGHEST)
+    second_low, grad_pool, small = call(
+        head_kernel,
+        [low, rows, ((tasks + 8, 512), F32)],
+        [fw_picks, where, facts] + crosses
+        + [heads, head_weight, errors, all_pack, second_out, section, norm_s, gains_plain,
+           biases_plain],
+        [pltpu.VMEM((1, tasks), F32), pltpu.VMEM((tasks, tasks), F32)],
+        name="head",
+    )
+
+    def summed(own, other):
+        got = partner(other)
+        both = own + got.astype(F32)
+        near = both[:2] + over("space", 1, both[2:].astype(BF16)).astype(F32)
+        mine = near[0] + over("space", 2, near[1].astype(BF16)).astype(F32)
+        final = mine.astype(BF16)
+        far = over("space", 2, final)
+        a = jnp.stack([final, far])
+        b = over("space", 1, a)
+        ax, ay = over("batch", 1, a), over("batch", 2, a)
+        bx, by = over("batch", 1, b), over("batch", 2, b)
+        axy, bxy = over("batch", 2, ax), over("batch", 1, by)
+        return [where, final, far, b, ax, ay, axy, bx, by, bxy]
+
+    def kernel_grad_of(act, low_grad, name):
+        own, other = call(
+            kernel_grad_kernel,
+            [((4, 9, 32, 256), F32), ((4, 9, 32, 256), BF16)],
+            [where, act, low_grad],
+            [pltpu.VMEM((9, 128, 1024), BF16)],
+            conv_flops // 4,
+            name,
+        )
+        return summed(own, other)
+
+    def assembled(blocks, name):
+        (out,) = call(assemble_kernel, [((9, 512, 256), F32)], blocks, name=name)
+        return out.reshape(3, 3, 512, 256)
+
+    second_blocks = kernel_grad_of(plain_act, second_low, "second_grad")
+    up_f, sum_f = call(
+        second_back_kernel,
+        [big, rows],
+        [facts, second_low, first_out, norm_f, gains_plain, biases_plain, conv_second],
+        [x_scratch, conv_scratch],
+        conv_flops,
+        "second_back",
+    )
+    other_sf = partner(sum_f)
+    first_low, up_j, sum_j = call(
+        first_back_kernel,
+        [low, big, rows],
+        [facts, up_f, first_out, norm_f, sum_f, other_sf, gains_plain, conv_first,
+         second_out, norm_s, section, biases_plain, grad_pool,
+         mid_out, short_out, norm_j, gains_down, biases_down],
+        [x_scratch, conv_scratch],
+        conv_flops,
+        "first_back",
+    )
+    other_sj = partner(sum_j)
+    first_blocks = kernel_grad_of(section, first_low, "first_grad")
+    mid_low, short_low, up_d, sum_d = call(
+        mid_back_kernel,
+        [low, low, big, rows],
+        [facts, up_j, mid_out, short_out, norm_j, sum_j, other_sj, gains_down, conv_mid,
+         down_out, norm_d, biases_down],
+        [x_scratch, conv_scratch],
+        conv_flops,
+        "mid_back",
+    )
+    other_sd = partner(sum_d)
+    mid_blocks = kernel_grad_of(down_act, mid_low, "mid_grad")
+    down_low, own_img, other_img = call(
+        down_back_kernel,
+        [low, ((4, 2, 2, 32, 256), BF16), ((4, 2, 2, 32, 256), BF16)],
+        [where, facts, up_d, down_out, norm_d, sum_d, other_sd, gains_down, short_low, conv_down,
+         shortcut],
+        [],
+        conv_flops // 8,
+        "down_back",
+    )
+    own, other = call(
+        down_grad_kernel,
+        [((4, 5, 32, 256), F32), ((4, 5, 32, 256), BF16)],
+        [where, img, down_low, short_low],
+        [pltpu.VMEM((5, 128, 1024), BF16)],
+        conv_flops // 8,
+        "down_grad",
+    )
+    down_blocks = summed(own, other)
+
+    got_img = partner(other_img)
+    image_pieces = []
+    for rel in range(4):
+        for block in (own_img, got_img):
+            part = block[rel]
+            image_pieces.append(part if rel == 0 else over("space", rel, part))
+    (images_grad,) = call(
+        image_grad_kernel,
+        [((16, 2, 64, 128), F32)],
+        [where] + image_pieces,
+        name="image_grad",
+    )
+
+    def own_lanes(x):
+        return lax.dynamic_slice_in_dim(x, pipe * 256, 256, x.ndim - 1)
+
+    pooled_mine = lax.dynamic_slice_in_dim(
+        all_pack[0].reshape(2, 4, 2, 512), batch, 1, 1
+    ).reshape(4, 512)
+    sums = jnp.concatenate(
+        [
+            small,
+            sum_f[0:2] + other_sf[0:2],
+            sum_j[0:3] + other_sj[0:3],
+            sum_d[0:2] + other_sd[0:2],
+        ]
+    )
+    sent = jnp.concatenate([own_lanes(sums), own_lanes(pooled_mine)])
+    parts = [sent] + [over("space", rel, sent) for rel in (1, 2, 3)]
+    summed_up = (parts[0] + parts[1]) + (parts[2] + parts[3])
+    pooled = by_index([part[-4:] for part in parts], zone).reshape(16, 256)
+    row = tasks + 8
+    second_sum, second_cross, head_b = (summed_up[tasks + i] for i in range(3))
+    first_sum, first_cross = summed_up[row], summed_up[row + 1]
+    join_sum, mid_cross, short_cross = (summed_up[row + 2 + i] for i in range(3))
+    down_sum, down_cross = summed_up[row + 5], summed_up[row + 6]
+    down_grad, short_grad = call(
+        assemble_down_kernel,
+        [((9, 256, 256), F32), ((256, 256), F32)],
+        down_blocks,
+        name="down_out",
+    )
+    return (
+        pooled,
+        images_grad,
+        down_grad.reshape(3, 3, 256, 256),
+        assembled(mid_blocks, "mid_out"),
+        short_grad,
+        jnp.stack([down_cross, mid_cross, short_cross]),
+        jnp.stack([down_sum, join_sum, join_sum]),
+        assembled(first_blocks, "first_out"),
+        assembled(second_blocks, "second_out"),
+        jnp.stack([first_cross, second_cross]),
+        jnp.stack([first_sum, second_sum]),
+        summed_up[:tasks].T,
+        lax.dynamic_slice_in_dim(head_b, pipe * (tasks // 2), tasks // 2, 0),
+    )
 
 
 def per_device(
@@ -156,6 +1024,13 @@
 ):
     layout = Layout(image_counts.shape[1])
     micros, zone = layout.micros, layout.zone
+    sizes = (images.shape, conv_down.shape, lax.axis_size("pipe"), lax.axis_size("batch"))
+    if layout.groups == 1 and sizes == ((16, 2, 64, 256), (3, 3, 256, 512), 2, 4):
+        return fast_device(
+            images, image_counts, labels, fw_picks, conv_down, conv_mid, shortcut, gains_down,
+            biases_down, conv_first, conv_second, gains_plain, biases_plain, head_weight,
+            head_bias,
+        )
     batches, pipes = lax.axis_size("batch"), lax.axis_size("pipe")
     batch = lax.axis_index("batch")
     pipe = lax.axis_index("pipe")

time: 595 us -> 381 us (0.64); the launches traced: 584 us -> 377 us
  Pallas kernels: 3.26 us -> 149 us
  blocking collectives: 135 us -> 0 us
  matrix products: 108 us -> 0.82 us
  waiting for transfers between devices: 207 us -> 104 us
  starting transfers between devices: 6.55 us -> 88.9 us
  other arithmetic: 57.1 us -> 8.59 us
  local copies, waits for them, and re-layouts: 50.8 us -> 20.5 us
  between operations: 16.2 us -> 4.53 us
    pallas_call x1 -> x21, Pallas kernels: 3.26 us -> 149 us  [call(): pl.pallas_call(kernel, out_shape=tuple((jax.ShapeDtypeStruct(shape, dtype...]
    all_gather x13 -> x0, waiting for transfers between devices: 120 us -> none  [the longest x4 48.3 us: total(): return lax.all_gather(summed, 'batch', axis=axis, tiled=True).astype(F32)]
    ppermute x0 -> x83, waiting for transfers between devices: none -> 104 us  [over(): return lax.ppermute(x, axis, [(i, i ^ rel) for i in range(size)])]
    ppermute x0 -> x83, starting transfers between devices: none -> 88.9 us  [over(): return lax.ppermute(x, axis, [(i, i ^ rel) for i in range(size)])]
    psum x1 -> x0, waiting for transfers between devices: 84.2 us -> none  [total(): summed = lax.psum(kernel.astype(BF16), 'space')]
    conv_general_dilated x7 -> x0, matrix products: 57.4 us -> none  [conv_valid(): lax.conv_general_dilated(extended, kernel, (stride, stride), 'VALID', dim...]
    psum x3 -> x0, blocking collectives: 55.5 us -> none  [the longest x1 20.4 us: per_device(): cross = lax.psum(cross, 'space', axis_index_groups=layout.inner)]
    dot_general x44 -> x1, matrix products: 48.6 us -> 0.82 us  [fast_device(): heads = jnp.dot(head_weight.T, head_weight, precision=HIGHEST)]
  transfers between devices with their start and end apart: 15 -> 83, of which waited for: 7 -> 35; matrix products, arithmetic and copies ran while one was open for 19% -> 5% of each run, Pallas kernels for 0% -> 20%
where the time goes in v2:
time: 381 us; the launch traced here: 377 us
  Pallas kernels  149 us (39%)
  waiting for transfers between devices  104 us (27%)
  starting transfers between devices  88.9 us (23%)
  local copies, waits for them, and re-layouts  20.5 us (5%)
  other arithmetic  8.59 us (2%)
  between operations  4.53 us (1%)
    pallas_call x21, Pallas kernels, call(): pl.pallas_call(kernel, out_shape=tuple((jax.ShapeDtypeStruct(shape, dtype...  149 us
    ppermute x83, waiting for transfers between devices, over(): return lax.ppermute(x, axis, [(i, i ^ rel) for i in range(size)])  104 us
    ppermute x83, starting transfers between devices, over(): return lax.ppermute(x, axis, [(i, i ^ rel) for i in range(size)])  88.9 us
    unnamed x158, local copies, waits for them, and re-layouts  10.7 us
  transfers between devices with their start and end apart: 83, of which 35 were waited for; matrix products, arithmetic and copies ran while one was open for 5% of the time, Pallas kernels for 20%

profile of v2, /device:TPU:0, one launch (start us, length us, event | category | flops | bytes accessed | tf_op | source)
XLA Modules:
  0.0 376.9 jit_solution(4112357439854232688)
XLA Ops:
  3.2 4.0 %collective-permute-start.2 = (s32[5,40]{1,0:T(8,128)S(1)}, s32[5,40]{1,0:T(8,128)S(1)}, u32[]{:S(2)}, u32[]{:S(2)}) collective-permute-start(s32[5,40]{1,0:T(8,128)S(1)} %get-tuple-element.130), channel_id=1, source_target_pairs={{0,12},{4,8},{8,4},{12,0},{1,13},{5,9},{9,5},{13,1},{2,14},{6,10},... | collective-permute-start | bytes 2408 | tf_op jit(solution)/shard_map/ppermute | solution.py:758
  8.5 2.1 pieces.1
  10.6 1.9 collective-permute-start.6
  14.1 1.6 collective-permute-start.3
  15.7 2.6 collective-permute-start.4
  20.8 6.6 %collective-permute-done.4.refs_2_ = bf16[2,2,32,512]{3,2,1,0:T(8,128)(2,1)S(1)} collective-permute-done((bf16[2,2,32,512]{3,2,1,0:T(8,128)(2,1)}, bf16[2,2,32,512]{3,2,1,0:T(8,128)(2,1)S(1)}, u32[]{:S(2)}, u32[]{:S(2)}) %collective-permute-start.4) | collective-permute-done | bytes 131104 | tf_op jit(solution)/shard_map/ppermute | solution.py:758
  32.1 1.7 collective-permute-done.7.refs_5_
  34.2 2.4 collective-permute-done.8.refs_6_
  37.3 2.0 collective-permute-done.9.refs_7_
  39.9 2.4 collective-permute-start.17
  47.7 9.5 %down.1 = (bf16[8,128,1024]{2,1,0:T(8,128)(2,1)}, f32[8,128,512]{2,1,0:T(8,128)}, f32[8,128,512]{2,1,0:T(8,128)}, f32[8,512]{1,0:T(8,128)}) custom-call(f32[16]{0:T(128)} %select_maximum_fusion.facts_ref.refs_0_, s32[4]{0:T(128)} %pad_add_fusion.1.where_ref, bf16[2,2,32,512]{3,2,1,0:T(8,128)(2,1)} %get-tuple-element.63.refs_0_, ...), custom_call_target="tpu_custom_call" | custom-call | flops 2415919104 | bytes 4718672 | tf_op jit(solution)/shard_map/down/pallas_call | solution.py:150
  59.3 11.1 %mid.1 = (bf16[8,128,512]{2,1,0:T(8,128)(2,1)}, f32[8,128,512]{2,1,0:T(8,128)}, f32[8,512]{1,0:T(8,128)}, f32[8,512]{1,0:T(8,128)}) custom-call(f32[16]{0:T(128)} %select_maximum_fusion.facts_ref.refs_0_, f32[8,128,512]{2,1,0:T(8,128)} %get-tuple-element.67.refs_1_.in_ref, f32[8,512]{1,0:T(8,128)} %get-tuple-element.68.refs_2_.own_d, f32[8,512]{1,0:T(8,128)} %copy-done.75, ...), custom_call_target="tpu_custom_call" | custom-call | flops 4831838208 | bytes 6860864 | tf_op jit(solution)/shard_map/mid/pallas_call | solution.py:150
  72.4 12.1 %first.1 = (bf16[8,128,512]{2,1,0:T(8,128)(2,1)}, f32[8,128,512]{2,1,0:T(8,128)}, f32[8,512]{1,0:T(8,128)}, f32[8,512]{1,0:T(8,128)}) custom-call(f32[16]{0:T(128)} %select_maximum_fusion.facts_ref.refs_0_, f32[8,128,512]{2,1,0:T(8,128)} %get-tuple-element.69.mid_ref, f32[8,128,512]{2,1,0:T(8,128)} %get-tuple-element.70.short_ref, ...), custom_call_target="tpu_custom_call" | custom-call | flops 4831838208 | bytes 8990784 | tf_op jit(solution)/shard_map/first/pallas_call | solution.py:150
  86.5 11.0 %second.1 = (bf16[8,128,512]{2,1,0:T(8,128)(2,1)}, f32[8,128,512]{2,1,0:T(8,128)}, f32[8,512]{1,0:T(8,128)}, f32[8,512]{1,0:T(8,128)}) custom-call(f32[16]{0:T(128)} %select_maximum_fusion.facts_ref.refs_0_, f32[8,128,512]{2,1,0:T(8,128)} %get-tuple-element.72.refs_1_.in_ref, f32[8,512]{1,0:T(8,128)} %get-tuple-element.73.refs_2_, f32[8,512]{1,0:T(8,128)} %copy-done.77, ...), custom_call_target="tpu_custom_call" | custom-call | flops 4831838208 | bytes 6856768 | tf_op jit(solution)/shard_map/second/pallas_call | solution.py:150
  99.5 4.2 %block.1 = (f32[24,512]{1,0:T(8,128)}, f32[8,512]{1,0:T(8,128)}) custom-call(f32[16]{0:T(128)} %select_maximum_fusion.facts_ref.refs_0_, f32[8,128,512]{2,1,0:T(8,128)} %get-tuple-element.74.in_ref.second_ref, bf16[8,128,512]{2,1,0:T(8,128)(2,1)} %get-tuple-element.75.section_ref.act_ref, f32[8,512]{1,0:T(8,128)} %get-tuple-element.76.own_ref, ...), custom_call_target="tpu_custom_call" | custom-call | bytes 3186752 | tf_op jit(solution)/shard_map/block/pallas_call | solution.py:150
  105.8 2.2 logits.1
  114.7 1.8 collective-permute-done.25.c3
  117.1 7.4 %head.1 = (bf16[8,128,512]{2,1,0:T(8,128)(2,1)}, f32[8,512]{1,0:T(8,128)}, f32[48,512]{1,0:T(8,128)}) custom-call(s32[20]{0:T(128)} %picks_ref.1, s32[4]{0:T(128)} %pad_add_fusion.1.where_ref, f32[16]{0:T(128)} %select_maximum_fusion.facts_ref.refs_0_, f32[40,40]{1,0:T(8,128)} %get-tuple-element.79.c0, f32[40,40]{1,0:T(8,128)} %copy-done.51, ...), custom_call_target="tpu_custom_call" | custom-call | bytes 3385248 | tf_op jit(solution)/shard_map/head/pallas_call | solution.py:150
  124.5 11.2 %second_back.1 = (f32[8,128,512]{2,1,0:T(8,128)}, f32[8,512]{1,0:T(8,128)}) custom-call(f32[16]{0:T(128)} %select_maximum_fusion.facts_ref.refs_0_, bf16[8,128,512]{2,1,0:T(8,128)(2,1)} %get-tuple-element.83.low_ref, f32[8,128,512]{2,1,0:T(8,128)} %get-tuple-element.72.refs_1_.in_ref, f32[8,512]{1,0:T(8,128)} %get-tuple-element.84.norm_ref, ...), custom_call_target="tpu_custom_call" | custom-call | flops 4831838208 | bytes 7888960 | tf_op jit(solution)/shard_map/second_back/pallas_call | solution.py:150
  135.8 6.1 %second_grad.1 = (f32[4,9,32,256]{3,2,1,0:T(8,128)}, bf16[4,9,32,256]{3,2,1,0:T(8,128)(2,1)}) custom-call(s32[4]{0:T(128)} %pad_add_fusion.1.where_ref, bf16[8,128,512]{2,1,0:T(8,128)(2,1)} %get-tuple-element.110.act_ref, bf16[8,128,512]{2,1,0:T(8,128)(2,1)} %get-tuple-element.83.low_ref), custom_call_target="tpu_custom_call" | custom-call | flops 1207959552 | bytes 2097168 | tf_op jit(solution)/shard_map/second_grad/pallas_call | solution.py:150
  143.0 16.3 %first_back.1 = (bf16[8,128,512]{2,1,0:T(8,128)(2,1)}, f32[8,128,512]{2,1,0:T(8,128)}, f32[8,512]{1,0:T(8,128)}) custom-call(f32[16]{0:T(128)} %select_maximum_fusion.facts_ref.refs_0_, f32[8,128,512]{2,1,0:T(8,128)} %get-tuple-element.86.up_in, f32[8,128,512]{2,1,0:T(8,128)} %get-tuple-element.72.refs_1_.in_ref, f32[8,512]{1,0:T(8,128)} %get-tuple-element.84.norm_ref, ...), custom_call_target="tpu_custom_call" | custom-call | flops 4831838208 | bytes 16371776 | tf_op jit(solution)/shard_map/first_back/pallas_call | solution.py:150
  159.3 6.1 %first_grad.1 = (f32[4,9,32,256]{3,2,1,0:T(8,128)}, bf16[4,9,32,256]{3,2,1,0:T(8,128)(2,1)}) custom-call(s32[4]{0:T(128)} %pad_add_fusion.1.where_ref, bf16[8,128,512]{2,1,0:T(8,128)(2,1)} %get-tuple-element.75.section_ref.act_ref, bf16[8,128,512]{2,1,0:T(8,128)(2,1)} %get-tuple-element.107.low_ref), custom_call_target="tpu_custom_call" | custom-call | flops 1207959552 | bytes 2097168 | tf_op jit(solution)/shard_map/first_grad/pallas_call | solution.py:150
  167.3 14.6 %mid_back.1 = (bf16[8,128,512]{2,1,0:T(8,128)(2,1)}, bf16[8,128,512]{2,1,0:T(8,128)(2,1)}, f32[8,128,512]{2,1,0:T(8,128)}, f32[8,512]{1,0:T(8,128)}) custom-call(f32[16]{0:T(128)} %select_maximum_fusion.facts_ref.refs_0_, f32[8,128,512]{2,1,0:T(8,128)} %get-tuple-element.90.up_in, f32[8,128,512]{2,1,0:T(8,128)} %get-tuple-element.69.mid_ref, ...), custom_call_target="tpu_custom_call" | custom-call | flops 4831838208 | bytes 13185088 | tf_op jit(solution)/shard_map/mid_back/pallas_call | solution.py:150
  181.9 6.1 %mid_grad.1 = (f32[4,9,32,256]{3,2,1,0:T(8,128)}, bf16[4,9,32,256]{3,2,1,0:T(8,128)(2,1)}) custom-call(s32[4]{0:T(128)} %pad_add_fusion.1.where_ref, bf16[8,128,512]{2,1,0:T(8,128)(2,1)} %get-tuple-element.102.act_ref, bf16[8,128,512]{2,1,0:T(8,128)(2,1)} %get-tuple-element.103.low_ref), custom_call_target="tpu_custom_call" | custom-call | flops 1207959552 | bytes 2097168 | tf_op jit(solution)/shard_map/mid_grad/pallas_call | solution.py:150
  189.4 1.6 collective-permute-start.31
  191.0 5.5 %down_back.1 = (bf16[8,128,512]{2,1,0:T(8,128)(2,1)}, bf16[4,2,2,32,256]{4,3,2,1,0:T(8,128)(2,1)}, bf16[4,2,2,32,256]{4,3,2,1,0:T(8,128)(2,1)}) custom-call(s32[4]{0:T(128)} %pad_add_fusion.1.where_ref, f32[16]{0:T(128)} %select_maximum_fusion.facts_ref.refs_0_, f32[8,128,512]{2,1,0:T(8,128)} %get-tuple-element.93.up_in, ...), custom_call_target="tpu_custom_call" | custom-call | flops 603979776 | bytes 7919696 | tf_op jit(solution)/shard_map/down_back/pallas_call | solution.py:150
  198.1 6.1 %down_grad.1 = (f32[4,5,32,256]{3,2,1,0:T(8,128)}, bf16[4,5,32,256]{3,2,1,0:T(8,128)(2,1)}) custom-call(s32[4]{0:T(128)} %pad_add_fusion.1.where_ref, bf16[8,128,1024]{2,1,0:T(8,128)(2,1)} %get-tuple-element.97.img_ref, bf16[8,128,512]{2,1,0:T(8,128)(2,1)} %get-tuple-element.98.low_ref, bf16[8,128,512]{2,1,0:T(8,128)(2,1)} %get-tuple-element.94.low_s_ref), custom_call_target="tpu_custom_call" | custom-call | flops 603979776 | bytes 4194320 | tf_op jit(solution)/shard_map/down_grad/pallas_call | solution.py:150
  204.3 2.8 collective-permute-start.29
  207.2 2.1 collective-permute-done.29
  209.4 1.8 collective-permute-done.39
  211.2 2.0 collective-permute-start.33
  215.2 5.3 %collective-permute-done.40 = bf16[2,5,32,256]{3,2,1,0:T(8,128)(2,1)S(1)} collective-permute-done((bf16[2,5,32,256]{3,2,1,0:T(8,128)(2,1)S(1)}, bf16[2,5,32,256]{3,2,1,0:T(8,128)(2,1)S(1)}, u32[]{:S(2)}, u32[]{:S(2)}) %collective-permute-start.40) | collective-permute-done | bytes 163872 | tf_op jit(solution)/shard_map/ppermute | solution.py:758
  221.2 2.3 collective-permute-start.37
  225.0 7.1 %collective-permute-done.41 = bf16[5,32,256]{2,1,0:T(8,128)(2,1)S(1)} collective-permute-done((bf16[5,32,256]{2,1,0:T(8,128)(2,1)S(1)}, bf16[5,32,256]{2,1,0:T(8,128)(2,1)S(1)}, u32[]{:S(2)}, u32[]{:S(2)}) %collective-permute-start.41) | collective-permute-done | bytes 81952 | tf_op jit(solution)/shard_map/ppermute | solution.py:758
  232.1 2.2 collective-permute-start.42
  234.6 4.4 %collective-permute-done.42.refs_1_ = bf16[5,32,256]{2,1,0:T(8,128)(2,1)S(1)} collective-permute-done((bf16[5,32,256]{2,1,0:T(8,128)(2,1)S(1)}, bf16[5,32,256]{2,1,0:T(8,128)(2,1)S(1)}, u32[]{:S(2)}, u32[]{:S(2)}) %collective-permute-start.42) | collective-permute-done | bytes 81952 | tf_op jit(solution)/shard_map/ppermute | solution.py:758
  239.0 2.6 collective-permute-start.62
  242.4 7.1 %collective-permute-done.62 = bf16[2,9,32,256]{3,2,1,0:T(8,128)(2,1)S(1)} collective-permute-done((bf16[2,9,32,256]{3,2,1,0:T(8,128)(2,1)S(1)}, bf16[2,9,32,256]{3,2,1,0:T(8,128)(2,1)S(1)}, u32[]{:S(2)}, u32[]{:S(2)}) %collective-permute-start.62) | collective-permute-done | bytes 294944 | tf_op jit(solution)/shard_map/ppermute | solution.py:758
  249.5 2.0 collective-permute-start.43
  251.7 4.1 %collective-permute-done.51 = bf16[2,9,32,256]{3,2,1,0:T(8,128)(2,1)S(1)} collective-permute-done((bf16[2,9,32,256]{3,2,1,0:T(8,128)(2,1)S(1)}, bf16[2,9,32,256]{3,2,1,0:T(8,128)(2,1)S(1)}, u32[]{:S(2)}, u32[]{:S(2)}) %collective-permute-start.51) | collective-permute-done | bytes 294944 | tf_op jit(solution)/shard_map/ppermute | solution.py:758
  255.8 2.7 collective-permute-start.74
  258.6 8.5 %collective-permute-done.74 = bf16[9,32,256]{2,1,0:T(8,128)(2,1)S(1)} collective-permute-done((bf16[9,32,256]{2,1,0:T(8,128)(2,1)S(1)}, bf16[9,32,256]{2,1,0:T(8,128)(2,1)S(1)}, u32[]{:S(2)}, u32[]{:S(2)}) %collective-permute-start.74) | collective-permute-done | bytes 147488 | tf_op jit(solution)/shard_map/ppermute | solution.py:758
  267.2 3.0 collective-permute-start.52
  270.2 9.6 %collective-permute-done.63 = bf16[9,32,256]{2,1,0:T(8,128)(2,1)S(1)} collective-permute-done((bf16[9,32,256]{2,1,0:T(8,128)(2,1)S(1)}, bf16[9,32,256]{2,1,0:T(8,128)(2,1)S(1)}, u32[]{:S(2)}, u32[]{:S(2)}) %collective-permute-start.63) | collective-permute-done | bytes 147488 | tf_op jit(solution)/shard_map/ppermute | solution.py:758
  279.8 2.1 collective-permute-start.34
  282.9 3.7 collective-permute-done.75.refs_1_
  286.6 3.1 collective-permute-start.38
  294.0 2.5 collective-permute-start.76
  299.2 1.7 collective-permute-start.49
  304.0 2.1 collective-permute-done.49.refs_8_
  307.1 1.7 collective-permute-done.53.refs_1_
  310.8 1.7 collective-permute-done.77.refs_3_
  316.1 2.7 collective-permute-done.66.refs_3_
  322.6 1.9 collective-permute-start.69
  326.6 8.4 %collective-permute-done.79.refs_5_ = bf16[2,9,32,256]{3,2,1,0:T(8,128)(2,1)S(1)} collective-permute-done((bf16[2,9,32,256]{3,2,1,0:T(8,128)(2,1)S(1)}, bf16[2,9,32,256]{3,2,1,0:T(8,128)(2,1)S(1)}, u32[]{:S(2)}, u32[]{:S(2)}) %collective-permute-start.79) | collective-permute-done | bytes 294944 | tf_op jit(solution)/shard_map/ppermute | solution.py:758
  337.1 1.9 collective-permute-start.82
  340.2 7.5 %collective-permute-done.68.refs_5_ = bf16[2,9,32,256]{3,2,1,0:T(8,128)(2,1)S(1)} collective-permute-done((bf16[2,9,32,256]{3,2,1,0:T(8,128)(2,1)S(1)}, bf16[2,9,32,256]{3,2,1,0:T(8,128)(2,1)S(1)}, u32[]{:S(2)}, u32[]{:S(2)}) %collective-permute-start.68) | collective-permute-done | bytes 294944 | tf_op jit(solution)/shard_map/ppermute | solution.py:758
  349.6 1.9 collective-permute-start.57
  353.1 2.0 collective-permute-start.60
  356.3 2.1 image_grad.1
  358.5 3.2 down_out.1
  361.8 4.1 %second_out.1 = f32[9,512,256]{2,1,0:T(8,128)} custom-call(s32[4]{0:T(128)} %pad_add_fusion.1.where_ref, bf16[9,32,256]{2,1,0:T(8,128)(2,1)} %copy-done.2, bf16[9,32,256]{2,1,0:T(8,128)(2,1)} %copy-done.10, bf16[2,9,32,256]{3,2,1,0:T(8,128)(2,1)} %copy-done.14, bf16[2,9,32,256]{3,2,1,0:T(8,128)(2,1)} %copy-done.15, bf16[2,9,32,256]{3,2,1,0:T(8,128)(2,1)} %copy-done.17, ...), custom_call_target="tpu_custom_call" | custom-call | bytes 2359312 | tf_op jit(solution)/shard_map/second_out/pallas_call | solution.py:150
  366.7 4.1 %first_out.1 = f32[9,512,256]{2,1,0:T(8,128)} custom-call(s32[4]{0:T(128)} %pad_add_fusion.1.where_ref, bf16[9,32,256]{2,1,0:T(8,128)(2,1)} %copy-done.3, bf16[9,32,256]{2,1,0:T(8,128)(2,1)} %copy-done.11, bf16[2,9,32,256]{3,2,1,0:T(8,128)(2,1)} %copy-done.16, bf16[2,9,32,256]{3,2,1,0:T(8,128)(2,1)} %copy-done.18, bf16[2,9,32,256]{3,2,1,0:T(8,128)(2,1)} %copy-done.20, ...), custom_call_target="tpu_custom_call" | custom-call | bytes 2359312 | tf_op jit(solution)/shard_map/first_out/pallas_call | solution.py:150
  372.5 4.1 %mid_out.1 = f32[9,512,256]{2,1,0:T(8,128)} custom-call(s32[4]{0:T(128)} %pad_add_fusion.1.where_ref, bf16[9,32,256]{2,1,0:T(8,128)(2,1)} %copy-done.4, bf16[9,32,256]{2,1,0:T(8,128)(2,1)} %copy-done.12, bf16[2,9,32,256]{3,2,1,0:T(8,128)(2,1)} %copy-done.19, bf16[2,9,32,256]{3,2,1,0:T(8,128)(2,1)} %copy-done.21, bf16[2,9,32,256]{3,2,1,0:T(8,128)(2,1)} %copy-done.29, ...), custom_call_target="tpu_custom_call" | custom-call | bytes 2359312 | tf_op jit(solution)/shard_map/mid_out/pallas_call | solution.py:150
  (360 shorter events, 79.8 us)
Async XLA Ops:
  3.2 10.8 %collective-permute-start.2 = (s32[5,40]{1,0:T(8,128)S(1)}, s32[5,40]{1,0:T(8,128)S(1)}, u32[]{:S(2)}, u32[]{:S(2)}) collective-permute-start(s32[5,40]{1,0:T(8,128)S(1)} %get-tuple-element.130), channel_id=1, source_target_pairs={{0,12},{4,8},{8,4},{12,0},{1,13},{5,9},{9,5},{13,1},{2,14},{6,10},... | collective-permute-start | bytes 2408 | tf_op jit(solution)/shard_map/ppermute | solution.py:758
  7.2 8.5 %collective-permute-start.1 = (s32[5,40]{1,0:T(8,128)S(1)}, s32[5,40]{1,0:T(8,128)S(1)}, u32[]{:S(2)}, u32[]{:S(2)}) collective-permute-start(s32[5,40]{1,0:T(8,128)S(1)} %get-tuple-element.130), channel_id=1, source_target_pairs={{0,8},{4,12},{8,0},{12,4},{1,9},{5,13},{9,1},{13,5},{2,10},{6,14},... | collective-permute-start | bytes 2408 | tf_op jit(solution)/shard_map/ppermute | solution.py:758
  7.7 10.6 %collective-permute-start = (s32[5,40]{1,0:T(8,128)S(1)}, s32[5,40]{1,0:T(8,128)S(1)}, u32[]{:S(2)}, u32[]{:S(2)}) collective-permute-start(s32[5,40]{1,0:T(8,128)S(1)} %get-tuple-element.130), channel_id=1, source_target_pairs={{0,4},{4,0},{8,12},{12,8},{1,5},{5,1},{9,13},{13,9},{2,6},{6,2},{1... | collective-permute-start | bytes 2408 | tf_op jit(solution)/shard_map/ppermute | solution.py:758
  10.6 17.9 %collective-permute-start.6 = (bf16[2,2,32,512]{3,2,1,0:T(8,128)(2,1)}, bf16[2,2,32,512]{3,2,1,0:T(8,128)(2,1)S(1)}, u32[]{:S(2)}, u32[]{:S(2)}) collective-permute-start(bf16[2,2,32,512]{3,2,1,0:T(8,128)(2,1)} %get-tuple-element.63.refs_0_), channel_id=1, source_target_pairs={{0,4},{4,0},{8,12},{12,8},{1,5},{5,1},{9,13},{13,9},{2,6},{6,2},{1... | collective-permute-start | bytes 393224 | tf_op jit(solution)/shard_map/ppermute | solution.py:758
  12.5 17.5 %collective-permute-start.10 = (bf16[2,2,32,512]{3,2,1,0:T(8,128)(2,1)}, bf16[2,2,32,512]{3,2,1,0:T(8,128)(2,1)S(1)}, u32[]{:S(2)}, u32[]{:S(2)}) collective-permute-start(bf16[2,2,32,512]{3,2,1,0:T(8,128)(2,1)} %get-tuple-element.63.refs_0_), channel_id=1, source_target_pairs={{0,8},{4,12},{8,0},{12,4},{1,9},{5,13},{9,1},{13,5},{2,10},{6,14},... | collective-permute-start | bytes 393224 | tf_op jit(solution)/shard_map/ppermute | solution.py:758
  15.7 11.7 %collective-permute-start.4 = (bf16[2,2,32,512]{3,2,1,0:T(8,128)(2,1)}, bf16[2,2,32,512]{3,2,1,0:T(8,128)(2,1)S(1)}, u32[]{:S(2)}, u32[]{:S(2)}) collective-permute-start(bf16[2,2,32,512]{3,2,1,0:T(8,128)(2,1)} %get-tuple-element.65), channel_id=1, source_target_pairs={{0,2},{1,3},{2,0},{3,1},{4,6},{5,7},{6,4},{7,5},{8,10},{9,11},{10,... | collective-permute-start | bytes 393224 | tf_op jit(solution)/shard_map/ppermute | solution.py:758
  18.3 9.6 %collective-permute-start.5 = (bf16[2,2,32,512]{3,2,1,0:T(8,128)(2,1)}, bf16[2,2,32,512]{3,2,1,0:T(8,128)(2,1)S(1)}, u32[]{:S(2)}, u32[]{:S(2)}) collective-permute-start(bf16[2,2,32,512]{3,2,1,0:T(8,128)(2,1)} %get-tuple-element.66), channel_id=1, source_target_pairs={{0,3},{1,2},{2,1},{3,0},{4,7},{5,6},{6,5},{7,4},{8,11},{9,10},{10,... | collective-permute-start | bytes 393224 | tf_op jit(solution)/shard_map/ppermute | solution.py:758
  20.4 10.2 %collective-permute-start.14 = (bf16[2,2,32,512]{3,2,1,0:T(8,128)(2,1)}, bf16[2,2,32,512]{3,2,1,0:T(8,128)(2,1)S(1)}, u32[]{:S(2)}, u32[]{:S(2)}) collective-permute-start(bf16[2,2,32,512]{3,2,1,0:T(8,128)(2,1)} %get-tuple-element.63.refs_0_), channel_id=1, source_target_pairs={{0,12},{4,8},{8,4},{12,0},{1,13},{5,9},{9,5},{13,1},{2,14},{6,10},... | collective-permute-start | bytes 393224 | tf_op jit(solution)/shard_map/ppermute | solution.py:758
  27.9 12.0 %collective-permute-start.11 = (bf16[2,2,32,512]{3,2,1,0:T(8,128)(2,1)S(1)}, bf16[2,2,32,512]{3,2,1,0:T(8,128)(2,1)S(1)}, u32[]{:S(2)}, u32[]{:S(2)}) collective-permute-start(bf16[2,2,32,512]{3,2,1,0:T(8,128)(2,1)S(1)} %collective-permute-done.3.refs_1_), channel_id=1, source_target_pairs={{0,8},{4,12},{8,0},{12,4},{1,9},{5,13},{9,1},{13,5},{2,10},{6,14},... | collective-permute-start | bytes 393224 | tf_op jit(solution)/shard_map/ppermute | solution.py:758
  28.5 8.1 %collective-permute-start.8 = (bf16[2,2,32,512]{3,2,1,0:T(8,128)(2,1)S(1)}, bf16[2,2,32,512]{3,2,1,0:T(8,128)(2,1)S(1)}, u32[]{:S(2)}, u32[]{:S(2)}) collective-permute-start(bf16[2,2,32,512]{3,2,1,0:T(8,128)(2,1)S(1)} %collective-permute-done.4.refs_2_), channel_id=1, source_target_pairs={{0,4},{4,0},{8,12},{12,8},{1,5},{5,1},{9,13},{13,9},{2,6},{6,2},{1... | collective-permute-start | bytes 393224 | tf_op jit(solution)/shard_map/ppermute | solution.py:758
  30.0 9.4 %collective-permute-start.9 = (bf16[2,2,32,512]{3,2,1,0:T(8,128)(2,1)S(1)}, bf16[2,2,32,512]{3,2,1,0:T(8,128)(2,1)S(1)}, u32[]{:S(2)}, u32[]{:S(2)}) collective-permute-start(bf16[2,2,32,512]{3,2,1,0:T(8,128)(2,1)S(1)} %collective-permute-done.5.refs_3_), channel_id=1, source_target_pairs={{0,4},{4,0},{8,12},{12,8},{1,5},{5,1},{9,13},{13,9},{2,6},{6,2},{1... | collective-permute-start | bytes 393224 | tf_op jit(solution)/shard_map/ppermute | solution.py:758
  30.5 15.7 %collective-permute-start.12 = (bf16[2,2,32,512]{3,2,1,0:T(8,128)(2,1)S(1)}, bf16[2,2,32,512]{3,2,1,0:T(8,128)(2,1)S(1)}, u32[]{:S(2)}, u32[]{:S(2)}) collective-permute-start(bf16[2,2,32,512]{3,2,1,0:T(8,128)(2,1)S(1)} %collective-permute-done.4.refs_2_), channel_id=1, source_target_pairs={{0,8},{4,12},{8,0},{12,4},{1,9},{5,13},{9,1},{13,5},{2,10},{6,14},... | collective-permute-start | bytes 393224 | tf_op jit(solution)/shard_map/ppermute | solution.py:758
  33.8 12.5 %collective-permute-start.13 = (bf16[2,2,32,512]{3,2,1,0:T(8,128)(2,1)S(1)}, bf16[2,2,32,512]{3,2,1,0:T(8,128)(2,1)S(1)}, u32[]{:S(2)}, u32[]{:S(2)}) collective-permute-start(bf16[2,2,32,512]{3,2,1,0:T(8,128)(2,1)S(1)} %collective-permute-done.5.refs_3_), channel_id=1, source_target_pairs={{0,8},{4,12},{8,0},{12,4},{1,9},{5,13},{9,1},{13,5},{2,10},{6,14},... | collective-permute-start | bytes 393224 | tf_op jit(solution)/shard_map/ppermute | solution.py:758
  36.6 9.7 %collective-permute-start.15 = (bf16[2,2,32,512]{3,2,1,0:T(8,128)(2,1)S(1)}, bf16[2,2,32,512]{3,2,1,0:T(8,128)(2,1)S(1)}, u32[]{:S(2)}, u32[]{:S(2)}) collective-permute-start(bf16[2,2,32,512]{3,2,1,0:T(8,128)(2,1)S(1)} %collective-permute-done.3.refs_1_), channel_id=1, source_target_pairs={{0,12},{4,8},{8,4},{12,0},{1,13},{5,9},{9,5},{13,1},{2,14},{6,10},... | collective-permute-start | bytes 393224 | tf_op jit(solution)/shard_map/ppermute | solution.py:758
  39.4 6.9 %collective-permute-start.16 = (bf16[2,2,32,512]{3,2,1,0:T(8,128)(2,1)S(1)}, bf16[2,2,32,512]{3,2,1,0:T(8,128)(2,1)S(1)}, u32[]{:S(2)}, u32[]{:S(2)}) collective-permute-start(bf16[2,2,32,512]{3,2,1,0:T(8,128)(2,1)S(1)} %collective-permute-done.4.refs_2_), channel_id=1, source_target_pairs={{0,12},{4,8},{8,4},{12,0},{1,13},{5,9},{9,5},{13,1},{2,14},{6,10},... | collective-permute-start | bytes 393224 | tf_op jit(solution)/shard_map/ppermute | solution.py:758
  141.9 79.2 %collective-permute-start.72 = (bf16[4,9,32,256]{3,2,1,0:T(8,128)(2,1)}, bf16[4,9,32,256]{3,2,1,0:T(8,128)(2,1)S(1)}, u32[]{:S(2)}, u32[]{:S(2)}) collective-permute-start(bf16[4,9,32,256]{3,2,1,0:T(8,128)(2,1)} %get-tuple-element.112), channel_id=1, source_target_pairs={{0,16},{16,0},{1,17},{17,1},{2,18},{18,2},{3,19},{19,3},{4,20},{20... | collective-permute-start | bytes 1769480 | tf_op jit(solution)/shard_map/ppermute | solution.py:758
  159.3 7.4 %collective-permute-start.27 = (f32[8,512]{1,0:T(8,128)}, f32[8,512]{1,0:T(8,128)S(1)}, u32[]{:S(2)}, u32[]{:S(2)}) collective-permute-start(f32[8,512]{1,0:T(8,128)} %get-tuple-element.89.own_ref), channel_id=1, source_target_pairs={{0,16},{16,0},{1,17},{17,1},{2,18},{18,2},{3,19},{19,3},{4,20},{20... | collective-permute-start | bytes 49160 | tf_op jit(solution)/shard_map/ppermute | solution.py:758
  165.5 58.2 %collective-permute-start.61 = (bf16[4,9,32,256]{3,2,1,0:T(8,128)(2,1)}, bf16[4,9,32,256]{3,2,1,0:T(8,128)(2,1)S(1)}, u32[]{:S(2)}, u32[]{:S(2)}) collective-permute-start(bf16[4,9,32,256]{3,2,1,0:T(8,128)(2,1)} %get-tuple-element.109), channel_id=1, source_target_pairs={{0,16},{16,0},{1,17},{17,1},{2,18},{18,2},{3,19},{19,3},{4,20},{20... | collective-permute-start | bytes 1769480 | tf_op jit(solution)/shard_map/ppermute | solution.py:758
  188.1 44.0 %collective-permute-start.50 = (bf16[4,9,32,256]{3,2,1,0:T(8,128)(2,1)}, bf16[4,9,32,256]{3,2,1,0:T(8,128)(2,1)S(1)}, u32[]{:S(2)}, u32[]{:S(2)}) collective-permute-start(bf16[4,9,32,256]{3,2,1,0:T(8,128)(2,1)} %get-tuple-element.105), channel_id=1, source_target_pairs={{0,16},{16,0},{1,17},{17,1},{2,18},{18,2},{3,19},{19,3},{4,20},{20... | collective-permute-start | bytes 1769480 | tf_op jit(solution)/shard_map/ppermute | solution.py:758
  189.4 14.9 %collective-permute-start.31 = (f32[59,256]{1,0:T(8,128)S(1)}, f32[59,256]{1,0:T(8,128)S(1)}, u32[]{:S(2)}, u32[]{:S(2)}) collective-permute-start(f32[59,256]{1,0:T(8,128)S(1)} %pad_maximum_fusion.4), channel_id=1, source_target_pairs={{0,3},{1,2},{2,1},{3,0},{4,7},{5,6},{6,5},{7,4},{8,11},{9,10},{10,... | collective-permute-start | bytes 181256 | tf_op jit(solution)/shard_map/ppermute | solution.py:758
  191.0 16.1 %collective-permute-start.30 = (f32[59,256]{1,0:T(8,128)S(1)}, f32[59,256]{1,0:T(8,128)S(1)}, u32[]{:S(2)}, u32[]{:S(2)}) collective-permute-start(f32[59,256]{1,0:T(8,128)S(1)} %pad_maximum_fusion.4), channel_id=1, source_target_pairs={{0,2},{1,3},{2,0},{3,1},{4,6},{5,7},{6,4},{7,5},{8,10},{9,11},{10,... | collective-permute-start | bytes 181256 | tf_op jit(solution)/shard_map/ppermute | solution.py:758
  207.1 7.3 %collective-permute-start.32 = (bf16[4,2,2,32,256]{4,3,2,1,0:T(8,128)(2,1)S(1)}, bf16[4,2,2,32,256]{4,3,2,1,0:T(8,128)(2,1)S(1)}, u32[]{:S(2)}, u32[]{:S(2)}) collective-permute-start(bf16[4,2,2,32,256]{4,3,2,1,0:T(8,128)(2,1)S(1)} %copy-done.59), channel_id=1, source_target_pairs={{0,16},{16,0},{1,17},{17,1},{2,18},{18,2},{3,19},{19,3},{4,20},{20... | collective-permute-start | bytes 786440 | tf_op jit(solution)/shard_map/ppermute | solution.py:758
  211.2 56.0 %collective-permute-start.33 = (bf16[2,2,32,256]{3,2,1,0:T(8,128)(2,1)S(1)}, bf16[2,2,32,256]{3,2,1,0:T(8,128)(2,1)S(1)}, u32[]{:S(2)}, u32[]{:S(2)}) collective-permute-start(bf16[2,2,32,256]{3,2,1,0:T(8,128)(2,1)S(1)} %get-tuple-element.119), channel_id=1, source_target_pairs={{0,1},{1,0},{2,3},{3,2},{4,5},{5,4},{6,7},{7,6},{8,9},{9,8},{10,11... | collective-permute-start | bytes 196616 | tf_op jit(solution)/shard_map/ppermute | solution.py:758
  220.4 59.3 %collective-permute-start.35 = (bf16[2,2,32,256]{3,2,1,0:T(8,128)(2,1)S(1)}, bf16[2,2,32,256]{3,2,1,0:T(8,128)(2,1)S(1)}, u32[]{:S(2)}, u32[]{:S(2)}) collective-permute-start(bf16[2,2,32,256]{3,2,1,0:T(8,128)(2,1)S(1)} %get-tuple-element.118), channel_id=1, source_target_pairs={{0,2},{1,3},{2,0},{3,1},{4,6},{5,7},{6,4},{7,5},{8,10},{9,11},{10,... | collective-permute-start | bytes 196616 | tf_op jit(solution)/shard_map/ppermute | solution.py:758
  221.2 60.7 %collective-permute-start.37 = (bf16[2,2,32,256]{3,2,1,0:T(8,128)(2,1)S(1)}, bf16[2,2,32,256]{3,2,1,0:T(8,128)(2,1)S(1)}, u32[]{:S(2)}, u32[]{:S(2)}) collective-permute-start(bf16[2,2,32,256]{3,2,1,0:T(8,128)(2,1)S(1)} %get-tuple-element.117), channel_id=1, source_target_pairs={{0,3},{1,2},{2,1},{3,0},{4,7},{5,6},{6,5},{7,4},{8,11},{9,10},{10,... | collective-permute-start | bytes 196616 | tf_op jit(solution)/shard_map/ppermute | solution.py:758
  223.7 8.3 %collective-permute-start.41 = (bf16[5,32,256]{2,1,0:T(8,128)(2,1)S(1)}, bf16[5,32,256]{2,1,0:T(8,128)(2,1)S(1)}, u32[]{:S(2)}, u32[]{:S(2)}) collective-permute-start(bf16[5,32,256]{2,1,0:T(8,128)(2,1)S(1)} %fusion.11), channel_id=1, source_target_pairs={{0,2},{1,3},{2,0},{3,1},{4,6},{5,7},{6,4},{7,5},{8,10},{9,11},{10,... | collective-permute-start | bytes 245768 | tf_op jit(solution)/shard_map/ppermute | solution.py:758
  232.1 10.3 %collective-permute-start.73 = (bf16[2,9,32,256]{3,2,1,0:T(8,128)(2,1)S(1)}, bf16[2,9,32,256]{3,2,1,0:T(8,128)(2,1)S(1)}, u32[]{:S(2)}, u32[]{:S(2)}) collective-permute-start(bf16[2,9,32,256]{3,2,1,0:T(8,128)(2,1)S(1)} %slice.322), channel_id=1, source_target_pairs={{0,1},{1,0},{2,3},{3,2},{4,5},{5,4},{6,7},{7,6},{8,9},{9,8},{10,11... | collective-permute-start | bytes 884744 | tf_op jit(solution)/shard_map/ppermute | solution.py:758
  232.1 6.9 %collective-permute-start.42 = (bf16[5,32,256]{2,1,0:T(8,128)(2,1)S(1)}, bf16[5,32,256]{2,1,0:T(8,128)(2,1)S(1)}, u32[]{:S(2)}, u32[]{:S(2)}) collective-permute-start(bf16[5,32,256]{2,1,0:T(8,128)(2,1)S(1)} %fusion.7.refs_0_), channel_id=1, source_target_pairs={{0,2},{1,3},{2,0},{3,1},{4,6},{5,7},{6,4},{7,5},{8,10},{9,11},{10,... | collective-permute-start | bytes 245768 | tf_op jit(solution)/shard_map/ppermute | solution.py:758
  239.0 10.5 %collective-permute-start.62 = (bf16[2,9,32,256]{3,2,1,0:T(8,128)(2,1)S(1)}, bf16[2,9,32,256]{3,2,1,0:T(8,128)(2,1)S(1)}, u32[]{:S(2)}, u32[]{:S(2)}) collective-permute-start(bf16[2,9,32,256]{3,2,1,0:T(8,128)(2,1)S(1)} %slice.323), channel_id=1, source_target_pairs={{0,1},{1,0},{2,3},{3,2},{4,5},{5,4},{6,7},{7,6},{8,9},{9,8},{10,11... | collective-permute-start | bytes 884744 | tf_op jit(solution)/shard_map/ppermute | solution.py:758
  242.3 13.4 %collective-permute-start.51 = (bf16[2,9,32,256]{3,2,1,0:T(8,128)(2,1)S(1)}, bf16[2,9,32,256]{3,2,1,0:T(8,128)(2,1)S(1)}, u32[]{:S(2)}, u32[]{:S(2)}) collective-permute-start(bf16[2,9,32,256]{3,2,1,0:T(8,128)(2,1)S(1)} %slice.324), channel_id=1, source_target_pairs={{0,1},{1,0},{2,3},{3,2},{4,5},{5,4},{6,7},{7,6},{8,9},{9,8},{10,11... | collective-permute-start | bytes 884744 | tf_op jit(solution)/shard_map/ppermute | solution.py:758
  249.5 41.9 %collective-permute-start.43 = (bf16[2,5,32,256]{3,2,1,0:T(8,128)(2,1)S(1)}, bf16[2,5,32,256]{3,2,1,0:T(8,128)(2,1)S(1)}, u32[]{:S(2)}, u32[]{:S(2)}) collective-permute-start(bf16[2,5,32,256]{3,2,1,0:T(8,128)(2,1)S(1)} %pad_maximum_fusion.3), channel_id=1, source_target_pairs={{0,1},{1,0},{2,3},{3,2},{4,5},{5,4},{6,7},{7,6},{8,9},{9,8},{10,11... | collective-permute-start | bytes 491528 | tf_op jit(solution)/shard_map/ppermute | solution.py:758
  255.8 11.3 %collective-permute-start.74 = (bf16[9,32,256]{2,1,0:T(8,128)(2,1)S(1)}, bf16[9,32,256]{2,1,0:T(8,128)(2,1)S(1)}, u32[]{:S(2)}, u32[]{:S(2)}) collective-permute-start(bf16[9,32,256]{2,1,0:T(8,128)(2,1)S(1)} %fusion.10), channel_id=1, source_target_pairs={{0,2},{1,3},{2,0},{3,1},{4,6},{5,7},{6,4},{7,5},{8,10},{9,11},{10,... | collective-permute-start | bytes 442376 | tf_op jit(solution)/shard_map/ppermute | solution.py:758
  267.1 12.6 %collective-permute-start.63 = (bf16[9,32,256]{2,1,0:T(8,128)(2,1)S(1)}, bf16[9,32,256]{2,1,0:T(8,128)(2,1)S(1)}, u32[]{:S(2)}, u32[]{:S(2)}) collective-permute-start(bf16[9,32,256]{2,1,0:T(8,128)(2,1)S(1)} %fusion.9), channel_id=1, source_target_pairs={{0,2},{1,3},{2,0},{3,1},{4,6},{5,7},{6,4},{7,5},{8,10},{9,11},{10,... | collective-permute-start | bytes 442376 | tf_op jit(solution)/shard_map/ppermute | solution.py:758
  267.2 26.8 %collective-permute-start.52 = (bf16[9,32,256]{2,1,0:T(8,128)(2,1)S(1)}, bf16[9,32,256]{2,1,0:T(8,128)(2,1)S(1)}, u32[]{:S(2)}, u32[]{:S(2)}) collective-permute-start(bf16[9,32,256]{2,1,0:T(8,128)(2,1)S(1)} %fusion.8), channel_id=1, source_target_pairs={{0,2},{1,3},{2,0},{3,1},{4,6},{5,7},{6,4},{7,5},{8,10},{9,11},{10,... | collective-permute-start | bytes 442376 | tf_op jit(solution)/shard_map/ppermute | solution.py:758
  279.7 6.9 %collective-permute-start.75 = (bf16[9,32,256]{2,1,0:T(8,128)(2,1)S(1)}, bf16[9,32,256]{2,1,0:T(8,128)(2,1)S(1)}, u32[]{:S(2)}, u32[]{:S(2)}) collective-permute-start(bf16[9,32,256]{2,1,0:T(8,128)(2,1)S(1)} %fusion.1.refs_0_), channel_id=1, source_target_pairs={{0,2},{1,3},{2,0},{3,1},{4,6},{5,7},{6,4},{7,5},{8,10},{9,11},{10,... | collective-permute-start | bytes 442376 | tf_op jit(solution)/shard_map/ppermute | solution.py:758
  279.8 9.9 %collective-permute-start.34 = (bf16[2,2,32,256]{3,2,1,0:T(8,128)(2,1)S(1)}, bf16[2,2,32,256]{3,2,1,0:T(8,128)(2,1)S(1)}, u32[]{:S(2)}, u32[]{:S(2)}) collective-permute-start(bf16[2,2,32,256]{3,2,1,0:T(8,128)(2,1)S(1)} %get-tuple-element.115), channel_id=1, source_target_pairs={{0,1},{1,0},{2,3},{3,2},{4,5},{5,4},{6,7},{7,6},{8,9},{9,8},{10,11... | collective-permute-start | bytes 196616 | tf_op jit(solution)/shard_map/ppermute | solution.py:758
  281.9 8.4 %collective-permute-start.36 = (bf16[2,2,32,256]{3,2,1,0:T(8,128)(2,1)S(1)}, bf16[2,2,32,256]{3,2,1,0:T(8,128)(2,1)S(1)}, u32[]{:S(2)}, u32[]{:S(2)}) collective-permute-start(bf16[2,2,32,256]{3,2,1,0:T(8,128)(2,1)S(1)} %get-tuple-element.114), channel_id=1, source_target_pairs={{0,2},{1,3},{2,0},{3,1},{4,6},{5,7},{6,4},{7,5},{8,10},{9,11},{10,... | collective-permute-start | bytes 196616 | tf_op jit(solution)/shard_map/ppermute | solution.py:758
  290.3 6.8 %collective-permute-start.45 = (bf16[2,5,32,256]{3,2,1,0:T(8,128)(2,1)S(1)}, bf16[2,5,32,256]{3,2,1,0:T(8,128)(2,1)S(1)}, u32[]{:S(2)}, u32[]{:S(2)}) collective-permute-start(bf16[2,5,32,256]{3,2,1,0:T(8,128)(2,1)S(1)} %pad_maximum_fusion.3), channel_id=1, source_target_pairs={{0,8},{4,12},{8,0},{12,4},{1,9},{5,13},{9,1},{13,5},{2,10},{6,14},... | collective-permute-start | bytes 491528 | tf_op jit(solution)/shard_map/ppermute | solution.py:758
  291.4 7.8 %collective-permute-start.48 = (bf16[2,5,32,256]{3,2,1,0:T(8,128)(2,1)S(1)}, bf16[2,5,32,256]{3,2,1,0:T(8,128)(2,1)S(1)}, u32[]{:S(2)}, u32[]{:S(2)}) collective-permute-start(bf16[2,5,32,256]{3,2,1,0:T(8,128)(2,1)S(1)} %collective-permute-done.43.refs_2_), channel_id=1, source_target_pairs={{0,8},{4,12},{8,0},{12,4},{1,9},{5,13},{9,1},{13,5},{2,10},{6,14},... | collective-permute-start | bytes 491528 | tf_op jit(solution)/shard_map/ppermute | solution.py:758
  293.4 8.0 %collective-permute-start.64 = (bf16[9,32,256]{2,1,0:T(8,128)(2,1)S(1)}, bf16[9,32,256]{2,1,0:T(8,128)(2,1)S(1)}, u32[]{:S(2)}, u32[]{:S(2)}) collective-permute-start(bf16[9,32,256]{2,1,0:T(8,128)(2,1)S(1)} %fusion.3.refs_0_), channel_id=1, source_target_pairs={{0,2},{1,3},{2,0},{3,1},{4,6},{5,7},{6,4},{7,5},{8,10},{9,11},{10,... | collective-permute-start | bytes 442376 | tf_op jit(solution)/shard_map/ppermute | solution.py:758
  294.0 15.5 %collective-permute-start.76 = (bf16[2,9,32,256]{3,2,1,0:T(8,128)(2,1)S(1)}, bf16[2,9,32,256]{3,2,1,0:T(8,128)(2,1)S(1)}, u32[]{:S(2)}, u32[]{:S(2)}) collective-permute-start(bf16[2,9,32,256]{3,2,1,0:T(8,128)(2,1)S(1)} %pad_maximum_fusion.2), channel_id=1, source_target_pairs={{0,1},{1,0},{2,3},{3,2},{4,5},{5,4},{6,7},{7,6},{8,9},{9,8},{10,11... | collective-permute-start | bytes 884744 | tf_op jit(solution)/shard_map/ppermute | solution.py:758
  296.6 7.4 %collective-permute-start.47 = (bf16[2,5,32,256]{3,2,1,0:T(8,128)(2,1)S(1)}, bf16[2,5,32,256]{3,2,1,0:T(8,128)(2,1)S(1)}, u32[]{:S(2)}, u32[]{:S(2)}) collective-permute-start(bf16[2,5,32,256]{3,2,1,0:T(8,128)(2,1)S(1)} %collective-permute-done.43.refs_2_), channel_id=1, source_target_pairs={{0,4},{4,0},{8,12},{12,8},{1,5},{5,1},{9,13},{13,9},{2,6},{6,2},{1... | collective-permute-start | bytes 491528 | tf_op jit(solution)/shard_map/ppermute | solution.py:758
  299.2 6.9 %collective-permute-start.49 = (bf16[2,5,32,256]{3,2,1,0:T(8,128)(2,1)S(1)}, bf16[2,5,32,256]{3,2,1,0:T(8,128)(2,1)S(1)}, u32[]{:S(2)}, u32[]{:S(2)}) collective-permute-start(bf16[2,5,32,256]{3,2,1,0:T(8,128)(2,1)S(1)} %collective-permute-done.48.refs_7_), channel_id=1, source_target_pairs={{0,4},{4,0},{8,12},{12,8},{1,5},{5,1},{9,13},{13,9},{2,6},{6,2},{1... | collective-permute-start | bytes 491528 | tf_op jit(solution)/shard_map/ppermute | solution.py:758
  301.4 7.4 %collective-permute-start.53 = (bf16[9,32,256]{2,1,0:T(8,128)(2,1)S(1)}, bf16[9,32,256]{2,1,0:T(8,128)(2,1)S(1)}, u32[]{:S(2)}, u32[]{:S(2)}) collective-permute-start(bf16[9,32,256]{2,1,0:T(8,128)(2,1)S(1)} %fusion.5.refs_0_), channel_id=1, source_target_pairs={{0,2},{1,3},{2,0},{3,1},{4,6},{5,7},{6,4},{7,5},{8,10},{9,11},{10,... | collective-permute-start | bytes 442376 | tf_op jit(solution)/shard_map/ppermute | solution.py:758
  302.5 10.0 %collective-permute-start.77 = (bf16[2,9,32,256]{3,2,1,0:T(8,128)(2,1)S(1)}, bf16[2,9,32,256]{3,2,1,0:T(8,128)(2,1)S(1)}, u32[]{:S(2)}, u32[]{:S(2)}) collective-permute-start(bf16[2,9,32,256]{3,2,1,0:T(8,128)(2,1)S(1)} %pad_maximum_fusion.2), channel_id=1, source_target_pairs={{0,4},{4,0},{8,12},{12,8},{1,5},{5,1},{9,13},{13,9},{2,6},{6,2},{1... | collective-permute-start | bytes 884744 | tf_op jit(solution)/shard_map/ppermute | solution.py:758
  304.0 10.1 %collective-permute-start.78 = (bf16[2,9,32,256]{3,2,1,0:T(8,128)(2,1)S(1)}, bf16[2,9,32,256]{3,2,1,0:T(8,128)(2,1)S(1)}, u32[]{:S(2)}, u32[]{:S(2)}) collective-permute-start(bf16[2,9,32,256]{3,2,1,0:T(8,128)(2,1)S(1)} %pad_maximum_fusion.2), channel_id=1, source_target_pairs={{0,8},{4,12},{8,0},{12,4},{1,9},{5,13},{9,1},{13,5},{2,10},{6,14},... | collective-permute-start | bytes 884744 | tf_op jit(solution)/shard_map/ppermute | solution.py:758
  306.1 9.2 %collective-permute-start.65 = (bf16[2,9,32,256]{3,2,1,0:T(8,128)(2,1)S(1)}, bf16[2,9,32,256]{3,2,1,0:T(8,128)(2,1)S(1)}, u32[]{:S(2)}, u32[]{:S(2)}) collective-permute-start(bf16[2,9,32,256]{3,2,1,0:T(8,128)(2,1)S(1)} %pad_maximum_fusion.1), channel_id=1, source_target_pairs={{0,1},{1,0},{2,3},{3,2},{4,5},{5,4},{6,7},{7,6},{8,9},{9,8},{10,11... | collective-permute-start | bytes 884744 | tf_op jit(solution)/shard_map/ppermute | solution.py:758
  308.8 9.9 %collective-permute-start.66 = (bf16[2,9,32,256]{3,2,1,0:T(8,128)(2,1)S(1)}, bf16[2,9,32,256]{3,2,1,0:T(8,128)(2,1)S(1)}, u32[]{:S(2)}, u32[]{:S(2)}) collective-permute-start(bf16[2,9,32,256]{3,2,1,0:T(8,128)(2,1)S(1)} %pad_maximum_fusion.1), channel_id=1, source_target_pairs={{0,4},{4,0},{8,12},{12,8},{1,5},{5,1},{9,13},{13,9},{2,6},{6,2},{1... | collective-permute-start | bytes 884744 | tf_op jit(solution)/shard_map/ppermute | solution.py:758
  309.5 10.7 %collective-permute-start.67 = (bf16[2,9,32,256]{3,2,1,0:T(8,128)(2,1)S(1)}, bf16[2,9,32,256]{3,2,1,0:T(8,128)(2,1)S(1)}, u32[]{:S(2)}, u32[]{:S(2)}) collective-permute-start(bf16[2,9,32,256]{3,2,1,0:T(8,128)(2,1)S(1)} %pad_maximum_fusion.1), channel_id=1, source_target_pairs={{0,8},{4,12},{8,0},{12,4},{1,9},{5,13},{9,1},{13,5},{2,10},{6,14},... | collective-permute-start | bytes 884744 | tf_op jit(solution)/shard_map/ppermute | solution.py:758
  312.5 10.1 %collective-permute-start.54 = (bf16[2,9,32,256]{3,2,1,0:T(8,128)(2,1)S(1)}, bf16[2,9,32,256]{3,2,1,0:T(8,128)(2,1)S(1)}, u32[]{:S(2)}, u32[]{:S(2)}) collective-permute-start(bf16[2,9,32,256]{3,2,1,0:T(8,128)(2,1)S(1)} %pad_maximum_fusion), channel_id=1, source_target_pairs={{0,1},{1,0},{2,3},{3,2},{4,5},{5,4},{6,7},{7,6},{8,9},{9,8},{10,11... | collective-permute-start | bytes 884744 | tf_op jit(solution)/shard_map/ppermute | solution.py:758
  314.1 11.0 %collective-permute-start.55 = (bf16[2,9,32,256]{3,2,1,0:T(8,128)(2,1)S(1)}, bf16[2,9,32,256]{3,2,1,0:T(8,128)(2,1)S(1)}, u32[]{:S(2)}, u32[]{:S(2)}) collective-permute-start(bf16[2,9,32,256]{3,2,1,0:T(8,128)(2,1)S(1)} %pad_maximum_fusion), channel_id=1, source_target_pairs={{0,4},{4,0},{8,12},{12,8},{1,5},{5,1},{9,13},{13,9},{2,6},{6,2},{1... | collective-permute-start | bytes 884744 | tf_op jit(solution)/shard_map/ppermute | solution.py:758
  315.3 21.2 %collective-permute-start.80 = (bf16[2,9,32,256]{3,2,1,0:T(8,128)(2,1)S(1)}, bf16[2,9,32,256]{3,2,1,0:T(8,128)(2,1)S(1)}, u32[]{:S(2)}, u32[]{:S(2)}) collective-permute-start(bf16[2,9,32,256]{3,2,1,0:T(8,128)(2,1)S(1)} %collective-permute-done.76.refs_2_), channel_id=1, source_target_pairs={{0,4},{4,0},{8,12},{12,8},{1,5},{5,1},{9,13},{13,9},{2,6},{6,2},{1... | collective-permute-start | bytes 884744 | tf_op jit(solution)/shard_map/ppermute | solution.py:758
  318.8 18.3 %collective-permute-start.81 = (bf16[2,9,32,256]{3,2,1,0:T(8,128)(2,1)S(1)}, bf16[2,9,32,256]{3,2,1,0:T(8,128)(2,1)S(1)}, u32[]{:S(2)}, u32[]{:S(2)}) collective-permute-start(bf16[2,9,32,256]{3,2,1,0:T(8,128)(2,1)S(1)} %collective-permute-done.76.refs_2_), channel_id=1, source_target_pairs={{0,8},{4,12},{8,0},{12,4},{1,9},{5,13},{9,1},{13,5},{2,10},{6,14},... | collective-permute-start | bytes 884744 | tf_op jit(solution)/shard_map/ppermute | solution.py:758
  320.3 14.8 %collective-permute-start.79 = (bf16[2,9,32,256]{3,2,1,0:T(8,128)(2,1)S(1)}, bf16[2,9,32,256]{3,2,1,0:T(8,128)(2,1)S(1)}, u32[]{:S(2)}, u32[]{:S(2)}) collective-permute-start(bf16[2,9,32,256]{3,2,1,0:T(8,128)(2,1)S(1)} %collective-permute-done.77.refs_3_), channel_id=1, source_target_pairs={{0,8},{4,12},{8,0},{12,4},{1,9},{5,13},{9,1},{13,5},{2,10},{6,14},... | collective-permute-start | bytes 884744 | tf_op jit(solution)/shard_map/ppermute | solution.py:758
  322.6 26.6 %collective-permute-start.69 = (bf16[2,9,32,256]{3,2,1,0:T(8,128)(2,1)S(1)}, bf16[2,9,32,256]{3,2,1,0:T(8,128)(2,1)S(1)}, u32[]{:S(2)}, u32[]{:S(2)}) collective-permute-start(bf16[2,9,32,256]{3,2,1,0:T(8,128)(2,1)S(1)} %collective-permute-done.65.refs_2_), channel_id=1, source_target_pairs={{0,4},{4,0},{8,12},{12,8},{1,5},{5,1},{9,13},{13,9},{2,6},{6,2},{1... | collective-permute-start | bytes 884744 | tf_op jit(solution)/shard_map/ppermute | solution.py:758
  325.1 24.5 %collective-permute-start.70 = (bf16[2,9,32,256]{3,2,1,0:T(8,128)(2,1)S(1)}, bf16[2,9,32,256]{3,2,1,0:T(8,128)(2,1)S(1)}, u32[]{:S(2)}, u32[]{:S(2)}) collective-permute-start(bf16[2,9,32,256]{3,2,1,0:T(8,128)(2,1)S(1)} %collective-permute-done.65.refs_2_), channel_id=1, source_target_pairs={{0,8},{4,12},{8,0},{12,4},{1,9},{5,13},{9,1},{13,5},{2,10},{6,14},... | collective-permute-start | bytes 884744 | tf_op jit(solution)/shard_map/ppermute | solution.py:758
  335.0 12.6 %collective-permute-start.68 = (bf16[2,9,32,256]{3,2,1,0:T(8,128)(2,1)S(1)}, bf16[2,9,32,256]{3,2,1,0:T(8,128)(2,1)S(1)}, u32[]{:S(2)}, u32[]{:S(2)}) collective-permute-start(bf16[2,9,32,256]{3,2,1,0:T(8,128)(2,1)S(1)} %collective-permute-done.66.refs_3_), channel_id=1, source_target_pairs={{0,8},{4,12},{8,0},{12,4},{1,9},{5,13},{9,1},{13,5},{2,10},{6,14},... | collective-permute-start | bytes 884744 | tf_op jit(solution)/shard_map/ppermute | solution.py:758
  336.5 16.6 %collective-permute-start.59 = (bf16[2,9,32,256]{3,2,1,0:T(8,128)(2,1)S(1)}, bf16[2,9,32,256]{3,2,1,0:T(8,128)(2,1)S(1)}, u32[]{:S(2)}, u32[]{:S(2)}) collective-permute-start(bf16[2,9,32,256]{3,2,1,0:T(8,128)(2,1)S(1)} %collective-permute-done.54.refs_2_), channel_id=1, source_target_pairs={{0,8},{4,12},{8,0},{12,4},{1,9},{5,13},{9,1},{13,5},{2,10},{6,14},... | collective-permute-start | bytes 884744 | tf_op jit(solution)/shard_map/ppermute | solution.py:758
  337.1 16.0 %collective-permute-start.82 = (bf16[2,9,32,256]{3,2,1,0:T(8,128)(2,1)S(1)}, bf16[2,9,32,256]{3,2,1,0:T(8,128)(2,1)S(1)}, u32[]{:S(2)}, u32[]{:S(2)}) collective-permute-start(bf16[2,9,32,256]{3,2,1,0:T(8,128)(2,1)S(1)} %collective-permute-done.81.refs_7_), channel_id=1, source_target_pairs={{0,4},{4,0},{8,12},{12,8},{1,5},{5,1},{9,13},{13,9},{2,6},{6,2},{1... | collective-permute-start | bytes 884744 | tf_op jit(solution)/shard_map/ppermute | solution.py:758
  347.7 23.1 %collective-permute-start.56 = (bf16[2,9,32,256]{3,2,1,0:T(8,128)(2,1)S(1)}, bf16[2,9,32,256]{3,2,1,0:T(8,128)(2,1)S(1)}, u32[]{:S(2)}, u32[]{:S(2)}) collective-permute-start(bf16[2,9,32,256]{3,2,1,0:T(8,128)(2,1)S(1)} %pad_maximum_fusion), channel_id=1, source_target_pairs={{0,8},{4,12},{8,0},{12,4},{1,9},{5,13},{9,1},{13,5},{2,10},{6,14},... | collective-permute-start | bytes 884744 | tf_op jit(solution)/shard_map/ppermute | solution.py:758
  349.2 21.7 %collective-permute-start.58 = (bf16[2,9,32,256]{3,2,1,0:T(8,128)(2,1)S(1)}, bf16[2,9,32,256]{3,2,1,0:T(8,128)(2,1)S(1)}, u32[]{:S(2)}, u32[]{:S(2)}) collective-permute-start(bf16[2,9,32,256]{3,2,1,0:T(8,128)(2,1)S(1)} %collective-permute-done.54.refs_2_), channel_id=1, source_target_pairs={{0,4},{4,0},{8,12},{12,8},{1,5},{5,1},{9,13},{13,9},{2,6},{6,2},{1... | collective-permute-start | bytes 884744 | tf_op jit(solution)/shard_map/ppermute | solution.py:758
  349.6 21.2 %collective-permute-start.57 = (bf16[2,9,32,256]{3,2,1,0:T(8,128)(2,1)S(1)}, bf16[2,9,32,256]{3,2,1,0:T(8,128)(2,1)S(1)}, u32[]{:S(2)}, u32[]{:S(2)}) collective-permute-start(bf16[2,9,32,256]{3,2,1,0:T(8,128)(2,1)S(1)} %collective-permute-done.55.refs_3_), channel_id=1, source_target_pairs={{0,8},{4,12},{8,0},{12,4},{1,9},{5,13},{9,1},{13,5},{2,10},{6,14},... | collective-permute-start | bytes 884744 | tf_op jit(solution)/shard_map/ppermute | solution.py:758
  353.1 12.9 %collective-permute-start.71 = (bf16[2,9,32,256]{3,2,1,0:T(8,128)(2,1)S(1)}, bf16[2,9,32,256]{3,2,1,0:T(8,128)(2,1)S(1)}, u32[]{:S(2)}, u32[]{:S(2)}) collective-permute-start(bf16[2,9,32,256]{3,2,1,0:T(8,128)(2,1)S(1)} %collective-permute-done.70.refs_7_), channel_id=1, source_target_pairs={{0,4},{4,0},{8,12},{12,8},{1,5},{5,1},{9,13},{13,9},{2,6},{6,2},{1... | collective-permute-start | bytes 884744 | tf_op jit(solution)/shard_map/ppermute | solution.py:758
  353.1 17.7 %collective-permute-start.60 = (bf16[2,9,32,256]{3,2,1,0:T(8,128)(2,1)S(1)}, bf16[2,9,32,256]{3,2,1,0:T(8,128)(2,1)S(1)}, u32[]{:S(2)}, u32[]{:S(2)}) collective-permute-start(bf16[2,9,32,256]{3,2,1,0:T(8,128)(2,1)S(1)} %collective-permute-done.59.refs_7_), channel_id=1, source_target_pairs={{0,4},{4,0},{8,12},{12,8},{1,5},{5,1},{9,13},{13,9},{2,6},{6,2},{1... | collective-permute-start | bytes 884744 | tf_op jit(solution)/shard_map/ppermute | solution.py:758
  (97 other events, 1605.6 us)

commit v3 on v2

--- a/solution.py
+++ b/solution.py
@@ -137,28 +137,40 @@
     return low, cross_sum, grad_sum
 
 
-MESH_LIMIT = 56 * 2**20
+KERNEL_LIMIT = 24 * 2**20
 VM = pl.BlockSpec(memory_space=pltpu.VMEM)
 SM = pl.BlockSpec(memory_space=pltpu.SMEM)
 NT = (((1,), (1,)), ((), ()))
 TN = (((0,), (0,)), ((), ()))
 OWN_PX, OTHER_PX, ALL_PX = 8, 9, 10
-
-
-def call(kernel, outs, operands, scratch=(), flops=0, name=None):
+G_DOWN, G_MID, G_SHORT, B_DOWN, B_MID, B_SHORT, G_FIRST, G_SECOND, B_FIRST, B_SECOND = range(10)
+
+
+def param(params_ref, row):
+    return params_ref[row : row + 1, :]
+
+
+def call(kernel, outs, operands, scratch=(), flops=0, name=None, after=(), specs=None):
+    count = len(operands)
     nbytes = sum(x.size * x.dtype.itemsize for x in operands)
+    specs = specs or {}
+
+    def body(*refs):
+        kernel(*refs[:count], *refs[count + len(after) :])
+
     return pl.pallas_call(
-        kernel,
+        body,
         out_shape=tuple(jax.ShapeDtypeStruct(shape, dtype) for shape, dtype in outs),
-        in_specs=[SM if x.ndim == 1 else VM for x in operands],
-        out_specs=tuple(VM for _ in outs),
+        in_specs=[specs.get(i, SM if x.ndim == 1 else VM) for i, x in enumerate(operands)]
+        + [pl.BlockSpec(memory_space=pl.ANY)] * len(after),
+        out_specs=tuple(SM if len(shape) == 1 else VM for shape, _ in outs),
         scratch_shapes=list(scratch),
-        compiler_params=pltpu.CompilerParams(vmem_limit_bytes=MESH_LIMIT),
+        compiler_params=pltpu.CompilerParams(vmem_limit_bytes=KERNEL_LIMIT),
         cost_estimate=pl.CostEstimate(
             flops=int(flops), bytes_accessed=int(nbytes), transcendentals=0
         ),
         name=name,
-    )(*operands)
+    )(*operands, *after)
 
 
 def fold(rows):
@@ -257,34 +269,49 @@
     return gate * (1.0 + values * (1.0 - gate))
 
 
-def pieces_kernel(where_ref, images_ref, o0, o1, o2, o3, wide):
+MARKS = 128
+
+
+def pieces_kernel(where_ref, images_ref, labels_ref, count_ref, o0, o1, o2, o3, wide):
     pipe, zone = where_ref[0], where_ref[2]
+    tasks = labels_ref.shape[1]
+    o0[MARKS:, :] = jnp.zeros((16, 512), BF16)
     for rel, out in enumerate((o0, o1, o2, o3)):
         first = (zone ^ rel) * 4 + pipe * 2
         for i in range(2):
             for row in range(2):
+                lines = slice((i * 2 + row) * 32, (i * 2 + row) * 32 + 32)
                 for part in range(2):
                     lanes = slice(part * 128, part * 128 + 128)
                     wide[...] = images_ref[first + i, row, :, lanes].astype(F32)
                     for par in range(2):
                         value = wide[pl.ds(par, 32, stride=2), :]
                         start = par * 256 + part * 128
-                        out[i, row, :, start : start + 128] = value.astype(BF16)
+                        out[lines, start : start + 128] = value.astype(BF16)
+    marks = jnp.concatenate(
+        [
+            labels_ref[...].astype(F32),
+            jnp.broadcast_to(count_ref[...].astype(F32), (4, tasks)),
+            jnp.zeros((8, tasks), F32),
+        ]
+    )
+    o0[MARKS:, 0:tasks] = marks.astype(BF16)
 
 
 def down_kernel(facts_ref, where_ref, *refs):
-    pieces, (w_ref, s_ref, img_ref, out_ref, short_ref, stat_ref, x_ref) = refs[:16], refs[16:]
+    pieces, (w_ref, s_ref, img_ref, out_ref, short_ref, stat_ref, x_ref) = refs[:12], refs[12:]
     batch, zone = where_ref[1], where_ref[2]
     for kb in range(4):
         for kz in range(4):
-            piece = pieces[kb * 4 + kz]
+            piece, base = pieces[kb * 3 + min(kz, 2)], (128 if kz == 3 else 0)
             row = zone ^ kz
             here = pl.ds(pl.multiple_of(row * 32, 32), 32)
             after = pl.ds(pl.multiple_of(((row + 1) % 4) * 32, 32), 32)
             for i in range(2):
                 image = (batch ^ kb) * 2 + i
-                odd = piece[i, 1]
-                img_ref[image, here, 0:512] = piece[i, 0]
+                start = base + i * 64
+                odd = piece[start + 32 : start + 64, :]
+                img_ref[image, here, 0:512] = piece[start : start + 32, :]
                 img_ref[image, here, 512:1024] = odd
                 x_ref[image, after, :] = jnp.where(row == 3, jnp.zeros_like(odd), odd)
     for part in range(2):
@@ -310,10 +337,10 @@
     stat_ref[4:8, :] = jnp.zeros((4, 512), F32)
 
 
-def layer_kernel(which, facts_ref, in_ref, own_ref, other_ref, g_ref, b_ref, w_ref,
+def layer_kernel(g_row, b_row, facts_ref, in_ref, own_ref, other_ref, params_ref, w_ref,
                  act_ref, out_ref, stat_ref, norm_ref, x_ref):
     mean, inverse = norm_of(facts_ref, own_ref, other_ref, 0)
-    gain, bias = g_ref[which : which + 1, :], b_ref[which : which + 1, :]
+    gain, bias = param(params_ref, g_row), param(params_ref, b_row)
 
     def activate(image, carry):
         for r in range(4):
@@ -332,12 +359,12 @@
     stat_ref[2:8, :] = jnp.zeros((6, 512), F32)
 
 
-def join_kernel(facts_ref, mid_ref, short_ref, own_m, other_m, own_d, other_d, g_ref, b_ref,
+def join_kernel(facts_ref, mid_ref, short_ref, own_m, other_m, own_d, other_d, params_ref,
                 w_ref, act_ref, out_ref, stat_ref, norm_ref, x_ref):
     mean_m, inv_m = norm_of(facts_ref, own_m, other_m, 0)
     mean_s, inv_s = norm_of(facts_ref, own_d, other_d, 2)
-    gain_m, gain_s = g_ref[1:2, :], g_ref[2:3, :]
-    bias_m, bias_s = b_ref[1:2, :], b_ref[2:3, :]
+    gain_m, gain_s = param(params_ref, G_MID), param(params_ref, G_SHORT)
+    bias_m, bias_s = param(params_ref, B_MID), param(params_ref, B_SHORT)
 
     def activate(image, carry):
         for r in range(4):
@@ -359,10 +386,10 @@
     stat_ref[2:8, :] = jnp.zeros((6, 512), F32)
 
 
-def block_kernel(facts_ref, in_ref, section_ref, own_ref, other_ref, g_ref, b_ref,
+def block_kernel(facts_ref, in_ref, section_ref, own_ref, other_ref, params_ref,
                  pack_ref, norm_ref):
     mean, inverse = norm_of(facts_ref, own_ref, other_ref, 0)
-    gain, bias = g_ref[1:2, :], b_ref[1:2, :]
+    gain, bias = param(params_ref, G_SECOND), param(params_ref, B_SECOND)
     norm_ref[0:1, :] = mean
     norm_ref[1:2, :] = inverse
     norm_ref[2:8, :] = jnp.zeros((6, 512), F32)
@@ -394,7 +421,9 @@
         all_ref[block, pl.ds(pl.multiple_of(pipe * 8, 8), 8), :] = own_ref[rows, :]
         all_ref[block, pl.ds(pl.multiple_of((1 - pipe) * 8, 8), 8), :] = other_ref[rows, :]
     logits = (
-        jnp.dot(all_ref[0], hw_ref[...], precision=HIGHEST, preferred_element_type=F32)
+        lax.dot_general(
+            all_ref[0], hw_ref[...], NT, precision=HIGHEST, preferred_element_type=F32
+        )
         + hb_ref[...]
     )
     errors = living_ref[...] * (sigmoid(logits) - labels_ref[...])
@@ -405,7 +434,7 @@
 
 
 def head_kernel(picks_ref, where_ref, facts_ref, c0, c1, c2, c3, heads_ref, hw_ref, errors_ref,
-                all_ref, in_ref, section_ref, norm_ref, g_ref, b_ref,
+                all_ref, in_ref, section_ref, norm_ref, params_ref,
                 low_ref, pool_ref, small_ref, alpha_ref, gram_ref):
     tasks = gram_ref.shape[0]
     pipe = where_ref[0]
@@ -414,9 +443,7 @@
     grad_logits = (128.0 * tasks) * alpha_ref[...] * errors_ref[...]
     pooled, slopes, crossed = all_ref[0], all_ref[1], all_ref[2]
     grad_pool = (
-        lax.dot_general(
-            grad_logits, hw_ref[...], NT, precision=HIGHEST, preferred_element_type=F32
-        )
+        jnp.dot(grad_logits, hw_ref[...], precision=HIGHEST, preferred_element_type=F32)
         / 128.0
     )
     grad_sum = total_row(grad_pool * slopes)
@@ -432,7 +459,7 @@
     pool_ref[...] = jnp.where(pipe == 0, grad_pool[0:8], grad_pool[8:16])
 
     mean, inverse = norm_ref[0:1, :], norm_ref[1:2, :]
-    gain, bias = g_ref[1:2, :], b_ref[1:2, :]
+    gain, bias = param(params_ref, G_SECOND), param(params_ref, B_SECOND)
     all_px = facts_ref[ALL_PX]
     front = gain * inverse
     mean_grad, mean_cross = grad_sum / all_px, cross_sum / all_px
@@ -470,7 +497,7 @@
     lax.fori_loop(0, 8, back, 0)
 
 
-def second_back_kernel(facts_ref, low_ref, in_ref, norm_ref, g_ref, b_ref, w_ref,
+def second_back_kernel(facts_ref, low_ref, in_ref, norm_ref, params_ref, w_ref,
                        up_ref, sum_ref, x_ref, conv_ref):
     def fill(image, carry):
         for r in range(4):
@@ -479,7 +506,8 @@
 
     lax.fori_loop(0, 8, fill, 0)
     conv_core(x_ref, w_ref, conv_ref, True)
-    slope_sums(facts_ref, in_ref, norm_ref, g_ref[0:1, :], b_ref[0:1, :], conv_ref, up_ref, sum_ref)
+    gain, bias = param(params_ref, G_FIRST), param(params_ref, B_FIRST)
+    slope_sums(facts_ref, in_ref, norm_ref, gain, bias, conv_ref, up_ref, sum_ref)
 
 
 def slope_sums(facts_ref, in_ref, norm_ref, gain, bias, conv_ref, up_ref, sum_ref):
@@ -503,22 +531,22 @@
     sum_ref[2:8, :] = jnp.zeros((6, 512), F32)
 
 
-def first_back_kernel(facts_ref, up_in, in_ref, norm_ref, own_ref, other_ref, gp_ref, w_ref,
-                      second_ref, norm2_ref, section_ref, bp_ref, pool_ref,
-                      mid_ref, short_ref, normd_ref, gd_ref, bd_ref,
+def first_back_kernel(facts_ref, up_in, in_ref, norm_ref, own_ref, other_ref, params_ref, w_ref,
+                      second_ref, norm2_ref, section_ref, pool_ref, mid_ref, short_ref, normd_ref,
                       low_ref, up_ref, sum_ref, x_ref, conv_ref):
     def keep(image, r, low):
         low_ref[image, band(r), :] = low
         put_band(x_ref, image, r, low)
 
-    back_norm(facts_ref, in_ref, up_in, norm_ref, own_ref, other_ref, gp_ref[0:1, :], 0, keep)
+    back_norm(facts_ref, in_ref, up_in, norm_ref, own_ref, other_ref, param(params_ref, G_FIRST),
+              0, keep)
     conv_core(x_ref, w_ref, conv_ref, True)
     mean2, inv2 = norm2_ref[0:1, :], norm2_ref[1:2, :]
-    gain2, bias2 = gp_ref[1:2, :], bp_ref[1:2, :]
+    gain2, bias2 = param(params_ref, G_SECOND), param(params_ref, B_SECOND)
     mean_m, inv_m = normd_ref[0:1, :], normd_ref[1:2, :]
     mean_s, inv_s = normd_ref[2:3, :], normd_ref[3:4, :]
-    gain_m, gain_s = gd_ref[1:2, :], gd_ref[2:3, :]
-    bias_m, bias_s = bd_ref[1:2, :], bd_ref[2:3, :]
+    gain_m, gain_s = param(params_ref, G_MID), param(params_ref, G_SHORT)
+    bias_m, bias_s = param(params_ref, B_MID), param(params_ref, B_SHORT)
 
     def join(image, carry):
         grads, cross_m, cross_s = carry
@@ -547,8 +575,8 @@
     sum_ref[3:8, :] = jnp.zeros((5, 512), F32)
 
 
-def mid_back_kernel(facts_ref, up_in, mid_ref, short_ref, normd_ref, own_ref, other_ref, gd_ref,
-                    w_ref, in_ref, norm1_ref, bd_ref,
+def mid_back_kernel(facts_ref, up_in, mid_ref, short_ref, normd_ref, own_ref, other_ref, params_ref,
+                    w_ref, in_ref, norm1_ref,
                     low_ref, low_s_ref, up_ref, sum_ref, x_ref, conv_ref):
     def keep(image, r, low):
         low_ref[image, band(r), :] = low
@@ -557,24 +585,23 @@
     def keep_short(image, r, low):
         low_s_ref[image, band(r), :] = low
 
-    back_norm(facts_ref, mid_ref, up_in, normd_ref, own_ref, other_ref, gd_ref[1:2, :], 0, keep)
-    back_norm(
-        facts_ref, short_ref, up_in, normd_ref, own_ref, other_ref, gd_ref[2:3, :], 2, keep_short
-    )
+    gain_m, gain_s = param(params_ref, G_MID), param(params_ref, G_SHORT)
+    back_norm(facts_ref, mid_ref, up_in, normd_ref, own_ref, other_ref, gain_m, 0, keep)
+    back_norm(facts_ref, short_ref, up_in, normd_ref, own_ref, other_ref, gain_s, 2, keep_short)
     conv_core(x_ref, w_ref, conv_ref, True)
-    slope_sums(
-        facts_ref, in_ref, norm1_ref, gd_ref[0:1, :], bd_ref[0:1, :], conv_ref, up_ref, sum_ref
-    )
-
-
-def down_back_kernel(where_ref, facts_ref, up_in, in_ref, norm1_ref, own_ref, other_ref, gd_ref,
-                     low_s_ref, w_ref, s_ref, low_ref, own_out, other_out):
+    gain, bias = param(params_ref, G_DOWN), param(params_ref, B_DOWN)
+    slope_sums(facts_ref, in_ref, norm1_ref, gain, bias, conv_ref, up_ref, sum_ref)
+
+
+def down_back_kernel(where_ref, facts_ref, up_in, in_ref, norm1_ref, own_ref, other_ref, params_ref,
+                     low_s_ref, w_ref, s_ref, low_ref, o0, o1, o2, o3, stage_ref):
     pipe, batch, zone = where_ref[0], where_ref[1], where_ref[2]
 
     def keep(image, r, low):
         low_ref[image, band(r), :] = low
 
-    back_norm(facts_ref, in_ref, up_in, norm1_ref, own_ref, other_ref, gd_ref[0:1, :], 0, keep)
+    gain = param(params_ref, G_DOWN)
+    back_norm(facts_ref, in_ref, up_in, norm1_ref, own_ref, other_ref, gain, 0, keep)
     mine = pl.ds(batch * 2, 2)
     here = low_ref[mine]
     below = jnp.concatenate([here[:, 32:], jnp.zeros((2, 32, 512), BF16)], axis=1)
@@ -596,27 +623,26 @@
     for row in range(2):
         for par in range(2):
             plane = planes[row][par].reshape(2, 4, 32, 256).astype(BF16)
-            halves = (plane[..., 0:128], plane[..., 128:256])
-            own = jnp.where(pipe == 0, halves[0], halves[1])
-            other = jnp.where(pipe == 0, halves[1], halves[0])
             lanes = slice(par * 128, par * 128 + 128)
-            for z in range(4):
-                own_out[z ^ zone, :, row, :, lanes] = own[:, z]
-                other_out[z ^ zone, :, row, :, lanes] = other[:, z]
-
-
-def image_grad_kernel(where_ref, *refs):
-    pieces, out_ref = refs[:8], refs[8]
+            for side in range(2):
+                half = plane[..., side * 128 : side * 128 + 128]
+                for z in range(4):
+                    stage_ref[z ^ zone, side ^ pipe, :, row, :, lanes] = half[:, z]
+    for rel, out in enumerate((o0, o1, o2, o3)):
+        out[...] = stage_ref[rel]
+
+
+def image_grad_kernel(where_ref, own_ref, got_ref, out_ref):
     pipe, zone = where_ref[0], where_ref[2]
     for rel in range(4):
-        for side in range(2):
+        for side, pieces in enumerate((own_ref, got_ref)):
             first = (zone ^ rel) * 4 + (pipe if side == 0 else 1 - pipe) * 2
             for i in range(2):
                 for row in range(2):
                     for par in range(2):
                         out_ref[first + i, row, pl.ds(par, 32, stride=2), :] = pieces[
-                            rel * 2 + side
-                        ][i, row, :, par * 128 : (par + 1) * 128].astype(F32)
+                            rel, i, row, :, par * 128 : (par + 1) * 128
+                        ].astype(F32)
 
 
 def slot_of(quarter, zone):
@@ -641,8 +667,7 @@
         other_ref[slot, unit] = result_other[rows].astype(BF16)
 
 
-def kernel_grad_kernel(where_ref, act_ref, low_ref, own_ref, other_ref, turned_ref):
-    pipe, batch, zone = where_ref[0], where_ref[1], where_ref[2]
+def turned_taps(batch, act_ref, turned_ref):
     lanes = pl.ds(pl.multiple_of(batch * 128, 128), 128)
 
     def turn(image, carry):
@@ -654,7 +679,10 @@
         return carry
 
     lax.fori_loop(0, 8, turn, 0)
-    lhs = turned_ref[...].reshape(9 * 128, 1024)
+
+
+def tap_products(pipe, zone, low_ref, turned_ref, own_ref, other_ref):
+    lhs = turned_ref[0:9].reshape(9 * 128, 1024)
     results = []
     for side in (pipe, 1 - pipe):
         columns = pl.ds(pl.multiple_of(side * 256, 256), 256)
@@ -663,6 +691,12 @@
     for unit in range(9):
         rows = slice(unit * 128, unit * 128 + 128)
         split_out(pipe, zone, unit, results[0][rows], results[1][rows], own_ref, other_ref)
+
+
+def kernel_grad_kernel(where_ref, act_ref, low_ref, own_ref, other_ref, turned_ref):
+    pipe, batch, zone = where_ref[0], where_ref[1], where_ref[2]
+    turned_taps(batch, act_ref, turned_ref)
+    tap_products(pipe, zone, low_ref, turned_ref, own_ref, other_ref)
 
 
 DOWN_UNITS = (
@@ -706,36 +740,32 @@
 
 
 def gathered_blocks(zone, batch, refs):
-    fin, near = refs[0], refs[1]
-    sets = {0: (None, refs[2]), 1: (refs[3], refs[6]), 2: (refs[4], refs[7]), 3: (refs[5], refs[8])}
+    a, b, ax, by, ayy, bxx = refs
+    sets = {0: (a, b, 0, 0), 1: (ax, bxx, 0, 0), 2: (ayy, by, 0, 0), 3: (ayy, bxx, 2, 2)}
     for kb in range(4):
-        first, second = sets[kb]
+        even, odd, base_even, base_odd = sets[kb]
         for rel in range(4):
-            owner, quarter = batch ^ kb, zone ^ rel
             if rel % 2 == 1:
-                yield owner, quarter, second, rel // 2
-            elif first is not None:
-                yield owner, quarter, first, rel // 2
+                yield batch ^ kb, zone ^ rel, odd, base_odd + rel // 2
             else:
-                yield owner, quarter, (fin if rel == 0 else near), None
+                yield batch ^ kb, zone ^ rel, even, base_even + rel // 2
 
 
 def assemble_kernel(where_ref, *refs):
-    pieces, out_ref = refs[:9], refs[9]
+    pieces, out_ref = refs[:6], refs[6]
     batch, zone = where_ref[1], where_ref[2]
     for owner, quarter, ref, index in gathered_blocks(zone, batch, pieces):
         rows = pl.ds(pl.multiple_of(owner * 128 + quarter * 32, 32), 32)
-        value = ref[...] if index is None else ref[index]
-        out_ref[:, rows, :] = value.astype(F32)
+        out_ref[:, rows, :] = ref[index].astype(F32)
 
 
 def assemble_down_kernel(where_ref, *refs):
-    pieces, (out_ref, short_ref) = refs[:9], refs[9:]
+    pieces, (out_ref, short_ref) = refs[:6], refs[6:]
     batch, zone = where_ref[1], where_ref[2]
     for owner, quarter, ref, index in gathered_blocks(zone, batch, pieces):
         upper, part = owner // 2, owner % 2
         rows = pl.ds(pl.multiple_of(part * 128 + quarter * 32, 32), 32)
-        value = (ref[...] if index is None else ref[index]).astype(F32)
+        value = ref[index].astype(F32)
         for kind in range(2):
 
             @pl.when(upper == kind)
@@ -747,6 +777,78 @@
                         out_ref[tap, rows, :] = value[unit]
 
 
+def facts_kernel(where_ref, p0, p1, p2, p3, hw_ref, facts_ref, living_ref, targets_ref, heads_ref):
+    pipe, batch = where_ref[0], where_ref[1]
+    tasks = hw_ref.shape[0]
+    alive = [jnp.float32(0.0), jnp.float32(0.0)]
+    for rel, piece in enumerate((p0, p1, p2, p3)):
+        owner = batch ^ rel
+        marks = piece[MARKS:, 0:tasks].astype(F32)
+        count = jnp.max(marks[4:5, :])
+        for slot in range(4):
+            side, place = slot // 2, owner * 2 + slot % 2
+            living = (count > slot + 0.5).astype(F32)
+            alive[side] = alive[side] + living
+            row = pl.ds(side * 8 + place, 1)
+            living_ref[row, :] = jnp.full((1, tasks), living)
+            targets_ref[row, :] = marks[slot : slot + 1, :]
+
+            @pl.when(pipe == side)
+            def _(place=place, living=living):
+                facts_ref[place] = living
+
+    own = jnp.where(pipe == 0, alive[0], alive[1])
+    facts_ref[OWN_PX] = own * 128.0
+    facts_ref[OTHER_PX] = (alive[0] + alive[1] - own) * 128.0
+    facts_ref[ALL_PX] = (alive[0] + alive[1]) * 128.0
+    for rest in range(ALL_PX + 1, 16):
+        facts_ref[rest] = jnp.float32(0.0)
+    heads_ref[...] = lax.dot_general(
+        hw_ref[...], hw_ref[...], NT, precision=HIGHEST, preferred_element_type=F32
+    )
+
+
+SMALL_ROWS = 64
+
+
+def small_kernel(where_ref, head_ref, all_ref, sum_f, other_f, sum_j, other_j, sum_d, other_d,
+                 sent_ref, wide_ref):
+    pipe, batch = where_ref[0], where_ref[1]
+    tasks = head_ref.shape[0] - 8
+    wide_ref[...] = jnp.zeros(wide_ref.shape, F32)
+    wide_ref[0 : tasks + 3, :] = head_ref[0 : tasks + 3, :]
+    at = tasks + 3
+    for own, other, count in ((sum_f, other_f, 2), (sum_j, other_j, 3), (sum_d, other_d, 2)):
+        wide_ref[at : at + count, :] = own[0:count, :] + other[0:count, :]
+        at += count
+    for side in range(2):
+        for slot in range(2):
+            row = side * 8 + batch * 2 + slot
+            at_row = SMALL_ROWS - 8 + side * 2 + slot
+            wide_ref[at_row : at_row + 1, :] = all_ref[0, pl.ds(row, 1), :]
+    sent_ref[...] = wide_ref[:, pl.ds(pl.multiple_of(pipe * 256, 256), 256)]
+
+
+def small_out_kernel(where_ref, p0, p1, p2, p3, pooled_ref, head_ref, gd_ref, bd_ref, gp_ref, bp_ref,
+                     headb_ref):
+    tasks = head_ref.shape[0]
+    zone = where_ref[2]
+    for rel, part in enumerate((p0, p1, p2, p3)):
+        pooled_ref[zone ^ rel] = part[SMALL_ROWS - 8 : SMALL_ROWS - 4, :]
+    total = (p0[...] + p1[...]) + (p2[...] + p3[...])
+    head_ref[...] = total[0:tasks]
+
+    def line(at):
+        return total[tasks + at : tasks + at + 1]
+
+    headb_ref[...] = line(2)
+    bp_ref[0:1, :], gp_ref[0:1, :] = line(3), line(4)
+    bp_ref[1:2, :], gp_ref[1:2, :] = line(0), line(1)
+    bd_ref[0:1, :], gd_ref[0:1, :] = line(8), line(9)
+    bd_ref[1:2, :], gd_ref[1:2, :] = line(5), line(6)
+    bd_ref[2:3, :], gd_ref[2:3, :] = line(5), line(7)
+
+
 def fast_device(images, image_counts, labels, fw_picks, conv_down, conv_mid, shortcut, gains_down,
                 biases_down, conv_first, conv_second, gains_plain, biases_plain, head_weight,
                 head_bias):
@@ -757,40 +859,28 @@
         size = lax.axis_size(axis)
         return lax.ppermute(x, axis, [(i, i ^ rel) for i in range(size)])
 
-    def by_index(parts, own):
-        stacked = jnp.stack(parts)
-        return jnp.take(stacked, jnp.arange(4) ^ own, axis=0)
-
     where = jnp.stack([pipe, batch, zone, zone]).astype(jnp.int32)
+    params = jnp.concatenate([gains_down, biases_down, gains_plain, biases_plain])
+    turned_heads = head_weight.T
+    bias_row = head_bias.reshape(1, tasks)
 
     pieces = call(
         pieces_kernel,
-        [((2, 2, 32, 512), BF16)] * 4,
-        [where, images],
+        [((144, 512), BF16)] + [((128, 512), BF16)] * 3,
+        [where, images, lax.dynamic_slice_in_dim(labels, zone * 4, 4, 0),
+         lax.dynamic_slice_in_dim(image_counts, zone, 1, 1)],
         [pltpu.VMEM((64, 128), F32)],
         name="pieces",
     )
-    moved = [pieces[0]] + [over("space", rel, pieces[rel]) for rel in (1, 2, 3)]
-    gathered = [[moved[rel] for rel in range(4)]]
-    for kb in (1, 2, 3):
-        gathered.append([over("batch", kb, moved[rel]) for rel in range(4)])
-
-    marks = lax.dynamic_slice_in_dim(labels, zone * 4, 4, 0)
-    count = lax.dynamic_slice_in_dim(image_counts, zone, 1, 1)
-    marks = jnp.concatenate([marks, jnp.broadcast_to(count, (1, tasks))], axis=0)
-    marks = by_index([marks] + [over("batch", kb, marks) for kb in (1, 2, 3)], batch)
-    counts = marks[:, 4, 0]
-    slots = jnp.arange(4, dtype=jnp.int32).reshape(2, 1, 2)
-    living = (slots < counts[None, :, None]).astype(F32).reshape(2, 8)
-    targets = marks[:, :4].reshape(4, 2, 2, tasks).transpose(1, 0, 2, 3).reshape(16, tasks)
-    targets = targets.astype(F32)
-    alive = jnp.sum(living, axis=1) * 128.0
-    mine = jnp.where(pipe == 0, living[0], living[1])
-    own_px = jnp.where(pipe == 0, alive[0], alive[1])
-    facts = jnp.concatenate(
-        [mine, jnp.stack([own_px, alive[0] + alive[1] - own_px, alive[0] + alive[1]])]
-    )
-    facts = jnp.pad(facts, (0, 5))
+    moved = [over("space", rel, pieces[rel]) for rel in (1, 2, 3)]
+    moved = [pieces[0], moved[0], jnp.concatenate([moved[1], moved[2]])]
+    gathered = [moved] + [[over("batch", kb, x) for x in moved] for kb in (1, 2, 3)]
+    facts, living, targets, heads = call(
+        facts_kernel,
+        [((16,), F32), ((16, tasks), F32), ((16, tasks), F32), ((tasks, tasks), F32)],
+        [where] + [line[0] for line in gathered] + [turned_heads],
+        name="facts",
+    )
 
     big = ((8, 128, 512), F32)
     low = ((8, 128, 512), BF16)
@@ -812,9 +902,9 @@
     )
     other_d = partner(stat_d)
     down_act, mid_out, stat_m, norm_d = call(
-        lambda *refs: layer_kernel(0, *refs),
+        lambda *refs: layer_kernel(G_DOWN, B_DOWN, *refs),
         [low, big, rows, rows],
-        [facts, down_out, stat_d, other_d, gains_down, biases_down, conv_mid],
+        [facts, down_out, stat_d, other_d, params, conv_mid],
         [x_scratch],
         conv_flops,
         "mid",
@@ -823,17 +913,16 @@
     section, first_out, stat_f, norm_j = call(
         join_kernel,
         [low, big, rows, rows],
-        [facts, mid_out, short_out, stat_m, other_m, stat_d, other_d, gains_down, biases_down,
-         conv_first],
+        [facts, mid_out, short_out, stat_m, other_m, stat_d, other_d, params, conv_first],
         [x_scratch],
         conv_flops,
         "first",
     )
     other_f = partner(stat_f)
     plain_act, second_out, stat_s, norm_f = call(
-        lambda *refs: layer_kernel(0, *refs),
+        lambda *refs: layer_kernel(G_FIRST, B_FIRST, *refs),
         [low, big, rows, rows],
-        [facts, first_out, stat_f, other_f, gains_plain, biases_plain, conv_second],
+        [facts, first_out, stat_f, other_f, params, conv_second],
         [x_scratch],
         conv_flops,
         "second",
@@ -842,166 +931,198 @@
     pack, norm_s = call(
         block_kernel,
         [((24, 512), F32), rows],
-        [facts, second_out, section, stat_s, other_s, gains_plain, biases_plain],
+        [facts, second_out, section, stat_s, other_s, params],
         name="block",
     )
     other_pack = partner(pack)
     all_pack, errors, cross = call(
         logits_kernel,
         [((3, 16, 512), F32), ((16, tasks), F32), ((tasks, tasks), F32)],
-        [where, pack, other_pack, living.reshape(16, 1), targets, head_weight,
-         head_bias.reshape(1, tasks)],
+        [where, pack, other_pack, living, targets, turned_heads, bias_row],
         name="logits",
     )
     crosses = [cross] + [over("space", rel, cross) for rel in (1, 2, 3)]
-    heads = jnp.dot(head_weight.T, head_weight, precision=HIGHEST)
     second_low, grad_pool, small = call(
         head_kernel,
         [low, rows, ((tasks + 8, 512), F32)],
         [fw_picks, where, facts] + crosses
-        + [heads, head_weight, errors, all_pack, second_out, section, norm_s, gains_plain,
-           biases_plain],
+        + [heads, turned_heads, errors, all_pack, second_out, section, norm_s, params],
         [pltpu.VMEM((1, tasks), F32), pltpu.VMEM((tasks, tasks), F32)],
         name="head",
     )
 
-    def summed(own, other):
-        got = partner(other)
-        both = own + got.astype(F32)
-        near = both[:2] + over("space", 1, both[2:].astype(BF16)).astype(F32)
-        mine = near[0] + over("space", 2, near[1].astype(BF16)).astype(F32)
-        final = mine.astype(BF16)
-        far = over("space", 2, final)
-        a = jnp.stack([final, far])
-        b = over("space", 1, a)
-        ax, ay = over("batch", 1, a), over("batch", 2, a)
-        bx, by = over("batch", 1, b), over("batch", 2, b)
-        axy, bxy = over("batch", 2, ax), over("batch", 1, by)
-        return [where, final, far, b, ax, ay, axy, bx, by, bxy]
-
-    def kernel_grad_of(act, low_grad, name):
-        own, other = call(
+    class Sum:
+        def __init__(self, own, other):
+            self.own, self.other = own, other
+
+        def cores(self):
+            self.both = self.own + partner(self.other).astype(F32)
+            self.sent = self.both[1:].astype(BF16)
+
+        def zones(self):
+            got = [over("space", rel, self.sent[slot]).astype(F32)
+                   for slot, rel in ((1, 1), (0, 2), (2, 3))]
+            self.final = ((self.both[0] + got[0]) + (got[1] + got[2])).astype(BF16)
+
+        def near(self):
+            self.far = over("space", 2, self.final)
+            self.a = jnp.stack([self.final, self.far])
+
+        def ends(self):
+            self.b = over("space", 1, self.a)
+
+        def plane(self):
+            self.ax, self.by = over("batch", 1, self.a), over("batch", 2, self.b)
+
+        def plane_far(self):
+            self.ayy = over("batch", 2, jnp.concatenate([self.a, self.ax]))
+            self.bxx = over("batch", 1, jnp.concatenate([self.b, self.by]))
+
+        def blocks(self):
+            return [where, self.a, self.b, self.ax, self.by, self.ayy, self.bxx]
+
+    def kernel_grad_of(act, low_grad, name, after=()):
+        return Sum(*call(
             kernel_grad_kernel,
             [((4, 9, 32, 256), F32), ((4, 9, 32, 256), BF16)],
             [where, act, low_grad],
             [pltpu.VMEM((9, 128, 1024), BF16)],
             conv_flops // 4,
             name,
-        )
-        return summed(own, other)
-
-    def assembled(blocks, name):
-        (out,) = call(assemble_kernel, [((9, 512, 256), F32)], blocks, name=name)
+            after,
+        ))
+
+    def assembled(blocks, name, after=()):
+        (out,) = call(assemble_kernel, [((9, 512, 256), F32)], blocks, name=name, after=after)
         return out.reshape(3, 3, 512, 256)
 
-    second_blocks = kernel_grad_of(plain_act, second_low, "second_grad")
+    second = kernel_grad_of(plain_act, second_low, "second_grad")
     up_f, sum_f = call(
         second_back_kernel,
         [big, rows],
-        [facts, second_low, first_out, norm_f, gains_plain, biases_plain, conv_second],
+        [facts, second_low, first_out, norm_f, params, conv_second],
         [x_scratch, conv_scratch],
         conv_flops,
         "second_back",
+        after=[second.other],
     )
     other_sf = partner(sum_f)
+    second.cores()
     first_low, up_j, sum_j = call(
         first_back_kernel,
         [low, big, rows],
-        [facts, up_f, first_out, norm_f, sum_f, other_sf, gains_plain, conv_first,
-         second_out, norm_s, section, biases_plain, grad_pool,
-         mid_out, short_out, norm_j, gains_down, biases_down],
+        [facts, up_f, first_out, norm_f, sum_f, other_sf, params, conv_first,
+         second_out, norm_s, section, grad_pool, mid_out, short_out, norm_j],
         [x_scratch, conv_scratch],
         conv_flops,
         "first_back",
+        after=[second.sent],
     )
     other_sj = partner(sum_j)
-    first_blocks = kernel_grad_of(section, first_low, "first_grad")
+    second.zones()
+    first = kernel_grad_of(section, first_low, "first_grad")
+    first.cores()
     mid_low, short_low, up_d, sum_d = call(
         mid_back_kernel,
         [low, low, big, rows],
-        [facts, up_j, mid_out, short_out, norm_j, sum_j, other_sj, gains_down, conv_mid,
-         down_out, norm_d, biases_down],
+        [facts, up_j, mid_out, short_out, norm_j, sum_j, other_sj, params, conv_mid,
+         down_out, norm_d],
         [x_scratch, conv_scratch],
         conv_flops,
         "mid_back",
+        after=[first.sent, second.final],
     )
     other_sd = partner(sum_d)
-    mid_blocks = kernel_grad_of(down_act, mid_low, "mid_grad")
-    down_low, own_img, other_img = call(
+    second.near()
+    first.zones()
+    mid = kernel_grad_of(down_act, mid_low, "mid_grad")
+    mid.cores()
+    second.ends()
+    down_low, *img_pieces = call(
         down_back_kernel,
-        [low, ((4, 2, 2, 32, 256), BF16), ((4, 2, 2, 32, 256), BF16)],
-        [where, facts, up_d, down_out, norm_d, sum_d, other_sd, gains_down, short_low, conv_down,
+        [low] + [((2, 2, 2, 32, 256), BF16)] * 4,
+        [where, facts, up_d, down_out, norm_d, sum_d, other_sd, params, short_low, conv_down,
          shortcut],
-        [],
+        [pltpu.VMEM((4, 2, 2, 2, 32, 256), BF16)],
         conv_flops // 8,
         "down_back",
-    )
-    own, other = call(
+        after=[second.a, mid.other],
+    )
+    down = Sum(*call(
         down_grad_kernel,
         [((4, 5, 32, 256), F32), ((4, 5, 32, 256), BF16)],
         [where, img, down_low, short_low],
         [pltpu.VMEM((5, 128, 1024), BF16)],
         conv_flops // 8,
         "down_grad",
-    )
-    down_blocks = summed(own, other)
-
-    got_img = partner(other_img)
-    image_pieces = []
-    for rel in range(4):
-        for block in (own_img, got_img):
-            part = block[rel]
-            image_pieces.append(part if rel == 0 else over("space", rel, part))
+        after=[second.b, mid.sent, first.final],
+    ))
+    down.cores()
+    first.near()
+    first.ends()
+    second.plane()
+    second.plane_far()
+    mid.zones()
+    first.plane()
+    first.plane_far()
+    mid.near()
+    mid.ends()
+    down.zones()
+    down.near()
+    down.ends()
+    mid.plane()
+    mid.plane_far()
+    down.plane()
+    down.plane_far()
+    second_out_grad = assembled(second.blocks(), "second_out")
+    first_out_grad = assembled(first.blocks(), "first_out")
+    mid_out_grad = assembled(mid.blocks(), "mid_out")
+
+    img_moved = [img_pieces[0]] + [over("space", rel, img_pieces[rel]) for rel in (1, 2, 3)]
+    img_moved = jnp.stack(img_moved)
+    img_got = partner(img_moved[:, 1])
     (images_grad,) = call(
         image_grad_kernel,
         [((16, 2, 64, 128), F32)],
-        [where] + image_pieces,
+        [where, img_moved[:, 0], img_got],
         name="image_grad",
     )
 
-    def own_lanes(x):
-        return lax.dynamic_slice_in_dim(x, pipe * 256, 256, x.ndim - 1)
-
-    pooled_mine = lax.dynamic_slice_in_dim(
-        all_pack[0].reshape(2, 4, 2, 512), batch, 1, 1
-    ).reshape(4, 512)
-    sums = jnp.concatenate(
-        [
-            small,
-            sum_f[0:2] + other_sf[0:2],
-            sum_j[0:3] + other_sj[0:3],
-            sum_d[0:2] + other_sd[0:2],
-        ]
-    )
-    sent = jnp.concatenate([own_lanes(sums), own_lanes(pooled_mine)])
+    (sent,) = call(
+        small_kernel,
+        [((SMALL_ROWS, 256), F32)],
+        [where, small, all_pack, sum_f, other_sf, sum_j, other_sj, sum_d, other_sd],
+        [pltpu.VMEM((SMALL_ROWS, 512), F32)],
+        name="small",
+    )
     parts = [sent] + [over("space", rel, sent) for rel in (1, 2, 3)]
-    summed_up = (parts[0] + parts[1]) + (parts[2] + parts[3])
-    pooled = by_index([part[-4:] for part in parts], zone).reshape(16, 256)
-    row = tasks + 8
-    second_sum, second_cross, head_b = (summed_up[tasks + i] for i in range(3))
-    first_sum, first_cross = summed_up[row], summed_up[row + 1]
-    join_sum, mid_cross, short_cross = (summed_up[row + 2 + i] for i in range(3))
-    down_sum, down_cross = summed_up[row + 5], summed_up[row + 6]
+    pooled, head_out, gains_d, sums_d, gains_p, sums_p, head_b = call(
+        small_out_kernel,
+        [((4, 4, 256), F32), ((tasks, 256), F32), ((3, 256), F32), ((3, 256), F32),
+         ((2, 256), F32), ((2, 256), F32), ((1, 256), F32)],
+        [where] + parts,
+        name="small_out",
+    )
     down_grad, short_grad = call(
         assemble_down_kernel,
         [((9, 256, 256), F32), ((256, 256), F32)],
-        down_blocks,
+        down.blocks(),
         name="down_out",
     )
     return (
-        pooled,
+        pooled.reshape(16, 256),
         images_grad,
         down_grad.reshape(3, 3, 256, 256),
-        assembled(mid_blocks, "mid_out"),
+        mid_out_grad,
         short_grad,
-        jnp.stack([down_cross, mid_cross, short_cross]),
-        jnp.stack([down_sum, join_sum, join_sum]),
-        assembled(first_blocks, "first_out"),
-        assembled(second_blocks, "second_out"),
-        jnp.stack([first_cross, second_cross]),
-        jnp.stack([first_sum, second_sum]),
-        summed_up[:tasks].T,
-        lax.dynamic_slice_in_dim(head_b, pipe * (tasks // 2), tasks // 2, 0),
+        gains_d,
+        sums_d,
+        first_out_grad,
+        second_out_grad,
+        gains_p,
+        sums_p,
+        head_out.T,
+        lax.dynamic_slice_in_dim(head_b[0], pipe * (tasks // 2), tasks // 2, 0),
     )
 
 

time: 381 us -> 295 us (0.77)
  Pallas kernels: 149 us -> 95.6 us
  waiting for transfers between devices: 104 us -> 83.4 us
    pallas_call x21 -> x24, Pallas kernels: 149 us -> 95.6 us  [call(): pl.pallas_call(body, out_shape=tuple((jax.ShapeDtypeStruct(shape, dtype)...]
    ppermute x83 -> x70, waiting for transfers between devices: 104 us -> 83.4 us  [over(): return lax.ppermute(x, axis, [(i, i ^ rel) for i in range(size)])]
    ppermute x83 -> x70, starting transfers between devices: 88.9 us -> 86.3 us  [over(): return lax.ppermute(x, axis, [(i, i ^ rel) for i in range(size)])]
    unnamed x158 -> x89, local copies, waits for them, and re-layouts: 10.7 us -> 13 us
  transfers between devices with their start and end apart: 83 -> 70, of which waited for: 35 -> 24; matrix products, arithmetic and copies ran while one was open for 5% -> 3% of each run, Pallas kernels for 20% -> 18%
where the time goes in v3:
time: 295 us; the launch traced here: 290 us
  Pallas kernels  95.6 us (32%)
  starting transfers between devices  86.3 us (29%)
  waiting for transfers between devices  83.4 us (28%)
  local copies, waits for them, and re-layouts  17.2 us (6%)
  other arithmetic  5.67 us (2%)
    pallas_call x24, Pallas kernels, call(): pl.pallas_call(body, out_shape=tuple((jax.ShapeDtypeStruct(shape, dtype)...  95.6 us
    ppermute x70, starting transfers between devices, over(): return lax.ppermute(x, axis, [(i, i ^ rel) for i in range(size)])  86.3 us
    ppermute x70, waiting for transfers between devices, over(): return lax.ppermute(x, axis, [(i, i ^ rel) for i in range(size)])  83.4 us
    unnamed x89, local copies, waits for them, and re-layouts  13 us
  transfers between devices with their start and end apart: 70, of which 24 were waited for; matrix products, arithmetic and copies ran while one was open for 3% of the time, Pallas kernels for 18%

profile of v3, /device:TPU:0, one launch (start us, length us, event | category | flops | bytes accessed | tf_op | source)
XLA Modules:
  0.0 290.0 jit_solution(11831580764238183889)
XLA Ops:
  5.4 4.1 %collective-permute-start.4 = (bf16[128,512]{1,0:T(8,128)(2,1)S(1)}, bf16[128,512]{1,0:T(8,128)(2,1)S(1)}, u32[]{:S(2)}, u32[]{:S(2)}) collective-permute-start(bf16[128,512]{1,0:T(8,128)(2,1)S(1)} %get-tuple-element.79), channel_id=1, source_target_pairs={{0,2},{1,3},{2,0},{3,1},{4,6},{5,7},{6,4},{7,5},{8,10},{9,11},{10,... | collective-permute-start | bytes 393224 | tf_op jit(solution)/shard_map/ppermute | solution.py:860
  10.8 1.5 collective-permute-start
  12.3 1.5 collective-permute-start.1
  14.3 5.1 %collective-permute-done.4 = bf16[128,512]{1,0:T(8,128)(2,1)S(1)} collective-permute-done((bf16[128,512]{1,0:T(8,128)(2,1)S(1)}, bf16[128,512]{1,0:T(8,128)(2,1)S(1)}, u32[]{:S(2)}, u32[]{:S(2)}) %collective-permute-start.4) | collective-permute-done | bytes 131104 | tf_op jit(solution)/shard_map/ppermute | solution.py:860
  19.4 1.9 collective-permute-start.7
  21.4 3.0 %collective-permute-done.3.refs_3_ = bf16[128,512]{1,0:T(8,128)(2,1)S(1)} collective-permute-done((bf16[128,512]{1,0:T(8,128)(2,1)S(1)}, bf16[128,512]{1,0:T(8,128)(2,1)S(1)}, u32[]{:S(2)}, u32[]{:S(2)}) %collective-permute-start.3) | collective-permute-done | bytes 131104 | tf_op jit(solution)/shard_map/ppermute | solution.py:860
  24.4 1.8 collective-permute-start.6
  26.2 1.5 collective-permute-start.9
  27.9 1.9 collective-permute-start.8
  29.7 1.8 collective-permute-done.6.refs_6_
  31.5 2.8 collective-permute-start.10
  35.7 6.5 %collective-permute-done.8.refs_9_ = bf16[128,512]{1,0:T(8,128)(2,1)S(1)} collective-permute-done((bf16[128,512]{1,0:T(8,128)(2,1)S(1)}, bf16[128,512]{1,0:T(8,128)(2,1)S(1)}, u32[]{:S(2)}, u32[]{:S(2)}) %collective-permute-start.8) | collective-permute-done | bytes 131104 | tf_op jit(solution)/shard_map/ppermute | solution.py:860
  42.3 1.7 copy-done.2
  43.9 4.7 %down.1 = (bf16[8,128,1024]{2,1,0:T(8,128)(2,1)S(1)}, f32[8,128,512]{2,1,0:T(8,128)S(1)}, f32[8,128,512]{2,1,0:T(8,128)S(1)}, f32[8,512]{1,0:T(8,128)S(1)}) custom-call(f32[16]{0:T(128)S(1)} %get-tuple-element.77.refs_0_.refs_2_.refs_1_, s32[4]{0:T(128)S(1)} %pad_add_fusion.refs_0_.refs_1_, bf16[144,512]{1,0:T(8,128)(2,1)S(1)} %get-tuple-element.76.refs_1_.refs_2_, ...), custom_call_target="tpu_custom_call" | custom-call | flops 2415919104 | bytes 4784208 | tf_op jit(solution)/shard_map/down/pallas_call | solution.py:161
  49.9 7.0 %mid.1 = (bf16[8,128,512]{2,1,0:T(8,128)(2,1)S(1)}, f32[8,128,512]{2,1,0:T(8,128)S(1)}, f32[8,512]{1,0:T(8,128)S(1)}, f32[8,512]{1,0:T(8,128)S(1)}) custom-call(f32[16]{0:T(128)S(1)} %get-tuple-element.77.refs_0_.refs_2_.refs_1_, f32[8,128,512]{2,1,0:T(8,128)S(1)} %get-tuple-element.81.refs_1_.refs_9_.refs_3_, ...), custom_call_target="tpu_custom_call" | custom-call | flops 4831838208 | bytes 6869056 | tf_op jit(solution)/shard_map/mid/pallas_call | solution.py:161
  58.2 7.4 %first.1 = (bf16[8,128,512]{2,1,0:T(8,128)(2,1)S(1)}, f32[8,128,512]{2,1,0:T(8,128)S(1)}, f32[8,512]{1,0:T(8,128)S(1)}, f32[8,512]{1,0:T(8,128)S(1)}) custom-call(f32[16]{0:T(128)S(1)} %get-tuple-element.77.refs_0_.refs_2_.refs_1_, f32[8,128,512]{2,1,0:T(8,128)S(1)} %get-tuple-element.83.refs_1_.refs_12_.refs_2_, ...), custom_call_target="tpu_custom_call" | custom-call | flops 4831838208 | bytes 8998976 | tf_op jit(solution)/shard_map/first/pallas_call | solution.py:161
  66.8 7.0 %second.1 = (bf16[8,128,512]{2,1,0:T(8,128)(2,1)S(1)}, f32[8,128,512]{2,1,0:T(8,128)S(1)}, f32[8,512]{1,0:T(8,128)S(1)}, f32[8,512]{1,0:T(8,128)S(1)}) custom-call(f32[16]{0:T(128)S(1)} %get-tuple-element.77.refs_0_.refs_2_.refs_1_, f32[8,128,512]{2,1,0:T(8,128)S(1)} %get-tuple-element.86.refs_1_.refs_2_, f32[8,512]{1,0:T(8,128)S(1)} %get-tuple-element.87.refs_2_, ...), custom_call_target="tpu_custom_call" | custom-call | flops 4831838208 | bytes 6869056 | tf_op jit(solution)/shard_map/second/pallas_call | solution.py:161
  75.1 2.2 block.1
  79.5 1.6 collective-permute-start.17
  81.1 4.0 %collective-permute-start.18 = (f32[40,40]{1,0:T(8,128)S(1)}, f32[40,40]{1,0:T(8,128)S(1)}, u32[]{:S(2)}, u32[]{:S(2)}) collective-permute-start(f32[40,40]{1,0:T(8,128)S(1)} %get-tuple-element.94.refs_3_), channel_id=1, source_target_pairs={{0,2},{1,3},{2,0},{3,1},{4,6},{5,7},{6,4},{7,5},{8,10},{9,11},{10,... | collective-permute-start | bytes 19208 | tf_op jit(solution)/shard_map/ppermute | solution.py:860
  85.2 1.7 collective-permute-done.18.refs_5_
  86.9 3.8 %collective-permute-done.19.refs_6_ = f32[40,40]{1,0:T(8,128)S(1)} collective-permute-done((f32[40,40]{1,0:T(8,128)S(1)}, f32[40,40]{1,0:T(8,128)S(1)}, u32[]{:S(2)}, u32[]{:S(2)}) %collective-permute-start.19) | collective-permute-done | bytes 6432 | tf_op jit(solution)/shard_map/ppermute | solution.py:860
  90.7 4.5 %head.1 = (bf16[8,128,512]{2,1,0:T(8,128)(2,1)S(1)}, f32[8,512]{1,0:T(8,128)S(1)}, f32[48,512]{1,0:T(8,128)S(1)}) custom-call(s32[20]{0:T(128)S(1)} %copy-done.34, s32[4]{0:T(128)S(1)} %pad_add_fusion.refs_0_.refs_1_, f32[16]{0:T(128)S(1)} %get-tuple-element.77.refs_0_.refs_2_.refs_1_, f32[40,40]{1,0:T(8,128)S(1)} %get-tuple-element.94.refs_3_, ...), custom_call_target="tpu_custom_call" | custom-call | bytes 3397536 | tf_op jit(solution)/shard_map/head/pallas_call | solution.py:161
  95.2 4.1 %second_grad.1 = (f32[4,9,32,256]{3,2,1,0:T(8,128)S(1)}, bf16[4,9,32,256]{3,2,1,0:T(8,128)(2,1)S(1)}) custom-call(s32[4]{0:T(128)S(1)} %pad_add_fusion.refs_0_.refs_1_, bf16[8,128,512]{2,1,0:T(8,128)(2,1)S(1)} %get-tuple-element.102.refs_1_, bf16[8,128,512]{2,1,0:T(8,128)(2,1)S(1)} %get-tuple-element.100.refs_2_.refs_1_), custom_call_target="tpu_custom_call" | custom-call | flops 1207959552 | bytes 2097168 | tf_op jit(solution)/shard_map/second_grad/pallas_call | solution.py:161
  99.4 7.2 %second_back.1 = (f32[8,128,512]{2,1,0:T(8,128)S(1)}, f32[8,512]{1,0:T(8,128)S(1)}) custom-call(f32[16]{0:T(128)S(1)} %get-tuple-element.77.refs_0_.refs_2_.refs_1_, bf16[8,128,512]{2,1,0:T(8,128)(2,1)S(1)} %get-tuple-element.100.refs_2_.refs_1_, f32[8,128,512]{2,1,0:T(8,128)S(1)} %get-tuple-element.86.refs_1_.refs_2_, ...), custom_call_target="tpu_custom_call" | custom-call | flops 4831838208 | bytes 7901248 | tf_op jit(solution)/shard_map/second_back/pallas_call | solution.py:161
  107.8 4.1 %collective-permute-start.24 = (bf16[9,32,256]{2,1,0:T(8,128)(2,1)S(1)}, bf16[9,32,256]{2,1,0:T(8,128)(2,1)S(1)}, u32[]{:S(2)}, u32[]{:S(2)}) collective-permute-start(bf16[9,32,256]{2,1,0:T(8,128)(2,1)S(1)} %get-tuple-element.153), channel_id=1, source_target_pairs={{0,1},{1,0},{2,3},{3,2},{4,5},{5,4},{6,7},{7,6},{8,9},{9,8},{10,11... | collective-permute-start | bytes 442376 | tf_op jit(solution)/shard_map/ppermute | solution.py:860
  111.9 9.6 %first_back.1 = (bf16[8,128,512]{2,1,0:T(8,128)(2,1)S(1)}, f32[8,128,512]{2,1,0:T(8,128)S(1)}, f32[8,512]{1,0:T(8,128)S(1)}) custom-call(f32[16]{0:T(128)S(1)} %get-tuple-element.77.refs_0_.refs_2_.refs_1_, f32[8,128,512]{2,1,0:T(8,128)S(1)} %get-tuple-element.105.refs_1_, f32[8,128,512]{2,1,0:T(8,128)S(1)} %get-tuple-element.86.refs_1_.refs_2_, ...), custom_call_target="tpu_custom_call" | custom-call | flops 4831838208 | bytes 16371776 | tf_op jit(solution)/shard_map/first_back/pallas_call | solution.py:161
  121.6 3.9 %first_grad.1 = (f32[4,9,32,256]{3,2,1,0:T(8,128)S(1)}, bf16[4,9,32,256]{3,2,1,0:T(8,128)(2,1)S(1)}) custom-call(s32[4]{0:T(128)S(1)} %pad_add_fusion.refs_0_.refs_1_, bf16[8,128,512]{2,1,0:T(8,128)(2,1)S(1)} %get-tuple-element.89.refs_2_.refs_12_.refs_10_.refs_1_, bf16[8,128,512]{2,1,0:T(8,128)(2,1)S(1)} %get-tuple-element.112.refs_2_), custom_call_target="tpu_custom_call" | custom-call | flops 1207959552 | bytes 2097168 | tf_op jit(solution)/shard_map/first_grad/pallas_call | solution.py:161
  126.3 9.2 %collective-permute-done.31 = bf16[9,32,256]{2,1,0:T(8,128)(2,1)S(1)} collective-permute-done((bf16[9,32,256]{2,1,0:T(8,128)(2,1)S(1)}, bf16[9,32,256]{2,1,0:T(8,128)(2,1)S(1)}, u32[]{:S(2)}, u32[]{:S(2)}) %collective-permute-start.31) | collective-permute-done | bytes 147488 | tf_op jit(solution)/shard_map/ppermute | solution.py:860
  136.5 8.5 %mid_back.1 = (bf16[8,128,512]{2,1,0:T(8,128)(2,1)S(1)}, bf16[8,128,512]{2,1,0:T(8,128)(2,1)S(1)}, f32[8,128,512]{2,1,0:T(8,128)S(1)}, f32[8,512]{1,0:T(8,128)S(1)}) custom-call(f32[16]{0:T(128)S(1)} %get-tuple-element.77.refs_0_.refs_2_.refs_1_, f32[8,128,512]{2,1,0:T(8,128)S(1)} %get-tuple-element.110.refs_1_, ...), custom_call_target="tpu_custom_call" | custom-call | flops 4831838208 | bytes 13193280 | tf_op jit(solution)/shard_map/mid_back/pallas_call | solution.py:161
  146.1 2.5 collective-permute-start.39
  149.6 3.9 %mid_grad.1 = (f32[4,9,32,256]{3,2,1,0:T(8,128)S(1)}, bf16[4,9,32,256]{3,2,1,0:T(8,128)(2,1)S(1)}) custom-call(s32[4]{0:T(128)S(1)} %pad_add_fusion.refs_0_.refs_1_, bf16[8,128,512]{2,1,0:T(8,128)(2,1)S(1)} %get-tuple-element.119.refs_1_, bf16[8,128,512]{2,1,0:T(8,128)(2,1)S(1)} %get-tuple-element.120.refs_2_), custom_call_target="tpu_custom_call" | custom-call | flops 1207959552 | bytes 2097168 | tf_op jit(solution)/shard_map/mid_grad/pallas_call | solution.py:161
  153.6 1.6 collective-permute-start.67
  155.8 2.1 down_back.1
  158.9 8.0 %collective-permute-done.39 = bf16[9,32,256]{2,1,0:T(8,128)(2,1)S(1)} collective-permute-done((bf16[9,32,256]{2,1,0:T(8,128)(2,1)S(1)}, bf16[9,32,256]{2,1,0:T(8,128)(2,1)S(1)}, u32[]{:S(2)}, u32[]{:S(2)}) %collective-permute-start.39) | collective-permute-done | bytes 147488 | tf_op jit(solution)/shard_map/ppermute | solution.py:860
  167.1 3.5 %collective-permute-start.60 = (bf16[9,32,256]{2,1,0:T(8,128)(2,1)S(1)}, bf16[9,32,256]{2,1,0:T(8,128)(2,1)S(1)}, u32[]{:S(2)}, u32[]{:S(2)}) collective-permute-start(bf16[9,32,256]{2,1,0:T(8,128)(2,1)S(1)} %fusion.5.refs_6_), channel_id=1, source_target_pairs={{0,2},{1,3},{2,0},{3,1},{4,6},{5,7},{6,4},{7,5},{8,10},{9,11},{10,... | collective-permute-start | bytes 442376 | tf_op jit(solution)/shard_map/ppermute | solution.py:860
  170.6 4.0 %collective-permute-done.33 = bf16[2,2,2,32,256]{4,3,2,1,0:T(8,128)(2,1)S(1)} collective-permute-done((bf16[2,2,2,32,256]{4,3,2,1,0:T(8,128)(2,1)S(1)}, bf16[2,2,2,32,256]{4,3,2,1,0:T(8,128)(2,1)S(1)}, u32[]{:S(2)}, u32[]{:S(2)}) %collective-permute-start.33) | collective-permute-done | bytes 131104 | tf_op jit(solution)/shard_map/ppermute | solution.py:860
  177.5 3.4 %collective-permute-start.51 = (bf16[9,32,256]{2,1,0:T(8,128)(2,1)S(1)}, bf16[9,32,256]{2,1,0:T(8,128)(2,1)S(1)}, u32[]{:S(2)}, u32[]{:S(2)}) collective-permute-start(bf16[9,32,256]{2,1,0:T(8,128)(2,1)S(1)} %get-tuple-element.147), channel_id=1, source_target_pairs={{0,1},{1,0},{2,3},{3,2},{4,5},{5,4},{6,7},{7,6},{8,9},{9,8},{10,11... | collective-permute-start | bytes 442376 | tf_op jit(solution)/shard_map/ppermute | solution.py:860
  180.9 3.2 %down_grad.1 = (f32[4,5,32,256]{3,2,1,0:T(8,128)S(1)}, bf16[4,5,32,256]{3,2,1,0:T(8,128)(2,1)S(1)}) custom-call(s32[4]{0:T(128)S(1)} %pad_add_fusion.refs_0_.refs_1_, bf16[8,128,1024]{2,1,0:T(8,128)(2,1)S(1)} %get-tuple-element.126.refs_1_, bf16[8,128,512]{2,1,0:T(8,128)(2,1)S(1)} %get-tuple-element.127.refs_2_, ...), custom_call_target="tpu_custom_call" | custom-call | flops 603979776 | bytes 4194320 | tf_op jit(solution)/shard_map/down_grad/pallas_call | solution.py:161
  184.2 2.7 collective-permute-done.60
  186.9 3.7 %collective-permute-start.28 = (f32[64,256]{1,0:T(8,128)S(1)}, f32[64,256]{1,0:T(8,128)S(1)}, u32[]{:S(2)}, u32[]{:S(2)}) collective-permute-start(f32[64,256]{1,0:T(8,128)S(1)} %small.1.refs_1_), channel_id=1, source_target_pairs={{0,1},{1,0},{2,3},{3,2},{4,5},{5,4},{6,7},{7,6},{8,9},{9,8},{10,11... | collective-permute-start | bytes 196616 | tf_op jit(solution)/shard_map/ppermute | solution.py:860
  190.6 1.9 collective-permute-done.52
  193.8 2.0 collective-permute-start.54
  196.6 5.7 %collective-permute-done.29.refs_3_ = f32[64,256]{1,0:T(8,128)S(1)} collective-permute-done((f32[64,256]{1,0:T(8,128)S(1)}, f32[64,256]{1,0:T(8,128)S(1)}, u32[]{:S(2)}, u32[]{:S(2)}) %collective-permute-start.29) | collective-permute-done | bytes 65568 | tf_op jit(solution)/shard_map/ppermute | solution.py:860
  203.6 2.1 collective-permute-start.44
  208.0 6.7 %collective-permute-done.44 = bf16[5,32,256]{2,1,0:T(8,128)(2,1)S(1)} collective-permute-done((bf16[5,32,256]{2,1,0:T(8,128)(2,1)S(1)}, bf16[5,32,256]{2,1,0:T(8,128)(2,1)S(1)}, u32[]{:S(2)}, u32[]{:S(2)}) %collective-permute-start.44) | collective-permute-done | bytes 81952 | tf_op jit(solution)/shard_map/ppermute | solution.py:860
  214.7 1.6 collective-permute-start.68
  216.3 1.5 collective-permute-start.62
  217.9 2.1 collective-permute-start.63
  220.0 2.4 collective-permute-start.45
  222.5 2.9 collective-permute-done.45
  227.0 4.2 %collective-permute-start.46 = (bf16[2,5,32,256]{3,2,1,0:T(8,128)(2,1)S(1)}, bf16[2,5,32,256]{3,2,1,0:T(8,128)(2,1)S(1)}, u32[]{:S(2)}, u32[]{:S(2)}) collective-permute-start(bf16[2,5,32,256]{3,2,1,0:T(8,128)(2,1)S(1)} %pad_maximum_fusion.12.refs_1_), channel_id=1, source_target_pairs={{0,1},{1,0},{2,3},{3,2},{4,5},{5,4},{6,7},{7,6},{8,9},{9,8},{10,11... | collective-permute-start | bytes 491528 | tf_op jit(solution)/shard_map/ppermute | solution.py:860
  231.2 1.7 collective-permute-start.57
  233.6 1.7 collective-permute-start.64
  236.1 2.4 collective-permute-start.47
  243.1 9.7 %collective-permute-done.47.refs_3_ = bf16[2,5,32,256]{3,2,1,0:T(8,128)(2,1)S(1)} collective-permute-done((bf16[2,5,32,256]{3,2,1,0:T(8,128)(2,1)S(1)}, bf16[2,5,32,256]{3,2,1,0:T(8,128)(2,1)S(1)}, u32[]{:S(2)}, u32[]{:S(2)}) %collective-permute-start.47) | collective-permute-done | bytes 163872 | tf_op jit(solution)/shard_map/ppermute | solution.py:860
  252.8 1.7 collective-permute-start.58
  254.5 2.8 collective-permute-done.48.refs_4_
  260.8 1.8 collective-permute-start.49
  273.2 1.6 image_grad.1
  274.8 3.0 %second_out.1 = f32[9,512,256]{2,1,0:T(8,128)} custom-call(s32[4]{0:T(128)S(1)} %pad_add_fusion.refs_0_.refs_1_, bf16[2,9,32,256]{3,2,1,0:T(8,128)(2,1)S(1)} %pad_maximum_fusion.9.refs_11_.refs_1_, bf16[2,9,32,256]{3,2,1,0:T(8,128)(2,1)S(1)} %collective-permute-done.36.refs_4_.refs_2_, bf16[2,9,32,256]{3,2,1,0:T(8,128)(2,1)S(1)} %collective-permute-done.66.refs_3_, ...), custom_call_target="tpu_custom_call" | custom-call | bytes 2359312 | tf_op jit(solution)/shard_map/second_out/pallas_call | solution.py:161
  277.8 3.6 %first_out.1 = f32[9,512,256]{2,1,0:T(8,128)} custom-call(s32[4]{0:T(128)S(1)} %pad_add_fusion.refs_0_.refs_1_, bf16[2,9,32,256]{3,2,1,0:T(8,128)(2,1)S(1)} %pad_maximum_fusion.11.refs_1_, bf16[2,9,32,256]{3,2,1,0:T(8,128)(2,1)S(1)} %collective-permute-done.61.refs_2_, bf16[2,9,32,256]{3,2,1,0:T(8,128)(2,1)S(1)} %collective-permute-done.62.refs_3_, ...), custom_call_target="tpu_custom_call" | custom-call | bytes 2359312 | tf_op jit(solution)/shard_map/first_out/pallas_call | solution.py:161
  282.9 2.9 down_out.1
  285.8 3.7 %mid_out.1 = f32[9,512,256]{2,1,0:T(8,128)} custom-call(s32[4]{0:T(128)S(1)} %pad_add_fusion.refs_0_.refs_1_, bf16[2,9,32,256]{3,2,1,0:T(8,128)(2,1)S(1)} %pad_maximum_fusion.10.refs_1_, bf16[2,9,32,256]{3,2,1,0:T(8,128)(2,1)S(1)} %collective-permute-done.55.refs_2_, bf16[2,9,32,256]{3,2,1,0:T(8,128)(2,1)S(1)} %collective-permute-done.56.refs_3_, ...), custom_call_target="tpu_custom_call" | custom-call | bytes 2359312 | tf_op jit(solution)/shard_map/mid_out/pallas_call | solution.py:161
  (227 shorter events, 54.1 us)
Async XLA Ops:
  5.4 14.0 %collective-permute-start.4 = (bf16[128,512]{1,0:T(8,128)(2,1)S(1)}, bf16[128,512]{1,0:T(8,128)(2,1)S(1)}, u32[]{:S(2)}, u32[]{:S(2)}) collective-permute-start(bf16[128,512]{1,0:T(8,128)(2,1)S(1)} %get-tuple-element.79), channel_id=1, source_target_pairs={{0,2},{1,3},{2,0},{3,1},{4,6},{5,7},{6,4},{7,5},{8,10},{9,11},{10,... | collective-permute-start | bytes 393224 | tf_op jit(solution)/shard_map/ppermute | solution.py:860
  9.5 10.0 %collective-permute-start.5 = (bf16[128,512]{1,0:T(8,128)(2,1)S(1)}, bf16[128,512]{1,0:T(8,128)(2,1)S(1)}, u32[]{:S(2)}, u32[]{:S(2)}) collective-permute-start(bf16[128,512]{1,0:T(8,128)(2,1)S(1)} %get-tuple-element.80), channel_id=1, source_target_pairs={{0,3},{1,2},{2,1},{3,0},{4,7},{5,6},{6,5},{7,4},{8,11},{9,10},{10,... | collective-permute-start | bytes 393224 | tf_op jit(solution)/shard_map/ppermute | solution.py:860
  10.8 15.4 %collective-permute-start = (bf16[144,512]{1,0:T(8,128)(2,1)S(1)}, bf16[144,512]{1,0:T(8,128)(2,1)S(1)}, u32[]{:S(2)}, u32[]{:S(2)}) collective-permute-start(bf16[144,512]{1,0:T(8,128)(2,1)S(1)} %get-tuple-element.76.refs_1_.refs_2_), channel_id=1, source_target_pairs={{0,4},{4,0},{8,12},{12,8},{1,5},{5,1},{9,13},{13,9},{2,6},{6,2},{1... | collective-permute-start | bytes 442376 | tf_op jit(solution)/shard_map/ppermute | solution.py:860
  12.3 15.4 %collective-permute-start.1 = (bf16[144,512]{1,0:T(8,128)(2,1)S(1)}, bf16[144,512]{1,0:T(8,128)(2,1)S(1)}, u32[]{:S(2)}, u32[]{:S(2)}) collective-permute-start(bf16[144,512]{1,0:T(8,128)(2,1)S(1)} %get-tuple-element.76.refs_1_.refs_2_), channel_id=1, source_target_pairs={{0,8},{4,12},{8,0},{12,4},{1,9},{5,13},{9,1},{13,5},{2,10},{6,14},... | collective-permute-start | bytes 442376 | tf_op jit(solution)/shard_map/ppermute | solution.py:860
  13.8 14.1 %collective-permute-start.2 = (bf16[144,512]{1,0:T(8,128)(2,1)S(1)}, bf16[144,512]{1,0:T(8,128)(2,1)S(1)}, u32[]{:S(2)}, u32[]{:S(2)}) collective-permute-start(bf16[144,512]{1,0:T(8,128)(2,1)S(1)} %get-tuple-element.76.refs_1_.refs_2_), channel_id=1, source_target_pairs={{0,12},{4,8},{8,4},{12,0},{1,13},{5,9},{9,5},{13,1},{2,14},{6,10},... | collective-permute-start | bytes 442376 | tf_op jit(solution)/shard_map/ppermute | solution.py:860
  19.4 22.8 %collective-permute-start.7 = (bf16[256,512]{1,0:T(8,128)(2,1)S(1)}, bf16[256,512]{1,0:T(8,128)(2,1)S(1)}, u32[]{:S(2)}, u32[]{:S(2)}) collective-permute-start(bf16[256,512]{1,0:T(8,128)(2,1)S(1)} %constant_dynamic-update-slice_fusion.refs_4_), channel_id=1, source_target_pairs={{0,4},{4,0},{8,12},{12,8},{1,5},{5,1},{9,13},{13,9},{2,6},{6,2},{1... | collective-permute-start | bytes 786440 | tf_op jit(solution)/shard_map/ppermute | solution.py:860
  24.4 7.2 %collective-permute-start.6 = (bf16[128,512]{1,0:T(8,128)(2,1)S(1)}, bf16[128,512]{1,0:T(8,128)(2,1)S(1)}, u32[]{:S(2)}, u32[]{:S(2)}) collective-permute-start(bf16[128,512]{1,0:T(8,128)(2,1)S(1)} %collective-permute-done.3.refs_3_), channel_id=1, source_target_pairs={{0,4},{4,0},{8,12},{12,8},{1,5},{5,1},{9,13},{13,9},{2,6},{6,2},{1... | collective-permute-start | bytes 393224 | tf_op jit(solution)/shard_map/ppermute | solution.py:860
  26.2 16.0 %collective-permute-start.9 = (bf16[256,512]{1,0:T(8,128)(2,1)S(1)}, bf16[256,512]{1,0:T(8,128)(2,1)S(1)}, u32[]{:S(2)}, u32[]{:S(2)}) collective-permute-start(bf16[256,512]{1,0:T(8,128)(2,1)S(1)} %constant_dynamic-update-slice_fusion.refs_4_), channel_id=1, source_target_pairs={{0,8},{4,12},{8,0},{12,4},{1,9},{5,13},{9,1},{13,5},{2,10},{6,14},... | collective-permute-start | bytes 786440 | tf_op jit(solution)/shard_map/ppermute | solution.py:860
  27.7 14.5 %collective-permute-start.11 = (bf16[256,512]{1,0:T(8,128)(2,1)S(1)}, bf16[256,512]{1,0:T(8,128)(2,1)S(1)}, u32[]{:S(2)}, u32[]{:S(2)}) collective-permute-start(bf16[256,512]{1,0:T(8,128)(2,1)S(1)} %constant_dynamic-update-slice_fusion.refs_4_), channel_id=1, source_target_pairs={{0,12},{4,8},{8,4},{12,0},{1,13},{5,9},{9,5},{13,1},{2,14},{6,10},... | collective-permute-start | bytes 786440 | tf_op jit(solution)/shard_map/ppermute | solution.py:860
  27.9 14.3 %collective-permute-start.8 = (bf16[128,512]{1,0:T(8,128)(2,1)S(1)}, bf16[128,512]{1,0:T(8,128)(2,1)S(1)}, u32[]{:S(2)}, u32[]{:S(2)}) collective-permute-start(bf16[128,512]{1,0:T(8,128)(2,1)S(1)} %collective-permute-done.3.refs_3_), channel_id=1, source_target_pairs={{0,8},{4,12},{8,0},{12,4},{1,9},{5,13},{9,1},{13,5},{2,10},{6,14},... | collective-permute-start | bytes 393224 | tf_op jit(solution)/shard_map/ppermute | solution.py:860
  31.5 10.7 %collective-permute-start.10 = (bf16[128,512]{1,0:T(8,128)(2,1)S(1)}, bf16[128,512]{1,0:T(8,128)(2,1)S(1)}, u32[]{:S(2)}, u32[]{:S(2)}) collective-permute-start(bf16[128,512]{1,0:T(8,128)(2,1)S(1)} %collective-permute-done.3.refs_3_), channel_id=1, source_target_pairs={{0,12},{4,8},{8,4},{12,0},{1,13},{5,9},{9,5},{13,1},{2,14},{6,10},... | collective-permute-start | bytes 393224 | tf_op jit(solution)/shard_map/ppermute | solution.py:860
  79.5 5.7 %collective-permute-start.17 = (f32[40,40]{1,0:T(8,128)S(1)}, f32[40,40]{1,0:T(8,128)S(1)}, u32[]{:S(2)}, u32[]{:S(2)}) collective-permute-start(f32[40,40]{1,0:T(8,128)S(1)} %get-tuple-element.94.refs_3_), channel_id=1, source_target_pairs={{0,1},{1,0},{2,3},{3,2},{4,5},{5,4},{6,7},{7,6},{8,9},{9,8},{10,11... | collective-permute-start | bytes 19208 | tf_op jit(solution)/shard_map/ppermute | solution.py:860
  81.1 5.8 %collective-permute-start.18 = (f32[40,40]{1,0:T(8,128)S(1)}, f32[40,40]{1,0:T(8,128)S(1)}, u32[]{:S(2)}, u32[]{:S(2)}) collective-permute-start(f32[40,40]{1,0:T(8,128)S(1)} %get-tuple-element.94.refs_3_), channel_id=1, source_target_pairs={{0,2},{1,3},{2,0},{3,1},{4,6},{5,7},{6,4},{7,5},{8,10},{9,11},{10,... | collective-permute-start | bytes 19208 | tf_op jit(solution)/shard_map/ppermute | solution.py:860
  85.2 5.6 %collective-permute-start.19 = (f32[40,40]{1,0:T(8,128)S(1)}, f32[40,40]{1,0:T(8,128)S(1)}, u32[]{:S(2)}, u32[]{:S(2)}) collective-permute-start(f32[40,40]{1,0:T(8,128)S(1)} %get-tuple-element.94.refs_3_), channel_id=1, source_target_pairs={{0,3},{1,2},{2,1},{3,0},{4,7},{5,6},{6,5},{7,4},{8,11},{9,10},{10,... | collective-permute-start | bytes 19208 | tf_op jit(solution)/shard_map/ppermute | solution.py:860
  99.3 7.8 %collective-permute-start.21 = (bf16[4,9,32,256]{3,2,1,0:T(8,128)(2,1)S(1)}, bf16[4,9,32,256]{3,2,1,0:T(8,128)(2,1)S(1)}, u32[]{:S(2)}, u32[]{:S(2)}) collective-permute-start(bf16[4,9,32,256]{3,2,1,0:T(8,128)(2,1)S(1)} %get-tuple-element.103.refs_6_), channel_id=1, source_target_pairs={{0,16},{16,0},{1,17},{17,1},{2,18},{18,2},{3,19},{19,3},{4,20},{20... | collective-permute-start | bytes 1769480 | tf_op jit(solution)/shard_map/ppermute | solution.py:860
  106.6 5.3 %collective-permute-start.20 = (f32[8,512]{1,0:T(8,128)S(1)}, f32[8,512]{1,0:T(8,128)S(1)}, u32[]{:S(2)}, u32[]{:S(2)}) collective-permute-start(f32[8,512]{1,0:T(8,128)S(1)} %get-tuple-element.104.refs_4_.refs_3_), channel_id=1, source_target_pairs={{0,16},{16,0},{1,17},{17,1},{2,18},{18,2},{3,19},{19,3},{4,20},{20... | collective-permute-start | bytes 49160 | tf_op jit(solution)/shard_map/ppermute | solution.py:860
  107.5 18.1 %collective-permute-start.26 = (bf16[9,32,256]{2,1,0:T(8,128)(2,1)S(1)}, bf16[9,32,256]{2,1,0:T(8,128)(2,1)S(1)}, u32[]{:S(2)}, u32[]{:S(2)}) collective-permute-start(bf16[9,32,256]{2,1,0:T(8,128)(2,1)S(1)} %get-tuple-element.154), channel_id=1, source_target_pairs={{0,3},{1,2},{2,1},{3,0},{4,7},{5,6},{6,5},{7,4},{8,11},{9,10},{10,... | collective-permute-start | bytes 442376 | tf_op jit(solution)/shard_map/ppermute | solution.py:860
  107.8 17.8 %collective-permute-start.25 = (bf16[9,32,256]{2,1,0:T(8,128)(2,1)S(1)}, bf16[9,32,256]{2,1,0:T(8,128)(2,1)S(1)}, u32[]{:S(2)}, u32[]{:S(2)}) collective-permute-start(bf16[9,32,256]{2,1,0:T(8,128)(2,1)S(1)} %get-tuple-element.155), channel_id=1, source_target_pairs={{0,2},{1,3},{2,0},{3,1},{4,6},{5,7},{6,4},{7,5},{8,10},{9,11},{10,... | collective-permute-start | bytes 442376 | tf_op jit(solution)/shard_map/ppermute | solution.py:860
  107.8 17.8 %collective-permute-start.24 = (bf16[9,32,256]{2,1,0:T(8,128)(2,1)S(1)}, bf16[9,32,256]{2,1,0:T(8,128)(2,1)S(1)}, u32[]{:S(2)}, u32[]{:S(2)}) collective-permute-start(bf16[9,32,256]{2,1,0:T(8,128)(2,1)S(1)} %get-tuple-element.153), channel_id=1, source_target_pairs={{0,1},{1,0},{2,3},{3,2},{4,5},{5,4},{6,7},{7,6},{8,9},{9,8},{10,11... | collective-permute-start | bytes 442376 | tf_op jit(solution)/shard_map/ppermute | solution.py:860
  125.5 10.7 %collective-permute-start.23 = (bf16[4,9,32,256]{3,2,1,0:T(8,128)(2,1)S(1)}, bf16[4,9,32,256]{3,2,1,0:T(8,128)(2,1)S(1)}, u32[]{:S(2)}, u32[]{:S(2)}) collective-permute-start(bf16[4,9,32,256]{3,2,1,0:T(8,128)(2,1)S(1)} %get-tuple-element.114), channel_id=1, source_target_pairs={{0,16},{16,0},{1,17},{17,1},{2,18},{18,2},{3,19},{19,3},{4,20},{20... | collective-permute-start | bytes 1769480 | tf_op jit(solution)/shard_map/ppermute | solution.py:860
  125.7 9.8 %collective-permute-start.31 = (bf16[9,32,256]{2,1,0:T(8,128)(2,1)S(1)}, bf16[9,32,256]{2,1,0:T(8,128)(2,1)S(1)}, u32[]{:S(2)}, u32[]{:S(2)}) collective-permute-start(bf16[9,32,256]{2,1,0:T(8,128)(2,1)S(1)} %fusion.8.refs_12_), channel_id=1, source_target_pairs={{0,2},{1,3},{2,0},{3,1},{4,6},{5,7},{6,4},{7,5},{8,10},{9,11},{10,... | collective-permute-start | bytes 442376 | tf_op jit(solution)/shard_map/ppermute | solution.py:860
  125.8 10.7 %collective-permute-start.22 = (f32[8,512]{1,0:T(8,128)S(1)}, f32[8,512]{1,0:T(8,128)S(1)}, u32[]{:S(2)}, u32[]{:S(2)}) collective-permute-start(f32[8,512]{1,0:T(8,128)S(1)} %get-tuple-element.109.refs_5_), channel_id=1, source_target_pairs={{0,16},{16,0},{1,17},{17,1},{2,18},{18,2},{3,19},{19,3},{4,20},{20... | collective-permute-start | bytes 49160 | tf_op jit(solution)/shard_map/ppermute | solution.py:860
  135.5 18.0 %collective-permute-start.36 = (bf16[2,9,32,256]{3,2,1,0:T(8,128)(2,1)S(1)}, bf16[2,9,32,256]{3,2,1,0:T(8,128)(2,1)S(1)}, u32[]{:S(2)}, u32[]{:S(2)}) collective-permute-start(bf16[2,9,32,256]{3,2,1,0:T(8,128)(2,1)S(1)} %pad_maximum_fusion.9.refs_11_.refs_1_), channel_id=1, source_target_pairs={{0,1},{1,0},{2,3},{3,2},{4,5},{5,4},{6,7},{7,6},{8,9},{9,8},{10,11... | collective-permute-start | bytes 884744 | tf_op jit(solution)/shard_map/ppermute | solution.py:860
  135.6 13.0 %collective-permute-start.66 = (bf16[2,9,32,256]{3,2,1,0:T(8,128)(2,1)S(1)}, bf16[2,9,32,256]{3,2,1,0:T(8,128)(2,1)S(1)}, u32[]{:S(2)}, u32[]{:S(2)}) collective-permute-start(bf16[2,9,32,256]{3,2,1,0:T(8,128)(2,1)S(1)} %pad_maximum_fusion.9.refs_11_.refs_1_), channel_id=1, source_target_pairs={{0,4},{4,0},{8,12},{12,8},{1,5},{5,1},{9,13},{13,9},{2,6},{6,2},{1... | collective-permute-start | bytes 884744 | tf_op jit(solution)/shard_map/ppermute | solution.py:860
  145.0 8.6 %collective-permute-start.27 = (f32[8,512]{1,0:T(8,128)S(1)}, f32[8,512]{1,0:T(8,128)S(1)}, u32[]{:S(2)}, u32[]{:S(2)}) collective-permute-start(f32[8,512]{1,0:T(8,128)S(1)} %get-tuple-element.115.refs_7_.refs_5_), channel_id=1, source_target_pairs={{0,16},{16,0},{1,17},{17,1},{2,18},{18,2},{3,19},{19,3},{4,20},{20... | collective-permute-start | bytes 49160 | tf_op jit(solution)/shard_map/ppermute | solution.py:860
  145.1 12.8 %collective-permute-start.40 = (bf16[9,32,256]{2,1,0:T(8,128)(2,1)S(1)}, bf16[9,32,256]{2,1,0:T(8,128)(2,1)S(1)}, u32[]{:S(2)}, u32[]{:S(2)}) collective-permute-start(bf16[9,32,256]{2,1,0:T(8,128)(2,1)S(1)} %get-tuple-element.151), channel_id=1, source_target_pairs={{0,3},{1,2},{2,1},{3,0},{4,7},{5,6},{6,5},{7,4},{8,11},{9,10},{10,... | collective-permute-start | bytes 442376 | tf_op jit(solution)/shard_map/ppermute | solution.py:860
  146.1 20.8 %collective-permute-start.39 = (bf16[9,32,256]{2,1,0:T(8,128)(2,1)S(1)}, bf16[9,32,256]{2,1,0:T(8,128)(2,1)S(1)}, u32[]{:S(2)}, u32[]{:S(2)}) collective-permute-start(bf16[9,32,256]{2,1,0:T(8,128)(2,1)S(1)} %get-tuple-element.152), channel_id=1, source_target_pairs={{0,2},{1,3},{2,0},{3,1},{4,6},{5,7},{6,4},{7,5},{8,10},{9,11},{10,... | collective-permute-start | bytes 442376 | tf_op jit(solution)/shard_map/ppermute | solution.py:860
  148.5 18.3 %collective-permute-start.38 = (bf16[9,32,256]{2,1,0:T(8,128)(2,1)S(1)}, bf16[9,32,256]{2,1,0:T(8,128)(2,1)S(1)}, u32[]{:S(2)}, u32[]{:S(2)}) collective-permute-start(bf16[9,32,256]{2,1,0:T(8,128)(2,1)S(1)} %get-tuple-element.150), channel_id=1, source_target_pairs={{0,1},{1,0},{2,3},{3,2},{4,5},{5,4},{6,7},{7,6},{8,9},{9,8},{10,11... | collective-permute-start | bytes 442376 | tf_op jit(solution)/shard_map/ppermute | solution.py:860
  153.5 22.6 %collective-permute-start.37 = (bf16[4,9,32,256]{3,2,1,0:T(8,128)(2,1)S(1)}, bf16[4,9,32,256]{3,2,1,0:T(8,128)(2,1)S(1)}, u32[]{:S(2)}, u32[]{:S(2)}) collective-permute-start(bf16[4,9,32,256]{3,2,1,0:T(8,128)(2,1)S(1)} %get-tuple-element.121.refs_12_), channel_id=1, source_target_pairs={{0,16},{16,0},{1,17},{17,1},{2,18},{18,2},{3,19},{19,3},{4,20},{20... | collective-permute-start | bytes 1769480 | tf_op jit(solution)/shard_map/ppermute | solution.py:860
  153.6 52.1 %collective-permute-start.67 = (bf16[2,9,32,256]{3,2,1,0:T(8,128)(2,1)S(1)}, bf16[2,9,32,256]{3,2,1,0:T(8,128)(2,1)S(1)}, u32[]{:S(2)}, u32[]{:S(2)}) collective-permute-start(bf16[2,9,32,256]{3,2,1,0:T(8,128)(2,1)S(1)} %collective-permute-done.36.refs_4_.refs_2_), channel_id=1, source_target_pairs={{0,8},{4,12},{8,0},{12,4},{1,9},{5,13},{9,1},{13,5},{2,10},{6,14},... | collective-permute-start | bytes 884744 | tf_op jit(solution)/shard_map/ppermute | solution.py:860
  157.8 9.2 %collective-permute-start.34 = (bf16[2,2,2,32,256]{4,3,2,1,0:T(8,128)(2,1)S(1)}, bf16[2,2,2,32,256]{4,3,2,1,0:T(8,128)(2,1)S(1)}, u32[]{:S(2)}, u32[]{:S(2)}) collective-permute-start(bf16[2,2,2,32,256]{4,3,2,1,0:T(8,128)(2,1)S(1)} %get-tuple-element.125), channel_id=1, source_target_pairs={{0,3},{1,2},{2,1},{3,0},{4,7},{5,6},{6,5},{7,4},{8,11},{9,10},{10,... | collective-permute-start | bytes 393224 | tf_op jit(solution)/shard_map/ppermute | solution.py:860
  166.8 7.8 %collective-permute-start.33 = (bf16[2,2,2,32,256]{4,3,2,1,0:T(8,128)(2,1)S(1)}, bf16[2,2,2,32,256]{4,3,2,1,0:T(8,128)(2,1)S(1)}, u32[]{:S(2)}, u32[]{:S(2)}) collective-permute-start(bf16[2,2,2,32,256]{4,3,2,1,0:T(8,128)(2,1)S(1)} %get-tuple-element.124), channel_id=1, source_target_pairs={{0,2},{1,3},{2,0},{3,1},{4,6},{5,7},{6,4},{7,5},{8,10},{9,11},{10,... | collective-permute-start | bytes 393224 | tf_op jit(solution)/shard_map/ppermute | solution.py:860
  166.9 8.5 %collective-permute-start.32 = (bf16[2,2,2,32,256]{4,3,2,1,0:T(8,128)(2,1)S(1)}, bf16[2,2,2,32,256]{4,3,2,1,0:T(8,128)(2,1)S(1)}, u32[]{:S(2)}, u32[]{:S(2)}) collective-permute-start(bf16[2,2,2,32,256]{4,3,2,1,0:T(8,128)(2,1)S(1)} %get-tuple-element.123), channel_id=1, source_target_pairs={{0,1},{1,0},{2,3},{3,2},{4,5},{5,4},{6,7},{7,6},{8,9},{9,8},{10,11... | collective-permute-start | bytes 393224 | tf_op jit(solution)/shard_map/ppermute | solution.py:860
  167.1 19.8 %collective-permute-start.60 = (bf16[9,32,256]{2,1,0:T(8,128)(2,1)S(1)}, bf16[9,32,256]{2,1,0:T(8,128)(2,1)S(1)}, u32[]{:S(2)}, u32[]{:S(2)}) collective-permute-start(bf16[9,32,256]{2,1,0:T(8,128)(2,1)S(1)} %fusion.5.refs_6_), channel_id=1, source_target_pairs={{0,2},{1,3},{2,0},{3,1},{4,6},{5,7},{6,4},{7,5},{8,10},{9,11},{10,... | collective-permute-start | bytes 442376 | tf_op jit(solution)/shard_map/ppermute | solution.py:860
  176.5 10.4 %collective-permute-start.53 = (bf16[9,32,256]{2,1,0:T(8,128)(2,1)S(1)}, bf16[9,32,256]{2,1,0:T(8,128)(2,1)S(1)}, u32[]{:S(2)}, u32[]{:S(2)}) collective-permute-start(bf16[9,32,256]{2,1,0:T(8,128)(2,1)S(1)} %get-tuple-element.148), channel_id=1, source_target_pairs={{0,3},{1,2},{2,1},{3,0},{4,7},{5,6},{6,5},{7,4},{8,11},{9,10},{10,... | collective-permute-start | bytes 442376 | tf_op jit(solution)/shard_map/ppermute | solution.py:860
  177.2 15.4 %collective-permute-start.52 = (bf16[9,32,256]{2,1,0:T(8,128)(2,1)S(1)}, bf16[9,32,256]{2,1,0:T(8,128)(2,1)S(1)}, u32[]{:S(2)}, u32[]{:S(2)}) collective-permute-start(bf16[9,32,256]{2,1,0:T(8,128)(2,1)S(1)} %get-tuple-element.149), channel_id=1, source_target_pairs={{0,2},{1,3},{2,0},{3,1},{4,6},{5,7},{6,4},{7,5},{8,10},{9,11},{10,... | collective-permute-start | bytes 442376 | tf_op jit(solution)/shard_map/ppermute | solution.py:860
  177.5 15.0 %collective-permute-start.51 = (bf16[9,32,256]{2,1,0:T(8,128)(2,1)S(1)}, bf16[9,32,256]{2,1,0:T(8,128)(2,1)S(1)}, u32[]{:S(2)}, u32[]{:S(2)}) collective-permute-start(bf16[9,32,256]{2,1,0:T(8,128)(2,1)S(1)} %get-tuple-element.147), channel_id=1, source_target_pairs={{0,1},{1,0},{2,3},{3,2},{4,5},{5,4},{6,7},{7,6},{8,9},{9,8},{10,11... | collective-permute-start | bytes 442376 | tf_op jit(solution)/shard_map/ppermute | solution.py:860
  186.9 7.0 %collective-permute-start.41 = (bf16[4,5,32,256]{3,2,1,0:T(8,128)(2,1)S(1)}, bf16[4,5,32,256]{3,2,1,0:T(8,128)(2,1)S(1)}, u32[]{:S(2)}, u32[]{:S(2)}) collective-permute-start(bf16[4,5,32,256]{3,2,1,0:T(8,128)(2,1)S(1)} %get-tuple-element.130), channel_id=1, source_target_pairs={{0,16},{16,0},{1,17},{17,1},{2,18},{18,2},{3,19},{19,3},{4,20},{20... | collective-permute-start | bytes 983048 | tf_op jit(solution)/shard_map/ppermute | solution.py:860
  186.9 9.1 %collective-permute-start.28 = (f32[64,256]{1,0:T(8,128)S(1)}, f32[64,256]{1,0:T(8,128)S(1)}, u32[]{:S(2)}, u32[]{:S(2)}) collective-permute-start(f32[64,256]{1,0:T(8,128)S(1)} %small.1.refs_1_), channel_id=1, source_target_pairs={{0,1},{1,0},{2,3},{3,2},{4,5},{5,4},{6,7},{7,6},{8,9},{9,8},{10,11... | collective-permute-start | bytes 196616 | tf_op jit(solution)/shard_map/ppermute | solution.py:860
  192.5 9.8 %collective-permute-start.29 = (f32[64,256]{1,0:T(8,128)S(1)}, f32[64,256]{1,0:T(8,128)S(1)}, u32[]{:S(2)}, u32[]{:S(2)}) collective-permute-start(f32[64,256]{1,0:T(8,128)S(1)} %small.1.refs_1_), channel_id=1, source_target_pairs={{0,2},{1,3},{2,0},{3,1},{4,6},{5,7},{6,4},{7,5},{8,10},{9,11},{10,... | collective-permute-start | bytes 196616 | tf_op jit(solution)/shard_map/ppermute | solution.py:860
  192.6 10.4 %collective-permute-start.30 = (f32[64,256]{1,0:T(8,128)S(1)}, f32[64,256]{1,0:T(8,128)S(1)}, u32[]{:S(2)}, u32[]{:S(2)}) collective-permute-start(f32[64,256]{1,0:T(8,128)S(1)} %small.1.refs_1_), channel_id=1, source_target_pairs={{0,3},{1,2},{2,1},{3,0},{4,7},{5,6},{6,5},{7,4},{8,11},{9,10},{10,... | collective-permute-start | bytes 196616 | tf_op jit(solution)/shard_map/ppermute | solution.py:860
  193.8 13.2 %collective-permute-start.54 = (bf16[9,32,256]{2,1,0:T(8,128)(2,1)S(1)}, bf16[9,32,256]{2,1,0:T(8,128)(2,1)S(1)}, u32[]{:S(2)}, u32[]{:S(2)}) collective-permute-start(bf16[9,32,256]{2,1,0:T(8,128)(2,1)S(1)} %fusion.2), channel_id=1, source_target_pairs={{0,2},{1,3},{2,0},{3,1},{4,6},{5,7},{6,4},{7,5},{8,10},{9,11},{10,... | collective-permute-start | bytes 442376 | tf_op jit(solution)/shard_map/ppermute | solution.py:860
  196.6 23.4 %collective-permute-start.35 = (bf16[4,2,2,32,256]{4,3,2,1,0:T(8,128)(2,1)S(1)}, bf16[4,2,2,32,256]{4,3,2,1,0:T(8,128)(2,1)S(1)}, u32[]{:S(2)}, u32[]{:S(2)}) collective-permute-start(bf16[4,2,2,32,256]{4,3,2,1,0:T(8,128)(2,1)S(1)} %get-tuple-element.156), channel_id=1, source_target_pairs={{0,16},{16,0},{1,17},{17,1},{2,18},{18,2},{3,19},{19,3},{4,20},{20... | collective-permute-start | bytes 786440 | tf_op jit(solution)/shard_map/ppermute | solution.py:860
  202.9 14.9 %collective-permute-start.61 = (bf16[2,9,32,256]{3,2,1,0:T(8,128)(2,1)S(1)}, bf16[2,9,32,256]{3,2,1,0:T(8,128)(2,1)S(1)}, u32[]{:S(2)}, u32[]{:S(2)}) collective-permute-start(bf16[2,9,32,256]{3,2,1,0:T(8,128)(2,1)S(1)} %pad_maximum_fusion.11.refs_1_), channel_id=1, source_target_pairs={{0,1},{1,0},{2,3},{3,2},{4,5},{5,4},{6,7},{7,6},{8,9},{9,8},{10,11... | collective-permute-start | bytes 884744 | tf_op jit(solution)/shard_map/ppermute | solution.py:860
  203.6 11.1 %collective-permute-start.44 = (bf16[5,32,256]{2,1,0:T(8,128)(2,1)S(1)}, bf16[5,32,256]{2,1,0:T(8,128)(2,1)S(1)}, u32[]{:S(2)}, u32[]{:S(2)}) collective-permute-start(bf16[5,32,256]{2,1,0:T(8,128)(2,1)S(1)} %get-tuple-element.159), channel_id=1, source_target_pairs={{0,3},{1,2},{2,1},{3,0},{4,7},{5,6},{6,5},{7,4},{8,11},{9,10},{10,... | collective-permute-start | bytes 245768 | tf_op jit(solution)/shard_map/ppermute | solution.py:860
  205.7 10.7 %collective-permute-start.43 = (bf16[5,32,256]{2,1,0:T(8,128)(2,1)S(1)}, bf16[5,32,256]{2,1,0:T(8,128)(2,1)S(1)}, u32[]{:S(2)}, u32[]{:S(2)}) collective-permute-start(bf16[5,32,256]{2,1,0:T(8,128)(2,1)S(1)} %get-tuple-element.160), channel_id=1, source_target_pairs={{0,2},{1,3},{2,0},{3,1},{4,6},{5,7},{6,4},{7,5},{8,10},{9,11},{10,... | collective-permute-start | bytes 245768 | tf_op jit(solution)/shard_map/ppermute | solution.py:860
  207.1 10.8 %collective-permute-start.42 = (bf16[5,32,256]{2,1,0:T(8,128)(2,1)S(1)}, bf16[5,32,256]{2,1,0:T(8,128)(2,1)S(1)}, u32[]{:S(2)}, u32[]{:S(2)}) collective-permute-start(bf16[5,32,256]{2,1,0:T(8,128)(2,1)S(1)} %get-tuple-element.158), channel_id=1, source_target_pairs={{0,1},{1,0},{2,3},{3,2},{4,5},{5,4},{6,7},{7,6},{8,9},{9,8},{10,11... | collective-permute-start | bytes 245768 | tf_op jit(solution)/shard_map/ppermute | solution.py:860
  214.7 18.2 %collective-permute-start.68 = (bf16[4,9,32,256]{3,2,1,0:T(8,128)(2,1)S(1)}, bf16[4,9,32,256]{3,2,1,0:T(8,128)(2,1)S(1)}, u32[]{:S(2)}, u32[]{:S(2)}) collective-permute-start(bf16[4,9,32,256]{3,2,1,0:T(8,128)(2,1)S(1)} %pad_maximum_fusion.4), channel_id=1, source_target_pairs={{0,8},{4,12},{8,0},{12,4},{1,9},{5,13},{9,1},{13,5},{2,10},{6,14},... | collective-permute-start | bytes 1769480 | tf_op jit(solution)/shard_map/ppermute | solution.py:860
  216.3 10.6 %collective-permute-start.62 = (bf16[2,9,32,256]{3,2,1,0:T(8,128)(2,1)S(1)}, bf16[2,9,32,256]{3,2,1,0:T(8,128)(2,1)S(1)}, u32[]{:S(2)}, u32[]{:S(2)}) collective-permute-start(bf16[2,9,32,256]{3,2,1,0:T(8,128)(2,1)S(1)} %pad_maximum_fusion.11.refs_1_), channel_id=1, source_target_pairs={{0,4},{4,0},{8,12},{12,8},{1,5},{5,1},{9,13},{13,9},{2,6},{6,2},{1... | collective-permute-start | bytes 884744 | tf_op jit(solution)/shard_map/ppermute | solution.py:860
  217.8 13.4 %collective-permute-start.55 = (bf16[2,9,32,256]{3,2,1,0:T(8,128)(2,1)S(1)}, bf16[2,9,32,256]{3,2,1,0:T(8,128)(2,1)S(1)}, u32[]{:S(2)}, u32[]{:S(2)}) collective-permute-start(bf16[2,9,32,256]{3,2,1,0:T(8,128)(2,1)S(1)} %pad_maximum_fusion.10.refs_1_), channel_id=1, source_target_pairs={{0,1},{1,0},{2,3},{3,2},{4,5},{5,4},{6,7},{7,6},{8,9},{9,8},{10,11... | collective-permute-start | bytes 884744 | tf_op jit(solution)/shard_map/ppermute | solution.py:860
  217.9 15.7 %collective-permute-start.63 = (bf16[2,9,32,256]{3,2,1,0:T(8,128)(2,1)S(1)}, bf16[2,9,32,256]{3,2,1,0:T(8,128)(2,1)S(1)}, u32[]{:S(2)}, u32[]{:S(2)}) collective-permute-start(bf16[2,9,32,256]{3,2,1,0:T(8,128)(2,1)S(1)} %collective-permute-done.61.refs_2_), channel_id=1, source_target_pairs={{0,8},{4,12},{8,0},{12,4},{1,9},{5,13},{9,1},{13,5},{2,10},{6,14},... | collective-permute-start | bytes 884744 | tf_op jit(solution)/shard_map/ppermute | solution.py:860
  220.0 5.4 %collective-permute-start.45 = (bf16[5,32,256]{2,1,0:T(8,128)(2,1)S(1)}, bf16[5,32,256]{2,1,0:T(8,128)(2,1)S(1)}, u32[]{:S(2)}, u32[]{:S(2)}) collective-permute-start(bf16[5,32,256]{2,1,0:T(8,128)(2,1)S(1)} %fusion.11), channel_id=1, source_target_pairs={{0,2},{1,3},{2,0},{3,1},{4,6},{5,7},{6,4},{7,5},{8,10},{9,11},{10,... | collective-permute-start | bytes 245768 | tf_op jit(solution)/shard_map/ppermute | solution.py:860
  225.4 10.7 %collective-permute-start.56 = (bf16[2,9,32,256]{3,2,1,0:T(8,128)(2,1)S(1)}, bf16[2,9,32,256]{3,2,1,0:T(8,128)(2,1)S(1)}, u32[]{:S(2)}, u32[]{:S(2)}) collective-permute-start(bf16[2,9,32,256]{3,2,1,0:T(8,128)(2,1)S(1)} %pad_maximum_fusion.10.refs_1_), channel_id=1, source_target_pairs={{0,4},{4,0},{8,12},{12,8},{1,5},{5,1},{9,13},{13,9},{2,6},{6,2},{1... | collective-permute-start | bytes 884744 | tf_op jit(solution)/shard_map/ppermute | solution.py:860
  227.0 11.6 %collective-permute-start.46 = (bf16[2,5,32,256]{3,2,1,0:T(8,128)(2,1)S(1)}, bf16[2,5,32,256]{3,2,1,0:T(8,128)(2,1)S(1)}, u32[]{:S(2)}, u32[]{:S(2)}) collective-permute-start(bf16[2,5,32,256]{3,2,1,0:T(8,128)(2,1)S(1)} %pad_maximum_fusion.12.refs_1_), channel_id=1, source_target_pairs={{0,1},{1,0},{2,3},{3,2},{4,5},{5,4},{6,7},{7,6},{8,9},{9,8},{10,11... | collective-permute-start | bytes 491528 | tf_op jit(solution)/shard_map/ppermute | solution.py:860
  231.2 9.9 %collective-permute-start.57 = (bf16[2,9,32,256]{3,2,1,0:T(8,128)(2,1)S(1)}, bf16[2,9,32,256]{3,2,1,0:T(8,128)(2,1)S(1)}, u32[]{:S(2)}, u32[]{:S(2)}) collective-permute-start(bf16[2,9,32,256]{3,2,1,0:T(8,128)(2,1)S(1)} %collective-permute-done.55.refs_2_), channel_id=1, source_target_pairs={{0,8},{4,12},{8,0},{12,4},{1,9},{5,13},{9,1},{13,5},{2,10},{6,14},... | collective-permute-start | bytes 884744 | tf_op jit(solution)/shard_map/ppermute | solution.py:860
  233.0 27.0 %collective-permute-start.69 = (bf16[4,9,32,256]{3,2,1,0:T(8,128)(2,1)S(1)}, bf16[4,9,32,256]{3,2,1,0:T(8,128)(2,1)S(1)}, u32[]{:S(2)}, u32[]{:S(2)}) collective-permute-start(bf16[4,9,32,256]{3,2,1,0:T(8,128)(2,1)S(1)} %pad_maximum_fusion.5), channel_id=1, source_target_pairs={{0,4},{4,0},{8,12},{12,8},{1,5},{5,1},{9,13},{13,9},{2,6},{6,2},{1... | collective-permute-start | bytes 1769480 | tf_op jit(solution)/shard_map/ppermute | solution.py:860
  233.6 29.0 %collective-permute-start.64 = (bf16[4,9,32,256]{3,2,1,0:T(8,128)(2,1)S(1)}, bf16[4,9,32,256]{3,2,1,0:T(8,128)(2,1)S(1)}, u32[]{:S(2)}, u32[]{:S(2)}) collective-permute-start(bf16[4,9,32,256]{3,2,1,0:T(8,128)(2,1)S(1)} %pad_maximum_fusion.2), channel_id=1, source_target_pairs={{0,8},{4,12},{8,0},{12,4},{1,9},{5,13},{9,1},{13,5},{2,10},{6,14},... | collective-permute-start | bytes 1769480 | tf_op jit(solution)/shard_map/ppermute | solution.py:860
  236.1 16.7 %collective-permute-start.47 = (bf16[2,5,32,256]{3,2,1,0:T(8,128)(2,1)S(1)}, bf16[2,5,32,256]{3,2,1,0:T(8,128)(2,1)S(1)}, u32[]{:S(2)}, u32[]{:S(2)}) collective-permute-start(bf16[2,5,32,256]{3,2,1,0:T(8,128)(2,1)S(1)} %pad_maximum_fusion.12.refs_1_), channel_id=1, source_target_pairs={{0,4},{4,0},{8,12},{12,8},{1,5},{5,1},{9,13},{13,9},{2,6},{6,2},{1... | collective-permute-start | bytes 491528 | tf_op jit(solution)/shard_map/ppermute | solution.py:860
  238.6 18.7 %collective-permute-start.48 = (bf16[2,5,32,256]{3,2,1,0:T(8,128)(2,1)S(1)}, bf16[2,5,32,256]{3,2,1,0:T(8,128)(2,1)S(1)}, u32[]{:S(2)}, u32[]{:S(2)}) collective-permute-start(bf16[2,5,32,256]{3,2,1,0:T(8,128)(2,1)S(1)} %collective-permute-done.46.refs_2_), channel_id=1, source_target_pairs={{0,8},{4,12},{8,0},{12,4},{1,9},{5,13},{9,1},{13,5},{2,10},{6,14},... | collective-permute-start | bytes 491528 | tf_op jit(solution)/shard_map/ppermute | solution.py:860
  241.1 36.7 %collective-permute-start.65 = (bf16[4,9,32,256]{3,2,1,0:T(8,128)(2,1)}, bf16[4,9,32,256]{3,2,1,0:T(8,128)(2,1)}, u32[]{:S(2)}, u32[]{:S(2)}) collective-permute-start(bf16[4,9,32,256]{3,2,1,0:T(8,128)(2,1)} %pad_maximum_fusion.3), channel_id=1, source_target_pairs={{0,4},{4,0},{8,12},{12,8},{1,5},{5,1},{9,13},{13,9},{2,6},{6,2},{1... | collective-permute-start | bytes 1769480 | tf_op jit(solution)/shard_map/ppermute | solution.py:860
  252.8 32.9 %collective-permute-start.58 = (bf16[4,9,32,256]{3,2,1,0:T(8,128)(2,1)}, bf16[4,9,32,256]{3,2,1,0:T(8,128)(2,1)}, u32[]{:S(2)}, u32[]{:S(2)}) collective-permute-start(bf16[4,9,32,256]{3,2,1,0:T(8,128)(2,1)} %pad_maximum_fusion), channel_id=1, source_target_pairs={{0,8},{4,12},{8,0},{12,4},{1,9},{5,13},{9,1},{13,5},{2,10},{6,14},... | collective-permute-start | bytes 1769480 | tf_op jit(solution)/shard_map/ppermute | solution.py:860
  257.3 28.5 %collective-permute-start.59 = (bf16[4,9,32,256]{3,2,1,0:T(8,128)(2,1)}, bf16[4,9,32,256]{3,2,1,0:T(8,128)(2,1)}, u32[]{:S(2)}, u32[]{:S(2)}) collective-permute-start(bf16[4,9,32,256]{3,2,1,0:T(8,128)(2,1)} %pad_maximum_fusion.1), channel_id=1, source_target_pairs={{0,4},{4,0},{8,12},{12,8},{1,5},{5,1},{9,13},{13,9},{2,6},{6,2},{1... | collective-permute-start | bytes 1769480 | tf_op jit(solution)/shard_map/ppermute | solution.py:860
  260.8 20.7 %collective-permute-start.49 = (bf16[4,5,32,256]{3,2,1,0:T(8,128)(2,1)}, bf16[4,5,32,256]{3,2,1,0:T(8,128)(2,1)}, u32[]{:S(2)}, u32[]{:S(2)}) collective-permute-start(bf16[4,5,32,256]{3,2,1,0:T(8,128)(2,1)} %pad_maximum_fusion.7), channel_id=1, source_target_pairs={{0,8},{4,12},{8,0},{12,4},{1,9},{5,13},{9,1},{13,5},{2,10},{6,14},... | collective-permute-start | bytes 983048 | tf_op jit(solution)/shard_map/ppermute | solution.py:860
  263.4 19.5 %collective-permute-start.50 = (bf16[4,5,32,256]{3,2,1,0:T(8,128)(2,1)}, bf16[4,5,32,256]{3,2,1,0:T(8,128)(2,1)}, u32[]{:S(2)}, u32[]{:S(2)}) collective-permute-start(bf16[4,5,32,256]{3,2,1,0:T(8,128)(2,1)} %pad_maximum_fusion.8), channel_id=1, source_target_pairs={{0,4},{4,0},{8,12},{12,8},{1,5},{5,1},{9,13},{13,9},{2,6},{6,2},{1... | collective-permute-start | bytes 983048 | tf_op jit(solution)/shard_map/ppermute | solution.py:860
  (50 other events, 315.6 us)

commit v4 on v3

--- a/solution.py
+++ b/solution.py
@@ -593,15 +593,16 @@
     slope_sums(facts_ref, in_ref, norm1_ref, gain, bias, conv_ref, up_ref, sum_ref)
 
 
-def down_back_kernel(where_ref, facts_ref, up_in, in_ref, norm1_ref, own_ref, other_ref, params_ref,
-                     low_s_ref, w_ref, s_ref, low_ref, o0, o1, o2, o3, stage_ref):
-    pipe, batch, zone = where_ref[0], where_ref[1], where_ref[2]
-
+def down_back_kernel(facts_ref, up_in, in_ref, norm1_ref, own_ref, other_ref, params_ref, low_ref):
     def keep(image, r, low):
         low_ref[image, band(r), :] = low
 
     gain = param(params_ref, G_DOWN)
     back_norm(facts_ref, in_ref, up_in, norm1_ref, own_ref, other_ref, gain, 0, keep)
+
+
+def image_back_kernel(where_ref, low_ref, low_s_ref, w_ref, s_ref, o0, o1, o2, o3, stage_ref):
+    pipe, batch, zone = where_ref[0], where_ref[1], where_ref[2]
     mine = pl.ds(batch * 2, 2)
     here = low_ref[mine]
     below = jnp.concatenate([here[:, 32:], jnp.zeros((2, 32, 512), BF16)], axis=1)
@@ -667,6 +668,11 @@
         other_ref[slot, unit] = result_other[rows].astype(BF16)
 
 
+def hand_out(other_ref, outs):
+    for slot, out in enumerate(outs):
+        out[...] = other_ref[slot]
+
+
 def turned_taps(batch, act_ref, turned_ref):
     lanes = pl.ds(pl.multiple_of(batch * 128, 128), 128)
 
@@ -693,10 +699,11 @@
         split_out(pipe, zone, unit, results[0][rows], results[1][rows], own_ref, other_ref)
 
 
-def kernel_grad_kernel(where_ref, act_ref, low_ref, own_ref, other_ref, turned_ref):
+def kernel_grad_kernel(where_ref, act_ref, low_ref, own_ref, o0, o1, o2, o3, turned_ref, other_ref):
     pipe, batch, zone = where_ref[0], where_ref[1], where_ref[2]
     turned_taps(batch, act_ref, turned_ref)
     tap_products(pipe, zone, low_ref, turned_ref, own_ref, other_ref)
+    hand_out(other_ref, (o0, o1, o2, o3))
 
 
 DOWN_UNITS = (
@@ -705,7 +712,8 @@
 )
 
 
-def down_grad_kernel(where_ref, img_ref, low_ref, low_s_ref, own_ref, other_ref, turned_ref):
+def down_grad_kernel(where_ref, img_ref, low_ref, low_s_ref, own_ref, o0, o1, o2, o3,
+                     turned_ref, other_ref):
     pipe, batch, zone = where_ref[0], where_ref[1], where_ref[2]
     upper, part = batch // 2, batch % 2
 
@@ -737,9 +745,42 @@
                 rhs = jnp.where(upper == 0, rhs_s, rhs)
             results.append(jnp.dot(lhs, rhs, preferred_element_type=F32))
         split_out(pipe, zone, unit, results[0], results[1], own_ref, other_ref)
+    hand_out(other_ref, (o0, o1, o2, o3))
+
+
+def add_cores_kernel(own_ref, g0, g1, g2, g3, keep_ref, send_ref):
+    for slot, got in enumerate((g0, g1)):
+        keep_ref[slot] = own_ref[slot] + got[...].astype(F32)
+    for slot, got in enumerate((g2, g3)):
+        send_ref[slot] = (own_ref[2 + slot] + got[...].astype(F32)).astype(BF16)
+
+
+def add_near_kernel(own_ref, got_ref, keep_ref, send_ref):
+    keep_ref[...] = own_ref[0] + got_ref[0].astype(F32)
+    send_ref[...] = (own_ref[1] + got_ref[1].astype(F32)).astype(BF16)
+
+
+def add_far_kernel(own_ref, got_ref, out_ref):
+    out_ref[...] = (own_ref[...] + got_ref[...].astype(F32)).astype(BF16)
+
+
+def join_kernel_of(*refs):
+    at = 0
+    for ref in refs[:-1]:
+        if len(ref.shape) == 3:
+            refs[-1][at] = ref[...]
+            at += 1
+        else:
+            refs[-1][at : at + ref.shape[0]] = ref[...]
+            at += ref.shape[0]
 
 
 def gathered_blocks(zone, batch, refs):
+    if len(refs) == 8:
+        for kb in range(4):
+            for rel in range(4):
+                yield batch ^ kb, zone ^ rel, refs[2 * kb + rel % 2], rel // 2
+        return
     a, b, ax, by, ayy, bxx = refs
     sets = {0: (a, b, 0, 0), 1: (ax, bxx, 0, 0), 2: (ayy, by, 0, 0), 3: (ayy, bxx, 2, 2)}
     for kb in range(4):
@@ -752,7 +793,7 @@
 
 
 def assemble_kernel(where_ref, *refs):
-    pieces, out_ref = refs[:6], refs[6]
+    pieces, out_ref = refs[:-1], refs[-1]
     batch, zone = where_ref[1], where_ref[2]
     for owner, quarter, ref, index in gathered_blocks(zone, batch, pieces):
         rows = pl.ds(pl.multiple_of(owner * 128 + quarter * 32, 32), 32)
@@ -760,7 +801,7 @@
 
 
 def assemble_down_kernel(where_ref, *refs):
-    pieces, (out_ref, short_ref) = refs[:6], refs[6:]
+    pieces, (out_ref, short_ref) = refs[:-2], refs[-2:]
     batch, zone = where_ref[1], where_ref[2]
     for owner, quarter, ref, index in gathered_blocks(zone, batch, pieces):
         upper, part = owner // 2, owner % 2
@@ -952,51 +993,92 @@
     )
 
     class Sum:
-        def __init__(self, own, other):
-            self.own, self.other = own, other
-
-        def cores(self):
-            self.both = self.own + partner(self.other).astype(F32)
-            self.sent = self.both[1:].astype(BF16)
-
-        def zones(self):
-            got = [over("space", rel, self.sent[slot]).astype(F32)
-                   for slot, rel in ((1, 1), (0, 2), (2, 3))]
-            self.final = ((self.both[0] + got[0]) + (got[1] + got[2])).astype(BF16)
-
-        def near(self):
-            self.far = over("space", 2, self.final)
-            self.a = jnp.stack([self.final, self.far])
-
-        def ends(self):
+        def __init__(self, kernel, units, operands, scratch, flops, name, after=()):
+            self.units, self.name = units, name
+            self.own, *self.other = call(
+                kernel,
+                [self.block(4, dtype=F32)] + [self.block()] * 4,
+                operands,
+                [scratch, pltpu.VMEM((4, units, 32, 256), BF16)],
+                flops,
+                name,
+                after,
+            )
+            self.got = [partner(x) for x in self.other]
+
+        def block(self, *lead, dtype=BF16):
+            return (lead + (self.units, 32, 256), dtype)
+
+        def cores(self, after=()):
+            self.keep, sent = call(
+                add_cores_kernel,
+                [self.block(2, dtype=F32), self.block(2)],
+                [self.own] + self.got,
+                name=self.name + "_cores",
+                after=after,
+            )
+            self.near = over("space", 1, sent)
+
+        def zone_near(self, after=()):
+            self.keep, sent = call(
+                add_near_kernel,
+                [self.block(dtype=F32), self.block()],
+                [self.keep, self.near],
+                name=self.name + "_near",
+                after=after,
+            )
+            self.far = over("space", 2, sent)
+
+        def zone_far(self, after=()):
+            (self.final,) = call(
+                add_far_kernel,
+                [self.block()],
+                [self.keep, self.far],
+                name=self.name + "_final",
+                after=after,
+            )
+            self.other_far = over("space", 2, self.final)
+
+        def pair(self, after=()):
+            (self.a,) = call(
+                join_kernel_of,
+                [self.block(2)],
+                [self.final, self.other_far],
+                name=self.name + "_pair",
+                after=after,
+            )
             self.b = over("space", 1, self.a)
+
+        def direct(self):
+            self.ra = [over("batch", rel, self.a) for rel in (1, 2, 3)]
+            self.rb = [over("batch", rel, self.b) for rel in (1, 2, 3)]
+            self.blocks = [where, self.a, self.b]
+            for x, y in zip(self.ra, self.rb):
+                self.blocks += [x, y]
 
         def plane(self):
             self.ax, self.by = over("batch", 1, self.a), over("batch", 2, self.b)
 
-        def plane_far(self):
-            self.ayy = over("batch", 2, jnp.concatenate([self.a, self.ax]))
-            self.bxx = over("batch", 1, jnp.concatenate([self.b, self.by]))
-
-        def blocks(self):
-            return [where, self.a, self.b, self.ax, self.by, self.ayy, self.bxx]
+        def plane_far(self, after=()):
+            self.fa, self.fb = [
+                call(join_kernel_of, [self.block(4)], pair, name=self.name + "_cross", after=after)[0]
+                for pair in ([self.a, self.ax], [self.b, self.by])
+            ]
+            self.ayy, self.bxx = over("batch", 2, self.fa), over("batch", 1, self.fb)
+            self.blocks = [where, self.a, self.b, self.ax, self.by, self.ayy, self.bxx]
 
     def kernel_grad_of(act, low_grad, name, after=()):
-        return Sum(*call(
-            kernel_grad_kernel,
-            [((4, 9, 32, 256), F32), ((4, 9, 32, 256), BF16)],
-            [where, act, low_grad],
-            [pltpu.VMEM((9, 128, 1024), BF16)],
-            conv_flops // 4,
-            name,
-            after,
-        ))
+        return Sum(
+            kernel_grad_kernel, 9, [where, act, low_grad], pltpu.VMEM((9, 128, 1024), BF16),
+            conv_flops // 4, name, after,
+        )
 
     def assembled(blocks, name, after=()):
         (out,) = call(assemble_kernel, [((9, 512, 256), F32)], blocks, name=name, after=after)
         return out.reshape(3, 3, 512, 256)
 
     second = kernel_grad_of(plain_act, second_low, "second_grad")
+    second.cores()
     up_f, sum_f = call(
         second_back_kernel,
         [big, rows],
@@ -1004,10 +1086,10 @@
         [x_scratch, conv_scratch],
         conv_flops,
         "second_back",
-        after=[second.other],
+        after=[second.keep],
     )
     other_sf = partner(sum_f)
-    second.cores()
+    second.zone_near(after=[sum_f])
     first_low, up_j, sum_j = call(
         first_back_kernel,
         [low, big, rows],
@@ -1016,12 +1098,14 @@
         [x_scratch, conv_scratch],
         conv_flops,
         "first_back",
-        after=[second.sent],
+        after=[second.keep],
     )
     other_sj = partner(sum_j)
-    second.zones()
-    first = kernel_grad_of(section, first_low, "first_grad")
-    first.cores()
+    second.zone_far(after=[sum_j])
+    first = kernel_grad_of(section, first_low, "first_grad", after=[second.final])
+    second.pair(after=first.other[0:1])
+    second.direct()
+    first.cores(after=[second.a])
     mid_low, short_low, up_d, sum_d = call(
         mid_back_kernel,
         [low, low, big, rows],
@@ -1030,53 +1114,50 @@
         [x_scratch, conv_scratch],
         conv_flops,
         "mid_back",
-        after=[first.sent, second.final],
+        after=[first.keep],
     )
     other_sd = partner(sum_d)
-    second.near()
-    first.zones()
-    mid = kernel_grad_of(down_act, mid_low, "mid_grad")
-    mid.cores()
-    second.ends()
-    down_low, *img_pieces = call(
+    first.zone_near(after=[sum_d, second.b])
+    mid = kernel_grad_of(down_act, mid_low, "mid_grad", after=[first.keep] + second.ra)
+    first.zone_far(after=mid.other[0:1])
+    mid.cores(after=[first.final])
+    (down_low,) = call(
         down_back_kernel,
-        [low] + [((2, 2, 2, 32, 256), BF16)] * 4,
-        [where, facts, up_d, down_out, norm_d, sum_d, other_sd, params, short_low, conv_down,
-         shortcut],
+        [low],
+        [facts, up_d, down_out, norm_d, sum_d, other_sd, params],
+        name="down_back",
+        after=[mid.keep],
+    )
+    down = Sum(
+        down_grad_kernel, 5, [where, img, down_low, short_low], pltpu.VMEM((5, 128, 1024), BF16),
+        conv_flops // 8, "down_grad",
+    )
+    first.pair(after=down.other[0:1])
+    down.cores(after=[first.a])
+    mid.zone_near(after=[down.keep])
+    first.plane()
+    second_out_grad = assembled(second.blocks, "second_out", after=[mid.keep])
+    down.zone_near(after=[second_out_grad])
+    mid.zone_far(after=[down.keep])
+    img_pieces = call(
+        image_back_kernel,
+        [((2, 2, 2, 32, 256), BF16)] * 4,
+        [where, down_low, short_low, conv_down, shortcut],
         [pltpu.VMEM((4, 2, 2, 2, 32, 256), BF16)],
         conv_flops // 8,
-        "down_back",
-        after=[second.a, mid.other],
-    )
-    down = Sum(*call(
-        down_grad_kernel,
-        [((4, 5, 32, 256), F32), ((4, 5, 32, 256), BF16)],
-        [where, img, down_low, short_low],
-        [pltpu.VMEM((5, 128, 1024), BF16)],
-        conv_flops // 8,
-        "down_grad",
-        after=[second.b, mid.sent, first.final],
-    ))
-    down.cores()
-    first.near()
-    first.ends()
-    second.plane()
-    second.plane_far()
-    mid.zones()
-    first.plane()
-    first.plane_far()
-    mid.near()
-    mid.ends()
-    down.zones()
-    down.near()
-    down.ends()
+        "image_back",
+        after=[mid.final],
+    )
+    first.plane_far(after=[img_pieces[0]])
+    down.zone_far(after=[first.fa, first.fb])
+    mid.pair(after=[down.final])
     mid.plane()
-    mid.plane_far()
+    down.pair(after=[mid.a])
     down.plane()
-    down.plane_far()
-    second_out_grad = assembled(second.blocks(), "second_out")
-    first_out_grad = assembled(first.blocks(), "first_out")
-    mid_out_grad = assembled(mid.blocks(), "mid_out")
+    first_out_grad = assembled(first.blocks, "first_out", after=[down.a])
+    mid.plane_far(after=[first_out_grad])
+    down.plane_far(after=[mid.fa, mid.fb])
+    mid_out_grad = assembled(mid.blocks, "mid_out", after=[down.fa])
 
     img_moved = [img_pieces[0]] + [over("space", rel, img_pieces[rel]) for rel in (1, 2, 3)]
     img_moved = jnp.stack(img_moved)
@@ -1094,6 +1175,7 @@
         [where, small, all_pack, sum_f, other_sf, sum_j, other_sj, sum_d, other_sd],
         [pltpu.VMEM((SMALL_ROWS, 512), F32)],
         name="small",
+        after=[down.final],
     )
     parts = [sent] + [over("space", rel, sent) for rel in (1, 2, 3)]
     pooled, head_out, gains_d, sums_d, gains_p, sums_p, head_b = call(
@@ -1106,7 +1188,7 @@
     down_grad, short_grad = call(
         assemble_down_kernel,
         [((9, 256, 256), F32), ((256, 256), F32)],
-        down.blocks(),
+        down.blocks,
         name="down_out",
     )
     return (

time: 295 us -> 274 us (0.929)
  starting transfers between devices: 86.3 us -> 73.9 us
  waiting for transfers between devices: 83.4 us -> 75.1 us
  other arithmetic: 5.67 us -> 0.17 us
  local copies, waits for them, and re-layouts: 17.2 us -> 21.1 us
    ppermute x70 -> x80, starting transfers between devices: 86.3 us -> 73.9 us  [over(): return lax.ppermute(x, axis, [(i, i ^ rel) for i in range(size)])]
    ppermute x70 -> x80, waiting for transfers between devices: 83.4 us -> 75.1 us  [over(): return lax.ppermute(x, axis, [(i, i ^ rel) for i in range(size)])]
    unnamed x89 -> x73, local copies, waits for them, and re-layouts: 13 us -> 17.9 us
    concatenate x8 -> x0, other arithmetic: 4.32 us -> none  [the longest x4 2.56 us: plane_far(): self.bxx = over('batch', 1, jnp.concatenate([self.b, self.by]))]
    pallas_call x24 -> x47, Pallas kernels: 95.6 us -> 97.9 us  [call(): pl.pallas_call(body, out_shape=tuple((jax.ShapeDtypeStruct(shape, dtype)...]
  transfers between devices with their start and end apart: 70 -> 80, of which waited for: 24 -> 34; matrix products, arithmetic and copies ran while one was open for 3% -> 1% of each run, Pallas kernels for 18% -> 20%
where the time goes in v4:
time: 274 us; the launch traced here: 270 us
  Pallas kernels  97.9 us (36%)
  waiting for transfers between devices  75.1 us (27%)
  starting transfers between devices  73.9 us (27%)
  local copies, waits for them, and re-layouts  21.1 us (8%)
    pallas_call x47, Pallas kernels, call(): pl.pallas_call(body, out_shape=tuple((jax.ShapeDtypeStruct(shape, dtype)...  97.9 us
    ppermute x80, waiting for transfers between devices, over(): return lax.ppermute(x, axis, [(i, i ^ rel) for i in range(size)])  75.1 us
    ppermute x80, starting transfers between devices, over(): return lax.ppermute(x, axis, [(i, i ^ rel) for i in range(size)])  73.9 us
    unnamed x73, local copies, waits for them, and re-layouts  17.9 us
  transfers between devices with their start and end apart: 80, of which 34 were waited for; matrix products, arithmetic and copies ran while one was open for 1% of the time, Pallas kernels for 20%

profile of v4, /device:TPU:0, one launch (start us, length us, event | category | flops | bytes accessed | tf_op | source)
XLA Modules:
  0.0 270.0 jit_solution(4924017390469612147)
XLA Ops:
  4.7 4.1 %collective-permute-start.4 = (bf16[128,512]{1,0:T(8,128)(2,1)S(1)}, bf16[128,512]{1,0:T(8,128)(2,1)S(1)}, u32[]{:S(2)}, u32[]{:S(2)}) collective-permute-start(bf16[128,512]{1,0:T(8,128)(2,1)S(1)} %get-tuple-element.106), channel_id=1, source_target_pairs={{0,2},{1,3},{2,0},{3,1},{4,6},{5,7},{6,4},{7,5},{8,10},{9,11},{10,... | collective-permute-start | bytes 393224 | tf_op jit(solution)/shard_map/ppermute | solution.py:901
  10.1 2.4 collective-permute-start.2
  13.6 5.1 %collective-permute-done.4 = bf16[128,512]{1,0:T(8,128)(2,1)S(1)} collective-permute-done((bf16[128,512]{1,0:T(8,128)(2,1)S(1)}, bf16[128,512]{1,0:T(8,128)(2,1)S(1)}, u32[]{:S(2)}, u32[]{:S(2)}) %collective-permute-start.4) | collective-permute-done | bytes 131104 | tf_op jit(solution)/shard_map/ppermute | solution.py:901
  18.8 2.9 %collective-permute-start.11 = (bf16[256,512]{1,0:T(8,128)(2,1)S(1)}, bf16[256,512]{1,0:T(8,128)(2,1)S(1)}, u32[]{:S(2)}, u32[]{:S(2)}) collective-permute-start(bf16[256,512]{1,0:T(8,128)(2,1)S(1)} %constant_dynamic-update-slice_fusion.refs_4_), channel_id=1, source_target_pairs={{0,12},{4,8},{8,4},{12,0},{1,13},{5,9},{9,5},{13,1},{2,14},{6,10},... | collective-permute-start | bytes 786440 | tf_op jit(solution)/shard_map/ppermute | solution.py:901
  21.6 2.1 collective-permute-done.3.refs_3_
  23.7 2.8 %collective-permute-start.10 = (bf16[128,512]{1,0:T(8,128)(2,1)S(1)}, bf16[128,512]{1,0:T(8,128)(2,1)S(1)}, u32[]{:S(2)}, u32[]{:S(2)}) collective-permute-start(bf16[128,512]{1,0:T(8,128)(2,1)S(1)} %collective-permute-done.3.refs_3_), channel_id=1, source_target_pairs={{0,12},{4,8},{8,4},{12,0},{1,13},{5,9},{9,5},{13,1},{2,14},{6,10},... | collective-permute-start | bytes 393224 | tf_op jit(solution)/shard_map/ppermute | solution.py:901
  27.2 1.9 collective-permute-start.8
  29.1 2.7 %collective-permute-done.10.refs_12_ = bf16[128,512]{1,0:T(8,128)(2,1)S(1)} collective-permute-done((bf16[128,512]{1,0:T(8,128)(2,1)S(1)}, bf16[128,512]{1,0:T(8,128)(2,1)S(1)}, u32[]{:S(2)}, u32[]{:S(2)}) %collective-permute-start.10) | collective-permute-done | bytes 131104 | tf_op jit(solution)/shard_map/ppermute | solution.py:901
  31.8 1.9 collective-permute-start.6
  35.9 2.9 %collective-permute-done.8.refs_9_ = bf16[128,512]{1,0:T(8,128)(2,1)S(1)} collective-permute-done((bf16[128,512]{1,0:T(8,128)(2,1)S(1)}, bf16[128,512]{1,0:T(8,128)(2,1)S(1)}, u32[]{:S(2)}, u32[]{:S(2)}) %collective-permute-start.8) | collective-permute-done | bytes 131104 | tf_op jit(solution)/shard_map/ppermute | solution.py:901
  38.9 1.7 copy-done.5
  40.6 4.7 %down.1 = (bf16[8,128,1024]{2,1,0:T(8,128)(2,1)S(1)}, f32[8,128,512]{2,1,0:T(8,128)S(1)}, f32[8,128,512]{2,1,0:T(8,128)S(1)}, f32[8,512]{1,0:T(8,128)S(1)}) custom-call(f32[16]{0:T(128)S(1)} %get-tuple-element.104.refs_0_.refs_2_, s32[4]{0:T(128)S(1)} %pad_add_fusion.refs_0_.refs_1_, bf16[144,512]{1,0:T(8,128)(2,1)S(1)} %get-tuple-element.103.refs_1_.refs_2_, ...), custom_call_target="tpu_custom_call" | custom-call | flops 2415919104 | bytes 4784208 | tf_op jit(solution)/shard_map/down/pallas_call | solution.py:161
  46.6 6.9 %mid.1 = (bf16[8,128,512]{2,1,0:T(8,128)(2,1)S(1)}, f32[8,128,512]{2,1,0:T(8,128)S(1)}, f32[8,512]{1,0:T(8,128)S(1)}, f32[8,512]{1,0:T(8,128)S(1)}) custom-call(f32[16]{0:T(128)S(1)} %get-tuple-element.104.refs_0_.refs_2_, f32[8,128,512]{2,1,0:T(8,128)S(1)} %get-tuple-element.108.refs_1_.refs_9_.refs_2_, f32[8,512]{1,0:T(8,128)S(1)} %get-tuple-element.109.refs_2_.refs_5_, ...), custom_call_target="tpu_custom_call" | custom-call | flops 4831838208 | bytes 6869056 | tf_op jit(solution)/shard_map/mid/pallas_call | solution.py:161
  54.8 7.4 %first.1 = (bf16[8,128,512]{2,1,0:T(8,128)(2,1)S(1)}, f32[8,128,512]{2,1,0:T(8,128)S(1)}, f32[8,512]{1,0:T(8,128)S(1)}, f32[8,512]{1,0:T(8,128)S(1)}) custom-call(f32[16]{0:T(128)S(1)} %get-tuple-element.104.refs_0_.refs_2_, f32[8,128,512]{2,1,0:T(8,128)S(1)} %get-tuple-element.110.refs_1_.refs_12_.refs_2_, ...), custom_call_target="tpu_custom_call" | custom-call | flops 4831838208 | bytes 8998976 | tf_op jit(solution)/shard_map/first/pallas_call | solution.py:161
  63.5 7.0 %second.1 = (bf16[8,128,512]{2,1,0:T(8,128)(2,1)S(1)}, f32[8,128,512]{2,1,0:T(8,128)S(1)}, f32[8,512]{1,0:T(8,128)S(1)}, f32[8,512]{1,0:T(8,128)S(1)}) custom-call(f32[16]{0:T(128)S(1)} %get-tuple-element.104.refs_0_.refs_2_, f32[8,128,512]{2,1,0:T(8,128)S(1)} %get-tuple-element.113.refs_1_.refs_2_, f32[8,512]{1,0:T(8,128)S(1)} %get-tuple-element.114.refs_2_, ...), custom_call_target="tpu_custom_call" | custom-call | flops 4831838208 | bytes 6869056 | tf_op jit(solution)/shard_map/second/pallas_call | solution.py:161
  71.8 2.2 block.1
  76.2 3.1 %collective-permute-start.19 = (f32[40,40]{1,0:T(8,128)S(1)}, f32[40,40]{1,0:T(8,128)S(1)}, u32[]{:S(2)}, u32[]{:S(2)}) collective-permute-start(f32[40,40]{1,0:T(8,128)S(1)} %get-tuple-element.121.refs_3_), channel_id=1, source_target_pairs={{0,3},{1,2},{2,1},{3,0},{4,7},{5,6},{6,5},{7,4},{8,11},{9,10},{10,... | collective-permute-start | bytes 19208 | tf_op jit(solution)/shard_map/ppermute | solution.py:901
  79.4 1.9 collective-permute-start.18
  81.8 2.3 collective-permute-done.18.refs_5_
  85.1 4.5 %head.1 = (bf16[8,128,512]{2,1,0:T(8,128)(2,1)S(1)}, f32[8,512]{1,0:T(8,128)S(1)}, f32[48,512]{1,0:T(8,128)S(1)}) custom-call(s32[20]{0:T(128)S(1)} %copy-done.20, s32[4]{0:T(128)S(1)} %pad_add_fusion.refs_0_.refs_1_, f32[16]{0:T(128)S(1)} %get-tuple-element.104.refs_0_.refs_2_, f32[40,40]{1,0:T(8,128)S(1)} %get-tuple-element.121.refs_3_, ...), custom_call_target="tpu_custom_call" | custom-call | bytes 3397536 | tf_op jit(solution)/shard_map/head/pallas_call | solution.py:161
  89.5 4.1 %second_grad.1 = (f32[4,9,32,256]{3,2,1,0:T(8,128)S(1)}, bf16[9,32,256]{2,1,0:T(8,128)(2,1)S(1)}, bf16[9,32,256]{2,1,0:T(8,128)(2,1)S(1)}, bf16[9,32,256]{2,1,0:T(8,128)(2,1)S(1)}, bf16[9,32,256]{2,1,0:T(8,128)(2,1)S(1)}) custom-call(s32[4]{0:T(128)S(1)} %pad_add_fusion.refs_0_.refs_1_, bf16[8,128,512]{2,1,0:T(8,128)(2,1)S(1)} %get-tuple-element.129.refs_1_, ...), custom_call_target="tpu_custom_call" | custom-call | flops 1207959552 | bytes 2097168 | tf_op jit(solution)/shard_map/second_grad/pallas_call | solution.py:161
  96.0 1.5 collective-permute-start.25
  97.4 7.2 %second_back.1 = (f32[8,128,512]{2,1,0:T(8,128)S(1)}, f32[8,512]{1,0:T(8,128)S(1)}) custom-call(f32[16]{0:T(128)S(1)} %get-tuple-element.104.refs_0_.refs_2_, bf16[8,128,512]{2,1,0:T(8,128)(2,1)S(1)} %get-tuple-element.127.refs_2_.refs_1_, f32[8,128,512]{2,1,0:T(8,128)S(1)} %get-tuple-element.113.refs_1_.refs_2_, f32[8,512]{1,0:T(8,128)S(1)} %get-tuple-element.128.refs_3_, ...), custom_call_target="tpu_custom_call" | custom-call | flops 4831838208 | bytes 7901248 | tf_op jit(solution)/shard_map/second_back/pallas_call | solution.py:161
  105.3 1.8 collective-permute-start.27
  107.1 1.7 copy-done.25
  108.8 9.7 %first_back.1 = (bf16[8,128,512]{2,1,0:T(8,128)(2,1)S(1)}, f32[8,128,512]{2,1,0:T(8,128)S(1)}, f32[8,512]{1,0:T(8,128)S(1)}) custom-call(f32[16]{0:T(128)S(1)} %get-tuple-element.104.refs_0_.refs_2_, f32[8,128,512]{2,1,0:T(8,128)S(1)} %get-tuple-element.137.refs_1_, f32[8,128,512]{2,1,0:T(8,128)S(1)} %copy-done.25, f32[8,512]{1,0:T(8,128)S(1)} %get-tuple-element.128.refs_3_, ...), custom_call_target="tpu_custom_call" | custom-call | flops 4831838208 | bytes 16371776 | tf_op jit(solution)/shard_map/first_back/pallas_call | solution.py:161
  119.9 3.9 %first_grad.1 = (f32[4,9,32,256]{3,2,1,0:T(8,128)S(1)}, bf16[9,32,256]{2,1,0:T(8,128)(2,1)S(1)}, bf16[9,32,256]{2,1,0:T(8,128)(2,1)S(1)}, bf16[9,32,256]{2,1,0:T(8,128)(2,1)S(1)}, bf16[9,32,256]{2,1,0:T(8,128)(2,1)S(1)}) custom-call(s32[4]{0:T(128)S(1)} %pad_add_fusion.refs_0_.refs_1_, ...), custom_call_target="tpu_custom_call" | custom-call | flops 1207959552 | bytes 2097168 | tf_op jit(solution)/shard_map/first_grad/pallas_call | solution.py:161
  124.9 3.7 %collective-permute-done.32.refs_1_ = bf16[9,32,256]{2,1,0:T(8,128)(2,1)S(1)} collective-permute-done((bf16[9,32,256]{2,1,0:T(8,128)(2,1)S(1)}, bf16[9,32,256]{2,1,0:T(8,128)(2,1)S(1)}, u32[]{:S(2)}, u32[]{:S(2)}) %collective-permute-start.32) | collective-permute-done | bytes 147488 | tf_op jit(solution)/shard_map/ppermute | solution.py:901
  128.6 2.4 collective-permute-start.38
  132.3 2.1 collective-permute-start.34
  134.4 8.5 %mid_back.1 = (bf16[8,128,512]{2,1,0:T(8,128)(2,1)S(1)}, bf16[8,128,512]{2,1,0:T(8,128)(2,1)S(1)}, f32[8,128,512]{2,1,0:T(8,128)S(1)}, f32[8,512]{1,0:T(8,128)S(1)}) custom-call(f32[16]{0:T(128)S(1)} %get-tuple-element.104.refs_0_.refs_2_, f32[8,128,512]{2,1,0:T(8,128)S(1)} %get-tuple-element.143.refs_1_, f32[8,128,512]{2,1,0:T(8,128)S(1)} %copy-done.23, ...), custom_call_target="tpu_custom_call" | custom-call | flops 4831838208 | bytes 13193280 | tf_op jit(solution)/shard_map/mid_back/pallas_call | solution.py:161
  142.9 4.2 %collective-permute-done.34.refs_1_ = bf16[2,9,32,256]{3,2,1,0:T(8,128)(2,1)S(1)} collective-permute-done((bf16[2,9,32,256]{3,2,1,0:T(8,128)(2,1)S(1)}, bf16[2,9,32,256]{3,2,1,0:T(8,128)(2,1)S(1)}, u32[]{:S(2)}, u32[]{:S(2)}) %collective-permute-start.34) | collective-permute-done | bytes 294944 | tf_op jit(solution)/shard_map/ppermute | solution.py:901
  147.2 3.9 %mid_grad.1 = (f32[4,9,32,256]{3,2,1,0:T(8,128)S(1)}, bf16[9,32,256]{2,1,0:T(8,128)(2,1)S(1)}, bf16[9,32,256]{2,1,0:T(8,128)(2,1)S(1)}, bf16[9,32,256]{2,1,0:T(8,128)(2,1)S(1)}, bf16[9,32,256]{2,1,0:T(8,128)(2,1)S(1)}) custom-call(s32[4]{0:T(128)S(1)} %pad_add_fusion.refs_0_.refs_1_, bf16[8,128,512]{2,1,0:T(8,128)(2,1)S(1)} %get-tuple-element.156.refs_1_, ...), custom_call_target="tpu_custom_call" | custom-call | flops 1207959552 | bytes 2097168 | tf_op jit(solution)/shard_map/mid_grad/pallas_call | solution.py:161
  152.2 3.5 %collective-permute-done.43.refs_1_ = bf16[9,32,256]{2,1,0:T(8,128)(2,1)S(1)} collective-permute-done((bf16[9,32,256]{2,1,0:T(8,128)(2,1)S(1)}, bf16[9,32,256]{2,1,0:T(8,128)(2,1)S(1)}, u32[]{:S(2)}, u32[]{:S(2)}) %collective-permute-start.43) | collective-permute-done | bytes 147488 | tf_op jit(solution)/shard_map/ppermute | solution.py:901
  158.1 3.3 %down_grad.1 = (f32[4,5,32,256]{3,2,1,0:T(8,128)S(1)}, bf16[5,32,256]{2,1,0:T(8,128)(2,1)S(1)}, bf16[5,32,256]{2,1,0:T(8,128)(2,1)S(1)}, bf16[5,32,256]{2,1,0:T(8,128)(2,1)S(1)}, bf16[5,32,256]{2,1,0:T(8,128)(2,1)S(1)}) custom-call(s32[4]{0:T(128)S(1)} %pad_add_fusion.refs_0_.refs_1_, bf16[8,128,1024]{2,1,0:T(8,128)(2,1)S(1)} %get-tuple-element.154.refs_1_, ...), custom_call_target="tpu_custom_call" | custom-call | flops 603979776 | bytes 4194320 | tf_op jit(solution)/shard_map/down_grad/pallas_call | solution.py:161
  163.1 1.7 collective-permute-done.48.refs_1_
  164.8 2.4 collective-permute-start.52
  169.8 2.2 collective-permute-done.53.refs_1_
  172.9 2.6 collective-permute-done.52.refs_8_
  175.6 1.5 collective-permute-start.55
  179.6 1.5 collective-permute-done.51.refs_6_
  181.9 3.0 %second_out.1 = f32[9,512,256]{2,1,0:T(8,128)} custom-call(s32[4]{0:T(128)S(1)} %pad_add_fusion.refs_0_.refs_1_, bf16[2,9,32,256]{3,2,1,0:T(8,128)(2,1)S(1)} %second_grad_pair.1.refs_5_.refs_1_, bf16[2,9,32,256]{3,2,1,0:T(8,128)(2,1)S(1)} %collective-permute-done.35.refs_3_.refs_2_, bf16[2,9,32,256]{3,2,1,0:T(8,128)(2,1)S(1)} %collective-permute-done.36.refs_4_.refs_3_, ...), custom_call_target="tpu_custom_call" | custom-call | bytes 2359312 | tf_op jit(solution)/shard_map/second_out/pallas_call | solution.py:161
  184.9 2.3 copy-done.4
  187.3 3.5 %collective-permute-done.56.refs_1_ = bf16[9,32,256]{2,1,0:T(8,128)(2,1)S(1)} collective-permute-done((bf16[9,32,256]{2,1,0:T(8,128)(2,1)S(1)}, bf16[9,32,256]{2,1,0:T(8,128)(2,1)S(1)}, u32[]{:S(2)}, u32[]{:S(2)}) %collective-permute-start.56) | collective-permute-done | bytes 147488 | tf_op jit(solution)/shard_map/ppermute | solution.py:901
  190.9 2.9 %collective-permute-start.54 = (bf16[5,32,256]{2,1,0:T(8,128)(2,1)S(1)}, bf16[5,32,256]{2,1,0:T(8,128)(2,1)S(1)}, u32[]{:S(2)}, u32[]{:S(2)}) collective-permute-start(bf16[5,32,256]{2,1,0:T(8,128)(2,1)S(1)} %get-tuple-element.178), channel_id=1, source_target_pairs={{0,2},{1,3},{2,0},{3,1},{4,6},{5,7},{6,4},{7,5},{8,10},{9,11},{10,... | collective-permute-start | bytes 245768 | tf_op jit(solution)/shard_map/ppermute | solution.py:901
  193.8 1.5 image_back.1
  195.4 1.5 collective-permute-start.72
  196.9 5.9 %collective-permute-done.54.refs_1_ = bf16[5,32,256]{2,1,0:T(8,128)(2,1)S(1)} collective-permute-done((bf16[5,32,256]{2,1,0:T(8,128)(2,1)S(1)}, bf16[5,32,256]{2,1,0:T(8,128)(2,1)S(1)}, u32[]{:S(2)}, u32[]{:S(2)}) %collective-permute-start.54) | collective-permute-done | bytes 81952 | tf_op jit(solution)/shard_map/ppermute | solution.py:901
  202.9 1.6 collective-permute-start.73
  205.0 6.8 %collective-permute-done.74.refs_0_.refs_2_ = bf16[2,9,32,256]{3,2,1,0:T(8,128)(2,1)S(1)} collective-permute-done((bf16[2,9,32,256]{3,2,1,0:T(8,128)(2,1)S(1)}, bf16[2,9,32,256]{3,2,1,0:T(8,128)(2,1)S(1)}, u32[]{:S(2)}, u32[]{:S(2)}) %collective-permute-start.74) | collective-permute-done | bytes 294944 | tf_op jit(solution)/shard_map/ppermute | solution.py:901
  214.7 4.5 %collective-permute-done.66.refs_1_ = bf16[5,32,256]{2,1,0:T(8,128)(2,1)S(1)} collective-permute-done((bf16[5,32,256]{2,1,0:T(8,128)(2,1)S(1)}, bf16[5,32,256]{2,1,0:T(8,128)(2,1)S(1)}, u32[]{:S(2)}, u32[]{:S(2)}) %collective-permute-start.66) | collective-permute-done | bytes 81952 | tf_op jit(solution)/shard_map/ppermute | solution.py:901
  219.3 5.3 %collective-permute-done.68.refs_0_.refs_2_ = bf16[2,5,32,256]{3,2,1,0:T(8,128)(2,1)S(1)} collective-permute-done((bf16[2,5,32,256]{3,2,1,0:T(8,128)(2,1)S(1)}, bf16[2,5,32,256]{3,2,1,0:T(8,128)(2,1)S(1)}, u32[]{:S(2)}, u32[]{:S(2)}) %collective-permute-start.68) | collective-permute-done | bytes 163872 | tf_op jit(solution)/shard_map/ppermute | solution.py:901
  225.4 2.1 collective-permute-start.62
  228.7 1.5 collective-permute-start.64
  232.2 3.0 %first_out.1 = f32[9,512,256]{2,1,0:T(8,128)} custom-call(s32[4]{0:T(128)S(1)} %pad_add_fusion.refs_0_.refs_1_, bf16[2,9,32,256]{3,2,1,0:T(8,128)(2,1)S(1)} %first_grad_pair.1.refs_5_.refs_0_.refs_1_, bf16[2,9,32,256]{3,2,1,0:T(8,128)(2,1)S(1)} %collective-permute-done.57.refs_0_.refs_2_, ...), custom_call_target="tpu_custom_call" | custom-call | bytes 2359312 | tf_op jit(solution)/shard_map/first_out/pallas_call | solution.py:161
  235.2 2.3 copy-done.2
  237.6 2.3 copy-done.3
  240.0 2.4 collective-permute-start.61
  243.0 1.5 collective-permute-start.79
  244.7 2.1 collective-permute-start.59
  257.0 2.0 image_grad.1
  259.0 3.0 %collective-permute-done.77.refs_6_ = bf16[4,5,32,256]{3,2,1,0:T(8,128)(2,1)} collective-permute-done((bf16[4,5,32,256]{3,2,1,0:T(8,128)(2,1)}, bf16[4,5,32,256]{3,2,1,0:T(8,128)(2,1)}, u32[]{:S(2)}, u32[]{:S(2)}) %collective-permute-start.77) | collective-permute-done | bytes 327712 | tf_op jit(solution)/shard_map/ppermute | solution.py:901
  262.9 2.9 %down_out.1 = (f32[9,256,256]{2,1,0:T(8,128)}, f32[256,256]{1,0:T(8,128)}) custom-call(s32[4]{0:T(128)S(1)} %pad_add_fusion.refs_0_.refs_1_, bf16[2,5,32,256]{3,2,1,0:T(8,128)(2,1)S(1)} %down_grad_pair.1.refs_7_.refs_0_.refs_1_, bf16[2,5,32,256]{3,2,1,0:T(8,128)(2,1)S(1)} %collective-permute-done.68.refs_0_.refs_2_, ...), custom_call_target="tpu_custom_call" | custom-call | bytes 1310736 | tf_op jit(solution)/shard_map/down_out/pallas_call | solution.py:161
  265.8 3.7 %mid_out.1 = f32[9,512,256]{2,1,0:T(8,128)} custom-call(s32[4]{0:T(128)S(1)} %pad_add_fusion.refs_0_.refs_1_, bf16[2,9,32,256]{3,2,1,0:T(8,128)(2,1)S(1)} %mid_grad_pair.1.refs_2_.refs_0_.refs_1_, bf16[2,9,32,256]{3,2,1,0:T(8,128)(2,1)S(1)} %collective-permute-done.74.refs_0_.refs_2_, bf16[2,9,32,256]{3,2,1,0:T(8,128)(2,1)S(1)} %collective-permute-done.71.refs_1_.refs_3_, ...), custom_call_target="tpu_custom_call" | custom-call | bytes 2359312 | tf_op jit(solution)/shard_map/mid_out/pallas_call | solution.py:161
  (228 shorter events, 56.6 us)
Async XLA Ops:
  4.7 14.0 %collective-permute-start.4 = (bf16[128,512]{1,0:T(8,128)(2,1)S(1)}, bf16[128,512]{1,0:T(8,128)(2,1)S(1)}, u32[]{:S(2)}, u32[]{:S(2)}) collective-permute-start(bf16[128,512]{1,0:T(8,128)(2,1)S(1)} %get-tuple-element.106), channel_id=1, source_target_pairs={{0,2},{1,3},{2,0},{3,1},{4,6},{5,7},{6,4},{7,5},{8,10},{9,11},{10,... | collective-permute-start | bytes 393224 | tf_op jit(solution)/shard_map/ppermute | solution.py:901
  8.8 10.0 %collective-permute-start.5 = (bf16[128,512]{1,0:T(8,128)(2,1)S(1)}, bf16[128,512]{1,0:T(8,128)(2,1)S(1)}, u32[]{:S(2)}, u32[]{:S(2)}) collective-permute-start(bf16[128,512]{1,0:T(8,128)(2,1)S(1)} %get-tuple-element.107), channel_id=1, source_target_pairs={{0,3},{1,2},{2,1},{3,0},{4,7},{5,6},{6,5},{7,4},{8,11},{9,10},{10,... | collective-permute-start | bytes 393224 | tf_op jit(solution)/shard_map/ppermute | solution.py:901
  10.1 16.4 %collective-permute-start.2 = (bf16[144,512]{1,0:T(8,128)(2,1)S(1)}, bf16[144,512]{1,0:T(8,128)(2,1)S(1)}, u32[]{:S(2)}, u32[]{:S(2)}) collective-permute-start(bf16[144,512]{1,0:T(8,128)(2,1)S(1)} %get-tuple-element.103.refs_1_.refs_2_), channel_id=1, source_target_pairs={{0,12},{4,8},{8,4},{12,0},{1,13},{5,9},{9,5},{13,1},{2,14},{6,10},... | collective-permute-start | bytes 442376 | tf_op jit(solution)/shard_map/ppermute | solution.py:901
  12.6 14.4 %collective-permute-start.1 = (bf16[144,512]{1,0:T(8,128)(2,1)S(1)}, bf16[144,512]{1,0:T(8,128)(2,1)S(1)}, u32[]{:S(2)}, u32[]{:S(2)}) collective-permute-start(bf16[144,512]{1,0:T(8,128)(2,1)S(1)} %get-tuple-element.103.refs_1_.refs_2_), channel_id=1, source_target_pairs={{0,8},{4,12},{8,0},{12,4},{1,9},{5,13},{9,1},{13,5},{2,10},{6,14},... | collective-permute-start | bytes 442376 | tf_op jit(solution)/shard_map/ppermute | solution.py:901
  13.1 14.1 %collective-permute-start = (bf16[144,512]{1,0:T(8,128)(2,1)S(1)}, bf16[144,512]{1,0:T(8,128)(2,1)S(1)}, u32[]{:S(2)}, u32[]{:S(2)}) collective-permute-start(bf16[144,512]{1,0:T(8,128)(2,1)S(1)} %get-tuple-element.103.refs_1_.refs_2_), channel_id=1, source_target_pairs={{0,4},{4,0},{8,12},{12,8},{1,5},{5,1},{9,13},{13,9},{2,6},{6,2},{1... | collective-permute-start | bytes 442376 | tf_op jit(solution)/shard_map/ppermute | solution.py:901
  18.7 5.0 %collective-permute-start.3 = (bf16[128,512]{1,0:T(8,128)(2,1)S(1)}, bf16[128,512]{1,0:T(8,128)(2,1)S(1)}, u32[]{:S(2)}, u32[]{:S(2)}) collective-permute-start(bf16[128,512]{1,0:T(8,128)(2,1)S(1)} %get-tuple-element.105), channel_id=1, source_target_pairs={{0,1},{1,0},{2,3},{3,2},{4,5},{5,4},{6,7},{7,6},{8,9},{9,8},{10,11... | collective-permute-start | bytes 393224 | tf_op jit(solution)/shard_map/ppermute | solution.py:901
  18.8 20.1 %collective-permute-start.11 = (bf16[256,512]{1,0:T(8,128)(2,1)S(1)}, bf16[256,512]{1,0:T(8,128)(2,1)S(1)}, u32[]{:S(2)}, u32[]{:S(2)}) collective-permute-start(bf16[256,512]{1,0:T(8,128)(2,1)S(1)} %constant_dynamic-update-slice_fusion.refs_4_), channel_id=1, source_target_pairs={{0,12},{4,8},{8,4},{12,0},{1,13},{5,9},{9,5},{13,1},{2,14},{6,10},... | collective-permute-start | bytes 786440 | tf_op jit(solution)/shard_map/ppermute | solution.py:901
  23.7 8.1 %collective-permute-start.10 = (bf16[128,512]{1,0:T(8,128)(2,1)S(1)}, bf16[128,512]{1,0:T(8,128)(2,1)S(1)}, u32[]{:S(2)}, u32[]{:S(2)}) collective-permute-start(bf16[128,512]{1,0:T(8,128)(2,1)S(1)} %collective-permute-done.3.refs_3_), channel_id=1, source_target_pairs={{0,12},{4,8},{8,4},{12,0},{1,13},{5,9},{9,5},{13,1},{2,14},{6,10},... | collective-permute-start | bytes 393224 | tf_op jit(solution)/shard_map/ppermute | solution.py:901
  26.5 12.4 %collective-permute-start.9 = (bf16[256,512]{1,0:T(8,128)(2,1)S(1)}, bf16[256,512]{1,0:T(8,128)(2,1)S(1)}, u32[]{:S(2)}, u32[]{:S(2)}) collective-permute-start(bf16[256,512]{1,0:T(8,128)(2,1)S(1)} %constant_dynamic-update-slice_fusion.refs_4_), channel_id=1, source_target_pairs={{0,8},{4,12},{8,0},{12,4},{1,9},{5,13},{9,1},{13,5},{2,10},{6,14},... | collective-permute-start | bytes 786440 | tf_op jit(solution)/shard_map/ppermute | solution.py:901
  27.0 11.9 %collective-permute-start.7 = (bf16[256,512]{1,0:T(8,128)(2,1)S(1)}, bf16[256,512]{1,0:T(8,128)(2,1)S(1)}, u32[]{:S(2)}, u32[]{:S(2)}) collective-permute-start(bf16[256,512]{1,0:T(8,128)(2,1)S(1)} %constant_dynamic-update-slice_fusion.refs_4_), channel_id=1, source_target_pairs={{0,4},{4,0},{8,12},{12,8},{1,5},{5,1},{9,13},{13,9},{2,6},{6,2},{1... | collective-permute-start | bytes 786440 | tf_op jit(solution)/shard_map/ppermute | solution.py:901
  27.2 11.6 %collective-permute-start.8 = (bf16[128,512]{1,0:T(8,128)(2,1)S(1)}, bf16[128,512]{1,0:T(8,128)(2,1)S(1)}, u32[]{:S(2)}, u32[]{:S(2)}) collective-permute-start(bf16[128,512]{1,0:T(8,128)(2,1)S(1)} %collective-permute-done.3.refs_3_), channel_id=1, source_target_pairs={{0,8},{4,12},{8,0},{12,4},{1,9},{5,13},{9,1},{13,5},{2,10},{6,14},... | collective-permute-start | bytes 393224 | tf_op jit(solution)/shard_map/ppermute | solution.py:901
  31.8 7.1 %collective-permute-start.6 = (bf16[128,512]{1,0:T(8,128)(2,1)S(1)}, bf16[128,512]{1,0:T(8,128)(2,1)S(1)}, u32[]{:S(2)}, u32[]{:S(2)}) collective-permute-start(bf16[128,512]{1,0:T(8,128)(2,1)S(1)} %collective-permute-done.3.refs_3_), channel_id=1, source_target_pairs={{0,4},{4,0},{8,12},{12,8},{1,5},{5,1},{9,13},{13,9},{2,6},{6,2},{1... | collective-permute-start | bytes 393224 | tf_op jit(solution)/shard_map/ppermute | solution.py:901
  76.2 5.6 %collective-permute-start.19 = (f32[40,40]{1,0:T(8,128)S(1)}, f32[40,40]{1,0:T(8,128)S(1)}, u32[]{:S(2)}, u32[]{:S(2)}) collective-permute-start(f32[40,40]{1,0:T(8,128)S(1)} %get-tuple-element.121.refs_3_), channel_id=1, source_target_pairs={{0,3},{1,2},{2,1},{3,0},{4,7},{5,6},{6,5},{7,4},{8,11},{9,10},{10,... | collective-permute-start | bytes 19208 | tf_op jit(solution)/shard_map/ppermute | solution.py:901
  79.4 4.8 %collective-permute-start.18 = (f32[40,40]{1,0:T(8,128)S(1)}, f32[40,40]{1,0:T(8,128)S(1)}, u32[]{:S(2)}, u32[]{:S(2)}) collective-permute-start(f32[40,40]{1,0:T(8,128)S(1)} %get-tuple-element.121.refs_3_), channel_id=1, source_target_pairs={{0,2},{1,3},{2,0},{3,1},{4,6},{5,7},{6,4},{7,5},{8,10},{9,11},{10,... | collective-permute-start | bytes 19208 | tf_op jit(solution)/shard_map/ppermute | solution.py:901
  96.0 9.3 %collective-permute-start.25 = (bf16[2,9,32,256]{3,2,1,0:T(8,128)(2,1)S(1)}, bf16[2,9,32,256]{3,2,1,0:T(8,128)(2,1)S(1)}, u32[]{:S(2)}, u32[]{:S(2)}) collective-permute-start(bf16[2,9,32,256]{3,2,1,0:T(8,128)(2,1)S(1)} %get-tuple-element.140), channel_id=1, source_target_pairs={{0,1},{1,0},{2,3},{3,2},{4,5},{5,4},{6,7},{7,6},{8,9},{9,8},{10,11... | collective-permute-start | bytes 884744 | tf_op jit(solution)/shard_map/ppermute | solution.py:901
  105.3 13.3 %collective-permute-start.27 = (bf16[9,32,256]{2,1,0:T(8,128)(2,1)S(1)}, bf16[9,32,256]{2,1,0:T(8,128)(2,1)S(1)}, u32[]{:S(2)}, u32[]{:S(2)}) collective-permute-start(bf16[9,32,256]{2,1,0:T(8,128)(2,1)S(1)} %get-tuple-element.146), channel_id=1, source_target_pairs={{0,2},{1,3},{2,0},{3,1},{4,6},{5,7},{6,4},{7,5},{8,10},{9,11},{10,... | collective-permute-start | bytes 442376 | tf_op jit(solution)/shard_map/ppermute | solution.py:901
  118.6 10.0 %collective-permute-start.32 = (bf16[9,32,256]{2,1,0:T(8,128)(2,1)S(1)}, bf16[9,32,256]{2,1,0:T(8,128)(2,1)S(1)}, u32[]{:S(2)}, u32[]{:S(2)}) collective-permute-start(bf16[9,32,256]{2,1,0:T(8,128)(2,1)S(1)} %second_grad_final.1.refs_3_.refs_0_), channel_id=1, source_target_pairs={{0,2},{1,3},{2,0},{3,1},{4,6},{5,7},{6,4},{7,5},{8,10},{9,11},{10,... | collective-permute-start | bytes 442376 | tf_op jit(solution)/shard_map/ppermute | solution.py:901
  123.8 4.8 %collective-permute-start.29 = (bf16[9,32,256]{2,1,0:T(8,128)(2,1)S(1)}, bf16[9,32,256]{2,1,0:T(8,128)(2,1)S(1)}, u32[]{:S(2)}, u32[]{:S(2)}) collective-permute-start(bf16[9,32,256]{2,1,0:T(8,128)(2,1)S(1)} %get-tuple-element.149), channel_id=1, source_target_pairs={{0,16},{16,0},{1,17},{17,1},{2,18},{18,2},{3,19},{19,3},{4,20},{20... | collective-permute-start | bytes 442376 | tf_op jit(solution)/shard_map/ppermute | solution.py:901
  123.9 7.1 %collective-permute-start.30 = (bf16[9,32,256]{2,1,0:T(8,128)(2,1)S(1)}, bf16[9,32,256]{2,1,0:T(8,128)(2,1)S(1)}, u32[]{:S(2)}, u32[]{:S(2)}) collective-permute-start(bf16[9,32,256]{2,1,0:T(8,128)(2,1)S(1)} %get-tuple-element.150), channel_id=1, source_target_pairs={{0,16},{16,0},{1,17},{17,1},{2,18},{18,2},{3,19},{19,3},{4,20},{20... | collective-permute-start | bytes 442376 | tf_op jit(solution)/shard_map/ppermute | solution.py:901
  124.4 7.2 %collective-permute-start.31 = (bf16[9,32,256]{2,1,0:T(8,128)(2,1)S(1)}, bf16[9,32,256]{2,1,0:T(8,128)(2,1)S(1)}, u32[]{:S(2)}, u32[]{:S(2)}) collective-permute-start(bf16[9,32,256]{2,1,0:T(8,128)(2,1)S(1)} %get-tuple-element.151), channel_id=1, source_target_pairs={{0,16},{16,0},{1,17},{17,1},{2,18},{18,2},{3,19},{19,3},{4,20},{20... | collective-permute-start | bytes 442376 | tf_op jit(solution)/shard_map/ppermute | solution.py:901
  124.5 7.7 %collective-permute-start.28 = (bf16[9,32,256]{2,1,0:T(8,128)(2,1)S(1)}, bf16[9,32,256]{2,1,0:T(8,128)(2,1)S(1)}, u32[]{:S(2)}, u32[]{:S(2)}) collective-permute-start(bf16[9,32,256]{2,1,0:T(8,128)(2,1)S(1)} %get-tuple-element.148.refs_2_), channel_id=1, source_target_pairs={{0,16},{16,0},{1,17},{17,1},{2,18},{18,2},{3,19},{19,3},{4,20},{20... | collective-permute-start | bytes 442376 | tf_op jit(solution)/shard_map/ppermute | solution.py:901
  128.6 18.6 %collective-permute-start.38 = (bf16[2,9,32,256]{3,2,1,0:T(8,128)(2,1)S(1)}, bf16[2,9,32,256]{3,2,1,0:T(8,128)(2,1)S(1)}, u32[]{:S(2)}, u32[]{:S(2)}) collective-permute-start(bf16[2,9,32,256]{3,2,1,0:T(8,128)(2,1)S(1)} %second_grad_pair.1.refs_5_.refs_1_), channel_id=1, source_target_pairs={{0,12},{4,8},{8,4},{12,0},{1,13},{5,9},{9,5},{13,1},{2,14},{6,10},... | collective-permute-start | bytes 884744 | tf_op jit(solution)/shard_map/ppermute | solution.py:901
  131.0 16.2 %collective-permute-start.37 = (bf16[2,9,32,256]{3,2,1,0:T(8,128)(2,1)S(1)}, bf16[2,9,32,256]{3,2,1,0:T(8,128)(2,1)S(1)}, u32[]{:S(2)}, u32[]{:S(2)}) collective-permute-start(bf16[2,9,32,256]{3,2,1,0:T(8,128)(2,1)S(1)} %second_grad_pair.1.refs_5_.refs_1_), channel_id=1, source_target_pairs={{0,8},{4,12},{8,0},{12,4},{1,9},{5,13},{9,1},{13,5},{2,10},{6,14},... | collective-permute-start | bytes 884744 | tf_op jit(solution)/shard_map/ppermute | solution.py:901
  131.6 15.6 %collective-permute-start.36 = (bf16[2,9,32,256]{3,2,1,0:T(8,128)(2,1)S(1)}, bf16[2,9,32,256]{3,2,1,0:T(8,128)(2,1)S(1)}, u32[]{:S(2)}, u32[]{:S(2)}) collective-permute-start(bf16[2,9,32,256]{3,2,1,0:T(8,128)(2,1)S(1)} %second_grad_pair.1.refs_5_.refs_1_), channel_id=1, source_target_pairs={{0,4},{4,0},{8,12},{12,8},{1,5},{5,1},{9,13},{13,9},{2,6},{6,2},{1... | collective-permute-start | bytes 884744 | tf_op jit(solution)/shard_map/ppermute | solution.py:901
  132.2 14.9 %collective-permute-start.35 = (bf16[2,9,32,256]{3,2,1,0:T(8,128)(2,1)S(1)}, bf16[2,9,32,256]{3,2,1,0:T(8,128)(2,1)S(1)}, u32[]{:S(2)}, u32[]{:S(2)}) collective-permute-start(bf16[2,9,32,256]{3,2,1,0:T(8,128)(2,1)S(1)} %second_grad_pair.1.refs_5_.refs_1_), channel_id=1, source_target_pairs={{0,1},{1,0},{2,3},{3,2},{4,5},{5,4},{6,7},{7,6},{8,9},{9,8},{10,11... | collective-permute-start | bytes 884744 | tf_op jit(solution)/shard_map/ppermute | solution.py:901
  132.3 14.8 %collective-permute-start.34 = (bf16[2,9,32,256]{3,2,1,0:T(8,128)(2,1)S(1)}, bf16[2,9,32,256]{3,2,1,0:T(8,128)(2,1)S(1)}, u32[]{:S(2)}, u32[]{:S(2)}) collective-permute-start(bf16[2,9,32,256]{3,2,1,0:T(8,128)(2,1)S(1)} %get-tuple-element.158), channel_id=1, source_target_pairs={{0,1},{1,0},{2,3},{3,2},{4,5},{5,4},{6,7},{7,6},{8,9},{9,8},{10,11... | collective-permute-start | bytes 884744 | tf_op jit(solution)/shard_map/ppermute | solution.py:901
  147.1 8.6 %collective-permute-start.43 = (bf16[9,32,256]{2,1,0:T(8,128)(2,1)S(1)}, bf16[9,32,256]{2,1,0:T(8,128)(2,1)S(1)}, u32[]{:S(2)}, u32[]{:S(2)}) collective-permute-start(bf16[9,32,256]{2,1,0:T(8,128)(2,1)S(1)} %get-tuple-element.165), channel_id=1, source_target_pairs={{0,2},{1,3},{2,0},{3,1},{4,6},{5,7},{6,4},{7,5},{8,10},{9,11},{10,... | collective-permute-start | bytes 442376 | tf_op jit(solution)/shard_map/ppermute | solution.py:901
  151.2 4.7 %collective-permute-start.40 = (bf16[9,32,256]{2,1,0:T(8,128)(2,1)S(1)}, bf16[9,32,256]{2,1,0:T(8,128)(2,1)S(1)}, u32[]{:S(2)}, u32[]{:S(2)}) collective-permute-start(bf16[9,32,256]{2,1,0:T(8,128)(2,1)S(1)} %get-tuple-element.162), channel_id=1, source_target_pairs={{0,16},{16,0},{1,17},{17,1},{2,18},{18,2},{3,19},{19,3},{4,20},{20... | collective-permute-start | bytes 442376 | tf_op jit(solution)/shard_map/ppermute | solution.py:901
  151.2 4.7 %collective-permute-start.41 = (bf16[9,32,256]{2,1,0:T(8,128)(2,1)S(1)}, bf16[9,32,256]{2,1,0:T(8,128)(2,1)S(1)}, u32[]{:S(2)}, u32[]{:S(2)}) collective-permute-start(bf16[9,32,256]{2,1,0:T(8,128)(2,1)S(1)} %get-tuple-element.163), channel_id=1, source_target_pairs={{0,16},{16,0},{1,17},{17,1},{2,18},{18,2},{3,19},{19,3},{4,20},{20... | collective-permute-start | bytes 442376 | tf_op jit(solution)/shard_map/ppermute | solution.py:901
  155.8 8.9 %collective-permute-start.48 = (bf16[9,32,256]{2,1,0:T(8,128)(2,1)S(1)}, bf16[9,32,256]{2,1,0:T(8,128)(2,1)S(1)}, u32[]{:S(2)}, u32[]{:S(2)}) collective-permute-start(bf16[9,32,256]{2,1,0:T(8,128)(2,1)S(1)} %first_grad_final.1.refs_5_.refs_0_), channel_id=1, source_target_pairs={{0,2},{1,3},{2,0},{3,1},{4,6},{5,7},{6,4},{7,5},{8,10},{9,11},{10,... | collective-permute-start | bytes 442376 | tf_op jit(solution)/shard_map/ppermute | solution.py:901
  161.4 5.8 %collective-permute-start.45 = (bf16[5,32,256]{2,1,0:T(8,128)(2,1)S(1)}, bf16[5,32,256]{2,1,0:T(8,128)(2,1)S(1)}, u32[]{:S(2)}, u32[]{:S(2)}) collective-permute-start(bf16[5,32,256]{2,1,0:T(8,128)(2,1)S(1)} %get-tuple-element.170), channel_id=1, source_target_pairs={{0,16},{16,0},{1,17},{17,1},{2,18},{18,2},{3,19},{19,3},{4,20},{20... | collective-permute-start | bytes 245768 | tf_op jit(solution)/shard_map/ppermute | solution.py:901
  161.6 5.6 %collective-permute-start.46 = (bf16[5,32,256]{2,1,0:T(8,128)(2,1)S(1)}, bf16[5,32,256]{2,1,0:T(8,128)(2,1)S(1)}, u32[]{:S(2)}, u32[]{:S(2)}) collective-permute-start(bf16[5,32,256]{2,1,0:T(8,128)(2,1)S(1)} %get-tuple-element.171), channel_id=1, source_target_pairs={{0,16},{16,0},{1,17},{17,1},{2,18},{18,2},{3,19},{19,3},{4,20},{20... | collective-permute-start | bytes 245768 | tf_op jit(solution)/shard_map/ppermute | solution.py:901
  162.0 6.0 %collective-permute-start.47 = (bf16[5,32,256]{2,1,0:T(8,128)(2,1)S(1)}, bf16[5,32,256]{2,1,0:T(8,128)(2,1)S(1)}, u32[]{:S(2)}, u32[]{:S(2)}) collective-permute-start(bf16[5,32,256]{2,1,0:T(8,128)(2,1)S(1)} %get-tuple-element.172), channel_id=1, source_target_pairs={{0,16},{16,0},{1,17},{17,1},{2,18},{18,2},{3,19},{19,3},{4,20},{20... | collective-permute-start | bytes 245768 | tf_op jit(solution)/shard_map/ppermute | solution.py:901
  162.1 9.8 %collective-permute-start.53 = (bf16[2,9,32,256]{3,2,1,0:T(8,128)(2,1)S(1)}, bf16[2,9,32,256]{3,2,1,0:T(8,128)(2,1)S(1)}, u32[]{:S(2)}, u32[]{:S(2)}) collective-permute-start(bf16[2,9,32,256]{3,2,1,0:T(8,128)(2,1)S(1)} %get-tuple-element.175), channel_id=1, source_target_pairs={{0,1},{1,0},{2,3},{3,2},{4,5},{5,4},{6,7},{7,6},{8,9},{9,8},{10,11... | collective-permute-start | bytes 884744 | tf_op jit(solution)/shard_map/ppermute | solution.py:901
  164.8 10.8 %collective-permute-start.52 = (bf16[2,9,32,256]{3,2,1,0:T(8,128)(2,1)S(1)}, bf16[2,9,32,256]{3,2,1,0:T(8,128)(2,1)S(1)}, u32[]{:S(2)}, u32[]{:S(2)}) collective-permute-start(bf16[2,9,32,256]{3,2,1,0:T(8,128)(2,1)S(1)} %collective-permute-done.35.refs_3_.refs_2_), channel_id=1, source_target_pairs={{0,12},{4,8},{8,4},{12,0},{1,13},{5,9},{9,5},{13,1},{2,14},{6,10},... | collective-permute-start | bytes 884744 | tf_op jit(solution)/shard_map/ppermute | solution.py:901
  167.2 11.1 %collective-permute-start.57 = (bf16[2,9,32,256]{3,2,1,0:T(8,128)(2,1)S(1)}, bf16[2,9,32,256]{3,2,1,0:T(8,128)(2,1)S(1)}, u32[]{:S(2)}, u32[]{:S(2)}) collective-permute-start(bf16[2,9,32,256]{3,2,1,0:T(8,128)(2,1)S(1)} %first_grad_pair.1.refs_5_.refs_0_.refs_1_), channel_id=1, source_target_pairs={{0,1},{1,0},{2,3},{3,2},{4,5},{5,4},{6,7},{7,6},{8,9},{9,8},{10,11... | collective-permute-start | bytes 884744 | tf_op jit(solution)/shard_map/ppermute | solution.py:901
  167.3 13.8 %collective-permute-start.51 = (bf16[2,9,32,256]{3,2,1,0:T(8,128)(2,1)S(1)}, bf16[2,9,32,256]{3,2,1,0:T(8,128)(2,1)S(1)}, u32[]{:S(2)}, u32[]{:S(2)}) collective-permute-start(bf16[2,9,32,256]{3,2,1,0:T(8,128)(2,1)S(1)} %collective-permute-done.35.refs_3_.refs_2_), channel_id=1, source_target_pairs={{0,8},{4,12},{8,0},{12,4},{1,9},{5,13},{9,1},{13,5},{2,10},{6,14},... | collective-permute-start | bytes 884744 | tf_op jit(solution)/shard_map/ppermute | solution.py:901
  169.2 12.7 %collective-permute-start.50 = (bf16[2,9,32,256]{3,2,1,0:T(8,128)(2,1)S(1)}, bf16[2,9,32,256]{3,2,1,0:T(8,128)(2,1)S(1)}, u32[]{:S(2)}, u32[]{:S(2)}) collective-permute-start(bf16[2,9,32,256]{3,2,1,0:T(8,128)(2,1)S(1)} %collective-permute-done.35.refs_3_.refs_2_), channel_id=1, source_target_pairs={{0,4},{4,0},{8,12},{12,8},{1,5},{5,1},{9,13},{13,9},{2,6},{6,2},{1... | collective-permute-start | bytes 884744 | tf_op jit(solution)/shard_map/ppermute | solution.py:901
  172.0 12.9 %collective-permute-start.49 = (bf16[2,5,32,256]{3,2,1,0:T(8,128)(2,1)S(1)}, bf16[2,5,32,256]{3,2,1,0:T(8,128)(2,1)S(1)}, u32[]{:S(2)}, u32[]{:S(2)}) collective-permute-start(bf16[2,5,32,256]{3,2,1,0:T(8,128)(2,1)S(1)} %get-tuple-element.174), channel_id=1, source_target_pairs={{0,1},{1,0},{2,3},{3,2},{4,5},{5,4},{6,7},{7,6},{8,9},{9,8},{10,11... | collective-permute-start | bytes 491528 | tf_op jit(solution)/shard_map/ppermute | solution.py:901
  175.6 19.7 %collective-permute-start.55 = (bf16[2,9,32,256]{3,2,1,0:T(8,128)(2,1)S(1)}, bf16[2,9,32,256]{3,2,1,0:T(8,128)(2,1)S(1)}, u32[]{:S(2)}, u32[]{:S(2)}) collective-permute-start(bf16[2,9,32,256]{3,2,1,0:T(8,128)(2,1)S(1)} %first_grad_pair.1.refs_5_.refs_0_.refs_1_), channel_id=1, source_target_pairs={{0,4},{4,0},{8,12},{12,8},{1,5},{5,1},{9,13},{13,9},{2,6},{6,2},{1... | collective-permute-start | bytes 884744 | tf_op jit(solution)/shard_map/ppermute | solution.py:901
  178.3 18.6 %collective-permute-start.58 = (bf16[2,9,32,256]{3,2,1,0:T(8,128)(2,1)S(1)}, bf16[2,9,32,256]{3,2,1,0:T(8,128)(2,1)S(1)}, u32[]{:S(2)}, u32[]{:S(2)}) collective-permute-start(bf16[2,9,32,256]{3,2,1,0:T(8,128)(2,1)S(1)} %collective-permute-done.57.refs_0_.refs_2_), channel_id=1, source_target_pairs={{0,8},{4,12},{8,0},{12,4},{1,9},{5,13},{9,1},{13,5},{2,10},{6,14},... | collective-permute-start | bytes 884744 | tf_op jit(solution)/shard_map/ppermute | solution.py:901
  181.1 9.7 %collective-permute-start.56 = (bf16[9,32,256]{2,1,0:T(8,128)(2,1)S(1)}, bf16[9,32,256]{2,1,0:T(8,128)(2,1)S(1)}, u32[]{:S(2)}, u32[]{:S(2)}) collective-permute-start(bf16[9,32,256]{2,1,0:T(8,128)(2,1)S(1)} %get-tuple-element.179), channel_id=1, source_target_pairs={{0,2},{1,3},{2,0},{3,1},{4,6},{5,7},{6,4},{7,5},{8,10},{9,11},{10,... | collective-permute-start | bytes 442376 | tf_op jit(solution)/shard_map/ppermute | solution.py:901
  190.8 12.0 %collective-permute-start.67 = (bf16[9,32,256]{2,1,0:T(8,128)(2,1)S(1)}, bf16[9,32,256]{2,1,0:T(8,128)(2,1)S(1)}, u32[]{:S(2)}, u32[]{:S(2)}) collective-permute-start(bf16[9,32,256]{2,1,0:T(8,128)(2,1)S(1)} %mid_grad_final.1.refs_5_.refs_0_), channel_id=1, source_target_pairs={{0,2},{1,3},{2,0},{3,1},{4,6},{5,7},{6,4},{7,5},{8,10},{9,11},{10,... | collective-permute-start | bytes 442376 | tf_op jit(solution)/shard_map/ppermute | solution.py:901
  190.9 11.9 %collective-permute-start.54 = (bf16[5,32,256]{2,1,0:T(8,128)(2,1)S(1)}, bf16[5,32,256]{2,1,0:T(8,128)(2,1)S(1)}, u32[]{:S(2)}, u32[]{:S(2)}) collective-permute-start(bf16[5,32,256]{2,1,0:T(8,128)(2,1)S(1)} %get-tuple-element.178), channel_id=1, source_target_pairs={{0,2},{1,3},{2,0},{3,1},{4,6},{5,7},{6,4},{7,5},{8,10},{9,11},{10,... | collective-permute-start | bytes 245768 | tf_op jit(solution)/shard_map/ppermute | solution.py:901
  195.4 32.1 %collective-permute-start.72 = (bf16[4,9,32,256]{3,2,1,0:T(8,128)(2,1)S(1)}, bf16[4,9,32,256]{3,2,1,0:T(8,128)(2,1)S(1)}, u32[]{:S(2)}, u32[]{:S(2)}) collective-permute-start(bf16[4,9,32,256]{3,2,1,0:T(8,128)(2,1)S(1)} %first_grad_cross.2.refs_2_), channel_id=1, source_target_pairs={{0,8},{4,12},{8,0},{12,4},{1,9},{5,13},{9,1},{13,5},{2,10},{6,14},... | collective-permute-start | bytes 1769480 | tf_op jit(solution)/shard_map/ppermute | solution.py:901
  202.9 9.0 %collective-permute-start.74 = (bf16[2,9,32,256]{3,2,1,0:T(8,128)(2,1)S(1)}, bf16[2,9,32,256]{3,2,1,0:T(8,128)(2,1)S(1)}, u32[]{:S(2)}, u32[]{:S(2)}) collective-permute-start(bf16[2,9,32,256]{3,2,1,0:T(8,128)(2,1)S(1)} %mid_grad_pair.1.refs_2_.refs_0_.refs_1_), channel_id=1, source_target_pairs={{0,1},{1,0},{2,3},{3,2},{4,5},{5,4},{6,7},{7,6},{8,9},{9,8},{10,11... | collective-permute-start | bytes 884744 | tf_op jit(solution)/shard_map/ppermute | solution.py:901
  202.9 27.3 %collective-permute-start.73 = (bf16[4,9,32,256]{3,2,1,0:T(8,128)(2,1)S(1)}, bf16[4,9,32,256]{3,2,1,0:T(8,128)(2,1)S(1)}, u32[]{:S(2)}, u32[]{:S(2)}) collective-permute-start(bf16[4,9,32,256]{3,2,1,0:T(8,128)(2,1)S(1)} %first_grad_cross.3.refs_3_), channel_id=1, source_target_pairs={{0,4},{4,0},{8,12},{12,8},{1,5},{5,1},{9,13},{13,9},{2,6},{6,2},{1... | collective-permute-start | bytes 1769480 | tf_op jit(solution)/shard_map/ppermute | solution.py:901
  204.5 20.9 %collective-permute-start.71 = (bf16[2,9,32,256]{3,2,1,0:T(8,128)(2,1)S(1)}, bf16[2,9,32,256]{3,2,1,0:T(8,128)(2,1)S(1)}, u32[]{:S(2)}, u32[]{:S(2)}) collective-permute-start(bf16[2,9,32,256]{3,2,1,0:T(8,128)(2,1)S(1)} %mid_grad_pair.1.refs_2_.refs_0_.refs_1_), channel_id=1, source_target_pairs={{0,4},{4,0},{8,12},{12,8},{1,5},{5,1},{9,13},{13,9},{2,6},{6,2},{1... | collective-permute-start | bytes 884744 | tf_op jit(solution)/shard_map/ppermute | solution.py:901
  211.9 16.8 %collective-permute-start.75 = (bf16[2,9,32,256]{3,2,1,0:T(8,128)(2,1)S(1)}, bf16[2,9,32,256]{3,2,1,0:T(8,128)(2,1)S(1)}, u32[]{:S(2)}, u32[]{:S(2)}) collective-permute-start(bf16[2,9,32,256]{3,2,1,0:T(8,128)(2,1)S(1)} %collective-permute-done.74.refs_0_.refs_2_), channel_id=1, source_target_pairs={{0,8},{4,12},{8,0},{12,4},{1,9},{5,13},{9,1},{13,5},{2,10},{6,14},... | collective-permute-start | bytes 884744 | tf_op jit(solution)/shard_map/ppermute | solution.py:901
  213.3 5.9 %collective-permute-start.66 = (bf16[5,32,256]{2,1,0:T(8,128)(2,1)S(1)}, bf16[5,32,256]{2,1,0:T(8,128)(2,1)S(1)}, u32[]{:S(2)}, u32[]{:S(2)}) collective-permute-start(bf16[5,32,256]{2,1,0:T(8,128)(2,1)S(1)} %down_grad_final.1.refs_9_.refs_2_.refs_0_), channel_id=1, source_target_pairs={{0,2},{1,3},{2,0},{3,1},{4,6},{5,7},{6,4},{7,5},{8,10},{9,11},{10,... | collective-permute-start | bytes 245768 | tf_op jit(solution)/shard_map/ppermute | solution.py:901
  219.3 5.4 %collective-permute-start.68 = (bf16[2,5,32,256]{3,2,1,0:T(8,128)(2,1)S(1)}, bf16[2,5,32,256]{3,2,1,0:T(8,128)(2,1)S(1)}, u32[]{:S(2)}, u32[]{:S(2)}) collective-permute-start(bf16[2,5,32,256]{3,2,1,0:T(8,128)(2,1)S(1)} %down_grad_pair.1.refs_7_.refs_0_.refs_1_), channel_id=1, source_target_pairs={{0,1},{1,0},{2,3},{3,2},{4,5},{5,4},{6,7},{7,6},{8,9},{9,8},{10,11... | collective-permute-start | bytes 491528 | tf_op jit(solution)/shard_map/ppermute | solution.py:901
  224.6 18.4 %collective-permute-start.69 = (bf16[2,5,32,256]{3,2,1,0:T(8,128)(2,1)S(1)}, bf16[2,5,32,256]{3,2,1,0:T(8,128)(2,1)S(1)}, u32[]{:S(2)}, u32[]{:S(2)}) collective-permute-start(bf16[2,5,32,256]{3,2,1,0:T(8,128)(2,1)S(1)} %down_grad_pair.1.refs_7_.refs_0_.refs_1_), channel_id=1, source_target_pairs={{0,4},{4,0},{8,12},{12,8},{1,5},{5,1},{9,13},{13,9},{2,6},{6,2},{1... | collective-permute-start | bytes 491528 | tf_op jit(solution)/shard_map/ppermute | solution.py:901
  225.4 14.6 %collective-permute-start.62 = (bf16[2,2,2,32,256]{4,3,2,1,0:T(8,128)(2,1)S(1)}, bf16[2,2,2,32,256]{4,3,2,1,0:T(8,128)(2,1)S(1)}, u32[]{:S(2)}, u32[]{:S(2)}) collective-permute-start(bf16[2,2,2,32,256]{4,3,2,1,0:T(8,128)(2,1)S(1)} %get-tuple-element.182), channel_id=1, source_target_pairs={{0,1},{1,0},{2,3},{3,2},{4,5},{5,4},{6,7},{7,6},{8,9},{9,8},{10,11... | collective-permute-start | bytes 393224 | tf_op jit(solution)/shard_map/ppermute | solution.py:901
  227.5 14.9 %collective-permute-start.63 = (bf16[2,2,2,32,256]{4,3,2,1,0:T(8,128)(2,1)S(1)}, bf16[2,2,2,32,256]{4,3,2,1,0:T(8,128)(2,1)S(1)}, u32[]{:S(2)}, u32[]{:S(2)}) collective-permute-start(bf16[2,2,2,32,256]{4,3,2,1,0:T(8,128)(2,1)S(1)} %get-tuple-element.183), channel_id=1, source_target_pairs={{0,2},{1,3},{2,0},{3,1},{4,6},{5,7},{6,4},{7,5},{8,10},{9,11},{10,... | collective-permute-start | bytes 393224 | tf_op jit(solution)/shard_map/ppermute | solution.py:901
  228.7 13.7 %collective-permute-start.64 = (bf16[2,2,2,32,256]{4,3,2,1,0:T(8,128)(2,1)S(1)}, bf16[2,2,2,32,256]{4,3,2,1,0:T(8,128)(2,1)S(1)}, u32[]{:S(2)}, u32[]{:S(2)}) collective-permute-start(bf16[2,2,2,32,256]{4,3,2,1,0:T(8,128)(2,1)S(1)} %get-tuple-element.184), channel_id=1, source_target_pairs={{0,3},{1,2},{2,1},{3,0},{4,7},{5,6},{6,5},{7,4},{8,11},{9,10},{10,... | collective-permute-start | bytes 393224 | tf_op jit(solution)/shard_map/ppermute | solution.py:901
  230.2 14.4 %collective-permute-start.70 = (bf16[2,5,32,256]{3,2,1,0:T(8,128)(2,1)S(1)}, bf16[2,5,32,256]{3,2,1,0:T(8,128)(2,1)S(1)}, u32[]{:S(2)}, u32[]{:S(2)}) collective-permute-start(bf16[2,5,32,256]{3,2,1,0:T(8,128)(2,1)S(1)} %collective-permute-done.68.refs_0_.refs_2_), channel_id=1, source_target_pairs={{0,8},{4,12},{8,0},{12,4},{1,9},{5,13},{9,1},{13,5},{2,10},{6,14},... | collective-permute-start | bytes 491528 | tf_op jit(solution)/shard_map/ppermute | solution.py:901
  240.0 7.5 %collective-permute-start.61 = (f32[64,256]{1,0:T(8,128)S(1)}, f32[64,256]{1,0:T(8,128)S(1)}, u32[]{:S(2)}, u32[]{:S(2)}) collective-permute-start(f32[64,256]{1,0:T(8,128)S(1)} %small.1.refs_1_), channel_id=1, source_target_pairs={{0,3},{1,2},{2,1},{3,0},{4,7},{5,6},{6,5},{7,4},{8,11},{9,10},{10,... | collective-permute-start | bytes 196616 | tf_op jit(solution)/shard_map/ppermute | solution.py:901
  242.4 6.2 %collective-permute-start.60 = (f32[64,256]{1,0:T(8,128)S(1)}, f32[64,256]{1,0:T(8,128)S(1)}, u32[]{:S(2)}, u32[]{:S(2)}) collective-permute-start(f32[64,256]{1,0:T(8,128)S(1)} %small.1.refs_1_), channel_id=1, source_target_pairs={{0,2},{1,3},{2,0},{3,1},{4,6},{5,7},{6,4},{7,5},{8,10},{9,11},{10,... | collective-permute-start | bytes 196616 | tf_op jit(solution)/shard_map/ppermute | solution.py:901
  242.4 23.4 %collective-permute-start.78 = (bf16[4,9,32,256]{3,2,1,0:T(8,128)(2,1)S(1)}, bf16[4,9,32,256]{3,2,1,0:T(8,128)(2,1)}, u32[]{:S(2)}, u32[]{:S(2)}) collective-permute-start(bf16[4,9,32,256]{3,2,1,0:T(8,128)(2,1)S(1)} %mid_grad_cross.2.refs_2_), channel_id=1, source_target_pairs={{0,8},{4,12},{8,0},{12,4},{1,9},{5,13},{9,1},{13,5},{2,10},{6,14},... | collective-permute-start | bytes 1769480 | tf_op jit(solution)/shard_map/ppermute | solution.py:901
  243.0 22.8 %collective-permute-start.79 = (bf16[4,9,32,256]{3,2,1,0:T(8,128)(2,1)S(1)}, bf16[4,9,32,256]{3,2,1,0:T(8,128)(2,1)}, u32[]{:S(2)}, u32[]{:S(2)}) collective-permute-start(bf16[4,9,32,256]{3,2,1,0:T(8,128)(2,1)S(1)} %mid_grad_cross.3.refs_3_), channel_id=1, source_target_pairs={{0,4},{4,0},{8,12},{12,8},{1,5},{5,1},{9,13},{13,9},{2,6},{6,2},{1... | collective-permute-start | bytes 1769480 | tf_op jit(solution)/shard_map/ppermute | solution.py:901
  244.7 6.8 %collective-permute-start.59 = (f32[64,256]{1,0:T(8,128)S(1)}, f32[64,256]{1,0:T(8,128)S(1)}, u32[]{:S(2)}, u32[]{:S(2)}) collective-permute-start(f32[64,256]{1,0:T(8,128)S(1)} %small.1.refs_1_), channel_id=1, source_target_pairs={{0,1},{1,0},{2,3},{3,2},{4,5},{5,4},{6,7},{7,6},{8,9},{9,8},{10,11... | collective-permute-start | bytes 196616 | tf_op jit(solution)/shard_map/ppermute | solution.py:901
  248.1 13.9 %collective-permute-start.77 = (bf16[4,5,32,256]{3,2,1,0:T(8,128)(2,1)}, bf16[4,5,32,256]{3,2,1,0:T(8,128)(2,1)}, u32[]{:S(2)}, u32[]{:S(2)}) collective-permute-start(bf16[4,5,32,256]{3,2,1,0:T(8,128)(2,1)} %down_grad_cross.3), channel_id=1, source_target_pairs={{0,4},{4,0},{8,12},{12,8},{1,5},{5,1},{9,13},{13,9},{2,6},{6,2},{1... | collective-permute-start | bytes 983048 | tf_op jit(solution)/shard_map/ppermute | solution.py:901
  249.2 12.7 %collective-permute-start.76 = (bf16[4,5,32,256]{3,2,1,0:T(8,128)(2,1)S(1)}, bf16[4,5,32,256]{3,2,1,0:T(8,128)(2,1)}, u32[]{:S(2)}, u32[]{:S(2)}) collective-permute-start(bf16[4,5,32,256]{3,2,1,0:T(8,128)(2,1)S(1)} %down_grad_cross.2.refs_7_), channel_id=1, source_target_pairs={{0,8},{4,12},{8,0},{12,4},{1,9},{5,13},{9,1},{13,5},{2,10},{6,14},... | collective-permute-start | bytes 983048 | tf_op jit(solution)/shard_map/ppermute | solution.py:901
  252.0 4.9 %collective-permute-start.65 = (bf16[4,2,2,32,256]{4,3,2,1,0:T(8,128)(2,1)}, bf16[4,2,2,32,256]{4,3,2,1,0:T(8,128)(2,1)}, u32[]{:S(2)}, u32[]{:S(2)}) collective-permute-start(bf16[4,2,2,32,256]{4,3,2,1,0:T(8,128)(2,1)} %get-tuple-element.193), channel_id=1, source_target_pairs={{0,16},{16,0},{1,17},{17,1},{2,18},{18,2},{3,19},{19,3},{4,20},{20... | collective-permute-start | bytes 786440 | tf_op jit(solution)/shard_map/ppermute | solution.py:901
  (52 other events, 308.7 us)

commit v5 on v4

--- a/solution.py
+++ b/solution.py
@@ -138,6 +138,7 @@
 
 
 KERNEL_LIMIT = 24 * 2**20
+PARTS, LAST_PARTS = 4, 1
 VM = pl.BlockSpec(memory_space=pltpu.VMEM)
 SM = pl.BlockSpec(memory_space=pltpu.SMEM)
 NT = (((1,), (1,)), ((), ()))
@@ -210,13 +211,13 @@
 
 
 def conv_core(x_ref, w_ref, out_ref, back):
-    for part in range(2):
-        images = slice(4 * part, 4 * part + 4)
+    for part in range(1):
+        images = slice(0, 8)
 
         def tap(col):
             value = None
             for row in range(3):
-                lhs = x_ref[images, :, row * 512 : (row + 1) * 512].reshape(512, 512)
+                lhs = x_ref[images, :, row * 512 : (row + 1) * 512].reshape(1024, 512)
                 if back:
                     term = lax.dot_general(
                         lhs, w_ref[2 - row, 2 - col], NT, preferred_element_type=F32
@@ -227,7 +228,7 @@
             return value
 
         out = columns_joined(tap(0), tap(1), tap(2))
-        out_ref[images] = out.reshape(4, 128, 512)
+        out_ref[images] = out.reshape(8, 128, 512)
 
 
 def stats_of(facts_ref, out_ref, stat_ref, row):
@@ -290,8 +291,8 @@
                         out[lines, start : start + 128] = value.astype(BF16)
     marks = jnp.concatenate(
         [
-            labels_ref[...].astype(F32),
-            jnp.broadcast_to(count_ref[...].astype(F32), (4, tasks)),
+            labels_ref[pl.ds(zone * 4, 4), :].astype(F32),
+            jnp.full((4, tasks), count_ref[0, zone].astype(F32)),
             jnp.zeros((8, tasks), F32),
         ]
     )
@@ -669,8 +670,9 @@
 
 
 def hand_out(other_ref, outs):
-    for slot, out in enumerate(outs):
-        out[...] = other_ref[slot]
+    each = 4 // len(outs)
+    for slot in range(4):
+        outs[slot // each][slot % each] = other_ref[slot]
 
 
 def turned_taps(batch, act_ref, turned_ref):
@@ -699,11 +701,12 @@
         split_out(pipe, zone, unit, results[0][rows], results[1][rows], own_ref, other_ref)
 
 
-def kernel_grad_kernel(where_ref, act_ref, low_ref, own_ref, o0, o1, o2, o3, turned_ref, other_ref):
+def kernel_grad_kernel(where_ref, act_ref, low_ref, own_ref, *refs):
+    outs, (turned_ref, other_ref) = refs[:-2], refs[-2:]
     pipe, batch, zone = where_ref[0], where_ref[1], where_ref[2]
     turned_taps(batch, act_ref, turned_ref)
     tap_products(pipe, zone, low_ref, turned_ref, own_ref, other_ref)
-    hand_out(other_ref, (o0, o1, o2, o3))
+    hand_out(other_ref, outs)
 
 
 DOWN_UNITS = (
@@ -712,8 +715,8 @@
 )
 
 
-def down_grad_kernel(where_ref, img_ref, low_ref, low_s_ref, own_ref, o0, o1, o2, o3,
-                     turned_ref, other_ref):
+def down_grad_kernel(where_ref, img_ref, low_ref, low_s_ref, own_ref, *refs):
+    outs, (turned_ref, other_ref) = refs[:-2], refs[-2:]
     pipe, batch, zone = where_ref[0], where_ref[1], where_ref[2]
     upper, part = batch // 2, batch % 2
 
@@ -745,14 +748,18 @@
                 rhs = jnp.where(upper == 0, rhs_s, rhs)
             results.append(jnp.dot(lhs, rhs, preferred_element_type=F32))
         split_out(pipe, zone, unit, results[0], results[1], own_ref, other_ref)
-    hand_out(other_ref, (o0, o1, o2, o3))
-
-
-def add_cores_kernel(own_ref, g0, g1, g2, g3, keep_ref, send_ref):
-    for slot, got in enumerate((g0, g1)):
-        keep_ref[slot] = own_ref[slot] + got[...].astype(F32)
-    for slot, got in enumerate((g2, g3)):
-        send_ref[slot] = (own_ref[2 + slot] + got[...].astype(F32)).astype(BF16)
+    hand_out(other_ref, outs)
+
+
+def add_cores_kernel(own_ref, *refs):
+    got, (keep_ref, send_ref) = refs[:-2], refs[-2:]
+    each = 4 // len(got)
+    for slot in range(4):
+        value = own_ref[slot] + got[slot // each][slot % each].astype(F32)
+        if slot < 2:
+            keep_ref[slot] = value
+        else:
+            send_ref[slot - 2] = value.astype(BF16)
 
 
 def add_near_kernel(own_ref, got_ref, keep_ref, send_ref):
@@ -908,10 +915,10 @@
     pieces = call(
         pieces_kernel,
         [((144, 512), BF16)] + [((128, 512), BF16)] * 3,
-        [where, images, lax.dynamic_slice_in_dim(labels, zone * 4, 4, 0),
-         lax.dynamic_slice_in_dim(image_counts, zone, 1, 1)],
+        [where, images, labels, image_counts],
         [pltpu.VMEM((64, 128), F32)],
         name="pieces",
+        specs={3: SM},
     )
     moved = [over("space", rel, pieces[rel]) for rel in (1, 2, 3)]
     moved = [pieces[0], moved[0], jnp.concatenate([moved[1], moved[2]])]
@@ -993,11 +1000,11 @@
     )
 
     class Sum:
-        def __init__(self, kernel, units, operands, scratch, flops, name, after=()):
+        def __init__(self, kernel, units, operands, scratch, flops, name, after=(), parts=4):
             self.units, self.name = units, name
             self.own, *self.other = call(
                 kernel,
-                [self.block(4, dtype=F32)] + [self.block()] * 4,
+                [self.block(4, dtype=F32)] + [self.block(4 // parts)] * parts,
                 operands,
                 [scratch, pltpu.VMEM((4, units, 32, 256), BF16)],
                 flops,
@@ -1067,10 +1074,10 @@
             self.ayy, self.bxx = over("batch", 2, self.fa), over("batch", 1, self.fb)
             self.blocks = [where, self.a, self.b, self.ax, self.by, self.ayy, self.bxx]
 
-    def kernel_grad_of(act, low_grad, name, after=()):
+    def kernel_grad_of(act, low_grad, name, after=(), parts=PARTS):
         return Sum(
             kernel_grad_kernel, 9, [where, act, low_grad], pltpu.VMEM((9, 128, 1024), BF16),
-            conv_flops // 4, name, after,
+            conv_flops // 4, name, after, parts,
         )
 
     def assembled(blocks, name, after=()):
@@ -1104,7 +1111,7 @@
     second.zone_far(after=[sum_j])
     first = kernel_grad_of(section, first_low, "first_grad", after=[second.final])
     second.pair(after=first.other[0:1])
-    second.direct()
+    second.plane()
     first.cores(after=[second.a])
     mid_low, short_low, up_d, sum_d = call(
         mid_back_kernel,
@@ -1117,28 +1124,26 @@
         after=[first.keep],
     )
     other_sd = partner(sum_d)
-    first.zone_near(after=[sum_d, second.b])
-    mid = kernel_grad_of(down_act, mid_low, "mid_grad", after=[first.keep] + second.ra)
+    first.zone_near(after=[sum_d, second.b, second.ax])
+    mid = kernel_grad_of(down_act, mid_low, "mid_grad", after=[first.keep])
     first.zone_far(after=mid.other[0:1])
     mid.cores(after=[first.final])
+    second.plane_far(after=[mid.keep])
     (down_low,) = call(
         down_back_kernel,
         [low],
         [facts, up_d, down_out, norm_d, sum_d, other_sd, params],
         name="down_back",
-        after=[mid.keep],
+        after=[second.fa, second.fb],
     )
     down = Sum(
         down_grad_kernel, 5, [where, img, down_low, short_low], pltpu.VMEM((5, 128, 1024), BF16),
-        conv_flops // 8, "down_grad",
+        conv_flops // 8, "down_grad", parts=LAST_PARTS,
     )
     first.pair(after=down.other[0:1])
-    down.cores(after=[first.a])
-    mid.zone_near(after=[down.keep])
     first.plane()
-    second_out_grad = assembled(second.blocks, "second_out", after=[mid.keep])
-    down.zone_near(after=[second_out_grad])
-    mid.zone_far(after=[down.keep])
+    mid.zone_near(after=[first.a])
+    down.cores(after=[mid.keep])
     img_pieces = call(
         image_back_kernel,
         [((2, 2, 2, 32, 256), BF16)] * 4,
@@ -1146,13 +1151,16 @@
         [pltpu.VMEM((4, 2, 2, 2, 32, 256), BF16)],
         conv_flops // 8,
         "image_back",
-        after=[mid.final],
-    )
-    first.plane_far(after=[img_pieces[0]])
-    down.zone_far(after=[first.fa, first.fb])
-    mid.pair(after=[down.final])
+        after=[down.keep],
+    )
+    mid.zone_far(after=[img_pieces[0]])
+    down.zone_near(after=[mid.final])
+    second_out_grad = assembled(second.blocks, "second_out", after=[down.keep, first.b])
+    first.plane_far(after=[second_out_grad])
+    mid.pair(after=[first.fa, first.fb])
     mid.plane()
-    down.pair(after=[mid.a])
+    down.zone_far(after=[mid.a])
+    down.pair()
     down.plane()
     first_out_grad = assembled(first.blocks, "first_out", after=[down.a])
     mid.plane_far(after=[first_out_grad])

time: 274 us -> 258 us (0.942)
  waiting for transfers between devices: 75.1 us -> 63.8 us
  starting transfers between devices: 73.9 us -> 70.5 us
    ppermute x80 -> x75, waiting for transfers between devices: 75.1 us -> 63.8 us  [over(): return lax.ppermute(x, axis, [(i, i ^ rel) for i in range(size)])]
    ppermute x80 -> x75, starting transfers between devices: 73.9 us -> 70.5 us  [over(): return lax.ppermute(x, axis, [(i, i ^ rel) for i in range(size)])]
    pallas_call x47 -> x49, Pallas kernels: 97.9 us -> 97 us  [call(): pl.pallas_call(body, out_shape=tuple((jax.ShapeDtypeStruct(shape, dtype)...]
    unnamed x73 -> x81, local copies, waits for them, and re-layouts: 17.9 us -> 18.7 us
  transfers between devices with their start and end apart: 80 -> 75, of which waited for: 34 -> 29; matrix products, arithmetic and copies ran while one was open for 1% -> 1% of each run, Pallas kernels for 20% -> 22%
where the time goes in v5:
time: 258 us; the launch traced here: 254 us
  Pallas kernels  97 us (38%)
  starting transfers between devices  70.5 us (27%)
  waiting for transfers between devices  63.8 us (25%)
  local copies, waits for them, and re-layouts  20.6 us (8%)
    pallas_call x49, Pallas kernels, call(): pl.pallas_call(body, out_shape=tuple((jax.ShapeDtypeStruct(shape, dtype)...  97 us
    ppermute x75, starting transfers between devices, over(): return lax.ppermute(x, axis, [(i, i ^ rel) for i in range(size)])  70.5 us
    ppermute x75, waiting for transfers between devices, over(): return lax.ppermute(x, axis, [(i, i ^ rel) for i in range(size)])  63.8 us
    unnamed x81, local copies, waits for them, and re-layouts  18.7 us
  transfers between devices with their start and end apart: 75, of which 29 were waited for; matrix products, arithmetic and copies ran while one was open for 1% of the time, Pallas kernels for 22%

profile of v5, /device:TPU:0, one launch (start us, length us, event | category | flops | bytes accessed | tf_op | source)
XLA Modules:
  0.0 254.0 jit_solution(10065711000810255447)
XLA Ops:
  4.1 4.1 %collective-permute-start.4 = (bf16[128,512]{1,0:T(8,128)(2,1)S(1)}, bf16[128,512]{1,0:T(8,128)(2,1)S(1)}, u32[]{:S(2)}, u32[]{:S(2)}) collective-permute-start(bf16[128,512]{1,0:T(8,128)(2,1)S(1)} %get-tuple-element.103), channel_id=1, source_target_pairs={{0,2},{1,3},{2,0},{3,1},{4,6},{5,7},{6,4},{7,5},{8,10},{9,11},{10,... | collective-permute-start | bytes 393224 | tf_op jit(solution)/shard_map/ppermute | solution.py:908
  9.5 2.4 collective-permute-start.2
  13.0 5.1 %collective-permute-done.4 = bf16[128,512]{1,0:T(8,128)(2,1)S(1)} collective-permute-done((bf16[128,512]{1,0:T(8,128)(2,1)S(1)}, bf16[128,512]{1,0:T(8,128)(2,1)S(1)}, u32[]{:S(2)}, u32[]{:S(2)}) %collective-permute-start.4) | collective-permute-done | bytes 131104 | tf_op jit(solution)/shard_map/ppermute | solution.py:908
  18.2 2.9 %collective-permute-start.11 = (bf16[256,512]{1,0:T(8,128)(2,1)S(1)}, bf16[256,512]{1,0:T(8,128)(2,1)S(1)}, u32[]{:S(2)}, u32[]{:S(2)}) collective-permute-start(bf16[256,512]{1,0:T(8,128)(2,1)S(1)} %constant_dynamic-update-slice_fusion.refs_4_), channel_id=1, source_target_pairs={{0,12},{4,8},{8,4},{12,0},{1,13},{5,9},{9,5},{13,1},{2,14},{6,10},... | collective-permute-start | bytes 786440 | tf_op jit(solution)/shard_map/ppermute | solution.py:908
  21.0 2.1 collective-permute-done.3.refs_3_
  23.1 2.8 %collective-permute-start.10 = (bf16[128,512]{1,0:T(8,128)(2,1)S(1)}, bf16[128,512]{1,0:T(8,128)(2,1)S(1)}, u32[]{:S(2)}, u32[]{:S(2)}) collective-permute-start(bf16[128,512]{1,0:T(8,128)(2,1)S(1)} %collective-permute-done.3.refs_3_), channel_id=1, source_target_pairs={{0,12},{4,8},{8,4},{12,0},{1,13},{5,9},{9,5},{13,1},{2,14},{6,10},... | collective-permute-start | bytes 393224 | tf_op jit(solution)/shard_map/ppermute | solution.py:908
  26.6 1.9 collective-permute-start.8
  28.5 2.7 %collective-permute-done.10.refs_12_ = bf16[128,512]{1,0:T(8,128)(2,1)S(1)} collective-permute-done((bf16[128,512]{1,0:T(8,128)(2,1)S(1)}, bf16[128,512]{1,0:T(8,128)(2,1)S(1)}, u32[]{:S(2)}, u32[]{:S(2)}) %collective-permute-start.10) | collective-permute-done | bytes 131104 | tf_op jit(solution)/shard_map/ppermute | solution.py:908
  31.2 1.9 collective-permute-start.6
  35.3 2.9 %collective-permute-done.8.refs_9_ = bf16[128,512]{1,0:T(8,128)(2,1)S(1)} collective-permute-done((bf16[128,512]{1,0:T(8,128)(2,1)S(1)}, bf16[128,512]{1,0:T(8,128)(2,1)S(1)}, u32[]{:S(2)}, u32[]{:S(2)}) %collective-permute-start.8) | collective-permute-done | bytes 131104 | tf_op jit(solution)/shard_map/ppermute | solution.py:908
  38.3 1.7 copy-done.3
  40.0 4.7 %down.1 = (bf16[8,128,1024]{2,1,0:T(8,128)(2,1)S(1)}, f32[8,128,512]{2,1,0:T(8,128)S(1)}, f32[8,128,512]{2,1,0:T(8,128)S(1)}, f32[8,512]{1,0:T(8,128)S(1)}) custom-call(f32[16]{0:T(128)S(1)} %get-tuple-element.101.refs_0_.refs_2_, s32[4]{0:T(128)S(1)} %pad_add_fusion.refs_0_.refs_1_, bf16[144,512]{1,0:T(8,128)(2,1)S(1)} %get-tuple-element.100.refs_1_.refs_2_, ...), custom_call_target="tpu_custom_call" | custom-call | flops 2415919104 | bytes 4784208 | tf_op jit(solution)/shard_map/down/pallas_call | solution.py:162
  46.0 6.9 %mid.1 = (bf16[8,128,512]{2,1,0:T(8,128)(2,1)S(1)}, f32[8,128,512]{2,1,0:T(8,128)S(1)}, f32[8,512]{1,0:T(8,128)S(1)}, f32[8,512]{1,0:T(8,128)S(1)}) custom-call(f32[16]{0:T(128)S(1)} %get-tuple-element.101.refs_0_.refs_2_, f32[8,128,512]{2,1,0:T(8,128)S(1)} %get-tuple-element.105.refs_1_.refs_9_.refs_2_, f32[8,512]{1,0:T(8,128)S(1)} %get-tuple-element.106.refs_2_.refs_5_, ...), custom_call_target="tpu_custom_call" | custom-call | flops 4831838208 | bytes 6869056 | tf_op jit(solution)/shard_map/mid/pallas_call | solution.py:162
  54.3 7.3 %first.1 = (bf16[8,128,512]{2,1,0:T(8,128)(2,1)S(1)}, f32[8,128,512]{2,1,0:T(8,128)S(1)}, f32[8,512]{1,0:T(8,128)S(1)}, f32[8,512]{1,0:T(8,128)S(1)}) custom-call(f32[16]{0:T(128)S(1)} %get-tuple-element.101.refs_0_.refs_2_, f32[8,128,512]{2,1,0:T(8,128)S(1)} %get-tuple-element.107.refs_1_.refs_12_.refs_2_, ...), custom_call_target="tpu_custom_call" | custom-call | flops 4831838208 | bytes 8998976 | tf_op jit(solution)/shard_map/first/pallas_call | solution.py:162
  62.9 6.9 %second.1 = (bf16[8,128,512]{2,1,0:T(8,128)(2,1)S(1)}, f32[8,128,512]{2,1,0:T(8,128)S(1)}, f32[8,512]{1,0:T(8,128)S(1)}, f32[8,512]{1,0:T(8,128)S(1)}) custom-call(f32[16]{0:T(128)S(1)} %get-tuple-element.101.refs_0_.refs_2_, f32[8,128,512]{2,1,0:T(8,128)S(1)} %get-tuple-element.110.refs_1_.refs_2_, f32[8,512]{1,0:T(8,128)S(1)} %get-tuple-element.111.refs_2_, ...), custom_call_target="tpu_custom_call" | custom-call | flops 4831838208 | bytes 6869056 | tf_op jit(solution)/shard_map/second/pallas_call | solution.py:162
  71.1 2.2 block.1
  75.5 3.1 %collective-permute-start.19 = (f32[40,40]{1,0:T(8,128)S(1)}, f32[40,40]{1,0:T(8,128)S(1)}, u32[]{:S(2)}, u32[]{:S(2)}) collective-permute-start(f32[40,40]{1,0:T(8,128)S(1)} %get-tuple-element.118.refs_3_), channel_id=1, source_target_pairs={{0,3},{1,2},{2,1},{3,0},{4,7},{5,6},{6,5},{7,4},{8,11},{9,10},{10,... | collective-permute-start | bytes 19208 | tf_op jit(solution)/shard_map/ppermute | solution.py:908
  78.7 1.9 collective-permute-start.18
  81.1 2.3 collective-permute-done.18.refs_5_
  84.4 4.5 %head.1 = (bf16[8,128,512]{2,1,0:T(8,128)(2,1)S(1)}, f32[8,512]{1,0:T(8,128)S(1)}, f32[48,512]{1,0:T(8,128)S(1)}) custom-call(s32[20]{0:T(128)S(1)} %copy-done.20, s32[4]{0:T(128)S(1)} %pad_add_fusion.refs_0_.refs_1_, f32[16]{0:T(128)S(1)} %get-tuple-element.101.refs_0_.refs_2_, f32[40,40]{1,0:T(8,128)S(1)} %get-tuple-element.118.refs_3_, ...), custom_call_target="tpu_custom_call" | custom-call | bytes 3397536 | tf_op jit(solution)/shard_map/head/pallas_call | solution.py:162
  88.9 4.1 %second_grad.1 = (f32[4,9,32,256]{3,2,1,0:T(8,128)S(1)}, bf16[1,9,32,256]{3,2,1,0:T(8,128)(2,1)S(1)}, bf16[1,9,32,256]{3,2,1,0:T(8,128)(2,1)S(1)}, bf16[1,9,32,2...) custom-call(s32[4]{0:T(128)S(1)} %pad_add_fusion.refs_0_.refs_1_, bf16[8,128,512]{2,1,0:T(8,128)(2,1)S(1)} %get-tuple-element.126.refs_1_, ...), custom_call_target="tpu_custom_call" | custom-call | flops 1207959552 | bytes 2097168 | tf_op jit(solution)/shard_map/second_grad/pallas_call | solution.py:162
  95.3 1.5 collective-permute-start.25
  96.8 7.2 %second_back.1 = (f32[8,128,512]{2,1,0:T(8,128)S(1)}, f32[8,512]{1,0:T(8,128)S(1)}) custom-call(f32[16]{0:T(128)S(1)} %get-tuple-element.101.refs_0_.refs_2_, bf16[8,128,512]{2,1,0:T(8,128)(2,1)S(1)} %get-tuple-element.124.refs_2_.refs_1_, f32[8,128,512]{2,1,0:T(8,128)S(1)} %get-tuple-element.110.refs_1_.refs_2_, f32[8,512]{1,0:T(8,128)S(1)} %get-tuple-element.125.refs_3_, ...), custom_call_target="tpu_custom_call" | custom-call | flops 4831838208 | bytes 7901248 | tf_op jit(solution)/shard_map/second_back/pallas_call | solution.py:162
  104.6 1.8 collective-permute-start.27
  106.4 1.7 copy-done.27
  108.1 9.6 %first_back.1 = (bf16[8,128,512]{2,1,0:T(8,128)(2,1)S(1)}, f32[8,128,512]{2,1,0:T(8,128)S(1)}, f32[8,512]{1,0:T(8,128)S(1)}) custom-call(f32[16]{0:T(128)S(1)} %get-tuple-element.101.refs_0_.refs_2_, f32[8,128,512]{2,1,0:T(8,128)S(1)} %get-tuple-element.134.refs_1_, f32[8,128,512]{2,1,0:T(8,128)S(1)} %copy-done.27, f32[8,512]{1,0:T(8,128)S(1)} %get-tuple-element.125.refs_3_, ...), custom_call_target="tpu_custom_call" | custom-call | flops 4831838208 | bytes 16371776 | tf_op jit(solution)/shard_map/first_back/pallas_call | solution.py:162
  119.1 3.9 %first_grad.1 = (f32[4,9,32,256]{3,2,1,0:T(8,128)S(1)}, bf16[1,9,32,256]{3,2,1,0:T(8,128)(2,1)S(1)}, bf16[1,9,32,256]{3,2,1,0:T(8,128)(2,1)S(1)}, bf16[1,9,32,25...) custom-call(s32[4]{0:T(128)S(1)} %pad_add_fusion.refs_0_.refs_1_, ...), custom_call_target="tpu_custom_call" | custom-call | flops 1207959552 | bytes 2097168 | tf_op jit(solution)/shard_map/first_grad/pallas_call | solution.py:162
  124.1 3.6 %collective-permute-done.32.refs_1_ = bf16[9,32,256]{2,1,0:T(8,128)(2,1)S(1)} collective-permute-done((bf16[9,32,256]{2,1,0:T(8,128)(2,1)S(1)}, bf16[9,32,256]{2,1,0:T(8,128)(2,1)S(1)}, u32[]{:S(2)}, u32[]{:S(2)}) %collective-permute-start.32) | collective-permute-done | bytes 147488 | tf_op jit(solution)/shard_map/ppermute | solution.py:908
  127.8 1.5 collective-permute-start.34
  129.5 2.0 collective-permute-start.35
  131.6 8.4 %mid_back.1 = (bf16[8,128,512]{2,1,0:T(8,128)(2,1)S(1)}, bf16[8,128,512]{2,1,0:T(8,128)(2,1)S(1)}, f32[8,128,512]{2,1,0:T(8,128)S(1)}, f32[8,512]{1,0:T(8,128)S(1)}) custom-call(f32[16]{0:T(128)S(1)} %get-tuple-element.101.refs_0_.refs_2_, f32[8,128,512]{2,1,0:T(8,128)S(1)} %get-tuple-element.140.refs_1_, f32[8,128,512]{2,1,0:T(8,128)S(1)} %copy-done.25, ...), custom_call_target="tpu_custom_call" | custom-call | flops 4831838208 | bytes 13193280 | tf_op jit(solution)/shard_map/mid_back/pallas_call | solution.py:162
  140.0 3.6 %collective-permute-done.35.refs_1_ = bf16[2,9,32,256]{3,2,1,0:T(8,128)(2,1)S(1)} collective-permute-done((bf16[2,9,32,256]{3,2,1,0:T(8,128)(2,1)S(1)}, bf16[2,9,32,256]{3,2,1,0:T(8,128)(2,1)S(1)}, u32[]{:S(2)}, u32[]{:S(2)}) %collective-permute-start.35) | collective-permute-done | bytes 294944 | tf_op jit(solution)/shard_map/ppermute | solution.py:908
  143.8 1.4 collective-permute-start.42
  145.2 3.9 %mid_grad.1 = (f32[4,9,32,256]{3,2,1,0:T(8,128)S(1)}, bf16[1,9,32,256]{3,2,1,0:T(8,128)(2,1)S(1)}, bf16[1,9,32,256]{3,2,1,0:T(8,128)(2,1)S(1)}, bf16[1,9,32,256]...) custom-call(s32[4]{0:T(128)S(1)} %pad_add_fusion.refs_0_.refs_1_, bf16[8,128,512]{2,1,0:T(8,128)(2,1)S(1)} %copy-done.29, ...), custom_call_target="tpu_custom_call" | custom-call | flops 1207959552 | bytes 2097168 | tf_op jit(solution)/shard_map/mid_grad/pallas_call | solution.py:162
  149.8 3.4 %collective-permute-done.41.refs_1_ = bf16[9,32,256]{2,1,0:T(8,128)(2,1)S(1)} collective-permute-done((bf16[9,32,256]{2,1,0:T(8,128)(2,1)S(1)}, bf16[9,32,256]{2,1,0:T(8,128)(2,1)S(1)}, u32[]{:S(2)}, u32[]{:S(2)}) %collective-permute-start.41) | collective-permute-done | bytes 147488 | tf_op jit(solution)/shard_map/ppermute | solution.py:908
  157.6 3.3 %down_grad.1 = (f32[4,5,32,256]{3,2,1,0:T(8,128)S(1)}, bf16[4,5,32,256]{3,2,1,0:T(8,128)(2,1)S(1)}) custom-call(s32[4]{0:T(128)S(1)} %pad_add_fusion.refs_0_.refs_1_, bf16[8,128,1024]{2,1,0:T(8,128)(2,1)S(1)} %get-tuple-element.151.refs_1_, bf16[8,128,512]{2,1,0:T(8,128)(2,1)S(1)} %down_back.1.refs_2_.refs_1_, ...), custom_call_target="tpu_custom_call" | custom-call | flops 603979776 | bytes 4194320 | tf_op jit(solution)/shard_map/down_grad/pallas_call | solution.py:162
  162.4 1.5 collective-permute-start.52
  164.0 1.5 collective-permute-start.53
  165.4 1.9 collective-permute-done.44.refs_1_
  167.6 1.6 collective-permute-start.46
  169.2 7.9 %collective-permute-done.53.refs_8_.refs_0_.refs_2_ = bf16[2,9,32,256]{3,2,1,0:T(8,128)(2,1)S(1)} collective-permute-done((bf16[2,9,32,256]{3,2,1,0:T(8,128)(2,1)S(1)}, bf16[2,9,32,256]{3,2,1,0:T(8,128)(2,1)S(1)}, u32[]{:S(2)}, u32[]{:S(2)}) %collective-permute-start.53) | collective-permute-done | bytes 294944 | tf_op jit(solution)/shard_map/ppermute | solution.py:908
  177.1 1.5 collective-permute-start.54
  178.5 1.5 collective-permute-start.50
  180.1 1.5 image_back.1
  181.7 3.0 %second_out.1 = f32[9,512,256]{2,1,0:T(8,128)} custom-call(s32[4]{0:T(128)S(1)} %pad_add_fusion.refs_0_.refs_1_, bf16[2,9,32,256]{3,2,1,0:T(8,128)(2,1)S(1)} %second_grad_pair.1.refs_5_.refs_0_.refs_1_, bf16[2,9,32,256]{3,2,1,0:T(8,128)(2,1)S(1)} %collective-permute-done.36.refs_3_.refs_0_.refs_2_, ...), custom_call_target="tpu_custom_call" | custom-call | bytes 2359312 | tf_op jit(solution)/shard_map/second_out/pallas_call | solution.py:162
  184.8 2.3 copy-done.2
  187.2 1.8 collective-permute-done.49.refs_1_
  190.0 1.5 collective-permute-start.68
  191.5 2.4 collective-permute-start.48
  194.3 4.7 %collective-permute-done.69.refs_0_.refs_2_ = bf16[2,9,32,256]{3,2,1,0:T(8,128)(2,1)S(1)} collective-permute-done((bf16[2,9,32,256]{3,2,1,0:T(8,128)(2,1)S(1)}, bf16[2,9,32,256]{3,2,1,0:T(8,128)(2,1)S(1)}, u32[]{:S(2)}, u32[]{:S(2)}) %collective-permute-start.69) | collective-permute-done | bytes 294944 | tf_op jit(solution)/shard_map/ppermute | solution.py:908
  200.2 5.1 %collective-permute-done.62.refs_1_ = bf16[5,32,256]{2,1,0:T(8,128)(2,1)S(1)} collective-permute-done((bf16[5,32,256]{2,1,0:T(8,128)(2,1)S(1)}, bf16[5,32,256]{2,1,0:T(8,128)(2,1)S(1)}, u32[]{:S(2)}, u32[]{:S(2)}) %collective-permute-start.62) | collective-permute-done | bytes 81952 | tf_op jit(solution)/shard_map/ppermute | solution.py:908
  205.4 5.3 %collective-permute-done.63.refs_0_.refs_2_ = bf16[2,5,32,256]{3,2,1,0:T(8,128)(2,1)S(1)} collective-permute-done((bf16[2,5,32,256]{3,2,1,0:T(8,128)(2,1)S(1)}, bf16[2,5,32,256]{3,2,1,0:T(8,128)(2,1)S(1)}, u32[]{:S(2)}, u32[]{:S(2)}) %collective-permute-start.63) | collective-permute-done | bytes 163872 | tf_op jit(solution)/shard_map/ppermute | solution.py:908
  210.7 1.5 collective-permute-start.64
  212.3 1.7 collective-permute-start.58
  214.7 2.0 collective-permute-start.60
  218.4 3.0 %first_out.1 = f32[9,512,256]{2,1,0:T(8,128)} custom-call(s32[4]{0:T(128)S(1)} %pad_add_fusion.refs_0_.refs_1_, bf16[2,9,32,256]{3,2,1,0:T(8,128)(2,1)S(1)} %first_grad_pair.1.refs_2_.refs_0_.refs_1_, bf16[2,9,32,256]{3,2,1,0:T(8,128)(2,1)S(1)} %collective-permute-done.53.refs_8_.refs_0_.refs_2_, ...), custom_call_target="tpu_custom_call" | custom-call | bytes 2359312 | tf_op jit(solution)/shard_map/first_out/pallas_call | solution.py:162
  221.5 2.3 copy-done
  223.8 2.3 copy-done.1
  226.2 2.2 collective-permute-start.57
  229.4 1.5 collective-permute-start.74
  231.0 1.9 collective-permute-start.55
  242.6 2.0 image_grad.1
  246.9 2.9 %down_out.1 = (f32[9,256,256]{2,1,0:T(8,128)}, f32[256,256]{1,0:T(8,128)}) custom-call(s32[4]{0:T(128)S(1)} %pad_add_fusion.refs_0_.refs_1_, bf16[2,5,32,256]{3,2,1,0:T(8,128)(2,1)S(1)} %down_grad_pair.1.refs_7_.refs_0_.refs_1_, bf16[2,5,32,256]{3,2,1,0:T(8,128)(2,1)S(1)} %collective-permute-done.63.refs_0_.refs_2_, ...), custom_call_target="tpu_custom_call" | custom-call | bytes 1310736 | tf_op jit(solution)/shard_map/down_out/pallas_call | solution.py:162
  249.8 3.7 %mid_out.1 = f32[9,512,256]{2,1,0:T(8,128)} custom-call(s32[4]{0:T(128)S(1)} %pad_add_fusion.refs_0_.refs_1_, bf16[2,9,32,256]{3,2,1,0:T(8,128)(2,1)S(1)} %mid_grad_pair.1.refs_2_.refs_0_.refs_1_, bf16[2,9,32,256]{3,2,1,0:T(8,128)(2,1)S(1)} %collective-permute-done.69.refs_0_.refs_2_, bf16[2,9,32,256]{3,2,1,0:T(8,128)(2,1)S(1)} %collective-permute-done.66.refs_1_.refs_3_, ...), custom_call_target="tpu_custom_call" | custom-call | bytes 2359312 | tf_op jit(solution)/shard_map/mid_out/pallas_call | solution.py:162
  (226 shorter events, 48.9 us)
Async XLA Ops:
  4.1 14.0 %collective-permute-start.4 = (bf16[128,512]{1,0:T(8,128)(2,1)S(1)}, bf16[128,512]{1,0:T(8,128)(2,1)S(1)}, u32[]{:S(2)}, u32[]{:S(2)}) collective-permute-start(bf16[128,512]{1,0:T(8,128)(2,1)S(1)} %get-tuple-element.103), channel_id=1, source_target_pairs={{0,2},{1,3},{2,0},{3,1},{4,6},{5,7},{6,4},{7,5},{8,10},{9,11},{10,... | collective-permute-start | bytes 393224 | tf_op jit(solution)/shard_map/ppermute | solution.py:908
  8.2 10.0 %collective-permute-start.5 = (bf16[128,512]{1,0:T(8,128)(2,1)S(1)}, bf16[128,512]{1,0:T(8,128)(2,1)S(1)}, u32[]{:S(2)}, u32[]{:S(2)}) collective-permute-start(bf16[128,512]{1,0:T(8,128)(2,1)S(1)} %get-tuple-element.104), channel_id=1, source_target_pairs={{0,3},{1,2},{2,1},{3,0},{4,7},{5,6},{6,5},{7,4},{8,11},{9,10},{10,... | collective-permute-start | bytes 393224 | tf_op jit(solution)/shard_map/ppermute | solution.py:908
  9.5 16.4 %collective-permute-start.2 = (bf16[144,512]{1,0:T(8,128)(2,1)S(1)}, bf16[144,512]{1,0:T(8,128)(2,1)S(1)}, u32[]{:S(2)}, u32[]{:S(2)}) collective-permute-start(bf16[144,512]{1,0:T(8,128)(2,1)S(1)} %get-tuple-element.100.refs_1_.refs_2_), channel_id=1, source_target_pairs={{0,12},{4,8},{8,4},{12,0},{1,13},{5,9},{9,5},{13,1},{2,14},{6,10},... | collective-permute-start | bytes 442376 | tf_op jit(solution)/shard_map/ppermute | solution.py:908
  12.0 14.4 %collective-permute-start.1 = (bf16[144,512]{1,0:T(8,128)(2,1)S(1)}, bf16[144,512]{1,0:T(8,128)(2,1)S(1)}, u32[]{:S(2)}, u32[]{:S(2)}) collective-permute-start(bf16[144,512]{1,0:T(8,128)(2,1)S(1)} %get-tuple-element.100.refs_1_.refs_2_), channel_id=1, source_target_pairs={{0,8},{4,12},{8,0},{12,4},{1,9},{5,13},{9,1},{13,5},{2,10},{6,14},... | collective-permute-start | bytes 442376 | tf_op jit(solution)/shard_map/ppermute | solution.py:908
  12.5 14.1 %collective-permute-start = (bf16[144,512]{1,0:T(8,128)(2,1)S(1)}, bf16[144,512]{1,0:T(8,128)(2,1)S(1)}, u32[]{:S(2)}, u32[]{:S(2)}) collective-permute-start(bf16[144,512]{1,0:T(8,128)(2,1)S(1)} %get-tuple-element.100.refs_1_.refs_2_), channel_id=1, source_target_pairs={{0,4},{4,0},{8,12},{12,8},{1,5},{5,1},{9,13},{13,9},{2,6},{6,2},{1... | collective-permute-start | bytes 442376 | tf_op jit(solution)/shard_map/ppermute | solution.py:908
  18.1 5.0 %collective-permute-start.3 = (bf16[128,512]{1,0:T(8,128)(2,1)S(1)}, bf16[128,512]{1,0:T(8,128)(2,1)S(1)}, u32[]{:S(2)}, u32[]{:S(2)}) collective-permute-start(bf16[128,512]{1,0:T(8,128)(2,1)S(1)} %get-tuple-element.102), channel_id=1, source_target_pairs={{0,1},{1,0},{2,3},{3,2},{4,5},{5,4},{6,7},{7,6},{8,9},{9,8},{10,11... | collective-permute-start | bytes 393224 | tf_op jit(solution)/shard_map/ppermute | solution.py:908
  18.2 20.1 %collective-permute-start.11 = (bf16[256,512]{1,0:T(8,128)(2,1)S(1)}, bf16[256,512]{1,0:T(8,128)(2,1)S(1)}, u32[]{:S(2)}, u32[]{:S(2)}) collective-permute-start(bf16[256,512]{1,0:T(8,128)(2,1)S(1)} %constant_dynamic-update-slice_fusion.refs_4_), channel_id=1, source_target_pairs={{0,12},{4,8},{8,4},{12,0},{1,13},{5,9},{9,5},{13,1},{2,14},{6,10},... | collective-permute-start | bytes 786440 | tf_op jit(solution)/shard_map/ppermute | solution.py:908
  23.1 8.1 %collective-permute-start.10 = (bf16[128,512]{1,0:T(8,128)(2,1)S(1)}, bf16[128,512]{1,0:T(8,128)(2,1)S(1)}, u32[]{:S(2)}, u32[]{:S(2)}) collective-permute-start(bf16[128,512]{1,0:T(8,128)(2,1)S(1)} %collective-permute-done.3.refs_3_), channel_id=1, source_target_pairs={{0,12},{4,8},{8,4},{12,0},{1,13},{5,9},{9,5},{13,1},{2,14},{6,10},... | collective-permute-start | bytes 393224 | tf_op jit(solution)/shard_map/ppermute | solution.py:908
  25.9 12.4 %collective-permute-start.9 = (bf16[256,512]{1,0:T(8,128)(2,1)S(1)}, bf16[256,512]{1,0:T(8,128)(2,1)S(1)}, u32[]{:S(2)}, u32[]{:S(2)}) collective-permute-start(bf16[256,512]{1,0:T(8,128)(2,1)S(1)} %constant_dynamic-update-slice_fusion.refs_4_), channel_id=1, source_target_pairs={{0,8},{4,12},{8,0},{12,4},{1,9},{5,13},{9,1},{13,5},{2,10},{6,14},... | collective-permute-start | bytes 786440 | tf_op jit(solution)/shard_map/ppermute | solution.py:908
  26.4 11.9 %collective-permute-start.7 = (bf16[256,512]{1,0:T(8,128)(2,1)S(1)}, bf16[256,512]{1,0:T(8,128)(2,1)S(1)}, u32[]{:S(2)}, u32[]{:S(2)}) collective-permute-start(bf16[256,512]{1,0:T(8,128)(2,1)S(1)} %constant_dynamic-update-slice_fusion.refs_4_), channel_id=1, source_target_pairs={{0,4},{4,0},{8,12},{12,8},{1,5},{5,1},{9,13},{13,9},{2,6},{6,2},{1... | collective-permute-start | bytes 786440 | tf_op jit(solution)/shard_map/ppermute | solution.py:908
  26.6 11.6 %collective-permute-start.8 = (bf16[128,512]{1,0:T(8,128)(2,1)S(1)}, bf16[128,512]{1,0:T(8,128)(2,1)S(1)}, u32[]{:S(2)}, u32[]{:S(2)}) collective-permute-start(bf16[128,512]{1,0:T(8,128)(2,1)S(1)} %collective-permute-done.3.refs_3_), channel_id=1, source_target_pairs={{0,8},{4,12},{8,0},{12,4},{1,9},{5,13},{9,1},{13,5},{2,10},{6,14},... | collective-permute-start | bytes 393224 | tf_op jit(solution)/shard_map/ppermute | solution.py:908
  31.2 7.1 %collective-permute-start.6 = (bf16[128,512]{1,0:T(8,128)(2,1)S(1)}, bf16[128,512]{1,0:T(8,128)(2,1)S(1)}, u32[]{:S(2)}, u32[]{:S(2)}) collective-permute-start(bf16[128,512]{1,0:T(8,128)(2,1)S(1)} %collective-permute-done.3.refs_3_), channel_id=1, source_target_pairs={{0,4},{4,0},{8,12},{12,8},{1,5},{5,1},{9,13},{13,9},{2,6},{6,2},{1... | collective-permute-start | bytes 393224 | tf_op jit(solution)/shard_map/ppermute | solution.py:908
  75.5 5.6 %collective-permute-start.19 = (f32[40,40]{1,0:T(8,128)S(1)}, f32[40,40]{1,0:T(8,128)S(1)}, u32[]{:S(2)}, u32[]{:S(2)}) collective-permute-start(f32[40,40]{1,0:T(8,128)S(1)} %get-tuple-element.118.refs_3_), channel_id=1, source_target_pairs={{0,3},{1,2},{2,1},{3,0},{4,7},{5,6},{6,5},{7,4},{8,11},{9,10},{10,... | collective-permute-start | bytes 19208 | tf_op jit(solution)/shard_map/ppermute | solution.py:908
  78.7 4.8 %collective-permute-start.18 = (f32[40,40]{1,0:T(8,128)S(1)}, f32[40,40]{1,0:T(8,128)S(1)}, u32[]{:S(2)}, u32[]{:S(2)}) collective-permute-start(f32[40,40]{1,0:T(8,128)S(1)} %get-tuple-element.118.refs_3_), channel_id=1, source_target_pairs={{0,2},{1,3},{2,0},{3,1},{4,6},{5,7},{6,4},{7,5},{8,10},{9,11},{10,... | collective-permute-start | bytes 19208 | tf_op jit(solution)/shard_map/ppermute | solution.py:908
  80.6 3.8 %collective-permute-start.17 = (f32[40,40]{1,0:T(8,128)S(1)}, f32[40,40]{1,0:T(8,128)S(1)}, u32[]{:S(2)}, u32[]{:S(2)}) collective-permute-start(f32[40,40]{1,0:T(8,128)S(1)} %get-tuple-element.118.refs_3_), channel_id=1, source_target_pairs={{0,1},{1,0},{2,3},{3,2},{4,5},{5,4},{6,7},{7,6},{8,9},{9,8},{10,11... | collective-permute-start | bytes 19208 | tf_op jit(solution)/shard_map/ppermute | solution.py:908
  95.3 9.3 %collective-permute-start.25 = (bf16[2,9,32,256]{3,2,1,0:T(8,128)(2,1)S(1)}, bf16[2,9,32,256]{3,2,1,0:T(8,128)(2,1)S(1)}, u32[]{:S(2)}, u32[]{:S(2)}) collective-permute-start(bf16[2,9,32,256]{3,2,1,0:T(8,128)(2,1)S(1)} %get-tuple-element.137), channel_id=1, source_target_pairs={{0,1},{1,0},{2,3},{3,2},{4,5},{5,4},{6,7},{7,6},{8,9},{9,8},{10,11... | collective-permute-start | bytes 884744 | tf_op jit(solution)/shard_map/ppermute | solution.py:908
  103.9 2.4 collective-permute-start.24
  104.6 13.2 %collective-permute-start.27 = (bf16[9,32,256]{2,1,0:T(8,128)(2,1)S(1)}, bf16[9,32,256]{2,1,0:T(8,128)(2,1)S(1)}, u32[]{:S(2)}, u32[]{:S(2)}) collective-permute-start(bf16[9,32,256]{2,1,0:T(8,128)(2,1)S(1)} %get-tuple-element.143), channel_id=1, source_target_pairs={{0,2},{1,3},{2,0},{3,1},{4,6},{5,7},{6,4},{7,5},{8,10},{9,11},{10,... | collective-permute-start | bytes 442376 | tf_op jit(solution)/shard_map/ppermute | solution.py:908
  117.8 9.9 %collective-permute-start.32 = (bf16[9,32,256]{2,1,0:T(8,128)(2,1)S(1)}, bf16[9,32,256]{2,1,0:T(8,128)(2,1)S(1)}, u32[]{:S(2)}, u32[]{:S(2)}) collective-permute-start(bf16[9,32,256]{2,1,0:T(8,128)(2,1)S(1)} %second_grad_final.1.refs_3_.refs_0_), channel_id=1, source_target_pairs={{0,2},{1,3},{2,0},{3,1},{4,6},{5,7},{6,4},{7,5},{8,10},{9,11},{10,... | collective-permute-start | bytes 442376 | tf_op jit(solution)/shard_map/ppermute | solution.py:908
  123.0 4.7 %collective-permute-start.29 = (bf16[1,9,32,256]{3,2,1,0:T(8,128)(2,1)S(1)}, bf16[1,9,32,256]{3,2,1,0:T(8,128)(2,1)S(1)}, u32[]{:S(2)}, u32[]{:S(2)}) collective-permute-start(bf16[1,9,32,256]{3,2,1,0:T(8,128)(2,1)S(1)} %get-tuple-element.146), channel_id=1, source_target_pairs={{0,16},{16,0},{1,17},{17,1},{2,18},{18,2},{3,19},{19,3},{4,20},{20... | collective-permute-start | bytes 442376 | tf_op jit(solution)/shard_map/ppermute | solution.py:908
  123.1 4.7 %collective-permute-start.30 = (bf16[1,9,32,256]{3,2,1,0:T(8,128)(2,1)S(1)}, bf16[1,9,32,256]{3,2,1,0:T(8,128)(2,1)S(1)}, u32[]{:S(2)}, u32[]{:S(2)}) collective-permute-start(bf16[1,9,32,256]{3,2,1,0:T(8,128)(2,1)S(1)} %get-tuple-element.147), channel_id=1, source_target_pairs={{0,16},{16,0},{1,17},{17,1},{2,18},{18,2},{3,19},{19,3},{4,20},{20... | collective-permute-start | bytes 442376 | tf_op jit(solution)/shard_map/ppermute | solution.py:908
  123.6 5.8 %collective-permute-start.31 = (bf16[1,9,32,256]{3,2,1,0:T(8,128)(2,1)S(1)}, bf16[1,9,32,256]{3,2,1,0:T(8,128)(2,1)S(1)}, u32[]{:S(2)}, u32[]{:S(2)}) collective-permute-start(bf16[1,9,32,256]{3,2,1,0:T(8,128)(2,1)S(1)} %get-tuple-element.148), channel_id=1, source_target_pairs={{0,16},{16,0},{1,17},{17,1},{2,18},{18,2},{3,19},{19,3},{4,20},{20... | collective-permute-start | bytes 442376 | tf_op jit(solution)/shard_map/ppermute | solution.py:908
  123.7 5.7 %collective-permute-start.28 = (bf16[1,9,32,256]{3,2,1,0:T(8,128)(2,1)S(1)}, bf16[1,9,32,256]{3,2,1,0:T(8,128)(2,1)S(1)}, u32[]{:S(2)}, u32[]{:S(2)}) collective-permute-start(bf16[1,9,32,256]{3,2,1,0:T(8,128)(2,1)S(1)} %get-tuple-element.145.refs_2_), channel_id=1, source_target_pairs={{0,16},{16,0},{1,17},{17,1},{2,18},{18,2},{3,19},{19,3},{4,20},{20... | collective-permute-start | bytes 442376 | tf_op jit(solution)/shard_map/ppermute | solution.py:908
  127.7 3.8 %collective-permute-start.26 = (f32[8,512]{1,0:T(8,128)S(1)}, f32[8,512]{1,0:T(8,128)S(1)}, u32[]{:S(2)}, u32[]{:S(2)}) collective-permute-start(f32[8,512]{1,0:T(8,128)S(1)} %get-tuple-element.139.refs_2_.refs_5_), channel_id=1, source_target_pairs={{0,16},{16,0},{1,17},{17,1},{2,18},{18,2},{3,19},{19,3},{4,20},{20... | collective-permute-start | bytes 49160 | tf_op jit(solution)/shard_map/ppermute | solution.py:908
  127.8 15.8 %collective-permute-start.36 = (bf16[2,9,32,256]{3,2,1,0:T(8,128)(2,1)S(1)}, bf16[2,9,32,256]{3,2,1,0:T(8,128)(2,1)S(1)}, u32[]{:S(2)}, u32[]{:S(2)}) collective-permute-start(bf16[2,9,32,256]{3,2,1,0:T(8,128)(2,1)S(1)} %second_grad_pair.1.refs_5_.refs_0_.refs_1_), channel_id=1, source_target_pairs={{0,1},{1,0},{2,3},{3,2},{4,5},{5,4},{6,7},{7,6},{8,9},{9,8},{10,11... | collective-permute-start | bytes 884744 | tf_op jit(solution)/shard_map/ppermute | solution.py:908
  127.8 15.7 %collective-permute-start.34 = (bf16[2,9,32,256]{3,2,1,0:T(8,128)(2,1)S(1)}, bf16[2,9,32,256]{3,2,1,0:T(8,128)(2,1)S(1)}, u32[]{:S(2)}, u32[]{:S(2)}) collective-permute-start(bf16[2,9,32,256]{3,2,1,0:T(8,128)(2,1)S(1)} %second_grad_pair.1.refs_5_.refs_0_.refs_1_), channel_id=1, source_target_pairs={{0,4},{4,0},{8,12},{12,8},{1,5},{5,1},{9,13},{13,9},{2,6},{6,2},{1... | collective-permute-start | bytes 884744 | tf_op jit(solution)/shard_map/ppermute | solution.py:908
  129.5 14.0 %collective-permute-start.35 = (bf16[2,9,32,256]{3,2,1,0:T(8,128)(2,1)S(1)}, bf16[2,9,32,256]{3,2,1,0:T(8,128)(2,1)S(1)}, u32[]{:S(2)}, u32[]{:S(2)}) collective-permute-start(bf16[2,9,32,256]{3,2,1,0:T(8,128)(2,1)S(1)} %get-tuple-element.155), channel_id=1, source_target_pairs={{0,1},{1,0},{2,3},{3,2},{4,5},{5,4},{6,7},{7,6},{8,9},{9,8},{10,11... | collective-permute-start | bytes 884744 | tf_op jit(solution)/shard_map/ppermute | solution.py:908
  143.6 9.5 %collective-permute-start.41 = (bf16[9,32,256]{2,1,0:T(8,128)(2,1)S(1)}, bf16[9,32,256]{2,1,0:T(8,128)(2,1)S(1)}, u32[]{:S(2)}, u32[]{:S(2)}) collective-permute-start(bf16[9,32,256]{2,1,0:T(8,128)(2,1)S(1)} %get-tuple-element.162), channel_id=1, source_target_pairs={{0,2},{1,3},{2,0},{3,1},{4,6},{5,7},{6,4},{7,5},{8,10},{9,11},{10,... | collective-permute-start | bytes 442376 | tf_op jit(solution)/shard_map/ppermute | solution.py:908
  143.8 11.6 %collective-permute-start.42 = (bf16[2,9,32,256]{3,2,1,0:T(8,128)(2,1)S(1)}, bf16[2,9,32,256]{3,2,1,0:T(8,128)(2,1)S(1)}, u32[]{:S(2)}, u32[]{:S(2)}) collective-permute-start(bf16[2,9,32,256]{3,2,1,0:T(8,128)(2,1)S(1)} %collective-permute-done.36.refs_3_.refs_0_.refs_2_), channel_id=1, source_target_pairs={{0,8},{4,12},{8,0},{12,4},{1,9},{5,13},{9,1},{13,5},{2,10},{6,14},... | collective-permute-start | bytes 884744 | tf_op jit(solution)/shard_map/ppermute | solution.py:908
  149.1 4.1 %collective-permute-start.38 = (bf16[1,9,32,256]{3,2,1,0:T(8,128)(2,1)S(1)}, bf16[1,9,32,256]{3,2,1,0:T(8,128)(2,1)S(1)}, u32[]{:S(2)}, u32[]{:S(2)}) collective-permute-start(bf16[1,9,32,256]{3,2,1,0:T(8,128)(2,1)S(1)} %get-tuple-element.159), channel_id=1, source_target_pairs={{0,16},{16,0},{1,17},{17,1},{2,18},{18,2},{3,19},{19,3},{4,20},{20... | collective-permute-start | bytes 442376 | tf_op jit(solution)/shard_map/ppermute | solution.py:908
  149.2 4.2 %collective-permute-start.39 = (bf16[1,9,32,256]{3,2,1,0:T(8,128)(2,1)S(1)}, bf16[1,9,32,256]{3,2,1,0:T(8,128)(2,1)S(1)}, u32[]{:S(2)}, u32[]{:S(2)}) collective-permute-start(bf16[1,9,32,256]{3,2,1,0:T(8,128)(2,1)S(1)} %get-tuple-element.160), channel_id=1, source_target_pairs={{0,16},{16,0},{1,17},{17,1},{2,18},{18,2},{3,19},{19,3},{4,20},{20... | collective-permute-start | bytes 442376 | tf_op jit(solution)/shard_map/ppermute | solution.py:908
  149.7 3.7 %collective-permute-start.40 = (bf16[1,9,32,256]{3,2,1,0:T(8,128)(2,1)S(1)}, bf16[1,9,32,256]{3,2,1,0:T(8,128)(2,1)S(1)}, u32[]{:S(2)}, u32[]{:S(2)}) collective-permute-start(bf16[1,9,32,256]{3,2,1,0:T(8,128)(2,1)S(1)} %get-tuple-element.161), channel_id=1, source_target_pairs={{0,16},{16,0},{1,17},{17,1},{2,18},{18,2},{3,19},{19,3},{4,20},{20... | collective-permute-start | bytes 442376 | tf_op jit(solution)/shard_map/ppermute | solution.py:908
  153.2 10.7 %collective-permute-start.45 = (bf16[9,32,256]{2,1,0:T(8,128)(2,1)S(1)}, bf16[9,32,256]{2,1,0:T(8,128)(2,1)S(1)}, u32[]{:S(2)}, u32[]{:S(2)}) collective-permute-start(bf16[9,32,256]{2,1,0:T(8,128)(2,1)S(1)} %first_grad_final.1.refs_5_.refs_0_), channel_id=1, source_target_pairs={{0,2},{1,3},{2,0},{3,1},{4,6},{5,7},{6,4},{7,5},{8,10},{9,11},{10,... | collective-permute-start | bytes 442376 | tf_op jit(solution)/shard_map/ppermute | solution.py:908
  154.7 12.7 %collective-permute-start.44 = (bf16[2,9,32,256]{3,2,1,0:T(8,128)(2,1)S(1)}, bf16[2,9,32,256]{3,2,1,0:T(8,128)(2,1)S(1)}, u32[]{:S(2)}, u32[]{:S(2)}) collective-permute-start(bf16[2,9,32,256]{3,2,1,0:T(8,128)(2,1)S(1)} %get-tuple-element.167), channel_id=1, source_target_pairs={{0,1},{1,0},{2,3},{3,2},{4,5},{5,4},{6,7},{7,6},{8,9},{9,8},{10,11... | collective-permute-start | bytes 884744 | tf_op jit(solution)/shard_map/ppermute | solution.py:908
  161.0 6.6 %collective-permute-start.43 = (bf16[4,5,32,256]{3,2,1,0:T(8,128)(2,1)S(1)}, bf16[4,5,32,256]{3,2,1,0:T(8,128)(2,1)S(1)}, u32[]{:S(2)}, u32[]{:S(2)}) collective-permute-start(bf16[4,5,32,256]{3,2,1,0:T(8,128)(2,1)S(1)} %get-tuple-element.166.refs_2_), channel_id=1, source_target_pairs={{0,16},{16,0},{1,17},{17,1},{2,18},{18,2},{3,19},{19,3},{4,20},{20... | collective-permute-start | bytes 983048 | tf_op jit(solution)/shard_map/ppermute | solution.py:908
  161.2 20.6 %collective-permute-start.51 = (bf16[4,9,32,256]{3,2,1,0:T(8,128)(2,1)S(1)}, bf16[4,9,32,256]{3,2,1,0:T(8,128)(2,1)S(1)}, u32[]{:S(2)}, u32[]{:S(2)}) collective-permute-start(bf16[4,9,32,256]{3,2,1,0:T(8,128)(2,1)S(1)} %second_grad_cross.2.refs_7_), channel_id=1, source_target_pairs={{0,8},{4,12},{8,0},{12,4},{1,9},{5,13},{9,1},{13,5},{2,10},{6,14},... | collective-permute-start | bytes 1769480 | tf_op jit(solution)/shard_map/ppermute | solution.py:908
  162.4 19.3 %collective-permute-start.52 = (bf16[4,9,32,256]{3,2,1,0:T(8,128)(2,1)S(1)}, bf16[4,9,32,256]{3,2,1,0:T(8,128)(2,1)S(1)}, u32[]{:S(2)}, u32[]{:S(2)}) collective-permute-start(bf16[4,9,32,256]{3,2,1,0:T(8,128)(2,1)S(1)} %second_grad_cross.3.refs_8_), channel_id=1, source_target_pairs={{0,4},{4,0},{8,12},{12,8},{1,5},{5,1},{9,13},{13,9},{2,6},{6,2},{1... | collective-permute-start | bytes 1769480 | tf_op jit(solution)/shard_map/ppermute | solution.py:908
  164.0 13.1 %collective-permute-start.53 = (bf16[2,9,32,256]{3,2,1,0:T(8,128)(2,1)S(1)}, bf16[2,9,32,256]{3,2,1,0:T(8,128)(2,1)S(1)}, u32[]{:S(2)}, u32[]{:S(2)}) collective-permute-start(bf16[2,9,32,256]{3,2,1,0:T(8,128)(2,1)S(1)} %first_grad_pair.1.refs_2_.refs_0_.refs_1_), channel_id=1, source_target_pairs={{0,1},{1,0},{2,3},{3,2},{4,5},{5,4},{6,7},{7,6},{8,9},{9,8},{10,11... | collective-permute-start | bytes 884744 | tf_op jit(solution)/shard_map/ppermute | solution.py:908
  167.5 11.1 %collective-permute-start.47 = (bf16[9,32,256]{2,1,0:T(8,128)(2,1)S(1)}, bf16[9,32,256]{2,1,0:T(8,128)(2,1)S(1)}, u32[]{:S(2)}, u32[]{:S(2)}) collective-permute-start(bf16[9,32,256]{2,1,0:T(8,128)(2,1)S(1)} %get-tuple-element.171), channel_id=1, source_target_pairs={{0,2},{1,3},{2,0},{3,1},{4,6},{5,7},{6,4},{7,5},{8,10},{9,11},{10,... | collective-permute-start | bytes 442376 | tf_op jit(solution)/shard_map/ppermute | solution.py:908
  167.6 14.0 %collective-permute-start.46 = (bf16[2,5,32,256]{3,2,1,0:T(8,128)(2,1)S(1)}, bf16[2,5,32,256]{3,2,1,0:T(8,128)(2,1)S(1)}, u32[]{:S(2)}, u32[]{:S(2)}) collective-permute-start(bf16[2,5,32,256]{3,2,1,0:T(8,128)(2,1)S(1)} %get-tuple-element.170), channel_id=1, source_target_pairs={{0,1},{1,0},{2,3},{3,2},{4,5},{5,4},{6,7},{7,6},{8,9},{9,8},{10,11... | collective-permute-start | bytes 491528 | tf_op jit(solution)/shard_map/ppermute | solution.py:908
  177.1 7.7 %collective-permute-start.54 = (bf16[2,9,32,256]{3,2,1,0:T(8,128)(2,1)S(1)}, bf16[2,9,32,256]{3,2,1,0:T(8,128)(2,1)S(1)}, u32[]{:S(2)}, u32[]{:S(2)}) collective-permute-start(bf16[2,9,32,256]{3,2,1,0:T(8,128)(2,1)S(1)} %collective-permute-done.53.refs_8_.refs_0_.refs_2_), channel_id=1, source_target_pairs={{0,8},{4,12},{8,0},{12,4},{1,9},{5,13},{9,1},{13,5},{2,10},{6,14},... | collective-permute-start | bytes 884744 | tf_op jit(solution)/shard_map/ppermute | solution.py:908
  178.5 8.6 %collective-permute-start.50 = (bf16[2,9,32,256]{3,2,1,0:T(8,128)(2,1)S(1)}, bf16[2,9,32,256]{3,2,1,0:T(8,128)(2,1)S(1)}, u32[]{:S(2)}, u32[]{:S(2)}) collective-permute-start(bf16[2,9,32,256]{3,2,1,0:T(8,128)(2,1)S(1)} %first_grad_pair.1.refs_2_.refs_0_.refs_1_), channel_id=1, source_target_pairs={{0,4},{4,0},{8,12},{12,8},{1,5},{5,1},{9,13},{13,9},{2,6},{6,2},{1... | collective-permute-start | bytes 884744 | tf_op jit(solution)/shard_map/ppermute | solution.py:908
  181.6 7.4 %collective-permute-start.49 = (bf16[9,32,256]{2,1,0:T(8,128)(2,1)S(1)}, bf16[9,32,256]{2,1,0:T(8,128)(2,1)S(1)}, u32[]{:S(2)}, u32[]{:S(2)}) collective-permute-start(bf16[9,32,256]{2,1,0:T(8,128)(2,1)S(1)} %mid_grad_final.1.refs_2_.refs_0_), channel_id=1, source_target_pairs={{0,2},{1,3},{2,0},{3,1},{4,6},{5,7},{6,4},{7,5},{8,10},{9,11},{10,... | collective-permute-start | bytes 442376 | tf_op jit(solution)/shard_map/ppermute | solution.py:908
  189.0 10.0 %collective-permute-start.69 = (bf16[2,9,32,256]{3,2,1,0:T(8,128)(2,1)S(1)}, bf16[2,9,32,256]{3,2,1,0:T(8,128)(2,1)S(1)}, u32[]{:S(2)}, u32[]{:S(2)}) collective-permute-start(bf16[2,9,32,256]{3,2,1,0:T(8,128)(2,1)S(1)} %mid_grad_pair.1.refs_2_.refs_0_.refs_1_), channel_id=1, source_target_pairs={{0,1},{1,0},{2,3},{3,2},{4,5},{5,4},{6,7},{7,6},{8,9},{9,8},{10,11... | collective-permute-start | bytes 884744 | tf_op jit(solution)/shard_map/ppermute | solution.py:908
  189.1 25.6 %collective-permute-start.67 = (bf16[4,9,32,256]{3,2,1,0:T(8,128)(2,1)S(1)}, bf16[4,9,32,256]{3,2,1,0:T(8,128)(2,1)S(1)}, u32[]{:S(2)}, u32[]{:S(2)}) collective-permute-start(bf16[4,9,32,256]{3,2,1,0:T(8,128)(2,1)S(1)} %first_grad_cross.2.refs_2_), channel_id=1, source_target_pairs={{0,8},{4,12},{8,0},{12,4},{1,9},{5,13},{9,1},{13,5},{2,10},{6,14},... | collective-permute-start | bytes 1769480 | tf_op jit(solution)/shard_map/ppermute | solution.py:908
  190.0 26.6 %collective-permute-start.68 = (bf16[4,9,32,256]{3,2,1,0:T(8,128)(2,1)S(1)}, bf16[4,9,32,256]{3,2,1,0:T(8,128)(2,1)S(1)}, u32[]{:S(2)}, u32[]{:S(2)}) collective-permute-start(bf16[4,9,32,256]{3,2,1,0:T(8,128)(2,1)S(1)} %first_grad_cross.3.refs_3_), channel_id=1, source_target_pairs={{0,4},{4,0},{8,12},{12,8},{1,5},{5,1},{9,13},{13,9},{2,6},{6,2},{1... | collective-permute-start | bytes 1769480 | tf_op jit(solution)/shard_map/ppermute | solution.py:908
  191.5 8.4 %collective-permute-start.48 = (bf16[5,32,256]{2,1,0:T(8,128)(2,1)S(1)}, bf16[5,32,256]{2,1,0:T(8,128)(2,1)S(1)}, u32[]{:S(2)}, u32[]{:S(2)}) collective-permute-start(bf16[5,32,256]{2,1,0:T(8,128)(2,1)S(1)} %get-tuple-element.174), channel_id=1, source_target_pairs={{0,2},{1,3},{2,0},{3,1},{4,6},{5,7},{6,4},{7,5},{8,10},{9,11},{10,... | collective-permute-start | bytes 245768 | tf_op jit(solution)/shard_map/ppermute | solution.py:908
  193.9 18.4 %collective-permute-start.66 = (bf16[2,9,32,256]{3,2,1,0:T(8,128)(2,1)S(1)}, bf16[2,9,32,256]{3,2,1,0:T(8,128)(2,1)S(1)}, u32[]{:S(2)}, u32[]{:S(2)}) collective-permute-start(bf16[2,9,32,256]{3,2,1,0:T(8,128)(2,1)S(1)} %mid_grad_pair.1.refs_2_.refs_0_.refs_1_), channel_id=1, source_target_pairs={{0,4},{4,0},{8,12},{12,8},{1,5},{5,1},{9,13},{13,9},{2,6},{6,2},{1... | collective-permute-start | bytes 884744 | tf_op jit(solution)/shard_map/ppermute | solution.py:908
  199.0 15.0 %collective-permute-start.70 = (bf16[2,9,32,256]{3,2,1,0:T(8,128)(2,1)S(1)}, bf16[2,9,32,256]{3,2,1,0:T(8,128)(2,1)S(1)}, u32[]{:S(2)}, u32[]{:S(2)}) collective-permute-start(bf16[2,9,32,256]{3,2,1,0:T(8,128)(2,1)S(1)} %collective-permute-done.69.refs_0_.refs_2_), channel_id=1, source_target_pairs={{0,8},{4,12},{8,0},{12,4},{1,9},{5,13},{9,1},{13,5},{2,10},{6,14},... | collective-permute-start | bytes 884744 | tf_op jit(solution)/shard_map/ppermute | solution.py:908
  199.9 5.4 %collective-permute-start.62 = (bf16[5,32,256]{2,1,0:T(8,128)(2,1)S(1)}, bf16[5,32,256]{2,1,0:T(8,128)(2,1)S(1)}, u32[]{:S(2)}, u32[]{:S(2)}) collective-permute-start(bf16[5,32,256]{2,1,0:T(8,128)(2,1)S(1)} %down_grad_final.1.refs_9_.refs_0_), channel_id=1, source_target_pairs={{0,2},{1,3},{2,0},{3,1},{4,6},{5,7},{6,4},{7,5},{8,10},{9,11},{10,... | collective-permute-start | bytes 245768 | tf_op jit(solution)/shard_map/ppermute | solution.py:908
  205.4 5.4 %collective-permute-start.63 = (bf16[2,5,32,256]{3,2,1,0:T(8,128)(2,1)S(1)}, bf16[2,5,32,256]{3,2,1,0:T(8,128)(2,1)S(1)}, u32[]{:S(2)}, u32[]{:S(2)}) collective-permute-start(bf16[2,5,32,256]{3,2,1,0:T(8,128)(2,1)S(1)} %down_grad_pair.1.refs_7_.refs_0_.refs_1_), channel_id=1, source_target_pairs={{0,1},{1,0},{2,3},{3,2},{4,5},{5,4},{6,7},{7,6},{8,9},{9,8},{10,11... | collective-permute-start | bytes 491528 | tf_op jit(solution)/shard_map/ppermute | solution.py:908
  210.7 18.6 %collective-permute-start.64 = (bf16[2,5,32,256]{3,2,1,0:T(8,128)(2,1)S(1)}, bf16[2,5,32,256]{3,2,1,0:T(8,128)(2,1)S(1)}, u32[]{:S(2)}, u32[]{:S(2)}) collective-permute-start(bf16[2,5,32,256]{3,2,1,0:T(8,128)(2,1)S(1)} %down_grad_pair.1.refs_7_.refs_0_.refs_1_), channel_id=1, source_target_pairs={{0,4},{4,0},{8,12},{12,8},{1,5},{5,1},{9,13},{13,9},{2,6},{6,2},{1... | collective-permute-start | bytes 491528 | tf_op jit(solution)/shard_map/ppermute | solution.py:908
  212.3 13.9 %collective-permute-start.58 = (bf16[2,2,2,32,256]{4,3,2,1,0:T(8,128)(2,1)S(1)}, bf16[2,2,2,32,256]{4,3,2,1,0:T(8,128)(2,1)S(1)}, u32[]{:S(2)}, u32[]{:S(2)}) collective-permute-start(bf16[2,2,2,32,256]{4,3,2,1,0:T(8,128)(2,1)S(1)} %get-tuple-element.176), channel_id=1, source_target_pairs={{0,1},{1,0},{2,3},{3,2},{4,5},{5,4},{6,7},{7,6},{8,9},{9,8},{10,11... | collective-permute-start | bytes 393224 | tf_op jit(solution)/shard_map/ppermute | solution.py:908
  214.0 14.4 %collective-permute-start.59 = (bf16[2,2,2,32,256]{4,3,2,1,0:T(8,128)(2,1)S(1)}, bf16[2,2,2,32,256]{4,3,2,1,0:T(8,128)(2,1)S(1)}, u32[]{:S(2)}, u32[]{:S(2)}) collective-permute-start(bf16[2,2,2,32,256]{4,3,2,1,0:T(8,128)(2,1)S(1)} %get-tuple-element.177), channel_id=1, source_target_pairs={{0,2},{1,3},{2,0},{3,1},{4,6},{5,7},{6,4},{7,5},{8,10},{9,11},{10,... | collective-permute-start | bytes 393224 | tf_op jit(solution)/shard_map/ppermute | solution.py:908
  214.7 13.8 %collective-permute-start.60 = (bf16[2,2,2,32,256]{4,3,2,1,0:T(8,128)(2,1)S(1)}, bf16[2,2,2,32,256]{4,3,2,1,0:T(8,128)(2,1)S(1)}, u32[]{:S(2)}, u32[]{:S(2)}) collective-permute-start(bf16[2,2,2,32,256]{4,3,2,1,0:T(8,128)(2,1)S(1)} %get-tuple-element.178), channel_id=1, source_target_pairs={{0,3},{1,2},{2,1},{3,0},{4,7},{5,6},{6,5},{7,4},{8,11},{9,10},{10,... | collective-permute-start | bytes 393224 | tf_op jit(solution)/shard_map/ppermute | solution.py:908
  216.7 14.4 %collective-permute-start.65 = (bf16[2,5,32,256]{3,2,1,0:T(8,128)(2,1)S(1)}, bf16[2,5,32,256]{3,2,1,0:T(8,128)(2,1)S(1)}, u32[]{:S(2)}, u32[]{:S(2)}) collective-permute-start(bf16[2,5,32,256]{3,2,1,0:T(8,128)(2,1)S(1)} %collective-permute-done.63.refs_0_.refs_2_), channel_id=1, source_target_pairs={{0,8},{4,12},{8,0},{12,4},{1,9},{5,13},{9,1},{13,5},{2,10},{6,14},... | collective-permute-start | bytes 491528 | tf_op jit(solution)/shard_map/ppermute | solution.py:908
  226.2 7.5 %collective-permute-start.57 = (f32[64,256]{1,0:T(8,128)S(1)}, f32[64,256]{1,0:T(8,128)S(1)}, u32[]{:S(2)}, u32[]{:S(2)}) collective-permute-start(f32[64,256]{1,0:T(8,128)S(1)} %small.1.refs_1_), channel_id=1, source_target_pairs={{0,3},{1,2},{2,1},{3,0},{4,7},{5,6},{6,5},{7,4},{8,11},{9,10},{10,... | collective-permute-start | bytes 196616 | tf_op jit(solution)/shard_map/ppermute | solution.py:908
  228.4 6.7 %collective-permute-start.56 = (f32[64,256]{1,0:T(8,128)S(1)}, f32[64,256]{1,0:T(8,128)S(1)}, u32[]{:S(2)}, u32[]{:S(2)}) collective-permute-start(f32[64,256]{1,0:T(8,128)S(1)} %small.1.refs_1_), channel_id=1, source_target_pairs={{0,2},{1,3},{2,0},{3,1},{4,6},{5,7},{6,4},{7,5},{8,10},{9,11},{10,... | collective-permute-start | bytes 196616 | tf_op jit(solution)/shard_map/ppermute | solution.py:908
  228.5 21.3 %collective-permute-start.73 = (bf16[4,9,32,256]{3,2,1,0:T(8,128)(2,1)S(1)}, bf16[4,9,32,256]{3,2,1,0:T(8,128)(2,1)}, u32[]{:S(2)}, u32[]{:S(2)}) collective-permute-start(bf16[4,9,32,256]{3,2,1,0:T(8,128)(2,1)S(1)} %mid_grad_cross.2.refs_2_), channel_id=1, source_target_pairs={{0,8},{4,12},{8,0},{12,4},{1,9},{5,13},{9,1},{13,5},{2,10},{6,14},... | collective-permute-start | bytes 1769480 | tf_op jit(solution)/shard_map/ppermute | solution.py:908
  229.4 20.4 %collective-permute-start.74 = (bf16[4,9,32,256]{3,2,1,0:T(8,128)(2,1)S(1)}, bf16[4,9,32,256]{3,2,1,0:T(8,128)(2,1)}, u32[]{:S(2)}, u32[]{:S(2)}) collective-permute-start(bf16[4,9,32,256]{3,2,1,0:T(8,128)(2,1)S(1)} %mid_grad_cross.3.refs_3_), channel_id=1, source_target_pairs={{0,4},{4,0},{8,12},{12,8},{1,5},{5,1},{9,13},{13,9},{2,6},{6,2},{1... | collective-permute-start | bytes 1769480 | tf_op jit(solution)/shard_map/ppermute | solution.py:908
  231.0 6.1 %collective-permute-start.55 = (f32[64,256]{1,0:T(8,128)S(1)}, f32[64,256]{1,0:T(8,128)S(1)}, u32[]{:S(2)}, u32[]{:S(2)}) collective-permute-start(f32[64,256]{1,0:T(8,128)S(1)} %small.1.refs_1_), channel_id=1, source_target_pairs={{0,1},{1,0},{2,3},{3,2},{4,5},{5,4},{6,7},{7,6},{8,9},{9,8},{10,11... | collective-permute-start | bytes 196616 | tf_op jit(solution)/shard_map/ppermute | solution.py:908
  234.3 11.7 %collective-permute-start.72 = (bf16[4,5,32,256]{3,2,1,0:T(8,128)(2,1)}, bf16[4,5,32,256]{3,2,1,0:T(8,128)(2,1)}, u32[]{:S(2)}, u32[]{:S(2)}) collective-permute-start(bf16[4,5,32,256]{3,2,1,0:T(8,128)(2,1)} %down_grad_cross.3), channel_id=1, source_target_pairs={{0,4},{4,0},{8,12},{12,8},{1,5},{5,1},{9,13},{13,9},{2,6},{6,2},{1... | collective-permute-start | bytes 983048 | tf_op jit(solution)/shard_map/ppermute | solution.py:908
  235.1 10.9 %collective-permute-start.71 = (bf16[4,5,32,256]{3,2,1,0:T(8,128)(2,1)S(1)}, bf16[4,5,32,256]{3,2,1,0:T(8,128)(2,1)}, u32[]{:S(2)}, u32[]{:S(2)}) collective-permute-start(bf16[4,5,32,256]{3,2,1,0:T(8,128)(2,1)S(1)} %down_grad_cross.2.refs_7_), channel_id=1, source_target_pairs={{0,8},{4,12},{8,0},{12,4},{1,9},{5,13},{9,1},{13,5},{2,10},{6,14},... | collective-permute-start | bytes 983048 | tf_op jit(solution)/shard_map/ppermute | solution.py:908
  237.7 4.9 %collective-permute-start.61 = (bf16[4,2,2,32,256]{4,3,2,1,0:T(8,128)(2,1)}, bf16[4,2,2,32,256]{4,3,2,1,0:T(8,128)(2,1)}, u32[]{:S(2)}, u32[]{:S(2)}) collective-permute-start(bf16[4,2,2,32,256]{4,3,2,1,0:T(8,128)(2,1)} %get-tuple-element.187), channel_id=1, source_target_pairs={{0,16},{16,0},{1,17},{17,1},{2,18},{18,2},{3,19},{19,3},{4,20},{20... | collective-permute-start | bytes 786440 | tf_op jit(solution)/shard_map/ppermute | solution.py:908
  (51 other events, 334.4 us)
